TPU v7x, 32 devices: a whole 2x2x4 slice. The times are simulated.
32 devices in a mesh: head: 4 (over y, x), tok: 8 (over z, core).
Axes of the slice: x: 2, y: 2, z: 4, core: 2. Of those that a mesh axis runs over, the one named last changes fastest.
Arguments:
- stretch_tokens: bfloat16 [8, 1024, 1792], P('tok', 'head'), may hold values from -6 to 6
- stretch_tail: bfloat16 [8, 2, 1792], P('tok'), may hold values from -6 to 6
- decode_tokens: bfloat16 [8, 32, 1792], P('tok'), may hold values from -6 to 6
- decode_tail: bfloat16 [8, 32, 2, 1792], P('tok'), may hold values from -6 to 6
- norm_gain: float32 [1792], replicated, may hold values from 0.1 to 1.9
- conv_taps: float32 [3, 1792], replicated, may hold values from -3 to 3
- qkv_weight: bfloat16 [1792, 16, 144], P(None, 'head'), may hold values from -0.125 to 0.125
- out_gain: float32 [1792], P('head'), may hold values from 0.1 to 1.9
- out_weight: bfloat16 [1792, 1792], P('head'), may hold values from -0.125 to 0.125
- state_cache: float32 [8, 16, 16, 112, 273], P('tok', None, 'head'), may hold values from -24 to 24
- stretch_len: int32 [8], P('tok'), may hold values from 1 to 1024, 4096 in all
- stretch_slot: int32 [8], P('tok'), may hold values from 0 to 15
- decode_slot: int32 [8, 32], P('tok'), may hold values from 0 to 15
- decode_owner: int32 [8, 32, 1], P('tok'), may hold values from 0 to 7; in each aligned block of 32 rows (0 to 31, 32 to 63, ..., all dimensions but the last counted through in order) at most 8 rows name the same one
Outputs:
- stretch_out: bfloat16 [8, 1024, 1792], P('tok', 'head')
- decode_out: bfloat16 [8, 32, 1792], P('tok', 'head')
- state_new: float32 [8, 16, 112, 273], P('tok', 'head')
Inputs may be any that keep to these rules, and one draw needn't show every extreme that they name: `decode_owner`: in the 32 decoders of one group at most 8 name the same owner group, a bound that some block reaches of them. `stretch_len`: some group's stretch is full.
All inputs are finite; a program needn't handle non-finite values.
Results may differ from a plain program's by a relative error of at most 0.014.
Values may be sent and summed in bfloat16 or wider, within the bound.
No kernel may reach another device: no remote copies, remote signals or barrier semaphores. Data moves between devices by JAX's collectives and lax.ppermute only.
A program may use at most 64 MiB of HBM per device.

v0:
```python
import math

import jax
import jax.numpy as jnp
from jax import lax
from jax.sharding import PartitionSpec as P

D = 1792
DH = 112
F = 16
STRETCH = 1024
DEC = 32


def from_behind(array, axis, by):
    peers = lax.axis_size(axis)
    pairs = [(i, i + by) for i in range(peers) if 0 <= i + by < peers]
    return lax.ppermute(array, axis, pairs)


def rms_rows(values, gain):
    values = values.astype(jnp.float32)
    factor = lax.rsqrt(jnp.mean(values * values, axis=-1, keepdims=True) + 1e-05)
    return values * factor * gain


def features(vectors):
    breadth = vectors.shape[-1]
    linear = vectors / math.sqrt(math.sqrt(breadth))
    outer = vectors[..., :, None] * vectors[..., None, :] / math.sqrt(2.0 * breadth)
    outer = outer.reshape(vectors.shape[:-1] + (breadth * breadth,))
    ones = jnp.ones(vectors.shape[:-1] + (1,), vectors.dtype)
    return jnp.concatenate([ones, linear, outer], axis=-1)


def convolve(tail, normed, conv_taps):
    joined = jnp.concatenate([tail, normed], axis=-2).astype(jnp.float32)
    span_rows = normed.shape[-2]
    total = conv_taps[0] * joined[..., 0:span_rows, :]
    total = total + conv_taps[1] * joined[..., 1 : span_rows + 1, :]
    total = total + conv_taps[2] * joined[..., 2 : span_rows + 2, :]
    return total.astype(jnp.bfloat16)


def decode_items(items, slot_items, cache_own, out_gain, head_count):
    item_count = items.shape[0]
    shaped = items.reshape(item_count, head_count, 2 * F + DH).astype(jnp.float32)
    queries = shaped[:, :, :F]
    key_feats = shaped[:, :, F : 2 * F]
    values = shaped[:, :, 2 * F :]
    slot_total = cache_own.shape[0]
    table = jnp.einsum(
        "nhp,shdp->nshd", features(queries), cache_own, precision=lax.Precision.HIGHEST
    )
    picker = (slot_items[:, None] == jnp.arange(slot_total)[None, :]).astype(jnp.float32)
    carried = jnp.einsum("ns,nshd->nhd", picker, table, precision=lax.Precision.HIGHEST)
    inner = jnp.sum(queries * key_feats, axis=-1) / math.sqrt(F)
    own_term = (1.0 + inner + 0.5 * inner * inner)[..., None] * values
    attended = rms_rows(carried + own_term, out_gain.reshape(head_count, DH))
    return attended.astype(jnp.bfloat16).reshape(item_count, head_count * DH)


def local(
    stretch_tokens,
    stretch_tail,
    decode_tokens,
    decode_tail,
    norm_gain,
    conv_taps,
    qkv_weight,
    out_gain,
    out_weight,
    state_cache,
    stretch_len,
    stretch_slot,
    decode_slot,
    decode_owner,
):
    head_count = qkv_weight.shape[1]
    block_width = qkv_weight.shape[2]
    rows_own = stretch_tokens.shape[1]
    w_flat = qkv_weight.reshape(D, head_count * block_width)
    gains = out_gain.reshape(head_count, DH)
    normed = rms_rows(stretch_tokens[0], norm_gain).astype(jnp.bfloat16)
    rim_rows = from_behind(normed[rows_own - 2 :], "head", 1)
    first_dev = lax.axis_index("head") == 0
    rim_rows = jnp.where(first_dev, stretch_tail[0], rim_rows)
    conved = convolve(rim_rows, normed, conv_taps)
    grouped = jnp.dot(
        lax.all_gather(conved, "head", axis=0, tiled=True),
        w_flat,
        preferred_element_type=jnp.float32,
    ).astype(jnp.bfloat16)
    grouped = grouped.reshape(STRETCH, head_count, block_width)
    queries = grouped[:, :, :F]
    key_feats = grouped[:, :, F : 2 * F]
    values = grouped[:, :, 2 * F :]
    length = stretch_len[0]
    positions = jnp.arange(STRETCH)
    valid_rows = positions < length
    state_old = lax.dynamic_index_in_dim(state_cache[0], stretch_slot[0], 0, keepdims=False)
    carried = jnp.einsum(
        "ihp,hdp->ihd",
        features(queries.astype(jnp.float32)),
        state_old,
        precision=lax.Precision.HIGHEST,
    )
    block_rows = min(512, STRETCH)
    pieces = []
    for anchor in range(0, STRETCH, block_rows):
        finish = anchor + block_rows
        inner = jnp.einsum(
            "ihf,jhf->hij",
            queries[anchor:finish],
            key_feats[:finish],
            preferred_element_type=jnp.float32,
        ) / math.sqrt(F)
        weights = 1.0 + inner + 0.5 * inner * inner
        allowed = (positions[None, :finish] <= positions[anchor:finish, None]) & valid_rows[
            None, :finish
        ]
        weights = jnp.where(allowed[None], weights, 0.0).astype(jnp.bfloat16)
        pieces.append(
            jnp.einsum("hij,jhd->ihd", weights, values[:finish], preferred_element_type=jnp.float32)
        )
    local_sum = jnp.concatenate(pieces, axis=0)
    attended = rms_rows(carried + local_sum, gains)
    attended = (
        jnp.where(valid_rows[:, None, None], attended, 0.0)
        .astype(jnp.bfloat16)
        .reshape(STRETCH, head_count * DH)
    )
    key_phi = jnp.where(
        valid_rows[:, None, None], features(key_feats.astype(jnp.float32)), 0.0
    ).astype(jnp.bfloat16)
    state_next = state_old + jnp.einsum(
        "jhd,jhp->hdp", values, key_phi, preferred_element_type=jnp.float32
    )
    part_rows = attended
    stretch_out = lax.psum_scatter(
        jnp.dot(part_rows, out_weight, preferred_element_type=jnp.float32).astype(jnp.bfloat16),
        "head",
        scatter_dimension=0,
        tiled=True,
    )
    dec_normed = rms_rows(decode_tokens[0], norm_gain).astype(jnp.bfloat16)
    dec_conved = convolve(decode_tail[0], dec_normed[:, None, :], conv_taps)[:, 0, :]
    dec_qkv = jnp.dot(dec_conved, w_flat, preferred_element_type=jnp.float32).astype(jnp.bfloat16)
    owners = decode_owner[0, :, 0]
    slots_here = decode_slot[0]
    groups = lax.axis_size("tok")
    capacity = max(2, 2 * DEC // groups)
    earlier = jnp.arange(DEC)[None, :] < jnp.arange(DEC)[:, None]
    same_owner = owners[None, :] == owners[:, None]
    rank_in = jnp.sum(earlier & same_owner, axis=1)
    target = owners * capacity + rank_in
    placing = jnp.arange(groups * capacity)[:, None] == target[None, :]
    sent_rows = jnp.dot(
        placing.astype(jnp.bfloat16), dec_qkv, preferred_element_type=jnp.float32
    ).astype(jnp.bfloat16)
    sent_rows = sent_rows.reshape(groups, capacity, head_count * block_width)
    sent_slots = jnp.sum(jnp.where(placing, slots_here[None, :] + 1, 0), axis=1) - 1
    sent_slots = sent_slots.reshape(groups, capacity)
    item_rows = lax.all_to_all(sent_rows, "tok", split_axis=0, concat_axis=0, tiled=True)
    item_slots = lax.all_to_all(sent_slots, "tok", split_axis=0, concat_axis=0, tiled=True)
    item_count = item_rows.shape[1]
    flat_out = decode_items(
        item_rows.reshape(groups * item_count, head_count * block_width),
        item_slots.reshape(groups * item_count),
        state_cache[0],
        out_gain,
        head_count,
    )
    served = flat_out.reshape(groups, item_count, head_count * DH)
    returned = lax.all_to_all(served, "tok", split_axis=0, concat_axis=0, tiled=True)
    dec_attended = jnp.dot(
        jnp.transpose(placing).astype(jnp.bfloat16),
        returned.reshape(groups * capacity, head_count * DH),
        preferred_element_type=jnp.float32,
    ).astype(jnp.bfloat16)
    part_rows = dec_attended
    decode_out = lax.psum_scatter(
        jnp.dot(part_rows, out_weight, preferred_element_type=jnp.float32).astype(jnp.bfloat16),
        "head",
        scatter_dimension=0,
        tiled=True,
    )
    return (stretch_out[None], decode_out[None], state_next[None])


def solution(mesh):
    in_specs = (
        P("tok", "head", None),
        P("tok", None, None),
        P("tok", None, None),
        P("tok", None, None, None),
        P(),
        P(),
        P(None, "head", None),
        P("head"),
        P("head", None),
        P("tok", None, "head", None, None),
        P("tok"),
        P("tok"),
        P("tok", None),
        P("tok", None, None),
    )
    out_specs = (P("tok", "head", None), P("tok", "head", None), P("tok", "head", None, None))
    return jax.shard_map(local, mesh=mesh, in_specs=in_specs, out_specs=out_specs, check_vma=False)
```

profile of v0, /device:TPU:0, one launch (start us, length us, event | category | flops | bytes accessed | tf_op | source)
XLA Modules:
  0.0 172.6 jit_solution(11819108801438909352)
XLA Ops:
  7.2 0.0 all-gather.2.cloned.1.call-start
  7.2 1.6 fusion.19
  8.8 1.5 fusion.21
  10.3 4.8 %collective-permute-start = (bf16[2,1792]{1,0:T(2,128)(2,1)S(1)}, bf16[2,1792]{1,0:T(2,128)(2,1)S(1)}, u32[]{:S(2)}, u32[]{:S(2)}) collective-permute-start(bf16[2,1792]{1,0:T(2,128)(2,1)S(1)} %slice.100), channel_id=1, source_target_pairs={{0,8},{8,16},{16,24},{1,9},{9,17},{17,25},{2,10},{10,18},{18,26},{... | collective-permute-start | bytes 21512 | tf_op jit(solution)/shard_map/ppermute | solution.py:18
  15.2 0.1 slice_reduce_fusion.2
  15.2 1.3 collective-permute-done
  16.5 0.2 maximum_convert_fusion
  16.8 1.5 fusion.23
  18.3 0.0 all-gather.2.cloned.1.call-update
  18.3 0.2 convert_reduce_fusion
  18.5 0.1 select_reduce_fusion
  18.6 0.7 sub.7
  19.3 4.9 %all-to-all-start = ((s32[8,1,8]{2,1,0:T(1,128)}), s32[8,1,8]{2,1,0:T(1,128)S(1)}, u32[]{:S(2)}, u32[]{:S(2)}) async-start(s32[8,1,8]{2,1,0:T(1,128)} %bitcast.16), calls=%async_computation.1 | async-start | bytes 8192 | tf_op jit(solution)/shard_map/all_to_all | solution.py:165
  25.5 0.1 mul.274
  25.7 0.1 fusion.51
  25.8 0.1 fusion.50
  26.0 1.5 fusion.39
  27.5 1.0 compare_and_fusion
  28.5 1.2 fusion.18
  29.7 5.1 %all-to-all-start.1 = ((bf16[8,8,576]{2,1,0:T(8,128)(2,1)}), bf16[8,8,576]{2,1,0:T(8,128)(2,1)S(1)}, u32[]{:S(2)}, u32[]{:S(2)}) async-start(bf16[8,8,576]{2,1,0:T(8,128)(2,1)} %fusion.39), calls=%async_computation.2 | async-start | bytes 163840 | tf_op jit(solution)/shard_map/all_to_all | solution.py:164
  34.8 0.5 broadcast.246
  35.3 0.7 reduce.10
  36.0 0.1 eq.51
  36.0 0.1 fusion.78
  36.1 4.8 %all-to-all-done.1 = bf16[8,8,576]{2,1,0:T(8,128)(2,1)S(1)} async-done(((bf16[8,8,576]{2,1,0:T(8,128)(2,1)}), bf16[8,8,576]{2,1,0:T(8,128)(2,1)S(1)}, u32[]{:S(2)}, u32[]{:S(2)}) %all-to-all-start.1) | async-done | bytes 73760 | tf_op jit(solution)/shard_map/all_to_all | solution.py:164
  40.9 0.2 reshape.277
  41.1 0.1 fusion.95
  41.3 0.1 copy.71
  41.4 0.1 fusion.57
  41.5 0.1 copy.76
  41.6 0.1 multiply_multiply_fusion.2
  41.7 0.2 copy.73
  41.8 10.5 %fusion.25 = f32[64,16,4,112]{3,0,1,2:T(8,128)S(1)} fusion(f32[16,4,112,273]{2,1,3,0:T(4,128)} %bitcast.85, f32[64,4,256]{2,0,1:T(8,128)S(1)} %copy.73, f32[64,4,16]{2,0,1:T(8,128)S(1)} %get-tuple-element.33, f32[273]{0:T(512)S(1)} %pad.10.clone), kind=kOutput, calls=%fused_computation.39 | convolution fusion | flops 1503011328 | bytes 9942084 | tf_op jit(solution)/shard_map/nhp,shdp->nshd/dot_general | solution.py:52
  52.4 2.4 %fusion.16 = f32[64,1,4,112]{3,1,2,0:T(1,128)S(1)} fusion(f32[64,16,4,112]{3,0,1,2:T(8,128)S(1)} %fusion.25, pred[64,16,1,1]{1,0,2,3:T(32,128)(4,1)S(1)} %fusion.78), kind=kOutput, calls=%fused_computation.23 | convolution fusion | flops 5505024 | bytes 1950720 | tf_op jit(solution)/shard_map/ns,nshd->nhd/dot_general | solution.py:56
  54.8 0.3 multiply_reduce_fusion.1
  55.1 0.3 multiply_convert_fusion
  55.4 0.7 reshape_reshape.4
  56.1 3.3 %all-to-all-start.2 = ((bf16[8,8,448]{2,1,0:T(8,128)(2,1)}), bf16[8,8,448]{2,1,0:T(8,128)(2,1)S(1)}, u32[]{:S(2)}, u32[]{:S(2)}) async-start(bf16[8,8,448]{2,1,0:T(8,128)(2,1)} %reshape_reshape.4), calls=%async_computation.3 | async-start | bytes 131072 | tf_op jit(solution)/shard_map/all_to_all | solution.py:175
  59.5 0.0 all-reduce.3.cloned.1.call-start
  59.5 1.1 constant_dynamic-slice_fusion
  60.6 4.7 %all-to-all-done.2 = bf16[8,8,448]{2,1,0:T(8,128)(2,1)S(1)} async-done(((bf16[8,8,448]{2,1,0:T(8,128)(2,1)}), bf16[8,8,448]{2,1,0:T(8,128)(2,1)S(1)}, u32[]{:S(2)}, u32[]{:S(2)}) %all-to-all-start.2) | async-done | bytes 57376 | tf_op jit(solution)/shard_map/all_to_all | solution.py:175
  65.3 2.6 %convolution_convert_fusion.1 = bf16[32,1792]{1,0:T(8,128)(2,1)} fusion(bf16[448,1792]{1,0:T(8,128)(2,1)} %param.22, bf16[8,8,448]{2,1,0:T(8,128)(2,1)S(1)} %all-to-all-done.2, s32[32]{0:T(128)S(1)} %multiply_add_fusion.1), kind=kOutput, calls=%fused_computation.22 | convolution fusion | flops 53288960 | bytes 1777792 | tf_op jit(solution)/shard_map/dot_general | solution.py:183
  68.0 0.2 reduce-scatter.2.cloned.1.call-start
  68.2 0.7 all-gather.2.cloned.1.call-done
  68.9 4.4 %convolution_convert_fusion.2 = bf16[1024,576]{0,1:T(8,128)(2,1)S(1)} fusion(bf16[1024,1792]{1,0:T(8,128)(2,1)} %all-gather.2.cloned.1.call-done, bf16[1792,576]{0,1:T(8,128)(2,1)S(1)} %bitcast.82), kind=kOutput, calls=%fused_computation.40 | convolution fusion | flops 2114519040 | bytes 6914048 | tf_op jit(solution)/shard_map/dot_general | solution.py:89
  73.3 1.0 copy-done.6
  74.3 0.1 broadcast_multiply_fusion
  74.4 5.4 %fusion.32 = f32[512,4,112]{0,2,1:T(8,128)} fusion(pred[512,1024]{1,0:T(8,128)(4,1)} %fusion.18, bf16[1024,4,144]{0,2,1:T(8,128)(2,1)} %bitcast.94), kind=kOutput, calls=%fused_computation.43 | convolution fusion | flops 551550976 | bytes 2555904 | tf_op jit(solution)/shard_map/hij,jhd->ihd/dot_general | solution.py:124
  79.8 3.8 %fusion.31 = f32[512,4,112]{0,2,1:T(8,128)} fusion(pred[512,512]{1,0:T(8,128)(4,1)} %compare_and_fusion, bf16[1024,4,144]{0,2,1:T(8,128)(2,1)} %bitcast.95), kind=kOutput, calls=%fused_computation.42 | convolution fusion | flops 275775488 | bytes 1769472 | tf_op jit(solution)/shard_map/hij,jhd->ihd/dot_general | solution.py:124
  83.6 0.6 multiply_multiply_fusion.1
  84.2 0.6 copy-done.2
  84.7 0.3 copy-done.3
  85.0 4.1 %multiply_reduce_fusion = (f32[1024,4]{0,1:T(4,128)S(1)}, f32[1024,4,112]{0,2,1:T(8,128)S(1)}) fusion(f32[512,4,112]{0,2,1:T(8,128)S(1)} %copy-done.2, f32[512,4,112]{0,2,1:T(8,128)S(1)} %copy-done.3, f32[1024,4,256]{0,2,1:T(8,128)S(1)} %bitcast.84, f32[1024,4,16]{0,2,1:T(8,128)S(1)} %broadcast_multiply_fusion.1, f32[273]{0:T(512)S(1)} %pad.10.clone, ...), kind=kOutput, calls=%fused_computation.38 | convolution fusion | flops 1506938880 | bytes 8633156 | tf_op jit(solution)/shard_map/ihp,hdp->ihd/dot_general | solution.py:102
  89.1 0.3 select_convert_fusion.3
  89.4 1.1 copy-done.1
  90.5 3.9 %convolution_convert_fusion = bf16[1024,1792]{1,0:T(8,128)(2,1)} fusion(bf16[1024,448]{0,1:T(8,128)(2,1)S(1)} %bitcast.90, bf16[448,1792]{1,0:T(8,128)(2,1)S(1)} %copy-done.1), kind=kOutput, calls=%fused_computation.15 | convolution fusion | flops 1646002176 | bytes 6193152 | tf_op jit(solution)/shard_map/dot_general | solution.py:141
  94.5 0.6 copy-done.14
  95.1 0.6 dynamic-slice.1
  96.3 16.8 %all-reduce.3.cloned.1.call-done = bf16[32,1792]{1,0:T(8,128)(2,1)} async-done(((bf16[32,1792]{1,0:T(8,128)(2,1)}), bf16[32,1792]{1,0:T(8,128)(2,1)}) %all-reduce.3.cloned.1.call-update) | async-done | bytes 114704
  113.2 1.5 dynamic-slice_bitcast_fusion
  114.6 0.6 multiply_multiply_fusion
  115.2 1.1 fusion.36
  116.3 1.0 copy.79
  117.3 48.8 %reduce-scatter.2.cloned.1.call-done = bf16[256,1792]{1,0:T(8,128)(2,1)} async-done(((bf16[1024,1792]{1,0:T(8,128)(2,1)}), bf16[256,1792]{1,0:T(8,128)(2,1)}) %reduce-scatter.2.cloned.1.call-update) | async-done | bytes 917520 | tf_op jit(solution)/shard_map/reduce_scatter | solution.py:140
  (48 shorter events, 0.3 us)
Async XLA Ops:
  7.2 18.8 %copy-start = (bf16[1792,4,144]{0,2,1:T(8,128)(2,1)S(1)}, bf16[1792,4,144]{0,2,1:T(8,128)(2,1)}, u32[]{:S(2)}) copy-start(bf16[1792,4,144]{0,2,1:T(8,128)(2,1)} %param.20) | copy-start | bytes 6193156
  7.2 8.0 %copy-start.9 = (f32[3,1792]{1,0:T(4,128)S(1)}, f32[3,1792]{1,0:T(4,128)}, u32[]{:S(2)}) copy-start(f32[3,1792]{1,0:T(4,128)} %param.19) | copy-start | bytes 64516
  7.2 9.3 %copy-start.10 = (bf16[1,2,1792]{2,1,0:T(2,128)(2,1)S(1)}, bf16[1,2,1792]{2,1,0:T(2,128)(2,1)}, u32[]{:S(2)}) copy-start(bf16[1,2,1792]{2,1,0:T(2,128)(2,1)} %param.15) | copy-start | bytes 21508
  7.2 61.7 %all-gather.2.cloned.1.call-start = ((), (), s32[]{:S(2)}) async-start(), calls=%async_computation.4 | async-start | bytes 4587520 | tf_op jit(solution)/shard_map/all_gather | solution.py:90
  10.3 6.2 %collective-permute-start = (bf16[2,1792]{1,0:T(2,128)(2,1)S(1)}, bf16[2,1792]{1,0:T(2,128)(2,1)S(1)}, u32[]{:S(2)}, u32[]{:S(2)}) collective-permute-start(bf16[2,1792]{1,0:T(2,128)(2,1)S(1)} %slice.100), channel_id=1, source_target_pairs={{0,8},{8,16},{16,24},{1,9},{9,17},{17,25},{2,10},{10,18},{18,26},{... | collective-permute-start | bytes 21512 | tf_op jit(solution)/shard_map/ppermute | solution.py:18
  16.7 1.6 copy-start.12
  16.7 1.6 copy-start.13
  16.7 8.8 %copy-start.11 = (f32[448]{0:T(512)S(1)}, f32[448]{0:T(512)}, u32[]{:S(2)}) copy-start(f32[448]{0:T(512)} %param.21) | copy-start | bytes 5380
  16.8 8.9 %copy-start.5 = (bf16[1,32,2,1792]{3,2,1,0:T(2,128)(2,1)S(1)}, bf16[1,32,2,1792]{3,2,1,0:T(2,128)(2,1)}, u32[]{:S(2)}) copy-start(bf16[1,32,2,1792]{3,2,1,0:T(2,128)(2,1)} %param.17) | copy-start | bytes 688132
  16.8 8.9 %copy-start.4 = (bf16[1,32,1792]{2,1,0:T(8,128)(2,1)S(1)}, bf16[1,32,1792]{2,1,0:T(8,128)(2,1)}, u32[]{:S(2)}) copy-start(bf16[1,32,1792]{2,1,0:T(8,128)(2,1)} %param.16) | copy-start | bytes 344068
  16.8 9.1 %copy-start.8 = (f32[1792]{0:T(1024)S(1)}, f32[1792]{0:T(1024)}, u32[]{:S(2)}) copy-start(f32[1792]{0:T(1024)} %param.18) | copy-start | bytes 21508
  19.3 10.4 %all-to-all-start = ((s32[8,1,8]{2,1,0:T(1,128)}), s32[8,1,8]{2,1,0:T(1,128)S(1)}, u32[]{:S(2)}, u32[]{:S(2)}) async-start(s32[8,1,8]{2,1,0:T(1,128)} %bitcast.16), calls=%async_computation.1 | async-start | bytes 8192 | tf_op jit(solution)/shard_map/all_to_all | solution.py:165
  29.7 11.2 %all-to-all-start.1 = ((bf16[8,8,576]{2,1,0:T(8,128)(2,1)}), bf16[8,8,576]{2,1,0:T(8,128)(2,1)S(1)}, u32[]{:S(2)}, u32[]{:S(2)}) async-start(bf16[8,8,576]{2,1,0:T(8,128)(2,1)} %fusion.39), calls=%async_computation.2 | async-start | bytes 163840 | tf_op jit(solution)/shard_map/all_to_all | solution.py:164
  56.1 9.2 %all-to-all-start.2 = ((bf16[8,8,448]{2,1,0:T(8,128)(2,1)}), bf16[8,8,448]{2,1,0:T(8,128)(2,1)S(1)}, u32[]{:S(2)}, u32[]{:S(2)}) async-start(bf16[8,8,448]{2,1,0:T(8,128)(2,1)} %reshape_reshape.4), calls=%async_computation.3 | async-start | bytes 131072 | tf_op jit(solution)/shard_map/all_to_all | solution.py:175
  59.5 53.7 %all-reduce.3.cloned.1.call-start = ((), (), s32[]{:S(2)}) async-start(), calls=%async_computation.6 | async-start | bytes 229376
  68.0 98.1 %reduce-scatter.2.cloned.1.call-start = ((), (), s32[]{:S(2)}) async-start(), calls=%async_computation.5 | async-start | bytes 4587520 | tf_op jit(solution)/shard_map/reduce_scatter | solution.py:140
  73.3 1.0 copy-start.6
  83.6 1.2 copy-start.2
  83.6 1.5 copy-start.3
  89.1 1.4 copy-start.1
  94.4 0.7 copy-start.14
  113.1 2.0 %copy-start.7 = (bf16[1024,576]{0,1:T(8,128)(2,1)S(1)}, bf16[1024,576]{0,1:T(8,128)(2,1)}, u32[]{:S(2)}) copy-start(bf16[1024,576]{0,1:T(8,128)(2,1)} %copy-done.6) | copy-start | bytes 3538948
Sparse Core Ops, SparseCore 0:
  18.4 50.4 all-gather.1
  71.8 41.3 all-reduce.2
  117.0 49.0 reduce-scatter.1
where the time goes:
time: 173 us
  waiting for transfers between devices  77.1 us (45%)
  matrix products  39.7 us (23%)
  starting transfers between devices  18.5 us (11%)
  between operations  16.1 us (9%)
  local copies, waits for them, and re-layouts  10.7 us (6%)
  other arithmetic  10.5 us (6%)
    reduce_scatter x1, waiting for transfers between devices, local(): lax.psum_scatter(jnp.dot(part_rows, out_weight, preferred_element_type=jn...  48.8 us
    unnamed x4, waiting for transfers between devices  16.9 us
    dot_general x1, matrix products, decode_items(): jnp.einsum('nhp,shdp->nshd', features(queries), cache_own, precision=lax....  10.5 us
    dot_general x2, matrix products, local(): jnp.einsum('hij,jhd->ihd', weights, values[:finish], preferred_element_ty...  9.2 us
    dot_general x2, matrix products, local(): jnp.dot(part_rows, out_weight, preferred_element_type=jnp.float32)  6.56 us
    unnamed x33, local copies, waits for them, and re-layouts  5.23 us
    all_to_all x1, starting transfers between devices, local(): lax.all_to_all(sent_rows, 'tok', split_axis=0, concat_axis=0, tiled=True)  5.1 us
    all_to_all x1, starting transfers between devices, local(): lax.all_to_all(sent_slots, 'tok', split_axis=0, concat_axis=0, tiled=True)  4.88 us
  transfers between devices with their start and end apart: 7, of which 6 were waited for; matrix products, arithmetic and copies ran while one was open for 30% of the time, Pallas kernels for 0%

commit v1 on v0

--- a/solution.py
+++ b/solution.py
@@ -1,8 +1,12 @@
+import functools
 import math
 
 import jax
 import jax.numpy as jnp
+import numpy as np
 from jax import lax
+from jax.experimental import pallas as pl
+from jax.experimental.pallas import tpu as pltpu
 from jax.sharding import PartitionSpec as P
 
 D = 1792
@@ -10,6 +14,356 @@
 F = 16
 STRETCH = 1024
 DEC = 32
+PHI = 1 + F + F * F
+WIDE = 128
+PHI_WIDE = 384
+MIB = 1 << 20
+
+
+def selectors():
+    first = np.zeros((F, PHI_WIDE), np.float32)
+    second = np.zeros((F, PHI_WIDE), np.float32)
+    for a in range(F):
+        first[a, 1 + a] = 1.0
+        for b in range(F):
+            first[a, 1 + F + a * F + b] = 1.0
+            second[b, 1 + F + a * F + b] = 1.0
+    return jnp.asarray(first, jnp.bfloat16), jnp.asarray(second, jnp.bfloat16)
+
+
+def dot(left, right, contract=((1,), (0,))):
+    return lax.dot_general(left, right, (contract, ((), ())), preferred_element_type=jnp.float32)
+
+
+def phi_of(vectors, first, second):
+    a = dot(vectors, first)
+    b = dot(vectors, second)
+    lane = lax.broadcasted_iota(jnp.int32, a.shape, 1)
+    scale = jnp.where(lane <= F, 1.0 / math.sqrt(math.sqrt(F)), b * (1.0 / math.sqrt(2.0 * F)))
+    return jnp.where(lane == 0, 1.0, a * scale)
+
+
+def unit_rows(values):
+    values = values.astype(jnp.float32)
+    total = jnp.sum(values * values, axis=-1, keepdims=True)
+    return values, lax.rsqrt(total * (1.0 / D) + 1e-05)
+
+
+def conv_kernel(first_ref, tokens_ref, rim_ref, tail_ref, gain_ref, taps_ref, out_ref):
+    rows = tokens_ref.shape[0]
+    _, factor = unit_rows(tokens_ref[...])
+    rim, rim_factor = unit_rows(rim_ref[...])
+    rim = (rim * rim_factor * gain_ref[...]).astype(jnp.bfloat16).astype(jnp.float32)
+    rim = jnp.where(first_ref[0] == 0, tail_ref[...].astype(jnp.float32), rim)
+    step = 256
+    row = lax.broadcasted_iota(jnp.int32, (rows, step), 0)
+    for at in range(0, D, step):
+        cols = slice(at, at + step)
+        normed = tokens_ref[:, cols].astype(jnp.float32) * factor * gain_ref[:, cols]
+        normed = normed.astype(jnp.bfloat16).astype(jnp.float32)
+        one = jnp.where(row == 0, rim[1:2, cols], pltpu.roll(normed, 1, 0))
+        two = pltpu.roll(normed, 2, 0)
+        two = jnp.where(row == 0, rim[0:1, cols], jnp.where(row == 1, rim[1:2, cols], two))
+        total = taps_ref[0:1, cols] * two + taps_ref[1:2, cols] * one + taps_ref[2:3, cols] * normed
+        out_ref[:, cols] = total.astype(jnp.bfloat16)
+
+
+def block_kernel(slot, heads, meta_ref, conved_ref, w_ref, a_ref, b_ref, q_ref, local_ref, sums_ref):
+    rows = conved_ref.shape[0]
+    qkv = dot(conved_ref[...], w_ref[...]).astype(jnp.bfloat16)
+    q_ref[...] = qkv[:, : heads * F]
+    live = meta_ref[1] - rows * (meta_ref[2] ^ slot)
+    row = lax.broadcasted_iota(jnp.int32, (rows, rows), 0)
+    col = lax.broadcasted_iota(jnp.int32, (rows, rows), 1)
+    allowed = (col <= row) & (col < live)
+    live_row = lax.broadcasted_iota(jnp.int32, (rows, PHI_WIDE), 0) < live
+    for head in range(heads):
+        q = qkv[:, head * F : head * F + F]
+        k = qkv[:, (heads + head) * F : (heads + head) * F + F]
+        at = 2 * heads * F + head * WIDE
+        v = qkv[:, at : at + WIDE]
+        inner = dot(q, k, ((1,), (1,))) * (1.0 / math.sqrt(F))
+        weights = jnp.where(allowed, 1.0 + inner + 0.5 * inner * inner, 0.0).astype(jnp.bfloat16)
+        local_ref[:, head * WIDE : (head + 1) * WIDE] = dot(weights, v)
+        key_phi = phi_of(k, a_ref[...], b_ref[...])
+        key_phi = jnp.where(live_row, key_phi, 0.0).astype(jnp.bfloat16)
+        total = dot(v, key_phi, ((0,), (0,)))
+        sums_ref[head] = total[:DH, :PHI]
+
+
+def finish_kernel(slots, heads, keep, meta_ref, *refs):
+    q_refs = refs[: len(slots)]
+    local_refs = refs[len(slots) : 2 * len(slots)]
+    sums_refs = refs[2 * len(slots) : 2 * len(slots) + 4]
+    old_ref, a_ref, b_ref, gain_ref, w_ref = refs[2 * len(slots) + 4 : 2 * len(slots) + 9]
+    outs = refs[2 * len(slots) + 9 :]
+    state = outs[-1]
+    mine = meta_ref[2]
+    rows = q_refs[0].shape[0]
+    state[...] = jnp.zeros_like(state)
+    for order, slot in enumerate(slots):
+        block = mine ^ slot
+        live = meta_ref[1] - rows * block
+        live_row = lax.broadcasted_iota(jnp.int32, (rows, WIDE), 0) < live
+        parts = []
+        for head in range(heads):
+            before = old_ref[0, 0, head]
+            for other in range(4):
+                if other != slot:
+                    use = ((mine ^ other) < block).astype(jnp.float32)
+                    before = before + use * sums_refs[other][head]
+            state[head, :DH, :PHI] = before.astype(jnp.bfloat16)
+            q = q_refs[order][:, head * F : head * F + F]
+            query_phi = phi_of(q, a_ref[...], b_ref[...]).astype(jnp.bfloat16)
+            total = local_refs[order][:, head * WIDE : (head + 1) * WIDE]
+            total = total + dot(query_phi, state[head], ((1,), (1,)))
+            square = jnp.sum(total * total, axis=-1, keepdims=True)
+            total = total * lax.rsqrt(square * (1.0 / DH) + 1e-05) * gain_ref[head : head + 1, :]
+            parts.append(jnp.where(live_row, total, 0.0).astype(jnp.bfloat16))
+        attended = jnp.concatenate(parts, axis=1)
+        outs[order][...] = dot(attended, w_ref[...]).astype(jnp.bfloat16)
+    if keep:
+        for head in range(heads):
+            after = old_ref[0, 0, head]
+            for other in range(4):
+                after = after + sums_refs[other][head]
+            outs[len(slots)][0, head] = after
+
+
+def send_kernel(
+    heads, capacity, tokens_ref, tail0_ref, tail1_ref, gain_ref, taps_ref, w_ref, col_ref, row_ref, slot_ref, out_ref
+):
+    tokens, factor = unit_rows(tokens_ref[...])
+    normed = (tokens * factor * gain_ref[...]).astype(jnp.bfloat16).astype(jnp.float32)
+    conved = taps_ref[0:1, :] * tail0_ref[...].astype(jnp.float32)
+    conved = conved + taps_ref[1:2, :] * tail1_ref[...].astype(jnp.float32)
+    conved = (conved + taps_ref[2:3, :] * normed).astype(jnp.bfloat16)
+    qkv = dot(conved, w_ref[...]).astype(jnp.bfloat16)
+    owners = row_ref[...]
+    m = lax.broadcasted_iota(jnp.int32, (DEC, DEC), 0)
+    n = lax.broadcasted_iota(jnp.int32, (DEC, DEC), 1)
+    rank = jnp.sum(jnp.where((m < n) & (col_ref[...] == owners), 1, 0), axis=0, keepdims=True)
+    target = owners * capacity + rank
+    total = out_ref.shape[0]
+    placing = lax.broadcasted_iota(jnp.int32, (total, DEC), 0) == target
+    sent = dot(jnp.where(placing, 1.0, 0.0).astype(jnp.bfloat16), qkv)
+    cache_slot = jnp.sum(jnp.where(placing, slot_ref[...] + 1, 0), axis=1, keepdims=True) - 1
+    lane = lax.broadcasted_iota(jnp.int32, sent.shape, 1)
+    mark = 2 * heads * F + DH
+    out_ref[...] = jnp.where(lane == mark, cache_slot.astype(jnp.float32), sent).astype(jnp.bfloat16)
+
+
+def serve_kernel(heads, items_ref, cache_ref, a_ref, b_ref, gain_ref, out_ref, phis, total, slots):
+    step = pl.program_id(0)
+    count = items_ref.shape[0]
+
+    @pl.when(step == 0)
+    def _():
+        total[...] = jnp.zeros_like(total)
+        for head in range(heads):
+            q = items_ref[:, head * F : head * F + F]
+            phis[head] = phi_of(q, a_ref[...], b_ref[...]).astype(jnp.bfloat16)
+        slab = items_ref[:, 2 * heads * F : 2 * heads * F + WIDE].astype(jnp.float32)
+        slots[...] = slab.T[DH : DH + 1, :]
+
+    here = slots[...] == step.astype(jnp.float32)
+    for head in range(heads):
+        state = cache_ref[0, 0, head].astype(jnp.bfloat16)
+        table = dot(state, phis[head][:, :PHI], ((1,), (1,)))
+        total[head, :DH, :] += jnp.where(here, table, 0.0)
+
+    @pl.when(step == pl.num_programs(0) - 1)
+    def _():
+        lane = lax.broadcasted_iota(jnp.int32, (count, WIDE), 1)
+        for head in range(heads):
+            q = items_ref[:, head * F : head * F + F].astype(jnp.float32)
+            k = items_ref[:, (heads + head) * F : (heads + head) * F + F].astype(jnp.float32)
+            at = 2 * heads * F + head * WIDE
+            v = items_ref[:, at : at + WIDE].astype(jnp.float32)
+            inner = jnp.sum(q * k, axis=-1, keepdims=True) * (1.0 / math.sqrt(F))
+            value = total[head].T + (1.0 + inner + 0.5 * inner * inner) * v
+            value = jnp.where(lane < DH, value, 0.0)
+            square = jnp.sum(value * value, axis=-1, keepdims=True)
+            value = value * lax.rsqrt(square * (1.0 / DH) + 1e-05) * gain_ref[head : head + 1, :]
+            out_ref[:, head * WIDE : (head + 1) * WIDE] = value.astype(jnp.bfloat16)
+
+
+def return_kernel(capacity, items_ref, col_ref, row_ref, w_ref, out_ref):
+    owners = col_ref[...]
+    n = lax.broadcasted_iota(jnp.int32, (DEC, DEC), 0)
+    m = lax.broadcasted_iota(jnp.int32, (DEC, DEC), 1)
+    rank = jnp.sum(jnp.where((m < n) & (row_ref[...] == owners), 1, 0), axis=1, keepdims=True)
+    target = owners * capacity + rank
+    placing = lax.broadcasted_iota(jnp.int32, (DEC, items_ref.shape[0]), 1) == target
+    attended = dot(jnp.where(placing, 1.0, 0.0).astype(jnp.bfloat16), items_ref[...]).astype(jnp.bfloat16)
+    out_ref[...] = dot(attended, w_ref[...]).astype(jnp.bfloat16)
+
+
+def whole(count):
+    return [pl.BlockSpec(memory_space=pltpu.VMEM)] * count
+
+
+def call(kernel, outs, flops, size, smem=0, scratch=(), vmem=24):
+    def run(*args):
+        many = isinstance(outs, (list, tuple))
+        return pl.pallas_call(
+            kernel,
+            out_shape=outs,
+            in_specs=[pl.BlockSpec(memory_space=pltpu.SMEM)] * smem + whole(len(args) - smem),
+            out_specs=whole(len(outs)) if many else whole(1)[0],
+            scratch_shapes=list(scratch),
+            compiler_params=pltpu.CompilerParams(vmem_limit_bytes=vmem * MIB),
+            cost_estimate=pl.CostEstimate(flops=flops, bytes_accessed=size, transcendentals=0),
+        )(*args)
+
+    return run
+
+
+def shape(*dims, dtype=jnp.bfloat16):
+    return jax.ShapeDtypeStruct(dims, dtype)
+
+
+def across(array, by):
+    return lax.ppermute(array, "head", [(i, i ^ by) for i in range(4)])
+
+
+def local_square(
+    stretch_tokens,
+    stretch_tail,
+    decode_tokens,
+    decode_tail,
+    norm_gain,
+    conv_taps,
+    qkv_weight,
+    out_gain,
+    out_weight,
+    state_cache,
+    stretch_len,
+    stretch_slot,
+    decode_slot,
+    decode_owner,
+):
+    heads = qkv_weight.shape[1]
+    rows = stretch_tokens.shape[1]
+    half = rows // 2
+    me = lax.axis_index("head")
+    meta = jnp.stack([stretch_slot[0], stretch_len[0], me]).astype(jnp.int32)
+    gain = norm_gain.reshape(1, D)
+    first, second = selectors()
+
+    rim = from_behind(stretch_tokens[0, rows - 2 :], "head", 1)
+
+    w_qk = [qkv_weight[:, :, :F].reshape(D, heads * F), qkv_weight[:, :, F : 2 * F].reshape(D, heads * F)]
+    w_v = jnp.pad(qkv_weight[:, :, 2 * F :], ((0, 0), (0, 0), (0, WIDE - DH))).reshape(D, heads * WIDE)
+    w_in = jnp.concatenate(w_qk + [w_v], axis=1)
+    wide = w_in.shape[1]
+    w_out = jnp.pad(out_weight.reshape(heads, DH, D), ((0, 0), (0, WIDE - DH), (0, 0))).reshape(heads * WIDE, D)
+    gains = jnp.pad(out_gain.reshape(heads, DH), ((0, 0), (0, WIDE - DH)))
+
+    conved = call(conv_kernel, shape(rows, D), 20 * rows * D, 4 * rows * D, smem=1)(
+        me.reshape(1), stretch_tokens[0], rim, stretch_tail[0], gain, conv_taps
+    )
+    from_x = across(conved, 1)
+    from_y = across(conved, 2)
+
+    groups = lax.axis_size("tok")
+    capacity = max(2, 2 * DEC // groups)
+    count = groups * capacity
+    owner_col = decode_owner[0]
+    owner_row = owner_col.reshape(1, DEC)
+    sent = call(functools.partial(send_kernel, heads, capacity), shape(count, wide), 2 * DEC * D * wide, 2 * D * wide)(
+        decode_tokens[0], decode_tail[0, :, 0], decode_tail[0, :, 1], gain, conv_taps, w_in, owner_col, owner_row, decode_slot
+    )
+    items = lax.all_to_all(sent.reshape(groups, capacity, wide), "tok", split_axis=0, concat_axis=0, tiled=True)
+    items = items.reshape(count, wide)
+    cache_slots = state_cache.shape[1]
+    served = pl.pallas_call(
+        functools.partial(serve_kernel, heads),
+        grid=(cache_slots,),
+        in_specs=[
+            pl.BlockSpec((count, wide), lambda i: (0, 0)),
+            pl.BlockSpec((1, 1, heads, DH, PHI), lambda i: (0, i, 0, 0, 0)),
+            pl.BlockSpec((F, PHI_WIDE), lambda i: (0, 0)),
+            pl.BlockSpec((F, PHI_WIDE), lambda i: (0, 0)),
+            pl.BlockSpec((heads, WIDE), lambda i: (0, 0)),
+        ],
+        out_specs=pl.BlockSpec((count, heads * WIDE), lambda i: (0, 0)),
+        out_shape=shape(count, heads * WIDE),
+        scratch_shapes=[
+            pltpu.VMEM((heads, count, PHI_WIDE), jnp.bfloat16),
+            pltpu.VMEM((heads, WIDE, count), jnp.float32),
+            pltpu.VMEM((1, count), jnp.float32),
+        ],
+        compiler_params=pltpu.CompilerParams(vmem_limit_bytes=24 * MIB),
+        cost_estimate=pl.CostEstimate(
+            flops=2 * cache_slots * heads * DH * PHI * count, bytes_accessed=4 * cache_slots * heads * DH * PHI_WIDE, transcendentals=0
+        ),
+    )(items, state_cache, first, second, gains)
+    returned = lax.all_to_all(
+        served.reshape(groups, capacity, heads * WIDE), "tok", split_axis=0, concat_axis=0, tiled=True
+    ).reshape(count, heads * WIDE)
+
+    def block(slot, block_rows):
+        return call(
+            functools.partial(block_kernel, slot, heads),
+            [shape(rows, heads * F), shape(rows, heads * WIDE, dtype=jnp.float32), shape(heads, DH, PHI, dtype=jnp.float32)],
+            2 * rows * D * wide + 6 * heads * rows * rows * WIDE,
+            2 * (rows * D + D * wide),
+            smem=1,
+        )(meta, block_rows, w_in, first, second)
+
+    blocks = [block(0, conved), block(1, from_x), block(2, from_y)]
+    from_xy = jnp.concatenate([across(from_x[:half], 2), across(from_y[half:], 1)], axis=0)
+    blocks.append(block(3, from_xy))
+
+    def finish(slots, keep=False):
+        outs = [shape(rows, D)] * len(slots)
+        if keep:
+            outs = outs + [shape(1, heads, DH, PHI, dtype=jnp.float32)]
+        args = [blocks[s][0] for s in slots] + [blocks[s][1] for s in slots] + [b[2] for b in blocks]
+        args = args + [state_cache, first, second, gains, w_out]
+
+        def fixed(dims):
+            return pl.BlockSpec(dims, lambda i, meta_ref: (0,) * len(dims))
+
+        specs = [fixed(a.shape) for a in args]
+        specs[-5] = pl.BlockSpec((1, 1, heads, DH, PHI), lambda i, meta_ref: (0, meta_ref[0], 0, 0, 0))
+        return pl.pallas_call(
+            functools.partial(finish_kernel, slots, heads, keep),
+            grid_spec=pltpu.PrefetchScalarGridSpec(
+                num_scalar_prefetch=1,
+                grid=(1,),
+                in_specs=specs,
+                out_specs=[fixed(o.shape) for o in outs],
+                scratch_shapes=[pltpu.VMEM((heads, WIDE, PHI_WIDE), jnp.bfloat16)],
+            ),
+            out_shape=outs,
+            compiler_params=pltpu.CompilerParams(vmem_limit_bytes=40 * MIB),
+            cost_estimate=pl.CostEstimate(
+                flops=len(slots) * 2 * rows * heads * WIDE * (D + PHI_WIDE), bytes_accessed=2 * rows * D * len(slots), transcendentals=0
+            ),
+        )(meta, *args)
+
+    (p3,) = finish((3,))
+    via_x = across(p3[:half], 1)
+    via_y = across(p3[half:], 2)
+    p1, p2 = finish((1, 2))
+    top_x = across(p1[:half], 1)
+    low_y = across(p2[half:], 2)
+    p0, state_next = finish((0,), keep=True)
+    f32 = jnp.float32
+    top_y = across((p2[:half].astype(f32) + via_x.astype(f32)).astype(jnp.bfloat16), 2)
+    low_x = across((p1[half:].astype(f32) + via_y.astype(f32)).astype(jnp.bfloat16), 1)
+    top = p0[:half].astype(f32) + top_x.astype(f32) + top_y.astype(f32)
+    low = p0[half:].astype(f32) + low_x.astype(f32) + low_y.astype(f32)
+    stretch_out = jnp.concatenate([top, low], axis=0).astype(jnp.bfloat16)
+
+    part = call(functools.partial(return_kernel, capacity), shape(DEC, D), 2 * DEC * heads * WIDE * D, 2 * heads * WIDE * D)(
+        returned, owner_col, owner_row, w_out
+    )
+    shares = lax.all_to_all(part.reshape(4, DEC // 4, D), "head", split_axis=0, concat_axis=0, tiled=True)
+    decode_out = jnp.sum(shares.astype(f32), axis=0).astype(jnp.bfloat16)
+    return (stretch_out[None], decode_out[None], state_next)
 
 
 def from_behind(array, axis, by):
@@ -206,4 +560,5 @@
         P("tok", None, None),
     )
     out_specs = (P("tok", "head", None), P("tok", "head", None), P("tok", "head", None, None))
-    return jax.shard_map(local, mesh=mesh, in_specs=in_specs, out_specs=out_specs, check_vma=False)
+    chosen = local_square if mesh.shape["head"] == 4 else local
+    return jax.shard_map(chosen, mesh=mesh, in_specs=in_specs, out_specs=out_specs, check_vma=False)

time: 173 us -> 136 us (0.79)
  waiting for transfers between devices: 77.1 us -> 0.66 us
  matrix products: 39.7 us -> 0 us
  local copies, waits for them, and re-layouts: 10.7 us -> 47.4 us
  Pallas kernels: 0 us -> 33 us
  blocking collectives: 0 us -> 27.2 us
  between operations: 16.1 us -> 2.26 us
  other arithmetic: 10.5 us -> 7.2 us
    reduce_scatter x1 -> x0, waiting for transfers between devices: 48.8 us -> none  [local(): lax.psum_scatter(jnp.dot(part_rows, out_weight, preferred_element_type=jn...]
    dot_general x10 -> x0, matrix products: 39.7 us -> none  [the longest x1 10.5 us: decode_items(): jnp.einsum('nhp,shdp->nshd', features(queries), cache_own, precision=lax....]
    pallas_call x0 -> x11, Pallas kernels: none -> 33 us  [the longest x7 15.4 us: run(): pl.pallas_call(kernel, out_shape=outs, in_specs=[pl.BlockSpec(memory_spac...]
    all_to_all x0 -> x3, blocking collectives: none -> 27.2 us  [the longest x1 10.8 us: local_square(): lax.all_to_all(sent.reshape(groups, capacity, wide), 'tok', split_axis=0,...]
    unnamed x33 -> x60, local copies, waits for them, and re-layouts: 5.23 us -> 26.9 us
    unnamed x4 -> x0, waiting for transfers between devices: 16.9 us -> none
    all_to_all x3 -> x0, starting transfers between devices: 13.3 us -> none  [the longest x1 5.1 us: local(): lax.all_to_all(sent_rows, 'tok', split_axis=0, concat_axis=0, tiled=True)]
    ppermute x0 -> x10, starting transfers between devices: none -> 12.3 us  [across(): return lax.ppermute(array, 'head', [(i, i ^ by) for i in range(4)])]
  transfers between devices with their start and end apart: 7 -> 11, of which waited for: 6 -> 1; matrix products, arithmetic and copies ran while one was open for 30% -> 27% of each run, Pallas kernels for 0% -> 19%
where the time goes in v1:
time: 136 us; the launch traced here: 135 us
  local copies, waits for them, and re-layouts  47.4 us (35%)
  Pallas kernels  33 us (24%)
  blocking collectives  27.2 us (20%)
  starting transfers between devices  17.2 us (13%)
  other arithmetic  7.2 us (5%)
  between operations  2.26 us (2%)
    unnamed x60, local copies, waits for them, and re-layouts  26.9 us
    pallas_call x7, Pallas kernels, run(): pl.pallas_call(kernel, out_shape=outs, in_specs=[pl.BlockSpec(memory_spac...  15.4 us
    ppermute x10, starting transfers between devices, across(): return lax.ppermute(array, 'head', [(i, i ^ by) for i in range(4)])  12.3 us
    pallas_call x3, Pallas kernels, finish(): pl.pallas_call(functools.partial(finish_kernel, slots, heads, keep), grid...  12.3 us
    all_to_all x1, blocking collectives, local_square(): lax.all_to_all(sent.reshape(groups, capacity, wide), 'tok', split_axis=0,...  10.8 us
    all_to_all x1, blocking collectives, local_square(): lax.all_to_all(served.reshape(groups, capacity, heads * WIDE), 'tok', spl...  8.3 us
    all_to_all x1, blocking collectives, local_square(): lax.all_to_all(part.reshape(4, DEC // 4, D), 'head', split_axis=0, concat...  8.16 us
    pallas_call x1, Pallas kernels, local_square(): pl.pallas_call(functools.partial(serve_kernel, heads), grid=(cache_slots,...  5.42 us
  transfers between devices with their start and end apart: 11, of which 1 were waited for; matrix products, arithmetic and copies ran while one was open for 27% of the time, Pallas kernels for 19%

profile of v1, /device:TPU:0, one launch (start us, length us, event | category | flops | bytes accessed | tf_op | source)
XLA Modules:
  0.0 135.0 jit_solution(4619443719673125605)
XLA Ops:
  0.6 0.8 slice_bitcast_fusion
  1.4 4.8 %collective-permute-start = (bf16[2,1792]{1,0:T(2,128)(2,1)S(1)}, bf16[2,1792]{1,0:T(2,128)(2,1)S(1)}, u32[]{:S(2)}, u32[]{:S(2)}) collective-permute-start(bf16[2,1792]{1,0:T(2,128)(2,1)S(1)} %slice_bitcast_fusion), channel_id=1, source_target_pairs={{0,8},{8,16},{16,24},{1,9},{9,17},{17,25},{2,10},{10,18},{18,26},{... | collective-permute-start | bytes 21512 | tf_op jit(solution)/shard_map/ppermute | solution.py:372
  6.2 0.7 reshape.74.gain_ref
  7.0 0.6 collective-permute-done.rim_ref
  7.6 1.2 copy-done.15
  8.8 0.7 copy-done.21
  9.5 0.7 copy-done.24
  10.2 1.5 %shard_map.175.conved_ref = bf16[256,1792]{1,0:T(8,128)(2,1)S(1)} custom-call(s32[1]{0:T(128)} %bitcast.first_ref, bf16[256,1792]{1,0:T(8,128)(2,1)S(1)} %bitcast.31, bf16[2,1792]{1,0:T(2,128)(2,1)S(1)} %collective-permute-done.rim_ref, bf16[2,1792]{1,0:T(2,128)(2,1)S(1)} %bitcast.38, f32[1,1792]{1,0:T(1,128)S(1)} %reshape.74.gain_ref, f32[3,1792]{1,0:T(4,128)S(1)} %copy-done.21), custom_call_target="tpu_custom_call" | custom-call | flops 9175040 | bytes 1835008 | tf_op jit(solution)/shard_map/pallas_call | solution.py:209
  11.7 0.0 copy-start.9
  11.7 3.3 %collective-permute-start.2 = (bf16[256,1792]{1,0:T(8,128)(2,1)S(1)}, bf16[256,1792]{1,0:T(8,128)(2,1)S(1)}, u32[]{:S(2)}, u32[]{:S(2)}) collective-permute-start(bf16[256,1792]{1,0:T(8,128)(2,1)S(1)} %shard_map.175.conved_ref), channel_id=1, source_target_pairs={{0,16},{8,24},{16,0},{24,8},{1,17},{9,25},{17,1},{25,9},{2,18},{10... | collective-permute-start | bytes 2752520 | tf_op jit(solution)/shard_map/ppermute | solution.py:227
  15.0 0.6 collective-permute-start.1
  16.9 0.8 reshape.78
  17.6 2.7 %slice.51 = bf16[1792,4,112]{0,2,1:T(8,128)(2,1)} slice(bf16[1792,4,144]{0,2,1:T(8,128)(2,1)} %param.22), slice={[0:1792], [0:4], [32:144]} | slice | bytes 3211264 | tf_op jit(solution)/shard_map/slice | solution.py:257
  20.3 1.8 %fusion.2 = (bf16[1792,4,16]{0,2,1:T(8,128)(2,1)S(1)}, bf16[1792,4,16]{0,2,1:T(8,128)(2,1)}) fusion(bf16[1792,4,144]{0,2,1:T(8,128)(2,1)} %param.22), kind=kLoop, calls=%fused_computation.13 | loop fusion | bytes 917504 | tf_op jit(solution)/shard_map/slice | solution.py:256
  22.1 1.2 copy.33
  23.3 1.0 copy.32
  24.3 2.8 %pad.12 = bf16[1792,4,128]{0,2,1:T(8,128)(2,1)} pad(bf16[1792,4,112]{0,2,1:T(8,128)(2,1)} %slice.51, bf16[]{:T(256)} %constant.14.clone.1), padding=0_0x0_0x0_16 | pad | bytes 3440642 | tf_op jit(solution)/shard_map/jit(_pad)/pad | solution.py:257
  27.1 3.8 %copy.43 = bf16[1792,512]{1,0:T(8,128)(2,1)} copy(bf16[1792,512]{0,1:T(8,128)(2,1)} %bitcast.42) | data formatting | bytes 3670016 | tf_op jit(solution)/shard_map/reshape | solution.py:257
  30.9 2.9 %pad.14 = bf16[4,128,1792]{2,1,0:T(8,128)(2,1)} pad(bf16[4,112,1792]{2,1,0:T(8,128)(2,1)} %bitcast.43, bf16[]{:T(256)} %constant.14.clone.1), padding=0_0x0_16x0_0 | pad | bytes 3440642 | tf_op jit(solution)/shard_map/jit(_pad)/pad | solution.py:260
  33.8 12.0 %copy.34.refs_6_.refs_8_.cache_ref = f32[1,16,4,112,273]{4,3,2,1,0:T(8,128)} copy(f32[1,16,4,112,273]{3,2,4,1,0:T(4,128)} %param.25) | data formatting | bytes 15654912 | tf_op args[9]
  45.8 0.1 pad_add_fusion.meta_ref
  46.0 1.5 %collective-permute-start.4 = (bf16[128,1792]{1,0:T(8,128)(2,1)S(1)}, bf16[128,1792]{1,0:T(8,128)(2,1)S(1)}, u32[]{:S(2)}, u32[]{:S(2)}) collective-permute-start(bf16[128,1792]{1,0:T(8,128)(2,1)S(1)} %slice.65), channel_id=1, source_target_pairs={{0,8},{8,0},{16,24},{24,16},{1,9},{9,1},{17,25},{25,17},{2,10},{10... | collective-permute-start | bytes 1376264 | tf_op jit(solution)/shard_map/ppermute | solution.py:227
  47.5 0.9 copy-done.11
  48.4 0.1 collective-permute-start.3
  48.5 1.6 %pad_maximum_fusion.w_ref = bf16[1792,640]{1,0:T(8,128)(2,1)S(1)} fusion(bf16[1792,512]{1,0:T(8,128)(2,1)S(1)} %copy-done.27, bf16[1792,64]{1,0:T(8,128)(2,1)S(1)} %copy.33, bf16[1792,64]{1,0:T(8,128)(2,1)} %copy.32), kind=kLoop, calls=%fused_computation | loop fusion | flops 6881280 | bytes 4587520 | tf_op jit(solution)/shard_map/concatenate | solution.py:258
  50.2 3.1 %shard_map.176 = (bf16[256,64]{1,0:T(8,128)(2,1)S(1)}, f32[256,512]{1,0:T(8,128)S(1)}, f32[4,112,273]{2,1,0:T(8,128)S(1)}) custom-call(s32[3]{0:T(128)S(1)} %pad_add_fusion.meta_ref, bf16[256,1792]{1,0:T(8,128)(2,1)S(1)} %copy-done.10, bf16[1792,640]{1,0:T(8,128)(2,1)S(1)} %pad_maximum_fusion.w_ref, bf16[16,384]{1,0:T(8,128)(2,1)S(1)} %copy-done.18, ...), custom_call_target="tpu_custom_call" | custom-call | flops 788529152 | bytes 3211264 | tf_op jit(solution)/shard_map/pallas_call | solution.py:209
  53.3 0.0 copy-start.19
  53.3 0.8 copy-done.19
  54.1 3.1 %shard_map.178 = (bf16[256,64]{1,0:T(8,128)(2,1)S(1)}, f32[256,512]{1,0:T(8,128)S(1)}, f32[4,112,273]{2,1,0:T(8,128)S(1)}) custom-call(s32[3]{0:T(128)S(1)} %pad_add_fusion.meta_ref, bf16[256,1792]{1,0:T(8,128)(2,1)S(1)} %copy-done.14, bf16[1792,640]{1,0:T(8,128)(2,1)S(1)} %pad_maximum_fusion.w_ref, bf16[16,384]{1,0:T(8,128)(2,1)S(1)} %copy-done.18, ...), custom_call_target="tpu_custom_call" | custom-call | flops 788529152 | bytes 3211264 | tf_op jit(solution)/shard_map/pallas_call | solution.py:209
  57.2 3.1 %shard_map.177 = (bf16[256,64]{1,0:T(8,128)(2,1)S(1)}, f32[256,512]{1,0:T(8,128)S(1)}, f32[4,112,273]{2,1,0:T(8,128)S(1)}) custom-call(s32[3]{0:T(128)S(1)} %pad_add_fusion.meta_ref, bf16[256,1792]{1,0:T(8,128)(2,1)S(1)} %copy-done.12, bf16[1792,640]{1,0:T(8,128)(2,1)S(1)} %pad_maximum_fusion.w_ref, bf16[16,384]{1,0:T(8,128)(2,1)S(1)} %copy-done.18, ...), custom_call_target="tpu_custom_call" | custom-call | flops 788529152 | bytes 3211264 | tf_op jit(solution)/shard_map/pallas_call | solution.py:209
  60.4 0.1 pad_maximum_fusion.1.conved_ref
  60.4 3.1 %shard_map.179 = (bf16[256,64]{1,0:T(8,128)(2,1)S(1)}, f32[256,512]{1,0:T(8,128)S(1)}, f32[4,112,273]{2,1,0:T(8,128)S(1)}) custom-call(s32[3]{0:T(128)S(1)} %pad_add_fusion.meta_ref, bf16[256,1792]{1,0:T(8,128)(2,1)S(1)} %pad_maximum_fusion.1.conved_ref, bf16[1792,640]{1,0:T(8,128)(2,1)S(1)} %pad_maximum_fusion.w_ref, bf16[16,384]{1,0:T(8,128)(2,1)S(1)} %copy-done.18, ...), custom_call_target="tpu_custom_call" | custom-call | flops 788529152 | bytes 3211264 | tf_op jit(solution)/shard_map/pallas_call | solution.py:209
  63.6 3.4 %shard_map.182 = bf16[256,1792]{1,0:T(8,128)(2,1)S(1)} custom-call(s32[3]{0:T(128)S(1)} %pad_add_fusion.meta_ref, bf16[256,64]{1,0:T(8,128)(2,1)S(1)} %get-tuple-element.32.refs_0_, f32[256,512]{1,0:T(8,128)S(1)} %get-tuple-element.33.refs_1_, f32[4,112,273]{2,1,0:T(8,128)S(1)} %get-tuple-element.21.refs_2_.refs_4_, ...), custom_call_target="tpu_custom_call" | custom-call | flops 570425344 | bytes 917504 | tf_op jit(solution)/shard_map/pallas_call | solution.py:331
  67.0 0.1 fusion.3
  67.1 1.0 collective-permute-start.6
  68.1 0.3 fusion.4
  68.4 1.8 %collective-permute-start.8 = (bf16[128,1792]{1,0:T(8,128)(2,1)S(1)}, bf16[128,1792]{1,0:T(8,128)(2,1)S(1)}, u32[]{:S(2)}, u32[]{:S(2)}) collective-permute-start(bf16[128,1792]{1,0:T(8,128)(2,1)S(1)} %get-tuple-element.46), channel_id=1, source_target_pairs={{0,16},{8,24},{16,0},{24,8},{1,17},{9,25},{17,1},{25,9},{2,18},{10... | collective-permute-start | bytes 1376264 | tf_op jit(solution)/shard_map/ppermute | solution.py:227
  70.2 5.2 %shard_map.181 = (bf16[256,1792]{1,0:T(8,128)(2,1)S(1)}, bf16[256,1792]{1,0:T(8,128)(2,1)S(1)}) custom-call(s32[3]{0:T(128)S(1)} %pad_add_fusion.meta_ref, bf16[256,64]{1,0:T(8,128)(2,1)S(1)} %get-tuple-element.26.refs_0_, bf16[256,64]{1,0:T(8,128)(2,1)S(1)} %get-tuple-element.27.refs_1_, f32[256,512]{1,0:T(8,128)S(1)} %get-tuple-element.28.refs_2_, ...), custom_call_target="tpu_custom_call" | custom-call | flops 1140850688 | bytes 1835008 | tf_op jit(solution)/shard_map/pallas_call | solution.py:331
  75.5 0.8 slice.55
  76.3 0.8 slice.61
  77.1 0.3 collective-permute-start.10
  77.4 1.1 collective-permute-start.5
  78.5 0.9 add_convert_fusion.3
  79.4 1.9 %collective-permute-start.7 = (bf16[128,1792]{1,0:T(8,128)(2,1)}, bf16[128,1792]{1,0:T(8,128)(2,1)}, u32[]{:S(2)}, u32[]{:S(2)}) collective-permute-start(bf16[128,1792]{1,0:T(8,128)(2,1)} %add_convert_fusion.3), channel_id=1, source_target_pairs={{0,16},{8,24},{16,0},{24,8},{1,17},{9,25},{17,1},{25,9},{2,18},{10... | collective-permute-start | bytes 1376264 | tf_op jit(solution)/shard_map/ppermute | solution.py:227
  81.2 0.9 add_convert_fusion.1
  82.1 0.8 collective-permute-start.9
  83.0 0.1 copy.39.col_ref
  83.1 0.7 shard_map.183
  83.8 10.8 %all_to_all.15 = bf16[8,8,640]{2,1,0:T(8,128)(2,1)S(1)} all-to-all(bf16[8,8,640]{2,1,0:T(8,128)(2,1)S(1)} %bitcast.34), channel_id=1, replica_groups=mesh['head'=4,'tok'=8] {'tok'}, dimensions={0} | all-to-all | bytes 163840 | tf_op jit(solution)/shard_map/all_to_all | solution.py:277
  94.6 4.1 %copy-done = f32[1,16,4,112,273]{4,3,2,1,0:T(8,128)S(1)} copy-done((f32[1,16,4,112,273]{4,3,2,1,0:T(8,128)S(1)}, f32[1,16,4,112,273]{4,3,2,1,0:T(8,128)}, u32[]{:S(2)}) %copy-start) | copy-done | bytes 7827480
  98.7 5.4 %shard_map.184 = bf16[64,512]{1,0:T(8,128)(2,1)S(1)} custom-call(bf16[64,640]{1,0:T(8,128)(2,1)S(1)} %bitcast.33, f32[1,16,4,112,273]{4,3,2,1,0:T(8,128)S(1)} %copy-done, bf16[16,384]{1,0:T(8,128)(2,1)S(1)} %copy-done.18, bf16[16,384]{1,0:T(8,128)(2,1)S(1)} %copy-done.17, f32[4,128]{1,0:T(4,128)S(1)} %pad.13.refs_9_.refs_11_.gain_ref), custom_call_target="tpu_custom_call" | custom-call | flops 250478592 | bytes 11010048 | tf_op jit(solution)/shard_map/pallas_call | solution.py:280
  104.1 8.3 %all_to_all.16 = bf16[8,8,512]{2,1,0:T(8,128)(2,1)S(1)} all-to-all(bf16[8,8,512]{2,1,0:T(8,128)(2,1)S(1)} %bitcast.35), channel_id=1, replica_groups=mesh['head'=4,'tok'=8] {'tok'}, dimensions={0} | all-to-all | bytes 131072 | tf_op jit(solution)/shard_map/all_to_all | solution.py:302
  112.4 0.7 shard_map.185
  113.1 8.2 %all_to_all.17 = bf16[4,8,1792]{2,1,0:T(8,128)(2,1)S(1)} all-to-all(bf16[4,8,1792]{2,1,0:T(8,128)(2,1)S(1)} %bitcast.32), channel_id=1, replica_groups=mesh['head'=4,'tok'=8] {'head'}, dimensions={0} | all-to-all | bytes 229376 | tf_op jit(solution)/shard_map/all_to_all | solution.py:364
  121.3 0.6 reduce_sum.12
  121.9 1.1 copy-done.4
  123.0 1.1 copy-done.6
  124.1 1.1 copy-done.8
  125.2 1.0 copy-done.20
  126.3 3.6 %shard_map.180 = (bf16[256,1792]{1,0:T(8,128)(2,1)S(1)}, f32[1,4,112,273]{3,2,1,0:T(8,128)S(1)}) custom-call(s32[3]{0:T(128)S(1)} %pad_add_fusion.meta_ref, bf16[256,64]{1,0:T(8,128)(2,1)S(1)} %get-tuple-element.19.refs_0_, f32[256,512]{1,0:T(8,128)S(1)} %copy-done.20, f32[4,112,273]{2,1,0:T(8,128)S(1)} %get-tuple-element.21.refs_2_.refs_4_, ...), custom_call_target="tpu_custom_call" | custom-call | flops 570425344 | bytes 917504 | tf_op jit(solution)/shard_map/pallas_call | solution.py:331
  129.9 0.9 copy-done.16
  130.8 1.1 copy.42
  131.9 2.0 %fusion = (bf16[1,128,1792]{2,1,0:T(8,128)(2,1)S(1)}, bf16[1,128,1792]{2,1,0:T(8,128)(2,1)S(1)}) fusion(bf16[128,1792]{1,0:T(8,128)(2,1)} %collective-permute-done.7, bf16[128,1792]{1,0:T(8,128)(2,1)} %collective-permute-done.5, bf16[256,1792]{1,0:T(8,128)(2,1)} %copy-done.16, bf16[128,1792]{1,0:T(8,128)(2,1)} %collective-permute-done.10, ...), kind=kLoop, calls=%fused_computation.7 | loop fusion | flops 2752512 | bytes 3670016 | tf_op jit(solution)/shard_map/concatenate | solution.py:359
  134.0 1.0 pad_maximum_fusion.2
  (59 shorter events, 0.2 us)
Async XLA Ops:
  1.4 6.2 %collective-permute-start = (bf16[2,1792]{1,0:T(2,128)(2,1)S(1)}, bf16[2,1792]{1,0:T(2,128)(2,1)S(1)}, u32[]{:S(2)}, u32[]{:S(2)}) collective-permute-start(bf16[2,1792]{1,0:T(2,128)(2,1)S(1)} %slice_bitcast_fusion), channel_id=1, source_target_pairs={{0,8},{8,16},{16,24},{1,9},{9,17},{17,25},{2,10},{10,18},{18,26},{... | collective-permute-start | bytes 21512 | tf_op jit(solution)/shard_map/ppermute | solution.py:372
  7.6 1.2 copy-start.15
  8.8 0.7 copy-start.21
  9.5 0.7 copy-start.24
  11.7 10.4 %copy-start.9 = (bf16[256,1792]{1,0:T(8,128)(2,1)}, bf16[256,1792]{1,0:T(8,128)(2,1)S(1)}, u32[]{:S(2)}) copy-start(bf16[256,1792]{1,0:T(8,128)(2,1)S(1)} %shard_map.175.conved_ref) | copy-start | bytes 2752516
  11.7 34.2 %collective-permute-start.2 = (bf16[256,1792]{1,0:T(8,128)(2,1)S(1)}, bf16[256,1792]{1,0:T(8,128)(2,1)S(1)}, u32[]{:S(2)}, u32[]{:S(2)}) collective-permute-start(bf16[256,1792]{1,0:T(8,128)(2,1)S(1)} %shard_map.175.conved_ref), channel_id=1, source_target_pairs={{0,16},{8,24},{16,0},{24,8},{1,17},{9,25},{17,1},{25,9},{2,18},{10... | collective-permute-start | bytes 2752520 | tf_op jit(solution)/shard_map/ppermute | solution.py:227
  15.0 32.5 %collective-permute-start.1 = (bf16[256,1792]{1,0:T(8,128)(2,1)S(1)}, bf16[256,1792]{1,0:T(8,128)(2,1)S(1)}, u32[]{:S(2)}, u32[]{:S(2)}) collective-permute-start(bf16[256,1792]{1,0:T(8,128)(2,1)S(1)} %shard_map.175.conved_ref), channel_id=1, source_target_pairs={{0,8},{8,0},{16,24},{24,16},{1,9},{9,1},{17,25},{25,17},{2,10},{10... | collective-permute-start | bytes 2752520 | tf_op jit(solution)/shard_map/ppermute | solution.py:227
  45.8 2.7 %copy-start.27 = (bf16[1792,512]{1,0:T(8,128)(2,1)S(1)}, bf16[1792,512]{1,0:T(8,128)(2,1)}, u32[]{:S(2)}) copy-start(bf16[1792,512]{1,0:T(8,128)(2,1)} %copy.43) | copy-start | bytes 5505028
  45.9 1.6 %copy-start.13 = (bf16[256,1792]{1,0:T(8,128)(2,1)}, bf16[256,1792]{1,0:T(8,128)(2,1)S(1)}, u32[]{:S(2)}) copy-start(bf16[256,1792]{1,0:T(8,128)(2,1)S(1)} %collective-permute-done.2.conved_ref) | copy-start | bytes 2752516
  46.0 14.4 %collective-permute-start.4 = (bf16[128,1792]{1,0:T(8,128)(2,1)S(1)}, bf16[128,1792]{1,0:T(8,128)(2,1)S(1)}, u32[]{:S(2)}, u32[]{:S(2)}) collective-permute-start(bf16[128,1792]{1,0:T(8,128)(2,1)S(1)} %slice.65), channel_id=1, source_target_pairs={{0,8},{8,0},{16,24},{24,16},{1,9},{9,1},{17,25},{25,17},{2,10},{10... | collective-permute-start | bytes 1376264 | tf_op jit(solution)/shard_map/ppermute | solution.py:227
  47.5 0.9 copy-start.11
  48.4 1.7 %copy-start.10 = (bf16[256,1792]{1,0:T(8,128)(2,1)S(1)}, bf16[256,1792]{1,0:T(8,128)(2,1)}, u32[]{:S(2)}) copy-start(bf16[256,1792]{1,0:T(8,128)(2,1)} %copy-done.9) | copy-start | bytes 2752516
  48.4 1.7 %copy-start.17 = (bf16[16,384]{1,0:T(8,128)(2,1)S(1)}, bf16[16,384]{1,0:T(8,128)(2,1)}, u32[]{:S(2)}) copy-start(bf16[16,384]{1,0:T(8,128)(2,1)} %constant.17.clone.b_ref.refs_8_.refs_10_) | copy-start | bytes 36868
  48.4 1.7 %copy-start.18 = (bf16[16,384]{1,0:T(8,128)(2,1)S(1)}, bf16[16,384]{1,0:T(8,128)(2,1)}, u32[]{:S(2)}) copy-start(bf16[16,384]{1,0:T(8,128)(2,1)} %constant.16.clone.a_ref.refs_7_.refs_9_) | copy-start | bytes 36868
  48.4 11.9 %collective-permute-start.3 = (bf16[128,1792]{1,0:T(8,128)(2,1)S(1)}, bf16[128,1792]{1,0:T(8,128)(2,1)S(1)}, u32[]{:S(2)}, u32[]{:S(2)}) collective-permute-start(bf16[128,1792]{1,0:T(8,128)(2,1)S(1)} %slice.64), channel_id=1, source_target_pairs={{0,16},{8,24},{16,0},{24,8},{1,17},{9,25},{17,1},{25,9},{2,18},{10... | collective-permute-start | bytes 1376264 | tf_op jit(solution)/shard_map/ppermute | solution.py:227
  50.1 3.9 %copy-start.14 = (bf16[256,1792]{1,0:T(8,128)(2,1)S(1)}, bf16[256,1792]{1,0:T(8,128)(2,1)}, u32[]{:S(2)}) copy-start(bf16[256,1792]{1,0:T(8,128)(2,1)} %copy-done.13) | copy-start | bytes 2752516
  53.3 0.8 copy-start.19
  54.1 3.1 %copy-start.12 = (bf16[256,1792]{1,0:T(8,128)(2,1)S(1)}, bf16[256,1792]{1,0:T(8,128)(2,1)}, u32[]{:S(2)}) copy-start(bf16[256,1792]{1,0:T(8,128)(2,1)} %copy-done.11) | copy-start | bytes 2752516
  57.2 13.0 %copy-start.3 = (f32[4,112,273]{2,1,0:T(8,128)}, f32[4,112,273]{2,1,0:T(8,128)S(1)}, u32[]{:S(2)}) copy-start(f32[4,112,273]{2,1,0:T(8,128)S(1)} %get-tuple-element.23.refs_4_.refs_6_) | copy-start | bytes 1467652
  60.3 9.9 %copy-start.5 = (f32[4,112,273]{2,1,0:T(8,128)}, f32[4,112,273]{2,1,0:T(8,128)S(1)}, u32[]{:S(2)}) copy-start(f32[4,112,273]{2,1,0:T(8,128)S(1)} %get-tuple-element.22.refs_3_.refs_5_) | copy-start | bytes 1467652
  60.4 3.1 %copy-start.1 = (bf16[4,128,1792]{2,1,0:T(8,128)(2,1)S(1)}, bf16[4,128,1792]{2,1,0:T(8,128)(2,1)}, u32[]{:S(2)}) copy-start(bf16[4,128,1792]{2,1,0:T(8,128)(2,1)} %pad.14) | copy-start | bytes 5505028
  63.6 6.7 %copy-start.7 = (f32[4,112,273]{2,1,0:T(8,128)}, f32[4,112,273]{2,1,0:T(8,128)S(1)}, u32[]{:S(2)}) copy-start(f32[4,112,273]{2,1,0:T(8,128)S(1)} %get-tuple-element.24.refs_5_.refs_7_) | copy-start | bytes 1467652
  67.0 1.1 copy-start.28
  67.1 11.4 %collective-permute-start.6 = (bf16[128,1792]{1,0:T(8,128)(2,1)S(1)}, bf16[128,1792]{1,0:T(8,128)(2,1)S(1)}, u32[]{:S(2)}, u32[]{:S(2)}) collective-permute-start(bf16[128,1792]{1,0:T(8,128)(2,1)S(1)} %get-tuple-element.45), channel_id=1, source_target_pairs={{0,8},{8,0},{16,24},{24,16},{1,9},{9,1},{17,25},{25,17},{2,10},{10... | collective-permute-start | bytes 1376264 | tf_op jit(solution)/shard_map/ppermute | solution.py:227
  68.4 12.8 %collective-permute-start.8 = (bf16[128,1792]{1,0:T(8,128)(2,1)S(1)}, bf16[128,1792]{1,0:T(8,128)(2,1)S(1)}, u32[]{:S(2)}, u32[]{:S(2)}) collective-permute-start(bf16[128,1792]{1,0:T(8,128)(2,1)S(1)} %get-tuple-element.46), channel_id=1, source_target_pairs={{0,16},{8,24},{16,0},{24,8},{1,17},{9,25},{17,1},{25,9},{2,18},{10... | collective-permute-start | bytes 1376264 | tf_op jit(solution)/shard_map/ppermute | solution.py:227
  76.3 6.7 %copy-start.25 = (s32[1,32,1]{1,2,0:T(1,128)S(1)}, s32[1,32,1]{1,2,0:T(1,128)}, u32[]{:S(2)}) copy-start(s32[1,32,1]{1,2,0:T(1,128)} %param.29) | copy-start | bytes 388
  76.3 6.8 %copy-start.22 = (f32[3,1792]{1,0:T(4,128)S(1)}, f32[3,1792]{1,0:T(4,128)}, u32[]{:S(2)}) copy-start(f32[3,1792]{1,0:T(4,128)} %taps_ref.3) | copy-start | bytes 64516
  76.3 6.8 %copy-start.23 = (bf16[1,32,1792]{2,1,0:T(8,128)(2,1)S(1)}, bf16[1,32,1792]{2,1,0:T(8,128)(2,1)}, u32[]{:S(2)}) copy-start(bf16[1,32,1792]{2,1,0:T(8,128)(2,1)} %param.18) | copy-start | bytes 344068
  76.3 6.8 %copy-start.26 = (s32[1,32]{1,0:T(1,128)S(1)}, s32[1,32]{1,0:T(1,128)}, u32[]{:S(2)}) copy-start(s32[1,32]{1,0:T(1,128)} %slot_ref.1) | copy-start | bytes 388
  77.1 54.8 %collective-permute-start.10 = (bf16[128,1792]{1,0:T(8,128)(2,1)}, bf16[128,1792]{1,0:T(8,128)(2,1)}, u32[]{:S(2)}, u32[]{:S(2)}) collective-permute-start(bf16[128,1792]{1,0:T(8,128)(2,1)} %slice.61), channel_id=1, source_target_pairs={{0,16},{8,24},{16,0},{24,8},{1,17},{9,25},{17,1},{25,9},{2,18},{10... | collective-permute-start | bytes 1376264 | tf_op jit(solution)/shard_map/ppermute | solution.py:227
  77.4 54.5 %collective-permute-start.5 = (bf16[128,1792]{1,0:T(8,128)(2,1)}, bf16[128,1792]{1,0:T(8,128)(2,1)}, u32[]{:S(2)}, u32[]{:S(2)}) collective-permute-start(bf16[128,1792]{1,0:T(8,128)(2,1)} %slice.55), channel_id=1, source_target_pairs={{0,8},{8,0},{16,24},{24,16},{1,9},{9,1},{17,25},{25,17},{2,10},{10... | collective-permute-start | bytes 1376264 | tf_op jit(solution)/shard_map/ppermute | solution.py:227
  79.4 52.6 %collective-permute-start.7 = (bf16[128,1792]{1,0:T(8,128)(2,1)}, bf16[128,1792]{1,0:T(8,128)(2,1)}, u32[]{:S(2)}, u32[]{:S(2)}) collective-permute-start(bf16[128,1792]{1,0:T(8,128)(2,1)} %add_convert_fusion.3), channel_id=1, source_target_pairs={{0,16},{8,24},{16,0},{24,8},{1,17},{9,25},{17,1},{25,9},{2,18},{10... | collective-permute-start | bytes 1376264 | tf_op jit(solution)/shard_map/ppermute | solution.py:227
  82.1 49.8 %collective-permute-start.9 = (bf16[128,1792]{1,0:T(8,128)(2,1)}, bf16[128,1792]{1,0:T(8,128)(2,1)}, u32[]{:S(2)}, u32[]{:S(2)}) collective-permute-start(bf16[128,1792]{1,0:T(8,128)(2,1)} %add_convert_fusion.1), channel_id=1, source_target_pairs={{0,8},{8,0},{16,24},{24,16},{1,9},{9,1},{17,25},{25,17},{2,10},{10... | collective-permute-start | bytes 1376264 | tf_op jit(solution)/shard_map/ppermute | solution.py:227
  94.6 4.1 %copy-start = (f32[1,16,4,112,273]{4,3,2,1,0:T(8,128)S(1)}, f32[1,16,4,112,273]{4,3,2,1,0:T(8,128)}, u32[]{:S(2)}) copy-start(f32[1,16,4,112,273]{4,3,2,1,0:T(8,128)} %copy.34.refs_6_.refs_8_.cache_ref) | copy-start | bytes 23482372
  98.7 13.7 %copy-start.2 = (bf16[4,128,1792]{2,1,0:T(8,128)(2,1)S(1)}, bf16[4,128,1792]{2,1,0:T(8,128)(2,1)}, u32[]{:S(2)}) copy-start(bf16[4,128,1792]{2,1,0:T(8,128)(2,1)} %pad.14) | copy-start | bytes 5505028
  121.9 1.1 copy-start.4
  123.0 1.1 copy-start.6
  124.1 1.1 copy-start.8
  125.2 1.0 copy-start.20
  129.9 0.9 copy-start.16

commit v2 on v0

--- a/solution.py
+++ b/solution.py
@@ -1,8 +1,12 @@
+import functools
 import math
 
 import jax
 import jax.numpy as jnp
+import numpy as np
 from jax import lax
+from jax.experimental import pallas as pl
+from jax.experimental.pallas import tpu as pltpu
 from jax.sharding import PartitionSpec as P
 
 D = 1792
@@ -10,6 +14,550 @@
 F = 16
 STRETCH = 1024
 DEC = 32
+QUAD = F * F
+PHI = 1 + F + QUAD
+WIDE = 128
+PHI_WIDE = QUAD + 128
+MIB = 1 << 20
+BF = jnp.bfloat16
+F32 = jnp.float32
+
+
+def lanes_of(size):
+    return lax.broadcasted_iota(jnp.int32, (F, size), 1), lax.broadcasted_iota(jnp.int32, (F, size), 0)
+
+
+def ones_where(mask):
+    return jnp.where(mask, 1.0, 0.0).astype(BF)
+
+
+def spreader():
+    lane, entry = lanes_of(PHI_WIDE)
+    return ones_where(jnp.where(lane < QUAD, lane >> 4, lane & (F - 1)) == entry)
+
+
+def dot(left, right, contract=((1,), (0,))):
+    return lax.dot_general(left, right, (contract, ((), ())), preferred_element_type=F32)
+
+
+def phi_of(vectors, pick):
+    spread = dot(vectors, pick)
+    a, b = spread[:, :QUAD], spread[:, QUAD:]
+    quad = a * jnp.concatenate([b] * (QUAD // 128), axis=1) * (1.0 / math.sqrt(2.0 * F))
+    lane = lax.broadcasted_iota(jnp.int32, b.shape, 1)
+    rest = jnp.where(lane < F, b * (1.0 / math.sqrt(math.sqrt(F))), jnp.where(lane == F, 1.0, 0.0))
+    return jnp.concatenate([quad, rest], axis=1)
+
+
+def unit_rows(values):
+    values = values.astype(F32)
+    total = jnp.sum(values * values, axis=-1, keepdims=True)
+    return values, lax.rsqrt(total * (1.0 / D) + 1e-05)
+
+
+def column(row):
+    size = row.shape[1]
+    same = lax.broadcasted_iota(jnp.int32, (size, size), 0) == lax.broadcasted_iota(jnp.int32, (size, size), 1)
+    return jnp.sum(jnp.where(same, row, 0), axis=1, keepdims=True)
+
+
+def projection(w_ref, heads):
+    pieces = [w_ref[h, :F, :] for h in range(heads)] + [w_ref[h, F : 2 * F, :] for h in range(heads)]
+    for h in range(heads):
+        pieces += [w_ref[h, 2 * F :, :], jnp.zeros((WIDE - DH, D), w_ref.dtype)]
+    return jnp.concatenate(pieces, axis=0)
+
+
+def out_projection(w_ref, heads):
+    pieces = []
+    for h in range(heads):
+        pieces += [w_ref[h * DH : (h + 1) * DH, :], jnp.zeros((WIDE - DH, D), w_ref.dtype)]
+    return jnp.concatenate(pieces, axis=0)
+
+
+def conv_kernel(tokens_ref, tail_ref, gain_ref, taps_ref, low, top, begin, end):
+    rows = tokens_ref.shape[0]
+    half = rows // 2
+    gain = gain_ref[...].reshape(1, D)
+    taps = taps_ref[...]
+    _, factor = unit_rows(tokens_ref[...])
+    step = 256
+    row = lax.broadcasted_iota(jnp.int32, (rows, step), 0)
+    for at in range(0, D, step):
+        cols = slice(at, at + step)
+        normed = tokens_ref[:, cols].astype(F32) * factor * gain[:, cols]
+        normed = normed.astype(BF)
+        begin[:, cols] = normed[:16]
+        end[:, cols] = normed[rows - 16 :]
+        normed = normed.astype(F32)
+        tail = tail_ref[:, cols].astype(F32)
+        one = jnp.where(row == 0, tail[1:2], pltpu.roll(normed, 1, 0))
+        two = pltpu.roll(normed, 2, 0)
+        two = jnp.where(row == 0, tail[0:1], jnp.where(row == 1, tail[1:2], two))
+        total = taps[0:1, cols] * two + taps[1:2, cols] * one + taps[2:3, cols] * normed
+        total = total.astype(BF)
+        top[:, cols] = total[:half]
+        low[:, cols] = total[half:]
+
+
+def rim_kernel(first_ref, top_ref, begin_ref, end_ref, taps_ref, out_ref, begin, end, taps, rows, sem):
+    copies = [
+        pltpu.make_async_copy(src, place, sem.at[n])
+        for n, (src, place) in enumerate([(begin_ref, begin), (end_ref, end), (taps_ref, taps)])
+    ]
+    for copy in copies:
+        copy.start()
+    for copy in copies:
+        copy.wait()
+    now = begin[...].astype(F32)
+    last = end[...].astype(F32)
+    row = lax.broadcasted_iota(jnp.int32, now.shape, 0)
+    one = jnp.where(row == 0, last[15:16], pltpu.roll(now, 1, 0))
+    two = jnp.where(row == 0, last[14:15], jnp.where(row == 1, last[15:16], pltpu.roll(now, 2, 0)))
+    rows[...] = (taps[0:1, :] * two + taps[1:2, :] * one + taps[2:3, :] * now).astype(BF)
+
+    @pl.when(first_ref[0] != 0)
+    def _():
+        back = pltpu.make_async_copy(rows, out_ref.at[:16], sem.at[3])
+        back.start()
+        back.wait()
+
+
+def block_part(slot, heads, length, conved, w_ref, sums, own, queries):
+    rows = conved.shape[0]
+    qkv = dot(conved, projection(w_ref, heads), ((1,), (1,))).astype(BF)
+    queries[...] = qkv[:, : heads * F]
+    live = length - rows * (lax.axis_index("head") ^ slot)
+    row = lax.broadcasted_iota(jnp.int32, (rows, rows), 0)
+    col = lax.broadcasted_iota(jnp.int32, (rows, rows), 1)
+    allowed = (col <= row) & (col < live)
+    live_row = lax.broadcasted_iota(jnp.int32, (rows, WIDE), 0) < live
+    pick = spreader()
+    for head in range(heads):
+        q = qkv[:, head * F : head * F + F]
+        k = qkv[:, (heads + head) * F : (heads + head) * F + F]
+        at = 2 * heads * F + head * WIDE
+        v = qkv[:, at : at + WIDE]
+        key_phi = phi_of(k, pick).astype(BF)
+        v_live = jnp.where(live_row, v.astype(F32), 0.0).astype(BF)
+        sums[head] = dot(key_phi, v_live, ((0,), (0,)))
+        inner = dot(q, k, ((1,), (1,))) * (1.0 / math.sqrt(F))
+        weights = jnp.where(allowed, 1.0 + inner + 0.5 * inner * inner, 0.0).astype(BF)
+        own[head] = dot(weights, v)
+
+
+def finish_part(slot, heads, length, states, own, queries, gain_ref, w_ref, top, low):
+    rows = queries.shape[0]
+    half = rows // 2
+    live = length - rows * (lax.axis_index("head") ^ slot)
+    live_row = lax.broadcasted_iota(jnp.int32, (rows, WIDE), 0) < live
+    pick = spreader()
+    gains = gain_ref[...].reshape(1, heads * DH)
+    zeros = jnp.zeros((1, WIDE - DH), F32)
+    parts = []
+    for head in range(heads):
+        query_phi = phi_of(queries[:, head * F : head * F + F], pick).astype(BF)
+        total = own[head] + dot(query_phi, states[head])
+        square = jnp.sum(total * total, axis=-1, keepdims=True)
+        gain = jnp.concatenate([gains[:, head * DH : (head + 1) * DH], zeros], axis=1)
+        total = total * lax.rsqrt(square * (1.0 / DH) + 1e-05) * gain
+        parts.append(jnp.where(live_row, total, 0.0).astype(BF))
+    attended = jnp.concatenate(parts, axis=1)
+    w_out = out_projection(w_ref, heads)
+    top[...] = dot(attended[:half], w_out).astype(BF)
+    top.push()
+    low[...] = dot(attended[half:], w_out).astype(BF)
+    low.push()
+
+
+def first_kernel(heads, len_ref, low, top, w_ref, sums, own, queries):
+    conved = jnp.concatenate([top[...], low[...]], axis=0)
+    block_part(0, heads, len_ref[0], conved, w_ref, sums, own, queries)
+
+
+def second_kernel(heads, len_ref, low1, top1, w_ref, low2, top2, sums1, own1, queries1, sums2, own2, queries2):
+    conved = jnp.concatenate([top1[...], low1[...]], axis=0)
+    block_part(1, heads, len_ref[0], conved, w_ref, sums1, own1, queries1)
+    for out in (sums1, own1, queries1):
+        out.push()
+    conved = jnp.concatenate([top2[...], low2[...]], axis=0)
+    block_part(2, heads, len_ref[0], conved, w_ref, sums2, own2, queries2)
+
+
+def third_kernel(heads, capacity, len_ref, low, top, w_ref, cache_ref, sums0, sums1, sums2, gain_ref, out_w_ref, items_ref, owner_ref,
+                 top3, low3, part, states, state_next, sums3, own3, queries3, states3):
+    length = len_ref[0]
+    mine = lax.axis_index("head")
+    conved = jnp.concatenate([top[...], low[...]], axis=0)
+    block_part(3, heads, length, conved, w_ref, sums3, own3, queries3)
+    sums = [sums0, sums1, sums2, sums3]
+    olds = []
+    pad = jnp.zeros((PHI_WIDE - PHI, DH), F32)
+    for head in range(heads):
+        old = [cache_ref[F + 1 :, head, :], cache_ref[1 : F + 1, head, :], cache_ref[0:1, head, :], pad]
+        old = jnp.concatenate([jnp.concatenate(old, axis=0), jnp.zeros((PHI_WIDE, WIDE - DH), F32)], axis=1)
+        olds.append(old)
+
+    def prefix(slot, head):
+        before = olds[head]
+        for other in range(4):
+            if other != slot:
+                before = before + ((mine ^ other) < (mine ^ slot)).astype(F32) * sums[other][head]
+        return before.astype(BF)
+
+    for head in range(heads):
+        states3[head] = prefix(3, head)
+    finish_part(3, heads, length, states3, own3, queries3, gain_ref, out_w_ref, top3, low3)
+    for slot in range(3):
+        for head in range(heads):
+            states[slot, head] = prefix(slot, head)
+    states.push()
+    return_part(heads, capacity, items_ref, owner_ref, out_w_ref, part)
+    part.push()
+    for head in range(heads):
+        total = olds[head] + (sums0[head] + sums1[head]) + (sums2[head] + sums3[head])
+        total = total[:, :DH]
+        state_next[0, F + 1 :, head, :] = total[:QUAD]
+        state_next[0, 1 : F + 1, head, :] = total[QUAD : QUAD + F]
+        state_next[0, 0:1, head, :] = total[QUAD + F : QUAD + F + 1]
+
+
+def fourth_kernel(heads, len_ref, states, queries1, own1, gain_ref, out_w_ref, queries2, own2, top1, low1, top2, low2):
+    finish_part(1, heads, len_ref[0], states.part(1), own1, queries1, gain_ref, out_w_ref, top1, low1)
+    finish_part(2, heads, len_ref[0], states.part(2), own2, queries2, gain_ref, out_w_ref, top2, low2)
+
+
+def fifth_kernel(heads, len_ref, states, queries0, own0, gain_ref, out_w_ref, top0, low0):
+    finish_part(0, heads, len_ref[0], states.part(0), own0, queries0, gain_ref, out_w_ref, top0, low0)
+
+
+def add_kernel(a_ref, b_ref, c_ref, d_ref, ab_ref, cd_ref):
+    ab_ref[...] = (a_ref[...].astype(F32) + b_ref[...].astype(F32)).astype(BF)
+    cd_ref[...] = (c_ref[...].astype(F32) + d_ref[...].astype(F32)).astype(BF)
+
+
+def total_kernel(*refs):
+    parts, out_ref = refs[:-1], refs[-1]
+    half = out_ref.shape[1] // 2
+    for order in range(2):
+        mine = [part[...].astype(F32) for part in parts[order::2]]
+        out_ref[0, order * half : (order + 1) * half, :] = functools.reduce(lambda a, b: a + b, mine).astype(BF)
+
+
+def placing_rank(owners_row, axis):
+    down = lax.broadcasted_iota(jnp.int32, (DEC, DEC), 0)
+    along = lax.broadcasted_iota(jnp.int32, (DEC, DEC), 1)
+    earlier = down < along if axis == 0 else along < down
+    return jnp.sum(jnp.where(earlier & (column(owners_row) == owners_row), 1, 0), axis=axis, keepdims=True)
+
+
+def send_kernel(heads, capacity, tokens_ref, tail_ref, gain_ref, taps_ref, owner_ref, slot_ref, w_ref, out):
+    tokens, factor = unit_rows(tokens_ref[...])
+    normed = (tokens * factor * gain_ref[...].reshape(1, D)).astype(BF).astype(F32)
+    tail = tail_ref[...].astype(F32)
+    taps = taps_ref[...]
+    conved = taps[0:1, :] * tail[:, 0, :] + taps[1:2, :] * tail[:, 1, :]
+    conved = (conved + taps[2:3, :] * normed).astype(BF)
+    owners = owner_ref[...]
+    target = owners * capacity + placing_rank(owners, 0)
+    placing = lax.broadcasted_iota(jnp.int32, (out.shape[0], DEC), 0) == target
+    cache_slot = jnp.sum(jnp.where(placing, slot_ref[...] + 1, 0), axis=1, keepdims=True) - 1
+    qkv = dot(conved, projection(w_ref, heads), ((1,), (1,))).astype(BF)
+    sent = dot(ones_where(placing), qkv)
+    lane = lax.broadcasted_iota(jnp.int32, sent.shape, 1)
+    mark = 2 * heads * F + DH
+    out[...] = jnp.where(lane == mark, cache_slot.astype(F32), sent).astype(BF)
+
+
+def cache_spreaders(heads):
+    lane, entry = lanes_of(PHI * heads)
+    feature = lane >> (heads.bit_length() - 1)
+    quad = feature - (1 + F)
+    a = jnp.where(quad < 0, feature - 1, quad >> 4)
+    return ones_where(a == entry), ones_where((quad >= 0) & ((quad & (F - 1)) == entry))
+
+
+def serve_kernel(heads, items_ref, gain_ref, cache_ref, wait_ref, out_ref, state, sem):
+    count = items_ref.shape[0]
+    mark = 2 * heads * F + DH
+    flying = 4
+    copies = [pltpu.make_async_copy(cache_ref.at[0, n], state.at[n], sem.at[n]) for n in range(state.shape[0])]
+    for copy in copies[:flying]:
+        copy.start()
+    first, second = cache_spreaders(heads)
+    phis = []
+    for head in range(heads):
+        q = items_ref[:, head * F : head * F + F]
+        a = dot(q, first)
+        b = dot(q, second)
+        lane = lax.broadcasted_iota(jnp.int32, a.shape, 1)
+        scale = jnp.where(lane < heads * (F + 1), 1.0 / math.sqrt(math.sqrt(F)), b * (1.0 / math.sqrt(2.0 * F)))
+        value = jnp.where(lane < heads, 1.0, a * scale)
+        phis.append(jnp.where((lane & (heads - 1)) == head, value, 0.0).astype(BF))
+    phis = jnp.concatenate(phis, axis=0)
+    slots = jnp.concatenate([items_ref[:, mark : mark + 1].astype(F32)] * heads, axis=0)
+    total = jnp.zeros((heads * count, DH), F32)
+    for n, copy in enumerate(copies):
+        copy.wait()
+        for later in copies[n + flying : n + flying + 1]:
+            later.start()
+        table = dot(phis, state[n].reshape(PHI * heads, DH).astype(BF))
+        total = total + jnp.where(slots == float(n), table, 0.0)
+    gains = gain_ref[...].reshape(1, heads * DH)
+    for head in range(heads):
+        q = items_ref[:, head * F : head * F + F].astype(F32)
+        k = items_ref[:, (heads + head) * F : (heads + head) * F + F].astype(F32)
+        at = 2 * heads * F + head * WIDE
+        v = items_ref[:, at : at + DH].astype(F32)
+        inner = jnp.sum(q * k, axis=-1, keepdims=True) * (1.0 / math.sqrt(F))
+        value = total[head * count : (head + 1) * count, :] + (1.0 + inner + 0.5 * inner * inner) * v
+        square = jnp.sum(value * value, axis=-1, keepdims=True)
+        value = value * lax.rsqrt(square * (1.0 / DH) + 1e-05) * gains[:, head * DH : (head + 1) * DH]
+        out_ref[:, head * WIDE : head * WIDE + DH] = value.astype(BF)
+        out_ref[:, head * WIDE + DH : (head + 1) * WIDE] = jnp.zeros((count, WIDE - DH), BF)
+
+
+def return_part(heads, capacity, items_ref, owner_ref, w_ref, out):
+    owners = owner_ref[...]
+    target = column(owners) * capacity + placing_rank(owners, 1)
+    placing = lax.broadcasted_iota(jnp.int32, (DEC, items_ref.shape[0]), 1) == target
+    attended = dot(ones_where(placing), items_ref[...]).astype(BF)
+    out[...] = dot(attended, out_projection(w_ref, heads)).astype(BF)
+
+
+class Fetched:
+    def __init__(self, copy, place):
+        self.copy, self.place, self.here = copy, place, False
+        self.shape, self.dtype = place.shape, place.dtype
+
+    def __getitem__(self, index):
+        if not self.here:
+            self.copy.wait()
+            self.here = True
+        return self.place[index]
+
+    def part(self, number):
+        self[0, 0]
+        return self.place.at[number]
+
+
+class Pushed:
+    def __init__(self, copy, place):
+        self.copy, self.place, self.gone = copy, place, False
+        self.shape, self.dtype = place.shape, place.dtype
+
+    def __getitem__(self, index):
+        return self.place[index]
+
+    def __setitem__(self, index, value):
+        self.place[index] = value
+
+    def push(self):
+        if not self.gone:
+            self.copy.start()
+            self.gone = True
+
+
+def hbm_call(kernel, outs, flops, size, scalars=(), picked=None, inner=(), waits=()):
+    def run(*args):
+        count, many = len(args), len(outs)
+
+        def shape_in(n):
+            return args[n].shape[2:] if n == picked else args[n].shape
+
+        def body(*refs):
+            numbers, sources = refs[: len(scalars)], refs[len(scalars) : len(scalars) + count]
+            rest = refs[len(scalars) + count + len(waits) :]
+            targets, places, results, own, sem = (
+                rest[:many],
+                rest[many : many + count],
+                rest[many + count : 2 * many + count],
+                rest[2 * many + count : -1],
+                rest[-1],
+            )
+            ins = []
+            for n, (source, place) in enumerate(zip(sources, places)):
+                if n == picked:
+                    source = source.at[0, numbers[-1][0]]
+                copy = pltpu.make_async_copy(source, place, sem.at[n])
+                copy.start()
+                ins.append(Fetched(copy, place))
+            done = [
+                Pushed(pltpu.make_async_copy(result, target, sem.at[count + n]), result)
+                for n, (result, target) in enumerate(zip(results, targets))
+            ]
+            kernel(*numbers[: len(scalars) - (picked is not None)], *ins, *done, *own)
+            for out in done:
+                out.push()
+            for one in ins:
+                if not one.here:
+                    one.copy.wait()
+            for out in done:
+                out.copy.wait()
+
+        hbm = pl.BlockSpec(memory_space=pltpu.HBM)
+        return pl.pallas_call(
+            body,
+            out_shape=[pltpu.HBM(o.shape, o.dtype) for o in outs],
+            in_specs=[pl.BlockSpec(memory_space=pltpu.SMEM)] * len(scalars)
+            + [hbm] * count
+            + [pl.BlockSpec(memory_space=pl.ANY)] * len(waits),
+            out_specs=[hbm] * many,
+            scratch_shapes=[pltpu.VMEM(shape_in(n), args[n].dtype) for n in range(count)]
+            + [pltpu.VMEM(o.shape, o.dtype) for o in outs]
+            + [pltpu.VMEM(o.shape, o.dtype) for o in inner]
+            + [pltpu.SemaphoreType.DMA((count + many,))],
+            compiler_params=pltpu.CompilerParams(vmem_limit_bytes=32 * MIB),
+            cost_estimate=pl.CostEstimate(flops=flops, bytes_accessed=size, transcendentals=0),
+        )(*scalars, *[pltpu.with_memory_space_constraint(a, pltpu.HBM) for a in args], *waits)
+
+    return run
+
+
+def call(kernel, outs, flops, size):
+    def run(*args):
+        many = isinstance(outs, (list, tuple))
+        spec = pl.BlockSpec(memory_space=pltpu.VMEM)
+        return pl.pallas_call(
+            kernel,
+            out_shape=outs,
+            in_specs=[spec] * len(args),
+            out_specs=[spec] * len(outs) if many else spec,
+            compiler_params=pltpu.CompilerParams(vmem_limit_bytes=16 * MIB),
+            cost_estimate=pl.CostEstimate(flops=flops, bytes_accessed=size, transcendentals=0),
+        )(*args)
+
+    return run
+
+
+def shape(*dims, dtype=BF):
+    return jax.ShapeDtypeStruct(dims, dtype)
+
+
+def across(array, by):
+    return lax.ppermute(array, "head", [(i, i ^ by) for i in range(4)])
+
+
+def local_square(
+    stretch_tokens,
+    stretch_tail,
+    decode_tokens,
+    decode_tail,
+    norm_gain,
+    conv_taps,
+    qkv_weight,
+    out_gain,
+    out_weight,
+    state_cache,
+    stretch_len,
+    stretch_slot,
+    decode_slot,
+    decode_owner,
+):
+    heads = qkv_weight.shape[1]
+    rows = stretch_tokens.shape[1]
+    half = rows // 2
+    wide = heads * (2 * F + WIDE)
+    me = lax.axis_index("head").reshape(1)
+    w_in = jnp.transpose(qkv_weight, (1, 2, 0))
+    cache = jnp.transpose(state_cache, (0, 1, 4, 2, 3))
+    hbm = pl.BlockSpec(memory_space=pltpu.HBM)
+    in_vmem = pl.BlockSpec(memory_space=pltpu.VMEM)
+    anywhere = pl.BlockSpec(memory_space=pl.ANY)
+    piece, ends = shape(half, D), shape(16, D)
+
+    low, top, begin, end = hbm_call(conv_kernel, [piece, piece, ends, ends], 20 * rows * D, 4 * rows * D)(
+        stretch_tokens[0], stretch_tail[0], norm_gain, conv_taps
+    )
+    low_x = across(low, 1)
+    low_y = across(low, 2)
+    end = from_behind(end, "head", 1)
+
+    groups = lax.axis_size("tok")
+    capacity = max(2, 2 * DEC // groups)
+    count = groups * capacity
+    owner_row = decode_owner.reshape(1, DEC)
+    (sent,) = hbm_call(functools.partial(send_kernel, heads, capacity), [shape(count, wide)], 2 * DEC * D * wide, 2 * D * wide)(
+        decode_tokens[0], decode_tail[0], norm_gain, conv_taps, owner_row, decode_slot, w_in
+    )
+    top = pl.pallas_call(
+        lambda first_ref, top_ref, begin_ref, end_ref, taps_ref, wait_ref, *refs: rim_kernel(
+            first_ref, top_ref, begin_ref, end_ref, taps_ref, *refs
+        ),
+        out_shape=pltpu.HBM((half, D), BF),
+        in_specs=[pl.BlockSpec(memory_space=pltpu.SMEM)] + [hbm] * 4 + [anywhere],
+        out_specs=hbm,
+        scratch_shapes=[pltpu.VMEM((16, D), BF), pltpu.VMEM((16, D), BF), pltpu.VMEM((3, D), F32), pltpu.VMEM((16, D), BF)]
+        + [pltpu.SemaphoreType.DMA((4,))],
+        input_output_aliases={1: 0},
+        compiler_params=pltpu.CompilerParams(vmem_limit_bytes=16 * MIB),
+        cost_estimate=pl.CostEstimate(flops=16 * D, bytes_accessed=128 * D, transcendentals=0),
+    )(me, *[pltpu.with_memory_space_constraint(a, pltpu.HBM) for a in (top, begin, end, conv_taps)], sent)
+    top_x = across(top, 1)
+    top_y = across(top, 2)
+    items = lax.all_to_all(sent.reshape(groups, capacity, wide), "tok", split_axis=0, concat_axis=0, tiled=True)
+
+    length = stretch_len.astype(jnp.int32)
+    slot = stretch_slot.astype(jnp.int32)
+    sums, own = shape(heads, PHI_WIDE, WIDE, dtype=F32), shape(heads, rows, WIDE, dtype=F32)
+    queries, states = shape(rows, heads * F), shape(heads, PHI_WIDE, WIDE)
+    block_flops = 2 * rows * D * wide + 6 * heads * rows * rows * WIDE
+    finish_flops = 2 * rows * heads * WIDE * (D + PHI_WIDE)
+    sums0, own0, queries0 = hbm_call(
+        functools.partial(first_kernel, heads), [sums, own, queries], block_flops, 4 * rows * D, scalars=[length], waits=[sent]
+    )(low, top, w_in)
+    served = pl.pallas_call(
+        functools.partial(serve_kernel, heads),
+        in_specs=[in_vmem, in_vmem, hbm, anywhere],
+        out_specs=in_vmem,
+        out_shape=shape(count, heads * WIDE),
+        scratch_shapes=[pltpu.VMEM(cache.shape[1:], F32), pltpu.SemaphoreType.DMA((cache.shape[1],))],
+        compiler_params=pltpu.CompilerParams(vmem_limit_bytes=32 * MIB),
+        cost_estimate=pl.CostEstimate(
+            flops=2 * cache.shape[1] * heads * heads * DH * PHI * count,
+            bytes_accessed=4 * cache.shape[1] * heads * WIDE * PHI,
+            transcendentals=0,
+        ),
+    )(items.reshape(count, wide), out_gain, pltpu.with_memory_space_constraint(cache, pltpu.HBM), queries0)
+    returned = lax.all_to_all(
+        served.reshape(groups, capacity, heads * WIDE), "tok", split_axis=0, concat_axis=0, tiled=True
+    ).reshape(count, heads * WIDE)
+    low_y, top_x = lax.optimization_barrier((low_y, top_x, served))[:2]
+    low_xy = across(low_y, 1)
+    top_xy = across(top_x, 2)
+    sums1, own1, queries1, sums2, own2, queries2 = hbm_call(
+        functools.partial(second_kernel, heads), [sums, own, queries] * 2, 2 * block_flops, 4 * rows * D, scalars=[length], waits=[served]
+    )(low_x, top_x, w_in, low_y, top_y)
+
+    returned, low_xy = lax.optimization_barrier((returned, low_xy, queries2))[:2]
+    top3, low3, part, all_states, state_next = hbm_call(
+        functools.partial(third_kernel, heads, capacity),
+        [piece, piece, shape(DEC, D), shape(3, *states.shape), shape(1, PHI, heads, DH, dtype=F32)],
+        block_flops + finish_flops,
+        8 * rows * D,
+        scalars=[length, slot],
+        picked=3,
+        inner=[sums, own, queries, states],
+    )(low_xy, top_xy, w_in, cache, sums0, sums1, sums2, out_gain, out_weight, returned, owner_row)
+    via_x = across(top3, 1)
+    via_y = across(low3, 2)
+    top1, low1, top2, low2 = hbm_call(
+        functools.partial(fourth_kernel, heads), [piece] * 4, 2 * finish_flops, 4 * rows * D, scalars=[length]
+    )(all_states, queries1, own1, out_gain, out_weight, queries2, own2)
+    one_x = across(top1, 1)
+    one_y = across(low2, 2)
+    part = lax.optimization_barrier((part, top1))[0]
+    shares = lax.all_to_all(part.reshape(4, DEC // 4, D), "head", split_axis=0, concat_axis=0, tiled=True)
+    two_y, two_x = call(add_kernel, [piece, piece], 0, 6 * rows * D)(top2, via_x, low1, via_y)
+    two_y = across(two_y, 2)
+    two_x = across(two_x, 1)
+    top0, low0 = hbm_call(
+        functools.partial(fifth_kernel, heads), [piece] * 2, finish_flops, 4 * rows * D, scalars=[length], waits=[two_x, two_y][:0]
+    )(all_states, queries0, own0, out_gain, out_weight)
+    state_next = jnp.transpose(state_next, (0, 2, 3, 1))
+    decode_out = jnp.sum(shares.astype(F32), axis=0).astype(BF)
+    stretch_out = call(total_kernel, shape(1, rows, D), 0, 8 * rows * D)(top0, low0, one_x, one_y, two_y, two_x)
+    return (stretch_out, decode_out[None], state_next)
 
 
 def from_behind(array, axis, by):
@@ -206,4 +754,5 @@
         P("tok", None, None),
     )
     out_specs = (P("tok", "head", None), P("tok", "head", None), P("tok", "head", None, None))
-    return jax.shard_map(local, mesh=mesh, in_specs=in_specs, out_specs=out_specs, check_vma=False)
+    chosen = local_square if mesh.shape["head"] == 4 else local
+    return jax.shard_map(chosen, mesh=mesh, in_specs=in_specs, out_specs=out_specs, check_vma=False)

time: 173 us -> 106 us (0.61)
  waiting for transfers between devices: 77.1 us -> 12.9 us
  Pallas kernels: 0 us -> 48.2 us
  matrix products: 39.7 us -> 0 us
  between operations: 16.1 us -> 2.23 us
  starting transfers between devices: 18.5 us -> 31.9 us
  other arithmetic: 10.5 us -> 0.63 us
    reduce_scatter x1 -> x0, waiting for transfers between devices: 48.8 us -> none  [local(): lax.psum_scatter(jnp.dot(part_rows, out_weight, preferred_element_type=jn...]
    pallas_call x0 -> x11, Pallas kernels: none -> 48.2 us  [the longest x7 38.7 us: run(): pl.pallas_call(body, out_shape=[pltpu.HBM(o.shape, o.dtype) for o in outs...]
    dot_general x10 -> x0, matrix products: 39.7 us -> none  [the longest x1 10.5 us: decode_items(): jnp.einsum('nhp,shdp->nshd', features(queries), cache_own, precision=lax....]
    unnamed x4 -> x0, waiting for transfers between devices: 16.9 us -> none
    ppermute x0 -> x12, starting transfers between devices: none -> 13.6 us  [across(): return lax.ppermute(array, 'head', [(i, i ^ by) for i in range(4)])]
    ppermute x0 -> x12, waiting for transfers between devices: none -> 4.94 us  [across(): return lax.ppermute(array, 'head', [(i, i ^ by) for i in range(4)])]
    unnamed x33 -> x34, local copies, waits for them, and re-layouts: 5.23 us -> 9.72 us
    convert_element_type x7 -> x0, other arithmetic: 3.83 us -> none  [the longest x1 1.49 us: convolve(): return total.astype(jnp.bfloat16)]
  transfers between devices with their start and end apart: 7 -> 16, of which waited for: 6 -> 3; matrix products, arithmetic and copies ran while one was open for 30% -> 1% of each run, Pallas kernels for 0% -> 33%
where the time goes in v2:
time: 106 us
  Pallas kernels  48.2 us (45%)
  starting transfers between devices  31.9 us (30%)
  waiting for transfers between devices  12.9 us (12%)
  local copies, waits for them, and re-layouts  9.72 us (9%)
  between operations  2.23 us (2%)
    pallas_call x7, Pallas kernels, run(): pl.pallas_call(body, out_shape=[pltpu.HBM(o.shape, o.dtype) for o in outs...  38.7 us
    ppermute x12, starting transfers between devices, across(): return lax.ppermute(array, 'head', [(i, i ^ by) for i in range(4)])  13.6 us
    unnamed x34, local copies, waits for them, and re-layouts  9.72 us
    all_to_all x1, waiting for transfers between devices, local_square(): lax.all_to_all(part.reshape(4, DEC // 4, D), 'head', split_axis=0, concat...  7.94 us
    pallas_call x1, Pallas kernels, local_square(): pl.pallas_call(functools.partial(serve_kernel, heads), in_specs=[in_vmem,...  7.09 us
    all_to_all x1, starting transfers between devices, local_square(): lax.all_to_all(served.reshape(groups, capacity, heads * WIDE), 'tok', spl...  5.04 us
    ppermute x1, starting transfers between devices, from_behind(): return lax.ppermute(array, axis, pairs)  4.98 us
    ppermute x12, waiting for transfers between devices, across(): return lax.ppermute(array, 'head', [(i, i ^ by) for i in range(4)])  4.94 us
  transfers between devices with their start and end apart: 16, of which 3 were waited for; matrix products, arithmetic and copies ran while one was open for 1% of the time, Pallas kernels for 33%

profile of v2, /device:TPU:0, one launch (start us, length us, event | category | flops | bytes accessed | tf_op | source)
XLA Modules:
  0.0 105.5 jit_solution(13839261151423049211)
XLA Ops:
  0.6 3.1 %shard_map.158 = (bf16[128,1792]{1,0:T(8,128)(2,1)}, bf16[128,1792]{1,0:T(8,128)(2,1)}, bf16[16,1792]{1,0:T(8,128)(2,1)}, bf16[16,1792]{1,0:T(8,128)(2,1)}) custom-call(bf16[256,1792]{1,0:T(8,128)(2,1)} %bitcast.23, bf16[2,1792]{1,0:T(2,128)(2,1)} %bitcast.28, f32[1792]{0:T(1024)} %refs_2_.3, f32[3,1792]{1,0:T(4,128)} %taps_ref.1), custom_call_target="tpu_custom_call" | custom-call | flops 9175040 | bytes 1835008 | tf_op jit(solution)/shard_map/pallas_call | solution.py:399
  3.8 0.0 copy-start.8
  3.8 5.0 %collective-permute-start = (bf16[16,1792]{1,0:T(8,128)(2,1)}, bf16[16,1792]{1,0:T(8,128)(2,1)S(1)}, u32[]{:S(2)}, u32[]{:S(2)}) collective-permute-start(bf16[16,1792]{1,0:T(8,128)(2,1)} %get-tuple-element.37), channel_id=1, source_target_pairs={{0,8},{8,16},{16,24},{1,9},{9,17},{17,25},{2,10},{10,18},{18,26},{... | collective-permute-start | bytes 172040 | tf_op jit(solution)/shard_map/ppermute | solution.py:566
  8.8 1.6 %collective-permute-start.1 = (bf16[128,1792]{1,0:T(8,128)(2,1)}, bf16[128,1792]{1,0:T(8,128)(2,1)S(1)}, u32[]{:S(2)}, u32[]{:S(2)}) collective-permute-start(bf16[128,1792]{1,0:T(8,128)(2,1)} %get-tuple-element.34.refs_1_), channel_id=1, source_target_pairs={{0,16},{8,24},{16,0},{24,8},{1,17},{9,25},{17,1},{25,9},{2,18},{10... | collective-permute-start | bytes 1376264 | tf_op jit(solution)/shard_map/ppermute | solution.py:438
  10.4 3.4 %shard_map.157.wait_ref.refs_4_ = bf16[64,640]{1,0:T(8,128)(2,1)} custom-call(bf16[32,1792]{1,0:T(8,128)(2,1)} %bitcast.26, bf16[32,2,1792]{2,1,0:T(2,128)(2,1)} %bitcast.25, f32[1792]{0:T(1024)} %refs_2_.3, f32[3,1792]{1,0:T(4,128)} %taps_ref.1, s32[1,32]{1,0:T(1,128)} %bitcast.29, s32[1,32]{1,0:T(1,128)} %refs_5_.3, bf16[4,144,1792]{2,1,0:T(8,128)(2,1)} %bitcast.19), custom_call_target="tpu_custom_call" | custom-call | flops 73400320 | bytes 2293760 | tf_op jit(solution)/shard_map/pallas_call | solution.py:399
  13.8 0.0 collective-permute-done.end_ref
  13.8 0.0 copy-start.12
  13.8 0.6 copy-done.12
  14.4 0.9 copy-done
  15.3 1.0 shard_map.159.refs_2_
  16.2 0.7 collective-permute-start.2
  16.9 4.9 %all-to-all-start = ((bf16[8,8,640]{2,1,0:T(8,128)(2,1)}), bf16[8,8,640]{2,1,0:T(8,128)(2,1)S(1)}, u32[]{:S(2)}, u32[]{:S(2)}) async-start(bf16[8,8,640]{2,1,0:T(8,128)(2,1)} %bitcast.15), calls=%async_computation | async-start | bytes 163840 | tf_op jit(solution)/shard_map/all_to_all | solution.py:498
  21.8 0.0 copy-done.8
  21.8 1.5 %collective-permute-start.4 = (bf16[128,1792]{1,0:T(8,128)(2,1)S(1)}, bf16[128,1792]{1,0:T(8,128)(2,1)S(1)}, u32[]{:S(2)}, u32[]{:S(2)}) collective-permute-start(bf16[128,1792]{1,0:T(8,128)(2,1)S(1)} %copy-done.8), channel_id=1, source_target_pairs={{0,8},{8,0},{16,24},{24,16},{1,9},{9,1},{17,25},{25,17},{2,10},{10... | collective-permute-start | bytes 1376264 | tf_op jit(solution)/shard_map/ppermute | solution.py:438
  23.9 1.2 %collective-permute-start.5 = (bf16[128,1792]{1,0:T(8,128)(2,1)}, bf16[128,1792]{1,0:T(8,128)(2,1)S(1)}, u32[]{:S(2)}, u32[]{:S(2)}) collective-permute-start(bf16[128,1792]{1,0:T(8,128)(2,1)} %shard_map.159.refs_2_), channel_id=1, source_target_pairs={{0,16},{8,24},{16,0},{24,8},{1,17},{9,25},{17,1},{25,9},{2,18},{10... | collective-permute-start | bytes 1376264 | tf_op jit(solution)/shard_map/ppermute | solution.py:438
  25.1 0.9 copy-done.1
  26.0 5.4 %shard_map.160 = (f32[4,384,128]{2,1,0:T(8,128)}, f32[4,256,128]{2,1,0:T(8,128)}, bf16[256,64]{1,0:T(8,128)(2,1)}) custom-call(s32[1]{0:T(128)S(6)} %copy.19.refs_0_, bf16[128,1792]{1,0:T(8,128)(2,1)} %get-tuple-element.34.refs_1_, bf16[128,1792]{1,0:T(8,128)(2,1)} %shard_map.159.refs_2_, bf16[4,144,1792]{2,1,0:T(8,128)(2,1)} %bitcast.20, ...), custom_call_target="tpu_custom_call" | custom-call | flops 788529152 | bytes 1835008 | tf_op jit(solution)/shard_map/pallas_call | solution.py:399
  31.4 0.0 all-to-all-done
  31.5 0.8 copy-done.6
  32.3 7.1 %shard_map.161.refs_6_ = bf16[64,512]{1,0:T(8,128)(2,1)} custom-call(bf16[64,640]{1,0:T(8,128)(2,1)S(1)} %bitcast.16, f32[448]{0:T(512)S(1)} %copy-done.7, f32[1,16,273,4,112]{4,3,2,1,0:T(4,128)} %bitcast.17, bf16[256,64]{1,0:T(8,128)(2,1)S(1)} %copy-done.6), custom_call_target="tpu_custom_call" | custom-call | flops 1001914368 | bytes 8945664 | tf_op jit(solution)/shard_map/pallas_call | solution.py:509
  39.4 0.0 collective-permute-done.1.refs_4_
  39.4 0.0 collective-permute-done.2.refs_2_
  39.4 1.5 %collective-permute-start.3 = (bf16[128,1792]{1,0:T(8,128)(2,1)S(1)}, bf16[128,1792]{1,0:T(8,128)(2,1)S(1)}, u32[]{:S(2)}, u32[]{:S(2)}) collective-permute-start(bf16[128,1792]{1,0:T(8,128)(2,1)S(1)} %collective-permute-done.1.refs_4_), channel_id=1, source_target_pairs={{0,8},{8,0},{16,24},{24,16},{1,9},{9,1},{17,25},{25,17},{2,10},{10... | collective-permute-start | bytes 1376264 | tf_op jit(solution)/shard_map/ppermute | solution.py:438
  41.0 0.0 collective-permute-start.6
  41.7 5.0 %all-to-all-start.1 = ((bf16[8,8,512]{2,1,0:T(8,128)(2,1)}), bf16[8,8,512]{2,1,0:T(8,128)(2,1)S(1)}, u32[]{:S(2)}, u32[]{:S(2)}) async-start(bf16[8,8,512]{2,1,0:T(8,128)(2,1)} %bitcast.10), calls=%async_computation.1 | async-start | bytes 131072 | tf_op jit(solution)/shard_map/all_to_all | solution.py:522
  46.7 0.0 collective-permute-done.4.refs_1_
  46.7 0.0 copy-start.15
  46.7 0.0 collective-permute-done.5.refs_5_
  46.7 0.0 copy-done.13
  46.7 0.0 copy-done.14
  46.7 0.7 copy-done.15
  47.5 0.8 copy-done.16
  48.2 7.9 %shard_map.162 = (f32[4,384,128]{2,1,0:T(8,128)}, f32[4,256,128]{2,1,0:T(8,128)}, bf16[256,64]{1,0:T(8,128)(2,1)}, f32[4,384,128]{2,1,0:T(8,128)}, f32[4,256,128]{2,1,0:T(8,128)}, /*index=5*/bf16[256,64]{1,0:T(8,128)(2,1)}) custom-call(s32[1]{0:T(128)S(6)} %copy.19.refs_0_, bf16[128,1792]{1,0:T(8,128)(2,1)} %copy-done.15, bf16[128,1792]{1,0:T(8,128)(2,1)} %copy-done.14, ...), custom_call_target="tpu_custom_call" | custom-call | flops 1577058304 | bytes 1835008 | tf_op jit(solution)/shard_map/pallas_call | solution.py:399
  56.1 0.0 all-to-all-done.1
  56.1 0.0 collective-permute-done.3.refs_2_
  56.2 0.0 collective-permute-done.6.refs_3_
  56.2 0.6 copy-done.11
  56.8 0.2 copy-done.9
  56.9 0.2 copy-done.10
  57.1 9.2 %shard_map.163 = (bf16[128,1792]{1,0:T(8,128)(2,1)}, bf16[128,1792]{1,0:T(8,128)(2,1)}, bf16[32,1792]{1,0:T(8,128)(2,1)}, bf16[3,4,384,128]{3,2,1,0:T(8,128)(2,1)}, f32[1,273,4,112]{3,2,1,0:T(4,128)}) custom-call(s32[1]{0:T(128)S(6)} %copy.19.refs_0_, s32[1]{0:T(128)S(6)} %copy.20.refs_1_, bf16[128,1792]{1,0:T(8,128)(2,1)} %copy-done.9, ...), custom_call_target="tpu_custom_call" | custom-call | flops 1358954496 | bytes 3670016 | tf_op jit(solution)/shard_map/pallas_call | solution.py:399
  66.3 1.5 %collective-permute-start.9 = (bf16[128,1792]{1,0:T(8,128)(2,1)}, bf16[128,1792]{1,0:T(8,128)(2,1)S(1)}, u32[]{:S(2)}, u32[]{:S(2)}) collective-permute-start(bf16[128,1792]{1,0:T(8,128)(2,1)} %get-tuple-element.57), channel_id=1, source_target_pairs={{0,8},{8,0},{16,24},{24,16},{1,9},{9,1},{17,25},{25,17},{2,10},{10... | collective-permute-start | bytes 1376264 | tf_op jit(solution)/shard_map/ppermute | solution.py:438
  67.8 1.1 %collective-permute-start.10 = (bf16[128,1792]{1,0:T(8,128)(2,1)}, bf16[128,1792]{1,0:T(8,128)(2,1)S(1)}, u32[]{:S(2)}, u32[]{:S(2)}) collective-permute-start(bf16[128,1792]{1,0:T(8,128)(2,1)} %get-tuple-element.59), channel_id=1, source_target_pairs={{0,16},{8,24},{16,0},{24,8},{1,17},{9,25},{17,1},{25,9},{2,18},{10... | collective-permute-start | bytes 1376264 | tf_op jit(solution)/shard_map/ppermute | solution.py:438
  68.9 5.7 %shard_map.165 = (bf16[128,1792]{1,0:T(8,128)(2,1)}, bf16[128,1792]{1,0:T(8,128)(2,1)}, bf16[128,1792]{1,0:T(8,128)(2,1)}, bf16[128,1792]{1,0:T(8,128)(2,1)}) custom-call(s32[1]{0:T(128)S(6)} %copy.19.refs_0_, bf16[3,4,384,128]{3,2,1,0:T(8,128)(2,1)} %get-tuple-element.47.refs_1_, bf16[256,64]{1,0:T(8,128)(2,1)} %get-tuple-element.51.refs_2_, ...), custom_call_target="tpu_custom_call" | custom-call | flops 1140850688 | bytes 1835008 | tf_op jit(solution)/shard_map/pallas_call | solution.py:399
  74.6 1.0 collective-permute-start.8
  75.6 0.9 collective-permute-start.7
  76.5 3.4 %collective-permute-done.9.b_ref = bf16[128,1792]{1,0:T(8,128)(2,1)S(1)} collective-permute-done((bf16[128,1792]{1,0:T(8,128)(2,1)}, bf16[128,1792]{1,0:T(8,128)(2,1)S(1)}, u32[]{:S(2)}, u32[]{:S(2)}) %collective-permute-start.9) | collective-permute-done | bytes 458784 | tf_op jit(solution)/shard_map/ppermute | solution.py:438
  79.9 1.5 %collective-permute-done.10.d_ref = bf16[128,1792]{1,0:T(8,128)(2,1)S(1)} collective-permute-done((bf16[128,1792]{1,0:T(8,128)(2,1)}, bf16[128,1792]{1,0:T(8,128)(2,1)S(1)}, u32[]{:S(2)}, u32[]{:S(2)}) %collective-permute-start.10) | collective-permute-done | bytes 458784 | tf_op jit(solution)/shard_map/ppermute | solution.py:438
  81.4 1.0 copy-done.4
  82.4 1.0 copy-done.5
  83.4 0.2 shard_map.166
  83.7 1.2 %collective-permute-start.11 = (bf16[128,1792]{1,0:T(8,128)(2,1)S(1)}, bf16[128,1792]{1,0:T(8,128)(2,1)S(1)}, u32[]{:S(2)}, u32[]{:S(2)}) collective-permute-start(bf16[128,1792]{1,0:T(8,128)(2,1)S(1)} %get-tuple-element.60), channel_id=1, source_target_pairs={{0,16},{8,24},{16,0},{24,8},{1,17},{9,25},{17,1},{25,9},{2,18},{10... | collective-permute-start | bytes 1376264 | tf_op jit(solution)/shard_map/ppermute | solution.py:438
  84.8 1.5 %collective-permute-start.12 = (bf16[128,1792]{1,0:T(8,128)(2,1)S(1)}, bf16[128,1792]{1,0:T(8,128)(2,1)S(1)}, u32[]{:S(2)}, u32[]{:S(2)}) collective-permute-start(bf16[128,1792]{1,0:T(8,128)(2,1)S(1)} %get-tuple-element.61), channel_id=1, source_target_pairs={{0,8},{8,0},{16,24},{24,16},{1,9},{9,1},{17,25},{25,17},{2,10},{10... | collective-permute-start | bytes 1376264 | tf_op jit(solution)/shard_map/ppermute | solution.py:438
  86.3 3.3 %all-to-all-start.2 = ((bf16[4,8,1792]{2,1,0:T(8,128)(2,1)}), bf16[4,8,1792]{2,1,0:T(8,128)(2,1)S(1)}, u32[]{:S(2)}, u32[]{:S(2)}) async-start(bf16[4,8,1792]{2,1,0:T(8,128)(2,1)} %bitcast.12), calls=%async_computation.2 | async-start | bytes 229376 | tf_op jit(solution)/shard_map/all_to_all | solution.py:550
  89.7 3.9 %shard_map.164 = (bf16[128,1792]{1,0:T(8,128)(2,1)}, bf16[128,1792]{1,0:T(8,128)(2,1)}) custom-call(s32[1]{0:T(128)S(6)} %copy.19.refs_0_, bf16[3,4,384,128]{3,2,1,0:T(8,128)(2,1)} %get-tuple-element.47.refs_1_, bf16[256,64]{1,0:T(8,128)(2,1)} %get-tuple-element.38.wait_ref.refs_2_, f32[4,256,128]{2,1,0:T(8,128)} %get-tuple-element.48.refs_3_, f32[448]{0:T(512)} %refs_4_.3, ...), custom_call_target="tpu_custom_call" | custom-call | flops 570425344 | bytes 1835008 | tf_op jit(solution)/shard_map/pallas_call | solution.py:399
  93.6 7.9 %all-to-all-done.2 = bf16[4,8,1792]{2,1,0:T(8,128)(2,1)S(1)} async-done(((bf16[4,8,1792]{2,1,0:T(8,128)(2,1)}), bf16[4,8,1792]{2,1,0:T(8,128)(2,1)S(1)}, u32[]{:S(2)}, u32[]{:S(2)}) %all-to-all-start.2) | async-done | bytes 114720 | tf_op jit(solution)/shard_map/all_to_all | solution.py:550
  101.6 0.6 reduce_sum.12
  102.2 0.0 collective-permute-done.8.refs_3_
  102.2 0.0 collective-permute-done.7.refs_2_
  102.2 0.0 collective-permute-done.11.refs_4_
  102.2 0.0 collective-permute-done.12.refs_5_
  102.2 0.0 copy-start.2
  102.2 1.0 copy-done.2
  103.2 1.0 copy-done.3
  104.2 1.2 %shard_map.167 = bf16[1,256,1792]{2,1,0:T(8,128)(2,1)} custom-call(bf16[128,1792]{1,0:T(8,128)(2,1)S(1)} %copy-done.2, bf16[128,1792]{1,0:T(8,128)(2,1)S(1)} %copy-done.3, bf16[128,1792]{1,0:T(8,128)(2,1)S(1)} %collective-permute-done.7.refs_2_, bf16[128,1792]{1,0:T(8,128)(2,1)S(1)} %collective-permute-done.8.refs_3_, ...), custom_call_target="tpu_custom_call" | custom-call | bytes 3670016 | tf_op jit(solution)/shard_map/pallas_call | solution.py:421
  (14 shorter events, 0.0 us)
Async XLA Ops:
  3.8 18.0 %copy-start.8 = (bf16[128,1792]{1,0:T(8,128)(2,1)S(1)}, bf16[128,1792]{1,0:T(8,128)(2,1)}, u32[]{:S(2)}) copy-start(bf16[128,1792]{1,0:T(8,128)(2,1)} %get-tuple-element.34.refs_1_) | copy-start | bytes 1376260
  3.8 10.0 %collective-permute-start = (bf16[16,1792]{1,0:T(8,128)(2,1)}, bf16[16,1792]{1,0:T(8,128)(2,1)S(1)}, u32[]{:S(2)}, u32[]{:S(2)}) collective-permute-start(bf16[16,1792]{1,0:T(8,128)(2,1)} %get-tuple-element.37), channel_id=1, source_target_pairs={{0,8},{8,16},{16,24},{1,9},{9,17},{17,25},{2,10},{10,18},{18,26},{... | collective-permute-start | bytes 172040 | tf_op jit(solution)/shard_map/ppermute | solution.py:566
  8.8 30.6 %collective-permute-start.1 = (bf16[128,1792]{1,0:T(8,128)(2,1)}, bf16[128,1792]{1,0:T(8,128)(2,1)S(1)}, u32[]{:S(2)}, u32[]{:S(2)}) collective-permute-start(bf16[128,1792]{1,0:T(8,128)(2,1)} %get-tuple-element.34.refs_1_), channel_id=1, source_target_pairs={{0,16},{8,24},{16,0},{24,8},{1,17},{9,25},{17,1},{25,9},{2,18},{10... | collective-permute-start | bytes 1376264 | tf_op jit(solution)/shard_map/ppermute | solution.py:438
  13.8 0.6 copy-start.12
  14.4 0.9 copy-start
  15.3 16.2 %copy-start.7 = (f32[448]{0:T(512)S(1)}, f32[448]{0:T(512)}, u32[]{:S(2)}) copy-start(f32[448]{0:T(512)} %refs_4_.3) | copy-start | bytes 5380
  16.2 23.2 %collective-permute-start.2 = (bf16[128,1792]{1,0:T(8,128)(2,1)}, bf16[128,1792]{1,0:T(8,128)(2,1)S(1)}, u32[]{:S(2)}, u32[]{:S(2)}) collective-permute-start(bf16[128,1792]{1,0:T(8,128)(2,1)} %shard_map.159.refs_2_), channel_id=1, source_target_pairs={{0,8},{8,0},{16,24},{24,16},{1,9},{9,1},{17,25},{25,17},{2,10},{10... | collective-permute-start | bytes 1376264 | tf_op jit(solution)/shard_map/ppermute | solution.py:438
  16.9 14.5 %all-to-all-start = ((bf16[8,8,640]{2,1,0:T(8,128)(2,1)}), bf16[8,8,640]{2,1,0:T(8,128)(2,1)S(1)}, u32[]{:S(2)}, u32[]{:S(2)}) async-start(bf16[8,8,640]{2,1,0:T(8,128)(2,1)} %bitcast.15), calls=%async_computation | async-start | bytes 163840 | tf_op jit(solution)/shard_map/all_to_all | solution.py:498
  21.8 24.9 %collective-permute-start.4 = (bf16[128,1792]{1,0:T(8,128)(2,1)S(1)}, bf16[128,1792]{1,0:T(8,128)(2,1)S(1)}, u32[]{:S(2)}, u32[]{:S(2)}) collective-permute-start(bf16[128,1792]{1,0:T(8,128)(2,1)S(1)} %copy-done.8), channel_id=1, source_target_pairs={{0,8},{8,0},{16,24},{24,16},{1,9},{9,1},{17,25},{25,17},{2,10},{10... | collective-permute-start | bytes 1376264 | tf_op jit(solution)/shard_map/ppermute | solution.py:438
  23.9 22.8 %collective-permute-start.5 = (bf16[128,1792]{1,0:T(8,128)(2,1)}, bf16[128,1792]{1,0:T(8,128)(2,1)S(1)}, u32[]{:S(2)}, u32[]{:S(2)}) collective-permute-start(bf16[128,1792]{1,0:T(8,128)(2,1)} %shard_map.159.refs_2_), channel_id=1, source_target_pairs={{0,16},{8,24},{16,0},{24,8},{1,17},{9,25},{17,1},{25,9},{2,18},{10... | collective-permute-start | bytes 1376264 | tf_op jit(solution)/shard_map/ppermute | solution.py:438
  25.1 0.9 copy-start.1
  31.4 0.8 copy-start.6
  39.4 7.3 %copy-start.13 = (bf16[128,1792]{1,0:T(8,128)(2,1)}, bf16[128,1792]{1,0:T(8,128)(2,1)S(1)}, u32[]{:S(2)}) copy-start(bf16[128,1792]{1,0:T(8,128)(2,1)S(1)} %collective-permute-done.1.refs_4_) | copy-start | bytes 1376260
  39.4 7.3 %copy-start.14 = (bf16[128,1792]{1,0:T(8,128)(2,1)}, bf16[128,1792]{1,0:T(8,128)(2,1)S(1)}, u32[]{:S(2)}) copy-start(bf16[128,1792]{1,0:T(8,128)(2,1)S(1)} %collective-permute-done.2.refs_2_) | copy-start | bytes 1376260
  39.4 16.7 %collective-permute-start.3 = (bf16[128,1792]{1,0:T(8,128)(2,1)S(1)}, bf16[128,1792]{1,0:T(8,128)(2,1)S(1)}, u32[]{:S(2)}, u32[]{:S(2)}) collective-permute-start(bf16[128,1792]{1,0:T(8,128)(2,1)S(1)} %collective-permute-done.1.refs_4_), channel_id=1, source_target_pairs={{0,8},{8,0},{16,24},{24,16},{1,9},{9,1},{17,25},{25,17},{2,10},{10... | collective-permute-start | bytes 1376264 | tf_op jit(solution)/shard_map/ppermute | solution.py:438
  41.0 15.2 %collective-permute-start.6 = (bf16[128,1792]{1,0:T(8,128)(2,1)S(1)}, bf16[128,1792]{1,0:T(8,128)(2,1)S(1)}, u32[]{:S(2)}, u32[]{:S(2)}) collective-permute-start(bf16[128,1792]{1,0:T(8,128)(2,1)S(1)} %collective-permute-done.2.refs_2_), channel_id=1, source_target_pairs={{0,16},{8,24},{16,0},{24,8},{1,17},{9,25},{17,1},{25,9},{2,18},{10... | collective-permute-start | bytes 1376264 | tf_op jit(solution)/shard_map/ppermute | solution.py:438
  41.7 14.5 %all-to-all-start.1 = ((bf16[8,8,512]{2,1,0:T(8,128)(2,1)}), bf16[8,8,512]{2,1,0:T(8,128)(2,1)S(1)}, u32[]{:S(2)}, u32[]{:S(2)}) async-start(bf16[8,8,512]{2,1,0:T(8,128)(2,1)} %bitcast.10), calls=%async_computation.1 | async-start | bytes 131072 | tf_op jit(solution)/shard_map/all_to_all | solution.py:522
  46.7 0.8 copy-start.15
  47.5 0.8 copy-start.16
  56.1 0.6 copy-start.11
  56.2 0.8 copy-start.9
  56.2 0.9 copy-start.10
  66.3 13.6 %collective-permute-start.9 = (bf16[128,1792]{1,0:T(8,128)(2,1)}, bf16[128,1792]{1,0:T(8,128)(2,1)S(1)}, u32[]{:S(2)}, u32[]{:S(2)}) collective-permute-start(bf16[128,1792]{1,0:T(8,128)(2,1)} %get-tuple-element.57), channel_id=1, source_target_pairs={{0,8},{8,0},{16,24},{24,16},{1,9},{9,1},{17,25},{25,17},{2,10},{10... | collective-permute-start | bytes 1376264 | tf_op jit(solution)/shard_map/ppermute | solution.py:438
  67.8 13.6 %collective-permute-start.10 = (bf16[128,1792]{1,0:T(8,128)(2,1)}, bf16[128,1792]{1,0:T(8,128)(2,1)S(1)}, u32[]{:S(2)}, u32[]{:S(2)}) collective-permute-start(bf16[128,1792]{1,0:T(8,128)(2,1)} %get-tuple-element.59), channel_id=1, source_target_pairs={{0,16},{8,24},{16,0},{24,8},{1,17},{9,25},{17,1},{25,9},{2,18},{10... | collective-permute-start | bytes 1376264 | tf_op jit(solution)/shard_map/ppermute | solution.py:438
  74.6 27.6 %collective-permute-start.8 = (bf16[128,1792]{1,0:T(8,128)(2,1)}, bf16[128,1792]{1,0:T(8,128)(2,1)S(1)}, u32[]{:S(2)}, u32[]{:S(2)}) collective-permute-start(bf16[128,1792]{1,0:T(8,128)(2,1)} %get-tuple-element.55), channel_id=1, source_target_pairs={{0,16},{8,24},{16,0},{24,8},{1,17},{9,25},{17,1},{25,9},{2,18},{10... | collective-permute-start | bytes 1376264 | tf_op jit(solution)/shard_map/ppermute | solution.py:438
  75.6 26.6 %collective-permute-start.7 = (bf16[128,1792]{1,0:T(8,128)(2,1)}, bf16[128,1792]{1,0:T(8,128)(2,1)S(1)}, u32[]{:S(2)}, u32[]{:S(2)}) collective-permute-start(bf16[128,1792]{1,0:T(8,128)(2,1)} %get-tuple-element.54), channel_id=1, source_target_pairs={{0,8},{8,0},{16,24},{24,16},{1,9},{9,1},{17,25},{25,17},{2,10},{10... | collective-permute-start | bytes 1376264 | tf_op jit(solution)/shard_map/ppermute | solution.py:438
  81.4 1.0 copy-start.4
  82.4 1.0 copy-start.5
  83.7 18.5 %collective-permute-start.11 = (bf16[128,1792]{1,0:T(8,128)(2,1)S(1)}, bf16[128,1792]{1,0:T(8,128)(2,1)S(1)}, u32[]{:S(2)}, u32[]{:S(2)}) collective-permute-start(bf16[128,1792]{1,0:T(8,128)(2,1)S(1)} %get-tuple-element.60), channel_id=1, source_target_pairs={{0,16},{8,24},{16,0},{24,8},{1,17},{9,25},{17,1},{25,9},{2,18},{10... | collective-permute-start | bytes 1376264 | tf_op jit(solution)/shard_map/ppermute | solution.py:438
  84.8 17.4 %collective-permute-start.12 = (bf16[128,1792]{1,0:T(8,128)(2,1)S(1)}, bf16[128,1792]{1,0:T(8,128)(2,1)S(1)}, u32[]{:S(2)}, u32[]{:S(2)}) collective-permute-start(bf16[128,1792]{1,0:T(8,128)(2,1)S(1)} %get-tuple-element.61), channel_id=1, source_target_pairs={{0,8},{8,0},{16,24},{24,16},{1,9},{9,1},{17,25},{25,17},{2,10},{10... | collective-permute-start | bytes 1376264 | tf_op jit(solution)/shard_map/ppermute | solution.py:438
  86.3 15.2 %all-to-all-start.2 = ((bf16[4,8,1792]{2,1,0:T(8,128)(2,1)}), bf16[4,8,1792]{2,1,0:T(8,128)(2,1)S(1)}, u32[]{:S(2)}, u32[]{:S(2)}) async-start(bf16[4,8,1792]{2,1,0:T(8,128)(2,1)} %bitcast.12), calls=%async_computation.2 | async-start | bytes 229376 | tf_op jit(solution)/shard_map/all_to_all | solution.py:550
  102.2 1.0 copy-start.2
  103.2 1.0 copy-start.3

commit v3 on v2

--- a/solution.py
+++ b/solution.py
@@ -18,6 +18,7 @@
 PHI = 1 + F + QUAD
 WIDE = 128
 PHI_WIDE = QUAD + 128
+TILE = 16
 MIB = 1 << 20
 BF = jnp.bfloat16
 F32 = jnp.float32
@@ -123,125 +124,134 @@
         back.wait()
 
 
-def block_part(slot, heads, length, conved, w_ref, sums, own, queries):
+def block_part(slot, heads, length, conved, w_ref, sums, own):
     rows = conved.shape[0]
     qkv = dot(conved, projection(w_ref, heads), ((1,), (1,))).astype(BF)
-    queries[...] = qkv[:, : heads * F]
     live = length - rows * (lax.axis_index("head") ^ slot)
     row = lax.broadcasted_iota(jnp.int32, (rows, rows), 0)
     col = lax.broadcasted_iota(jnp.int32, (rows, rows), 1)
     allowed = (col <= row) & (col < live)
     live_row = lax.broadcasted_iota(jnp.int32, (rows, WIDE), 0) < live
     pick = spreader()
+    keys = [qkv[:, (heads + head) * F : (heads + head) * F + F] for head in range(heads)]
+    values = [qkv[:, 2 * heads * F + head * WIDE : 2 * heads * F + (head + 1) * WIDE] for head in range(heads)]
     for head in range(heads):
-        q = qkv[:, head * F : head * F + F]
-        k = qkv[:, (heads + head) * F : (heads + head) * F + F]
-        at = 2 * heads * F + head * WIDE
-        v = qkv[:, at : at + WIDE]
-        key_phi = phi_of(k, pick).astype(BF)
-        v_live = jnp.where(live_row, v.astype(F32), 0.0).astype(BF)
-        sums[head] = dot(key_phi, v_live, ((0,), (0,)))
-        inner = dot(q, k, ((1,), (1,))) * (1.0 / math.sqrt(F))
+        live_values = jnp.where(live_row, values[head].astype(F32), 0.0).astype(BF)
+        sums[head] = dot(phi_of(keys[head], pick).astype(BF), live_values, ((0,), (0,)))
+        sums.push(head)
+    for head in range(heads):
+        inner = dot(qkv[:, head * F : head * F + F], keys[head], ((1,), (1,))) * (1.0 / math.sqrt(F))
         weights = jnp.where(allowed, 1.0 + inner + 0.5 * inner * inner, 0.0).astype(BF)
-        own[head] = dot(weights, v)
-
-
-def finish_part(slot, heads, length, states, own, queries, gain_ref, w_ref, top, low):
-    rows = queries.shape[0]
-    half = rows // 2
+        own[head] = dot(weights, values[head])
+        own.push(head)
+    return qkv[:, : heads * F]
+
+
+def old_state(cache_ref, head):
+    pad = jnp.zeros((PHI_WIDE - PHI, DH), F32)
+    old = [cache_ref[F + 1 :, head, :], cache_ref[1 : F + 1, head, :], cache_ref[0:1, head, :], pad]
+    return jnp.concatenate([jnp.concatenate(old, axis=0), jnp.zeros((PHI_WIDE, WIDE - DH), F32)], axis=1)
+
+
+def attend_part(slot, head, heads, length, q, own, state, gain_ref, pick):
+    rows = q.shape[0]
+    total = own + dot(phi_of(q, pick).astype(BF), state)
+    square = jnp.sum(total * total, axis=-1, keepdims=True)
+    gain = gain_ref[...].reshape(1, heads * DH)[:, head * DH : (head + 1) * DH]
+    gain = jnp.concatenate([gain, jnp.zeros((1, WIDE - DH), F32)], axis=1)
+    total = total * lax.rsqrt(square * (1.0 / DH) + 1e-05) * gain
     live = length - rows * (lax.axis_index("head") ^ slot)
     live_row = lax.broadcasted_iota(jnp.int32, (rows, WIDE), 0) < live
+    return jnp.where(live_row, total, 0.0).astype(BF)
+
+
+def project_part(parts, heads, w_ref, top, low, others=()):
+    attended = jnp.concatenate(parts, axis=1)
+    half = low.shape[0]
+    w_out = out_projection(w_ref, heads)
+    for order, (out, rows) in enumerate(((top, attended[:half]), (low, attended[half:]))):
+        total = dot(rows, w_out)
+        if others:
+            total = total + others[order][...].astype(F32)
+        out[...] = total.astype(BF)
+        out.push()
+
+
+def first_kernel(heads, len_ref, low, top, w_ref, sums, own, queries):
+    conved = jnp.concatenate([top[...], low[...]], axis=0)
+    queries[...] = block_part(0, heads, len_ref[0], conved, w_ref, sums, own)
+
+
+def second_kernel(
+    heads, len_ref, low1, top1, w_ref, low2, top2, cache, sums0, own1, queries1, own2, queries2, state3, bases, sums1, sums2
+):
+    conved = jnp.concatenate([top1[...], low1[...]], axis=0)
+    sums1, sums2 = Near(sums1), Near(sums2)
+    queries1[...] = block_part(1, heads, len_ref[0], conved, w_ref, sums1, own1)
+    queries1.push()
+    conved = jnp.concatenate([top2[...], low2[...]], axis=0)
+    queries2[...] = block_part(2, heads, len_ref[0], conved, w_ref, sums2, own2)
+    queries2.push()
+    mine = lax.axis_index("head")
+    for head in range(heads):
+        old, sums = old_state(cache, head), (sums0[head], sums1[head], sums2[head])
+        for slot in range(4):
+            total = old
+            for other in range(3):
+                if other != slot:
+                    total = total + ((mine ^ other) < (mine ^ slot)).astype(F32) * sums[other]
+            if slot == 3:
+                state3[head] = total.astype(BF)
+            else:
+                bases[slot, head] = total
+        bases[3, head] = old + (sums[0] + (sums[1] + sums[2]))
+
+
+def third_kernel(heads, len_ref, low, top, w_ref, state3, gain_ref, out_w_ref, top3, low3, sums3, own):
+    length = len_ref[0]
+    conved = jnp.concatenate([top[...], low[...]], axis=0)
+    own = Near(own)
+    queries = block_part(3, heads, length, conved, w_ref, sums3, own)
     pick = spreader()
-    gains = gain_ref[...].reshape(1, heads * DH)
-    zeros = jnp.zeros((1, WIDE - DH), F32)
     parts = []
     for head in range(heads):
-        query_phi = phi_of(queries[:, head * F : head * F + F], pick).astype(BF)
-        total = own[head] + dot(query_phi, states[head])
-        square = jnp.sum(total * total, axis=-1, keepdims=True)
-        gain = jnp.concatenate([gains[:, head * DH : (head + 1) * DH], zeros], axis=1)
-        total = total * lax.rsqrt(square * (1.0 / DH) + 1e-05) * gain
-        parts.append(jnp.where(live_row, total, 0.0).astype(BF))
-    attended = jnp.concatenate(parts, axis=1)
-    w_out = out_projection(w_ref, heads)
-    top[...] = dot(attended[:half], w_out).astype(BF)
-    top.push()
-    low[...] = dot(attended[half:], w_out).astype(BF)
-    low.push()
-
-
-def first_kernel(heads, len_ref, low, top, w_ref, sums, own, queries):
-    conved = jnp.concatenate([top[...], low[...]], axis=0)
-    block_part(0, heads, len_ref[0], conved, w_ref, sums, own, queries)
-
-
-def second_kernel(heads, len_ref, low1, top1, w_ref, low2, top2, sums1, own1, queries1, sums2, own2, queries2):
-    conved = jnp.concatenate([top1[...], low1[...]], axis=0)
-    block_part(1, heads, len_ref[0], conved, w_ref, sums1, own1, queries1)
-    for out in (sums1, own1, queries1):
-        out.push()
-    conved = jnp.concatenate([top2[...], low2[...]], axis=0)
-    block_part(2, heads, len_ref[0], conved, w_ref, sums2, own2, queries2)
-
-
-def third_kernel(heads, capacity, len_ref, low, top, w_ref, cache_ref, sums0, sums1, sums2, gain_ref, out_w_ref, items_ref, owner_ref,
-                 top3, low3, part, states, state_next, sums3, own3, queries3, states3):
-    length = len_ref[0]
+        q = queries[:, head * F : head * F + F]
+        parts.append(attend_part(3, head, heads, length, q, own[head], state3[head], gain_ref, pick))
+    project_part(parts, heads, out_w_ref, top3, low3)
+
+
+def attend_kernel(heads, slots, adds, len_ref, bases, sums3, gain_ref, out_w_ref, *refs):
+    queries, own, refs = refs[: len(slots)], refs[len(slots) : 2 * len(slots)], refs[2 * len(slots) :]
+    others, outs = refs[:adds], refs[adds:]
     mine = lax.axis_index("head")
-    conved = jnp.concatenate([top[...], low[...]], axis=0)
-    block_part(3, heads, length, conved, w_ref, sums3, own3, queries3)
-    sums = [sums0, sums1, sums2, sums3]
-    olds = []
-    pad = jnp.zeros((PHI_WIDE - PHI, DH), F32)
-    for head in range(heads):
-        old = [cache_ref[F + 1 :, head, :], cache_ref[1 : F + 1, head, :], cache_ref[0:1, head, :], pad]
-        old = jnp.concatenate([jnp.concatenate(old, axis=0), jnp.zeros((PHI_WIDE, WIDE - DH), F32)], axis=1)
-        olds.append(old)
-
-    def prefix(slot, head):
-        before = olds[head]
-        for other in range(4):
-            if other != slot:
-                before = before + ((mine ^ other) < (mine ^ slot)).astype(F32) * sums[other][head]
-        return before.astype(BF)
-
-    for head in range(heads):
-        states3[head] = prefix(3, head)
-    finish_part(3, heads, length, states3, own3, queries3, gain_ref, out_w_ref, top3, low3)
-    for slot in range(3):
+    pick = spreader()
+    for order, slot in enumerate(slots):
+        parts = []
         for head in range(heads):
-            states[slot, head] = prefix(slot, head)
-    states.push()
-    return_part(heads, capacity, items_ref, owner_ref, out_w_ref, part)
-    part.push()
-    for head in range(heads):
-        total = olds[head] + (sums0[head] + sums1[head]) + (sums2[head] + sums3[head])
-        total = total[:, :DH]
-        state_next[0, F + 1 :, head, :] = total[:QUAD]
-        state_next[0, 1 : F + 1, head, :] = total[QUAD : QUAD + F]
-        state_next[0, 0:1, head, :] = total[QUAD + F : QUAD + F + 1]
-
-
-def fourth_kernel(heads, len_ref, states, queries1, own1, gain_ref, out_w_ref, queries2, own2, top1, low1, top2, low2):
-    finish_part(1, heads, len_ref[0], states.part(1), own1, queries1, gain_ref, out_w_ref, top1, low1)
-    finish_part(2, heads, len_ref[0], states.part(2), own2, queries2, gain_ref, out_w_ref, top2, low2)
-
-
-def fifth_kernel(heads, len_ref, states, queries0, own0, gain_ref, out_w_ref, top0, low0):
-    finish_part(0, heads, len_ref[0], states.part(0), own0, queries0, gain_ref, out_w_ref, top0, low0)
-
-
-def add_kernel(a_ref, b_ref, c_ref, d_ref, ab_ref, cd_ref):
-    ab_ref[...] = (a_ref[...].astype(F32) + b_ref[...].astype(F32)).astype(BF)
-    cd_ref[...] = (c_ref[...].astype(F32) + d_ref[...].astype(F32)).astype(BF)
-
-
-def total_kernel(*refs):
-    parts, out_ref = refs[:-1], refs[-1]
-    half = out_ref.shape[1] // 2
-    for order in range(2):
-        mine = [part[...].astype(F32) for part in parts[order::2]]
-        out_ref[0, order * half : (order + 1) * half, :] = functools.reduce(lambda a, b: a + b, mine).astype(BF)
+            q = queries[order][:, head * F : (head + 1) * F]
+            state = bases[slot, head] + ((mine ^ 3) < (mine ^ slot)).astype(F32) * sums3[head]
+            parts.append(attend_part(slot, head, heads, len_ref[0], q, own[order][head], state.astype(BF), gain_ref, pick))
+        project_part(parts, heads, out_w_ref, outs[2 * order], outs[2 * order + 1], others)
+    if len(outs) > 2 * len(slots):
+        state_next = outs[-1]
+        for head in range(heads):
+            new = (bases[3, head] + sums3[head])[:, :DH]
+            state_next[0, F + 1 :, head, :] = new[:QUAD]
+            state_next[0, 1 : F + 1, head, :] = new[QUAD : QUAD + F]
+            state_next[0, 0:1, head, :] = new[QUAD + F : QUAD + F + 1]
+
+
+def add_kernel(top2, via_x, low1, via_y, two_y, two_x):
+    two_y[...] = (top2[...].astype(F32) + via_x[...].astype(F32)).astype(BF)
+    two_x[...] = (low1[...].astype(F32) + via_y[...].astype(F32)).astype(BF)
+
+
+def total_kernel(dec0, dec1, dec2, dec3, top0, low0, two_y, two_x, out, decode_out):
+    half = low0.shape[0]
+    out[0, :half, :] = (top0[...].astype(F32) + two_y[...].astype(F32)).astype(BF)
+    out[0, half:, :] = (low0[...].astype(F32) + two_x[...].astype(F32)).astype(BF)
+    total = (dec0[...].astype(F32) + dec1[...].astype(F32)) + (dec2[...].astype(F32) + dec3[...].astype(F32))
+    decode_out[0] = total[: DEC // 4].astype(BF)
 
 
 def placing_rank(owners_row, axis):
@@ -277,17 +287,17 @@
     return ones_where(a == entry), ones_where((quad >= 0) & ((quad & (F - 1)) == entry))
 
 
-def serve_kernel(heads, items_ref, gain_ref, cache_ref, wait_ref, out_ref, state, sem):
-    count = items_ref.shape[0]
-    mark = 2 * heads * F + DH
-    flying = 4
+def serve_kernel(heads, items, gain_ref, cache_ref, out, state, sem):
+    flying = 6
     copies = [pltpu.make_async_copy(cache_ref.at[0, n], state.at[n], sem.at[n]) for n in range(state.shape[0])]
     for copy in copies[:flying]:
         copy.start()
+    count = items.shape[0]
+    mark = 2 * heads * F + DH
     first, second = cache_spreaders(heads)
     phis = []
     for head in range(heads):
-        q = items_ref[:, head * F : head * F + F]
+        q = items[:, head * F : head * F + F]
         a = dot(q, first)
         b = dot(q, second)
         lane = lax.broadcasted_iota(jnp.int32, a.shape, 1)
@@ -295,55 +305,77 @@
         value = jnp.where(lane < heads, 1.0, a * scale)
         phis.append(jnp.where((lane & (heads - 1)) == head, value, 0.0).astype(BF))
     phis = jnp.concatenate(phis, axis=0)
-    slots = jnp.concatenate([items_ref[:, mark : mark + 1].astype(F32)] * heads, axis=0)
-    total = jnp.zeros((heads * count, DH), F32)
-    for n, copy in enumerate(copies):
-        copy.wait()
-        for later in copies[n + flying : n + flying + 1]:
-            later.start()
-        table = dot(phis, state[n].reshape(PHI * heads, DH).astype(BF))
-        total = total + jnp.where(slots == float(n), table, 0.0)
+    slots = jnp.concatenate([items[:, mark : mark + 1].astype(F32)] * heads, axis=0)
+    zeros = jnp.zeros((PHI * heads, WIDE - DH), BF)
+    total = jnp.zeros((heads * count, WIDE), F32)
+    for n in range(0, len(copies), 2):
+        pair = []
+        for place in (n, n + 1):
+            copies[place].wait()
+            for later in copies[place + flying : place + flying + 1]:
+                later.start()
+            pair += [state[place].reshape(PHI * heads, DH).astype(BF), zeros]
+        table = dot(phis, jnp.concatenate(pair, axis=1))
+        total = total + jnp.where(slots == float(n), table[:, :WIDE], 0.0)
+        total = total + jnp.where(slots == float(n + 1), table[:, WIDE:], 0.0)
     gains = gain_ref[...].reshape(1, heads * DH)
     for head in range(heads):
-        q = items_ref[:, head * F : head * F + F].astype(F32)
-        k = items_ref[:, (heads + head) * F : (heads + head) * F + F].astype(F32)
+        q = items[:, head * F : head * F + F].astype(F32)
+        k = items[:, (heads + head) * F : (heads + head) * F + F].astype(F32)
         at = 2 * heads * F + head * WIDE
-        v = items_ref[:, at : at + DH].astype(F32)
+        v = items[:, at : at + DH].astype(F32)
         inner = jnp.sum(q * k, axis=-1, keepdims=True) * (1.0 / math.sqrt(F))
-        value = total[head * count : (head + 1) * count, :] + (1.0 + inner + 0.5 * inner * inner) * v
+        value = total[head * count : (head + 1) * count, :DH] + (1.0 + inner + 0.5 * inner * inner) * v
         square = jnp.sum(value * value, axis=-1, keepdims=True)
         value = value * lax.rsqrt(square * (1.0 / DH) + 1e-05) * gains[:, head * DH : (head + 1) * DH]
-        out_ref[:, head * WIDE : head * WIDE + DH] = value.astype(BF)
-        out_ref[:, head * WIDE + DH : (head + 1) * WIDE] = jnp.zeros((count, WIDE - DH), BF)
-
-
-def return_part(heads, capacity, items_ref, owner_ref, w_ref, out):
+        out[:, head * WIDE : head * WIDE + DH] = value.astype(BF)
+        out[:, head * WIDE + DH : (head + 1) * WIDE] = jnp.zeros((count, WIDE - DH), BF)
+
+
+def return_kernel(heads, capacity, items_ref, owner_ref, w_ref, *outs):
     owners = owner_ref[...]
     target = column(owners) * capacity + placing_rank(owners, 1)
     placing = lax.broadcasted_iota(jnp.int32, (DEC, items_ref.shape[0]), 1) == target
     attended = dot(ones_where(placing), items_ref[...]).astype(BF)
-    out[...] = dot(attended, out_projection(w_ref, heads)).astype(BF)
+    row = lax.broadcasted_iota(jnp.int32, (4 * TILE, DEC), 0)
+    entry = lax.broadcasted_iota(jnp.int32, (4 * TILE, DEC), 1)
+    device = lax.axis_index("head") ^ (row // TILE)
+    wanted = ((row % TILE) < DEC // 4) & (entry == device * (DEC // 4) + row % TILE)
+    attended = dot(ones_where(wanted), attended).astype(BF)
+    shares = dot(attended, out_projection(w_ref, heads)).astype(BF)
+    for slot, out in enumerate(outs):
+        out[...] = shares[slot * TILE : (slot + 1) * TILE]
+
+
+def far_off(array):
+    return pltpu.with_memory_space_constraint(array, pltpu.HBM)
+
+
+def entries(ref):
+    return [ref.at[n] for n in range(ref.shape[0])]
 
 
 class Fetched:
-    def __init__(self, copy, place):
-        self.copy, self.place, self.here = copy, place, False
+    def __init__(self, copies, place):
+        self.copies, self.place, self.here = copies, place, set()
         self.shape, self.dtype = place.shape, place.dtype
 
     def __getitem__(self, index):
-        if not self.here:
-            self.copy.wait()
-            self.here = True
+        entry = index[0] if isinstance(index, tuple) else index
+        wanted = [entry] if len(self.copies) > 1 and isinstance(entry, int) else range(len(self.copies))
+        for n in wanted:
+            self.wait(n)
         return self.place[index]
 
-    def part(self, number):
-        self[0, 0]
-        return self.place.at[number]
+    def wait(self, n):
+        if n not in self.here:
+            self.copies[n].wait()
+            self.here.add(n)
 
 
 class Pushed:
-    def __init__(self, copy, place):
-        self.copy, self.place, self.gone = copy, place, False
+    def __init__(self, copies, place):
+        self.copies, self.place, self.gone = copies, place, set()
         self.shape, self.dtype = place.shape, place.dtype
 
     def __getitem__(self, index):
@@ -352,80 +384,98 @@
     def __setitem__(self, index, value):
         self.place[index] = value
 
-    def push(self):
-        if not self.gone:
-            self.copy.start()
-            self.gone = True
-
-
-def hbm_call(kernel, outs, flops, size, scalars=(), picked=None, inner=(), waits=()):
+    def push(self, entry=0):
+        if entry not in self.gone:
+            self.copies[entry].start()
+            self.gone.add(entry)
+
+
+class Near:
+    def __init__(self, ref):
+        self.ref, self.shape, self.dtype, self.copies = ref, ref.shape, ref.dtype, []
+
+    def __getitem__(self, index):
+        return self.ref[index]
+
+    def __setitem__(self, index, value):
+        self.ref[index] = value
+
+    def push(self, entry=0):
+        pass
+
+
+def hbm_call(kernel, outs, flops, size, scalars=(), picked=None, waits=(), loose=(), here=(), near=(), split=(), split_out=(), raw=(), scratch=()):
     def run(*args):
         count, many = len(args), len(outs)
+        moved = [n for n in range(count) if n not in here and n not in raw]
+        far = [n for n in range(many) if n not in near]
 
         def shape_in(n):
             return args[n].shape[2:] if n == picked else args[n].shape
 
+        pieces = sum(shape_in(n)[0] if n in split else 1 for n in moved)
+        pieces += sum(outs[n].shape[0] if n in split_out else 1 for n in far)
+
         def body(*refs):
-            numbers, sources = refs[: len(scalars)], refs[len(scalars) : len(scalars) + count]
-            rest = refs[len(scalars) + count + len(waits) :]
-            targets, places, results, own, sem = (
-                rest[:many],
-                rest[many : many + count],
-                rest[many + count : 2 * many + count],
-                rest[2 * many + count : -1],
-                rest[-1],
-            )
+            refs = list(refs)
+
+            def take(number):
+                taken = refs[:number]
+                del refs[:number]
+                return taken
+
+            numbers, sources, _, targets = take(len(scalars)), take(count), take(len(waits)), take(many)
+            places, results, own, (sem,) = dict(zip(moved, take(len(moved)))), dict(zip(far, take(len(far)))), take(len(scratch)), refs
+            used = iter(range(pieces))
+
+            def copies(source, target, apart):
+                pairs = zip(entries(source), entries(target)) if apart else [(source, target)]
+                return [pltpu.make_async_copy(a, b, sem.at[next(used)]) for a, b in pairs]
+
             ins = []
-            for n, (source, place) in enumerate(zip(sources, places)):
+            for n, source in enumerate(sources):
+                if n in here or n in raw:
+                    ins.append(source)
+                    continue
                 if n == picked:
                     source = source.at[0, numbers[-1][0]]
-                copy = pltpu.make_async_copy(source, place, sem.at[n])
-                copy.start()
-                ins.append(Fetched(copy, place))
+                fetched = Fetched(copies(source, places[n], n in split), places[n])
+                for copy in fetched.copies:
+                    copy.start()
+                ins.append(fetched)
             done = [
-                Pushed(pltpu.make_async_copy(result, target, sem.at[count + n]), result)
-                for n, (result, target) in enumerate(zip(results, targets))
+                Pushed(copies(results[n], target, n in split_out), results[n]) if n in far else Near(target)
+                for n, target in enumerate(targets)
             ]
             kernel(*numbers[: len(scalars) - (picked is not None)], *ins, *done, *own)
-            for out in done:
-                out.push()
-            for one in ins:
-                if not one.here:
-                    one.copy.wait()
-            for out in done:
-                out.copy.wait()
+            for n in far:
+                for entry in range(len(done[n].copies)):
+                    done[n].push(entry)
+            for n in moved:
+                for entry in range(len(ins[n].copies)):
+                    ins[n].wait(entry)
+            for n in far:
+                for copy in done[n].copies:
+                    copy.wait()
 
         hbm = pl.BlockSpec(memory_space=pltpu.HBM)
+        in_vmem = pl.BlockSpec(memory_space=pltpu.VMEM)
+        anywhere = pl.BlockSpec(memory_space=pl.ANY)
+        free = set(loose) | set(here)
         return pl.pallas_call(
             body,
-            out_shape=[pltpu.HBM(o.shape, o.dtype) for o in outs],
+            out_shape=[o if n in near else pltpu.HBM(o.shape, o.dtype) for n, o in enumerate(outs)],
             in_specs=[pl.BlockSpec(memory_space=pltpu.SMEM)] * len(scalars)
-            + [hbm] * count
-            + [pl.BlockSpec(memory_space=pl.ANY)] * len(waits),
-            out_specs=[hbm] * many,
-            scratch_shapes=[pltpu.VMEM(shape_in(n), args[n].dtype) for n in range(count)]
-            + [pltpu.VMEM(o.shape, o.dtype) for o in outs]
-            + [pltpu.VMEM(o.shape, o.dtype) for o in inner]
-            + [pltpu.SemaphoreType.DMA((count + many,))],
-            compiler_params=pltpu.CompilerParams(vmem_limit_bytes=32 * MIB),
+            + [in_vmem if n in here else anywhere if n in loose else hbm for n in range(count)]
+            + [hbm] * len(waits),
+            out_specs=[in_vmem if n in near else hbm for n in range(many)],
+            scratch_shapes=[pltpu.VMEM(shape_in(n), args[n].dtype) for n in moved]
+            + [pltpu.VMEM(outs[n].shape, outs[n].dtype) for n in far]
+            + list(scratch)
+            + [pltpu.SemaphoreType.DMA((pieces,))],
+            compiler_params=pltpu.CompilerParams(vmem_limit_bytes=40 * MIB),
             cost_estimate=pl.CostEstimate(flops=flops, bytes_accessed=size, transcendentals=0),
-        )(*scalars, *[pltpu.with_memory_space_constraint(a, pltpu.HBM) for a in args], *waits)
-
-    return run
-
-
-def call(kernel, outs, flops, size):
-    def run(*args):
-        many = isinstance(outs, (list, tuple))
-        spec = pl.BlockSpec(memory_space=pltpu.VMEM)
-        return pl.pallas_call(
-            kernel,
-            out_shape=outs,
-            in_specs=[spec] * len(args),
-            out_specs=[spec] * len(outs) if many else spec,
-            compiler_params=pltpu.CompilerParams(vmem_limit_bytes=16 * MIB),
-            cost_estimate=pl.CostEstimate(flops=flops, bytes_accessed=size, transcendentals=0),
-        )(*args)
+        )(*scalars, *[a if n in free else far_off(a) for n, a in enumerate(args)], *map(far_off, waits))
 
     return run
 
@@ -458,15 +508,17 @@
     rows = stretch_tokens.shape[1]
     half = rows // 2
     wide = heads * (2 * F + WIDE)
-    me = lax.axis_index("head").reshape(1)
     w_in = jnp.transpose(qkv_weight, (1, 2, 0))
     cache = jnp.transpose(state_cache, (0, 1, 4, 2, 3))
+    length = stretch_len.astype(jnp.int32)
+    slot = stretch_slot.astype(jnp.int32)
     hbm = pl.BlockSpec(memory_space=pltpu.HBM)
-    in_vmem = pl.BlockSpec(memory_space=pltpu.VMEM)
-    anywhere = pl.BlockSpec(memory_space=pl.ANY)
-    piece, ends = shape(half, D), shape(16, D)
-
-    low, top, begin, end = hbm_call(conv_kernel, [piece, piece, ends, ends], 20 * rows * D, 4 * rows * D)(
+    piece = shape(half, D)
+    block_flops = 2 * rows * D * wide + 6 * heads * rows * rows * WIDE
+    attend_flops = 2 * rows * heads * WIDE * (D + PHI_WIDE)
+    size = 4 * rows * D
+
+    low, top, begin, end = hbm_call(conv_kernel, [piece, piece, shape(TILE, D), shape(TILE, D)], 20 * rows * D, size)(
         stretch_tokens[0], stretch_tail[0], norm_gain, conv_taps
     )
     low_x = across(low, 1)
@@ -485,79 +537,107 @@
             first_ref, top_ref, begin_ref, end_ref, taps_ref, *refs
         ),
         out_shape=pltpu.HBM((half, D), BF),
-        in_specs=[pl.BlockSpec(memory_space=pltpu.SMEM)] + [hbm] * 4 + [anywhere],
+        in_specs=[pl.BlockSpec(memory_space=pltpu.SMEM), hbm, hbm, pl.BlockSpec(memory_space=pl.ANY), hbm, hbm],
         out_specs=hbm,
-        scratch_shapes=[pltpu.VMEM((16, D), BF), pltpu.VMEM((16, D), BF), pltpu.VMEM((3, D), F32), pltpu.VMEM((16, D), BF)]
+        scratch_shapes=[pltpu.VMEM((TILE, D), BF), pltpu.VMEM((TILE, D), BF), pltpu.VMEM((3, D), F32), pltpu.VMEM((TILE, D), BF)]
         + [pltpu.SemaphoreType.DMA((4,))],
         input_output_aliases={1: 0},
-        compiler_params=pltpu.CompilerParams(vmem_limit_bytes=16 * MIB),
+        compiler_params=pltpu.CompilerParams(vmem_limit_bytes=40 * MIB),
         cost_estimate=pl.CostEstimate(flops=16 * D, bytes_accessed=128 * D, transcendentals=0),
-    )(me, *[pltpu.with_memory_space_constraint(a, pltpu.HBM) for a in (top, begin, end, conv_taps)], sent)
+    )(lax.axis_index("head").reshape(1), far_off(top), far_off(begin), end, far_off(conv_taps), far_off(sent))
     top_x = across(top, 1)
     top_y = across(top, 2)
     items = lax.all_to_all(sent.reshape(groups, capacity, wide), "tok", split_axis=0, concat_axis=0, tiled=True)
 
-    length = stretch_len.astype(jnp.int32)
-    slot = stretch_slot.astype(jnp.int32)
-    sums, own = shape(heads, PHI_WIDE, WIDE, dtype=F32), shape(heads, rows, WIDE, dtype=F32)
-    queries, states = shape(rows, heads * F), shape(heads, PHI_WIDE, WIDE)
-    block_flops = 2 * rows * D * wide + 6 * heads * rows * rows * WIDE
-    finish_flops = 2 * rows * heads * WIDE * (D + PHI_WIDE)
+    sums, own, queries = shape(heads, PHI_WIDE, WIDE, dtype=F32), shape(heads, rows, WIDE, dtype=F32), shape(rows, heads * F)
     sums0, own0, queries0 = hbm_call(
-        functools.partial(first_kernel, heads), [sums, own, queries], block_flops, 4 * rows * D, scalars=[length], waits=[sent]
+        functools.partial(first_kernel, heads),
+        [sums, own, queries],
+        block_flops,
+        size,
+        scalars=[length],
+        split_out=(0, 1),
     )(low, top, w_in)
-    served = pl.pallas_call(
+    (served,) = hbm_call(
         functools.partial(serve_kernel, heads),
-        in_specs=[in_vmem, in_vmem, hbm, anywhere],
-        out_specs=in_vmem,
-        out_shape=shape(count, heads * WIDE),
-        scratch_shapes=[pltpu.VMEM(cache.shape[1:], F32), pltpu.SemaphoreType.DMA((cache.shape[1],))],
-        compiler_params=pltpu.CompilerParams(vmem_limit_bytes=32 * MIB),
-        cost_estimate=pl.CostEstimate(
-            flops=2 * cache.shape[1] * heads * heads * DH * PHI * count,
-            bytes_accessed=4 * cache.shape[1] * heads * WIDE * PHI,
-            transcendentals=0,
-        ),
-    )(items.reshape(count, wide), out_gain, pltpu.with_memory_space_constraint(cache, pltpu.HBM), queries0)
+        [shape(count, heads * WIDE)],
+        2 * cache.shape[1] * heads * heads * DH * PHI * count,
+        4 * cache.shape[1] * heads * WIDE * PHI,
+        loose=(0,),
+        raw=(2,),
+        scratch=[pltpu.VMEM(cache.shape[1:], F32), pltpu.SemaphoreType.DMA((cache.shape[1],))],
+        waits=[queries0],
+    )(items.reshape(count, wide), out_gain, cache)
+    low_y, top_x = lax.optimization_barrier((low_y, top_x, served))[:2]
+    low_xy = across(low_y, 1)
+    top_xy = across(top_x, 2)
+    own1, queries1, own2, queries2, state3, bases = hbm_call(
+        functools.partial(second_kernel, heads),
+        [own, queries, own, queries, shape(heads, PHI_WIDE, WIDE), shape(4, heads, PHI_WIDE, WIDE, dtype=F32)],
+        2 * block_flops,
+        2 * size,
+        scalars=[length, slot],
+        picked=5,
+        waits=[served],
+        loose=(0, 1, 3, 4),
+        split=(6,),
+        split_out=(0, 2),
+        scratch=[pltpu.VMEM(sums.shape, F32)] * 2,
+    )(low_x, top_x, w_in, low_y, top_y, cache, sums0)
+    top3, low3, sums3 = hbm_call(
+        functools.partial(third_kernel, heads),
+        [piece, piece, sums],
+        block_flops + attend_flops,
+        size,
+        scalars=[length],
+        loose=(0, 1),
+        near=(0, 1),
+        split=(3,),
+        split_out=(2,),
+        scratch=[pltpu.VMEM(own.shape, F32)],
+        waits=[queries2],
+    )(low_xy, top_xy, w_in, state3, out_gain, out_weight)
+
+    def attend(slots, *blocks, others=(), keep=False, waits=()):
+        ins = 4 + 2 * len(slots)
+        return hbm_call(
+            functools.partial(attend_kernel, heads, slots, len(others)),
+            [piece] * (2 * len(slots)) + [shape(1, PHI, heads, DH, dtype=F32)] * keep,
+            len(slots) * attend_flops,
+            size,
+            scalars=[length],
+            split=(0, 1),
+            loose=range(ins, ins + len(others)),
+            waits=waits,
+        )(bases, sums3, out_gain, out_weight, *[b[0] for b in blocks], *[b[1] for b in blocks], *others)
+
+    via_x = across(top3, 1)
+    via_y = across(low3, 2)
+    served = lax.optimization_barrier((served, top3))[0]
     returned = lax.all_to_all(
         served.reshape(groups, capacity, heads * WIDE), "tok", split_axis=0, concat_axis=0, tiled=True
     ).reshape(count, heads * WIDE)
-    low_y, top_x = lax.optimization_barrier((low_y, top_x, served))[:2]
-    low_xy = across(low_y, 1)
-    top_xy = across(top_x, 2)
-    sums1, own1, queries1, sums2, own2, queries2 = hbm_call(
-        functools.partial(second_kernel, heads), [sums, own, queries] * 2, 2 * block_flops, 4 * rows * D, scalars=[length], waits=[served]
-    )(low_x, top_x, w_in, low_y, top_y)
-
-    returned, low_xy = lax.optimization_barrier((returned, low_xy, queries2))[:2]
-    top3, low3, part, all_states, state_next = hbm_call(
-        functools.partial(third_kernel, heads, capacity),
-        [piece, piece, shape(DEC, D), shape(3, *states.shape), shape(1, PHI, heads, DH, dtype=F32)],
-        block_flops + finish_flops,
-        8 * rows * D,
-        scalars=[length, slot],
-        picked=3,
-        inner=[sums, own, queries, states],
-    )(low_xy, top_xy, w_in, cache, sums0, sums1, sums2, out_gain, out_weight, returned, owner_row)
-    via_x = across(top3, 1)
-    via_y = across(low3, 2)
-    top1, low1, top2, low2 = hbm_call(
-        functools.partial(fourth_kernel, heads), [piece] * 4, 2 * finish_flops, 4 * rows * D, scalars=[length]
-    )(all_states, queries1, own1, out_gain, out_weight, queries2, own2)
+    top1, low1, top2, low2 = attend((1, 2), (queries1, own1), (queries2, own2))
     one_x = across(top1, 1)
     one_y = across(low2, 2)
-    part = lax.optimization_barrier((part, top1))[0]
-    shares = lax.all_to_all(part.reshape(4, DEC // 4, D), "head", split_axis=0, concat_axis=0, tiled=True)
-    two_y, two_x = call(add_kernel, [piece, piece], 0, 6 * rows * D)(top2, via_x, low1, via_y)
+    two_y, two_x = hbm_call(add_kernel, [piece, piece], 0, size, here=(1, 3), near=(0, 1), waits=[top1])(top2, via_x, low1, via_y)
+    top0, low0, state_next = attend((0,), (queries0, own0), others=(one_x, one_y), keep=True, waits=[top1])
+    decoded = hbm_call(
+        functools.partial(return_kernel, heads, capacity),
+        [shape(TILE, D)] * 4,
+        2 * DEC * heads * WIDE * D,
+        2 * heads * WIDE * D,
+        loose=(0,),
+        waits=[top0],
+    )(returned, owner_row, out_weight)
+    shares = [decoded[0]] + [across(decoded[by], by) for by in (1, 2, 3)]
     two_y = across(two_y, 2)
     two_x = across(two_x, 1)
-    top0, low0 = hbm_call(
-        functools.partial(fifth_kernel, heads), [piece] * 2, finish_flops, 4 * rows * D, scalars=[length], waits=[two_x, two_y][:0]
-    )(all_states, queries0, own0, out_gain, out_weight)
     state_next = jnp.transpose(state_next, (0, 2, 3, 1))
-    decode_out = jnp.sum(shares.astype(F32), axis=0).astype(BF)
-    stretch_out = call(total_kernel, shape(1, rows, D), 0, 8 * rows * D)(top0, low0, one_x, one_y, two_y, two_x)
-    return (stretch_out, decode_out[None], state_next)
+    stretch_out, decode_out = hbm_call(
+        total_kernel, [shape(1, rows, D), shape(1, DEC // 4, D)], 0, 8 * rows * D, loose=(1, 2, 3, 6, 7)
+    )(*shares, top0, low0, two_y, two_x)
+    return (stretch_out, decode_out, state_next)
 
 
 def from_behind(array, axis, by):

time: 106 us -> 99.9 us (0.942)
  local copies, waits for them, and re-layouts: 9.72 us -> 0.01 us
  Pallas kernels: 48.2 us -> 56.9 us
  waiting for transfers between devices: 12.9 us -> 8.92 us
    unnamed x34 -> x2, local copies, waits for them, and re-layouts: 9.72 us -> 0.01 us
    pallas_call x10 -> x11, Pallas kernels: 47.2 us -> 56 us  [run(): pl.pallas_call(body, out_shape=[o if n in near else pltpu.HBM(o.shape, o....]
    all_to_all x1 -> x0, waiting for transfers between devices: 7.94 us -> none  [local_square(): lax.all_to_all(part.reshape(4, DEC // 4, D), 'head', split_axis=0, concat...]
    ppermute x12 -> x15, waiting for transfers between devices: 4.94 us -> 8.92 us  [across(): return lax.ppermute(array, 'head', [(i, i ^ by) for i in range(4)])]
    all_to_all x1 -> x0, starting transfers between devices: 3.31 us -> none  [local_square(): lax.all_to_all(part.reshape(4, DEC // 4, D), 'head', split_axis=0, concat...]
    ppermute x12 -> x15, starting transfers between devices: 13.6 us -> 16.3 us  [across(): return lax.ppermute(array, 'head', [(i, i ^ by) for i in range(4)])]
  transfers between devices with their start and end apart: 16 -> 18, of which waited for: 3 -> 6; matrix products, arithmetic and copies ran while one was open for 1% -> 0% of each run, Pallas kernels for 33% -> 44%
where the time goes in v3:
time: 99.9 us; the launch traced here: 99.3 us
  Pallas kernels  56.9 us (57%)
  starting transfers between devices  31.2 us (31%)
  waiting for transfers between devices  8.92 us (9%)
  between operations  2.29 us (2%)
    pallas_call x11, Pallas kernels, run(): pl.pallas_call(body, out_shape=[o if n in near else pltpu.HBM(o.shape, o....  56 us
    ppermute x15, starting transfers between devices, across(): return lax.ppermute(array, 'head', [(i, i ^ by) for i in range(4)])  16.3 us
    ppermute x15, waiting for transfers between devices, across(): return lax.ppermute(array, 'head', [(i, i ^ by) for i in range(4)])  8.92 us
    all_to_all x1, starting transfers between devices, local_square(): lax.all_to_all(served.reshape(groups, capacity, heads * WIDE), 'tok', spl...  5.04 us
    ppermute x1, starting transfers between devices, from_behind(): return lax.ppermute(array, axis, pairs)  4.98 us
    all_to_all x1, starting transfers between devices, local_square(): lax.all_to_all(sent.reshape(groups, capacity, wide), 'tok', split_axis=0,...  4.88 us
  transfers between devices with their start and end apart: 18, of which 6 were waited for; matrix products, arithmetic and copies ran while one was open for 0% of the time, Pallas kernels for 44%

profile of v3, /device:TPU:0, one launch (start us, length us, event | category | flops | bytes accessed | tf_op | source)
XLA Modules:
  0.0 99.3 jit_solution(5802002949889417116)
XLA Ops:
  0.6 3.1 %shard_map.158 = (bf16[128,1792]{1,0:T(8,128)(2,1)}, bf16[128,1792]{1,0:T(8,128)(2,1)}, bf16[16,1792]{1,0:T(8,128)(2,1)}, bf16[16,1792]{1,0:T(8,128)(2,1)}) custom-call(bf16[256,1792]{1,0:T(8,128)(2,1)} %bitcast.21, bf16[2,1792]{1,0:T(2,128)(2,1)} %bitcast.25, f32[1792]{0:T(1024)} %refs_2_.4, f32[3,1792]{1,0:T(4,128)} %taps_ref.1), custom_call_target="tpu_custom_call" | custom-call | flops 9175040 | bytes 1835008 | tf_op jit(solution)/shard_map/pallas_call | solution.py:465
  3.8 0.0 copy-start
  3.8 5.0 %collective-permute-start = (bf16[16,1792]{1,0:T(8,128)(2,1)}, bf16[16,1792]{1,0:T(8,128)(2,1)S(1)}, u32[]{:S(2)}, u32[]{:S(2)}) collective-permute-start(bf16[16,1792]{1,0:T(8,128)(2,1)} %get-tuple-element.40), channel_id=1, source_target_pairs={{0,8},{8,16},{16,24},{1,9},{9,17},{17,25},{2,10},{10,18},{18,26},{... | collective-permute-start | bytes 172040 | tf_op jit(solution)/shard_map/ppermute | solution.py:646
  8.8 1.6 %collective-permute-start.1 = (bf16[128,1792]{1,0:T(8,128)(2,1)}, bf16[128,1792]{1,0:T(8,128)(2,1)S(1)}, u32[]{:S(2)}, u32[]{:S(2)}) collective-permute-start(bf16[128,1792]{1,0:T(8,128)(2,1)} %get-tuple-element.37.refs_1_), channel_id=1, source_target_pairs={{0,16},{8,24},{16,0},{24,8},{1,17},{9,25},{17,1},{25,9},{2,18},{10... | collective-permute-start | bytes 1376264 | tf_op jit(solution)/shard_map/ppermute | solution.py:488
  10.4 3.4 %shard_map.157.wait_ref = bf16[64,640]{1,0:T(8,128)(2,1)} custom-call(bf16[32,1792]{1,0:T(8,128)(2,1)} %bitcast.24, bf16[32,2,1792]{2,1,0:T(2,128)(2,1)} %bitcast.23, f32[1792]{0:T(1024)} %refs_2_.4, f32[3,1792]{1,0:T(4,128)} %taps_ref.1, s32[1,32]{1,0:T(1,128)} %bitcast.26, s32[1,32]{1,0:T(1,128)} %refs_5_.2, bf16[4,144,1792]{2,1,0:T(8,128)(2,1)} %bitcast.17), custom_call_target="tpu_custom_call" | custom-call | flops 73400320 | bytes 2293760 | tf_op jit(solution)/shard_map/pallas_call | solution.py:465
  13.8 0.0 collective-permute-done.end_ref
  13.8 0.9 shard_map.159.refs_2_
  14.7 0.7 collective-permute-start.2
  15.4 4.9 %all-to-all-start = ((bf16[8,8,640]{2,1,0:T(8,128)(2,1)}), bf16[8,8,640]{2,1,0:T(8,128)(2,1)S(1)}, u32[]{:S(2)}, u32[]{:S(2)}) async-start(bf16[8,8,640]{2,1,0:T(8,128)(2,1)} %bitcast.22), calls=%async_computation | async-start | bytes 163840 | tf_op jit(solution)/shard_map/all_to_all | solution.py:550
  20.3 0.0 copy-done
  20.3 1.5 %collective-permute-start.5 = (bf16[128,1792]{1,0:T(8,128)(2,1)S(1)}, bf16[128,1792]{1,0:T(8,128)(2,1)S(1)}, u32[]{:S(2)}, u32[]{:S(2)}) collective-permute-start(bf16[128,1792]{1,0:T(8,128)(2,1)S(1)} %copy-done), channel_id=1, source_target_pairs={{0,8},{8,0},{16,24},{24,16},{1,9},{9,1},{17,25},{25,17},{2,10},{10... | collective-permute-start | bytes 1376264 | tf_op jit(solution)/shard_map/ppermute | solution.py:488
  22.4 1.2 %collective-permute-start.6 = (bf16[128,1792]{1,0:T(8,128)(2,1)}, bf16[128,1792]{1,0:T(8,128)(2,1)S(1)}, u32[]{:S(2)}, u32[]{:S(2)}) collective-permute-start(bf16[128,1792]{1,0:T(8,128)(2,1)} %shard_map.159.refs_2_), channel_id=1, source_target_pairs={{0,16},{8,24},{16,0},{24,8},{1,17},{9,25},{17,1},{25,9},{2,18},{10... | collective-permute-start | bytes 1376264 | tf_op jit(solution)/shard_map/ppermute | solution.py:488
  23.6 4.9 %shard_map.160 = (f32[4,384,128]{2,1,0:T(8,128)}, f32[4,256,128]{2,1,0:T(8,128)}, bf16[256,64]{1,0:T(8,128)(2,1)}) custom-call(s32[1]{0:T(128)S(6)} %copy.19.refs_0_, bf16[128,1792]{1,0:T(8,128)(2,1)} %get-tuple-element.37.refs_1_, bf16[128,1792]{1,0:T(8,128)(2,1)} %shard_map.159.refs_2_, bf16[4,144,1792]{2,1,0:T(8,128)(2,1)} %bitcast.18), custom_call_target="tpu_custom_call" | custom-call | flops 788529152 | bytes 1835008 | tf_op jit(solution)/shard_map/pallas_call | solution.py:465
  28.5 0.0 all-to-all-done
  28.6 6.6 %shard_map.161.refs_9_ = bf16[64,512]{1,0:T(8,128)(2,1)} custom-call(bf16[64,640]{1,0:T(8,128)(2,1)S(1)} %bitcast.13, f32[448]{0:T(512)} %refs_3_.7, f32[1,16,273,4,112]{4,3,2,1,0:T(4,128)} %bitcast.15, bf16[256,64]{1,0:T(8,128)(2,1)} %get-tuple-element.41.refs_3_.refs_5_), custom_call_target="tpu_custom_call" | custom-call | flops 1001914368 | bytes 8945664 | tf_op jit(solution)/shard_map/pallas_call | solution.py:465
  35.2 0.0 collective-permute-done.1.refs_5_
  35.2 0.0 collective-permute-done.2.refs_3_
  35.2 1.6 %collective-permute-start.3 = (bf16[128,1792]{1,0:T(8,128)(2,1)S(1)}, bf16[128,1792]{1,0:T(8,128)(2,1)S(1)}, u32[]{:S(2)}, u32[]{:S(2)}) collective-permute-start(bf16[128,1792]{1,0:T(8,128)(2,1)S(1)} %collective-permute-done.1.refs_5_), channel_id=1, source_target_pairs={{0,8},{8,0},{16,24},{24,16},{1,9},{9,1},{17,25},{25,17},{2,10},{10... | collective-permute-start | bytes 1376264 | tf_op jit(solution)/shard_map/ppermute | solution.py:488
  36.7 0.0 collective-permute-start.4
  37.4 0.0 collective-permute-done.5.refs_2_
  37.4 0.0 collective-permute-done.6.refs_6_
  37.4 9.5 %shard_map.162 = (f32[4,256,128]{2,1,0:T(8,128)}, bf16[256,64]{1,0:T(8,128)(2,1)}, f32[4,256,128]{2,1,0:T(8,128)}, bf16[256,64]{1,0:T(8,128)(2,1)}, bf16[4,384,1...) custom-call(s32[1]{0:T(128)S(6)} %copy.19.refs_0_, s32[1]{0:T(128)S(6)} %copy.20.refs_1_, ...), custom_call_target="tpu_custom_call" | custom-call | flops 1577058304 | bytes 3670016 | tf_op jit(solution)/shard_map/pallas_call | solution.py:465
  46.9 0.6 collective-permute-done.3.refs_1_
  47.6 1.2 %collective-permute-done.4.refs_2_ = bf16[128,1792]{1,0:T(8,128)(2,1)S(1)} collective-permute-done((bf16[128,1792]{1,0:T(8,128)(2,1)S(1)}, bf16[128,1792]{1,0:T(8,128)(2,1)S(1)}, u32[]{:S(2)}, u32[]{:S(2)}) %collective-permute-start.4) | collective-permute-done | bytes 458784 | tf_op jit(solution)/shard_map/ppermute | solution.py:488
  48.8 7.1 %shard_map.163 = (bf16[128,1792]{1,0:T(8,128)(2,1)S(1)}, bf16[128,1792]{1,0:T(8,128)(2,1)S(1)}, f32[4,384,128]{2,1,0:T(8,128)}) custom-call(s32[1]{0:T(128)S(6)} %copy.19.refs_0_, bf16[128,1792]{1,0:T(8,128)(2,1)S(1)} %collective-permute-done.3.refs_1_, bf16[128,1792]{1,0:T(8,128)(2,1)S(1)} %collective-permute-done.4.refs_2_, ...), custom_call_target="tpu_custom_call" | custom-call | flops 1358954496 | bytes 1835008 | tf_op jit(solution)/shard_map/pallas_call | solution.py:465
  55.9 0.6 collective-permute-start.12
  56.5 0.9 collective-permute-start.13
  57.4 7.9 %shard_map.164 = (bf16[128,1792]{1,0:T(8,128)(2,1)}, bf16[128,1792]{1,0:T(8,128)(2,1)}, bf16[128,1792]{1,0:T(8,128)(2,1)}, bf16[128,1792]{1,0:T(8,128)(2,1)}) custom-call(s32[1]{0:T(128)S(6)} %copy.19.refs_0_, f32[4,4,384,128]{3,2,1,0:T(8,128)} %get-tuple-element.49.refs_1_, f32[4,384,128]{2,1,0:T(8,128)} %get-tuple-element.50.refs_2_, f32[448]{0:T(512)} %refs_3_.7, ...), custom_call_target="tpu_custom_call" | custom-call | flops 1140850688 | bytes 1835008 | tf_op jit(solution)/shard_map/pallas_call | solution.py:465
  65.3 0.9 collective-permute-start.7
  66.2 1.7 %collective-permute-start.8 = (bf16[128,1792]{1,0:T(8,128)(2,1)}, bf16[128,1792]{1,0:T(8,128)(2,1)S(1)}, u32[]{:S(2)}, u32[]{:S(2)}) collective-permute-start(bf16[128,1792]{1,0:T(8,128)(2,1)} %get-tuple-element.56), channel_id=1, source_target_pairs={{0,16},{8,24},{16,0},{24,8},{1,17},{9,25},{17,1},{25,9},{2,18},{10... | collective-permute-start | bytes 1376264 | tf_op jit(solution)/shard_map/ppermute | solution.py:488
  68.0 0.0 collective-permute-done.12.refs_1_
  68.0 0.0 collective-permute-done.13.refs_3_
  68.0 1.3 %shard_map.167 = (bf16[128,1792]{1,0:T(8,128)(2,1)S(1)}, bf16[128,1792]{1,0:T(8,128)(2,1)S(1)}) custom-call(bf16[128,1792]{1,0:T(8,128)(2,1)} %get-tuple-element.63.refs_0_, bf16[128,1792]{1,0:T(8,128)(2,1)S(1)} %collective-permute-done.12.refs_1_, bf16[128,1792]{1,0:T(8,128)(2,1)} %get-tuple-element.64.refs_2_, ...), custom_call_target="tpu_custom_call" | custom-call | bytes 1835008 | tf_op jit(solution)/shard_map/pallas_call | solution.py:465
  69.3 0.4 collective-permute-start.14
  69.6 1.7 %collective-permute-start.15 = (bf16[128,1792]{1,0:T(8,128)(2,1)S(1)}, bf16[128,1792]{1,0:T(8,128)(2,1)S(1)}, u32[]{:S(2)}, u32[]{:S(2)}) collective-permute-start(bf16[128,1792]{1,0:T(8,128)(2,1)S(1)} %get-tuple-element.67), channel_id=1, source_target_pairs={{0,8},{8,0},{16,24},{24,16},{1,9},{9,1},{17,25},{25,17},{2,10},{10... | collective-permute-start | bytes 1376264 | tf_op jit(solution)/shard_map/ppermute | solution.py:488
  71.3 5.0 %all-to-all-start.1 = ((bf16[8,8,512]{2,1,0:T(8,128)(2,1)}), bf16[8,8,512]{2,1,0:T(8,128)(2,1)S(1)}, u32[]{:S(2)}, u32[]{:S(2)}) async-start(bf16[8,8,512]{2,1,0:T(8,128)(2,1)} %bitcast.10), calls=%async_computation.1 | async-start | bytes 131072 | tf_op jit(solution)/shard_map/all_to_all | solution.py:617
  76.4 2.7 %collective-permute-done.7.refs_7_ = bf16[128,1792]{1,0:T(8,128)(2,1)S(1)} collective-permute-done((bf16[128,1792]{1,0:T(8,128)(2,1)}, bf16[128,1792]{1,0:T(8,128)(2,1)S(1)}, u32[]{:S(2)}, u32[]{:S(2)}) %collective-permute-start.7) | collective-permute-done | bytes 458784 | tf_op jit(solution)/shard_map/ppermute | solution.py:488
  79.0 0.9 collective-permute-done.8.refs_8_
  79.9 6.9 %shard_map.165 = (bf16[128,1792]{1,0:T(8,128)(2,1)}, bf16[128,1792]{1,0:T(8,128)(2,1)}, f32[1,273,4,112]{3,2,1,0:T(4,128)}) custom-call(s32[1]{0:T(128)S(6)} %copy.19.refs_0_, f32[4,4,384,128]{3,2,1,0:T(8,128)} %get-tuple-element.49.refs_1_, f32[4,384,128]{2,1,0:T(8,128)} %get-tuple-element.50.refs_2_, f32[448]{0:T(512)} %refs_3_.7, ...), custom_call_target="tpu_custom_call" | custom-call | flops 570425344 | bytes 1835008 | tf_op jit(solution)/shard_map/pallas_call | solution.py:465
  86.8 0.0 all-to-all-done.1
  86.8 2.7 %shard_map.166 = (bf16[16,1792]{1,0:T(8,128)(2,1)}, bf16[16,1792]{1,0:T(8,128)(2,1)}, bf16[16,1792]{1,0:T(8,128)(2,1)}, bf16[16,1792]{1,0:T(8,128)(2,1)}) custom-call(bf16[64,512]{1,0:T(8,128)(2,1)S(1)} %bitcast.14, s32[1,32]{1,0:T(1,128)} %bitcast.27, bf16[448,1792]{1,0:T(8,128)(2,1)} %refs_2_.5, bf16[128,1792]{1,0:T(8,128)(2,1)} %get-tuple-element.57.refs_3_.refs_4_), custom_call_target="tpu_custom_call" | custom-call | flops 58720256 | bytes 1835008 | tf_op jit(solution)/shard_map/pallas_call | solution.py:465
  89.5 1.8 %collective-permute-start.10 = (bf16[16,1792]{1,0:T(8,128)(2,1)}, bf16[16,1792]{1,0:T(8,128)(2,1)S(1)}, u32[]{:S(2)}, u32[]{:S(2)}) collective-permute-start(bf16[16,1792]{1,0:T(8,128)(2,1)} %get-tuple-element.60), channel_id=1, source_target_pairs={{0,16},{8,24},{16,0},{24,8},{1,17},{9,25},{17,1},{25,9},{2,18},{10... | collective-permute-start | bytes 172040 | tf_op jit(solution)/shard_map/ppermute | solution.py:488
  91.3 0.9 collective-permute-start.11
  92.2 0.9 collective-permute-start.9
  93.0 0.9 collective-permute-done.10.refs_2_
  93.9 2.6 %collective-permute-done.11.refs_3_ = bf16[16,1792]{1,0:T(8,128)(2,1)S(1)} collective-permute-done((bf16[16,1792]{1,0:T(8,128)(2,1)}, bf16[16,1792]{1,0:T(8,128)(2,1)S(1)}, u32[]{:S(2)}, u32[]{:S(2)}) %collective-permute-start.11) | collective-permute-done | bytes 57376 | tf_op jit(solution)/shard_map/ppermute | solution.py:488
  96.6 0.0 collective-permute-done.9.refs_1_
  96.6 0.0 collective-permute-done.14.refs_6_
  96.6 0.0 collective-permute-done.15.refs_7_
  96.6 2.5 %shard_map.168 = (bf16[1,256,1792]{2,1,0:T(8,128)(2,1)}, bf16[1,8,1792]{2,1,0:T(8,128)(2,1)}) custom-call(bf16[16,1792]{1,0:T(8,128)(2,1)} %get-tuple-element.58.refs_0_, bf16[16,1792]{1,0:T(8,128)(2,1)S(1)} %collective-permute-done.9.refs_1_, bf16[16,1792]{1,0:T(8,128)(2,1)S(1)} %collective-permute-done.10.refs_2_, ...), custom_call_target="tpu_custom_call" | custom-call | bytes 3670016 | tf_op jit(solution)/shard_map/pallas_call | solution.py:465
Async XLA Ops:
  3.8 16.5 %copy-start = (bf16[128,1792]{1,0:T(8,128)(2,1)S(1)}, bf16[128,1792]{1,0:T(8,128)(2,1)}, u32[]{:S(2)}) copy-start(bf16[128,1792]{1,0:T(8,128)(2,1)} %get-tuple-element.37.refs_1_) | copy-start | bytes 1376260
  3.8 10.0 %collective-permute-start = (bf16[16,1792]{1,0:T(8,128)(2,1)}, bf16[16,1792]{1,0:T(8,128)(2,1)S(1)}, u32[]{:S(2)}, u32[]{:S(2)}) collective-permute-start(bf16[16,1792]{1,0:T(8,128)(2,1)} %get-tuple-element.40), channel_id=1, source_target_pairs={{0,8},{8,16},{16,24},{1,9},{9,17},{17,25},{2,10},{10,18},{18,26},{... | collective-permute-start | bytes 172040 | tf_op jit(solution)/shard_map/ppermute | solution.py:646
  8.8 26.4 %collective-permute-start.1 = (bf16[128,1792]{1,0:T(8,128)(2,1)}, bf16[128,1792]{1,0:T(8,128)(2,1)S(1)}, u32[]{:S(2)}, u32[]{:S(2)}) collective-permute-start(bf16[128,1792]{1,0:T(8,128)(2,1)} %get-tuple-element.37.refs_1_), channel_id=1, source_target_pairs={{0,16},{8,24},{16,0},{24,8},{1,17},{9,25},{17,1},{25,9},{2,18},{10... | collective-permute-start | bytes 1376264 | tf_op jit(solution)/shard_map/ppermute | solution.py:488
  14.7 20.5 %collective-permute-start.2 = (bf16[128,1792]{1,0:T(8,128)(2,1)}, bf16[128,1792]{1,0:T(8,128)(2,1)S(1)}, u32[]{:S(2)}, u32[]{:S(2)}) collective-permute-start(bf16[128,1792]{1,0:T(8,128)(2,1)} %shard_map.159.refs_2_), channel_id=1, source_target_pairs={{0,8},{8,0},{16,24},{24,16},{1,9},{9,1},{17,25},{25,17},{2,10},{10... | collective-permute-start | bytes 1376264 | tf_op jit(solution)/shard_map/ppermute | solution.py:488
  15.4 13.2 %all-to-all-start = ((bf16[8,8,640]{2,1,0:T(8,128)(2,1)}), bf16[8,8,640]{2,1,0:T(8,128)(2,1)S(1)}, u32[]{:S(2)}, u32[]{:S(2)}) async-start(bf16[8,8,640]{2,1,0:T(8,128)(2,1)} %bitcast.22), calls=%async_computation | async-start | bytes 163840 | tf_op jit(solution)/shard_map/all_to_all | solution.py:550
  20.3 17.1 %collective-permute-start.5 = (bf16[128,1792]{1,0:T(8,128)(2,1)S(1)}, bf16[128,1792]{1,0:T(8,128)(2,1)S(1)}, u32[]{:S(2)}, u32[]{:S(2)}) collective-permute-start(bf16[128,1792]{1,0:T(8,128)(2,1)S(1)} %copy-done), channel_id=1, source_target_pairs={{0,8},{8,0},{16,24},{24,16},{1,9},{9,1},{17,25},{25,17},{2,10},{10... | collective-permute-start | bytes 1376264 | tf_op jit(solution)/shard_map/ppermute | solution.py:488
  22.4 15.0 %collective-permute-start.6 = (bf16[128,1792]{1,0:T(8,128)(2,1)}, bf16[128,1792]{1,0:T(8,128)(2,1)S(1)}, u32[]{:S(2)}, u32[]{:S(2)}) collective-permute-start(bf16[128,1792]{1,0:T(8,128)(2,1)} %shard_map.159.refs_2_), channel_id=1, source_target_pairs={{0,16},{8,24},{16,0},{24,8},{1,17},{9,25},{17,1},{25,9},{2,18},{10... | collective-permute-start | bytes 1376264 | tf_op jit(solution)/shard_map/ppermute | solution.py:488
  35.2 12.4 %collective-permute-start.3 = (bf16[128,1792]{1,0:T(8,128)(2,1)S(1)}, bf16[128,1792]{1,0:T(8,128)(2,1)S(1)}, u32[]{:S(2)}, u32[]{:S(2)}) collective-permute-start(bf16[128,1792]{1,0:T(8,128)(2,1)S(1)} %collective-permute-done.1.refs_5_), channel_id=1, source_target_pairs={{0,8},{8,0},{16,24},{24,16},{1,9},{9,1},{17,25},{25,17},{2,10},{10... | collective-permute-start | bytes 1376264 | tf_op jit(solution)/shard_map/ppermute | solution.py:488
  36.7 12.0 %collective-permute-start.4 = (bf16[128,1792]{1,0:T(8,128)(2,1)S(1)}, bf16[128,1792]{1,0:T(8,128)(2,1)S(1)}, u32[]{:S(2)}, u32[]{:S(2)}) collective-permute-start(bf16[128,1792]{1,0:T(8,128)(2,1)S(1)} %collective-permute-done.2.refs_3_), channel_id=1, source_target_pairs={{0,16},{8,24},{16,0},{24,8},{1,17},{9,25},{17,1},{25,9},{2,18},{10... | collective-permute-start | bytes 1376264 | tf_op jit(solution)/shard_map/ppermute | solution.py:488
  55.9 12.1 %collective-permute-start.12 = (bf16[128,1792]{1,0:T(8,128)(2,1)S(1)}, bf16[128,1792]{1,0:T(8,128)(2,1)S(1)}, u32[]{:S(2)}, u32[]{:S(2)}) collective-permute-start(bf16[128,1792]{1,0:T(8,128)(2,1)S(1)} %get-tuple-element.47), channel_id=1, source_target_pairs={{0,8},{8,0},{16,24},{24,16},{1,9},{9,1},{17,25},{25,17},{2,10},{10... | collective-permute-start | bytes 1376264 | tf_op jit(solution)/shard_map/ppermute | solution.py:488
  56.5 11.5 %collective-permute-start.13 = (bf16[128,1792]{1,0:T(8,128)(2,1)S(1)}, bf16[128,1792]{1,0:T(8,128)(2,1)S(1)}, u32[]{:S(2)}, u32[]{:S(2)}) collective-permute-start(bf16[128,1792]{1,0:T(8,128)(2,1)S(1)} %get-tuple-element.65), channel_id=1, source_target_pairs={{0,16},{8,24},{16,0},{24,8},{1,17},{9,25},{17,1},{25,9},{2,18},{10... | collective-permute-start | bytes 1376264 | tf_op jit(solution)/shard_map/ppermute | solution.py:488
  65.3 13.7 %collective-permute-start.7 = (bf16[128,1792]{1,0:T(8,128)(2,1)}, bf16[128,1792]{1,0:T(8,128)(2,1)S(1)}, u32[]{:S(2)}, u32[]{:S(2)}) collective-permute-start(bf16[128,1792]{1,0:T(8,128)(2,1)} %get-tuple-element.55.refs_9_.refs_4_), channel_id=1, source_target_pairs={{0,8},{8,0},{16,24},{24,16},{1,9},{9,1},{17,25},{25,17},{2,10},{10... | collective-permute-start | bytes 1376264 | tf_op jit(solution)/shard_map/ppermute | solution.py:488
  66.2 13.7 %collective-permute-start.8 = (bf16[128,1792]{1,0:T(8,128)(2,1)}, bf16[128,1792]{1,0:T(8,128)(2,1)S(1)}, u32[]{:S(2)}, u32[]{:S(2)}) collective-permute-start(bf16[128,1792]{1,0:T(8,128)(2,1)} %get-tuple-element.56), channel_id=1, source_target_pairs={{0,16},{8,24},{16,0},{24,8},{1,17},{9,25},{17,1},{25,9},{2,18},{10... | collective-permute-start | bytes 1376264 | tf_op jit(solution)/shard_map/ppermute | solution.py:488
  69.3 27.3 %collective-permute-start.14 = (bf16[128,1792]{1,0:T(8,128)(2,1)S(1)}, bf16[128,1792]{1,0:T(8,128)(2,1)S(1)}, u32[]{:S(2)}, u32[]{:S(2)}) collective-permute-start(bf16[128,1792]{1,0:T(8,128)(2,1)S(1)} %get-tuple-element.66), channel_id=1, source_target_pairs={{0,16},{8,24},{16,0},{24,8},{1,17},{9,25},{17,1},{25,9},{2,18},{10... | collective-permute-start | bytes 1376264 | tf_op jit(solution)/shard_map/ppermute | solution.py:488
  69.6 27.0 %collective-permute-start.15 = (bf16[128,1792]{1,0:T(8,128)(2,1)S(1)}, bf16[128,1792]{1,0:T(8,128)(2,1)S(1)}, u32[]{:S(2)}, u32[]{:S(2)}) collective-permute-start(bf16[128,1792]{1,0:T(8,128)(2,1)S(1)} %get-tuple-element.67), channel_id=1, source_target_pairs={{0,8},{8,0},{16,24},{24,16},{1,9},{9,1},{17,25},{25,17},{2,10},{10... | collective-permute-start | bytes 1376264 | tf_op jit(solution)/shard_map/ppermute | solution.py:488
  71.3 15.5 %all-to-all-start.1 = ((bf16[8,8,512]{2,1,0:T(8,128)(2,1)}), bf16[8,8,512]{2,1,0:T(8,128)(2,1)S(1)}, u32[]{:S(2)}, u32[]{:S(2)}) async-start(bf16[8,8,512]{2,1,0:T(8,128)(2,1)} %bitcast.10), calls=%async_computation.1 | async-start | bytes 131072 | tf_op jit(solution)/shard_map/all_to_all | solution.py:617
  89.5 4.5 %collective-permute-start.10 = (bf16[16,1792]{1,0:T(8,128)(2,1)}, bf16[16,1792]{1,0:T(8,128)(2,1)S(1)}, u32[]{:S(2)}, u32[]{:S(2)}) collective-permute-start(bf16[16,1792]{1,0:T(8,128)(2,1)} %get-tuple-element.60), channel_id=1, source_target_pairs={{0,16},{8,24},{16,0},{24,8},{1,17},{9,25},{17,1},{25,9},{2,18},{10... | collective-permute-start | bytes 172040 | tf_op jit(solution)/shard_map/ppermute | solution.py:488
  91.3 5.3 %collective-permute-start.11 = (bf16[16,1792]{1,0:T(8,128)(2,1)}, bf16[16,1792]{1,0:T(8,128)(2,1)S(1)}, u32[]{:S(2)}, u32[]{:S(2)}) collective-permute-start(bf16[16,1792]{1,0:T(8,128)(2,1)} %get-tuple-element.61), channel_id=1, source_target_pairs={{0,24},{8,16},{16,8},{24,0},{1,25},{9,17},{17,9},{25,1},{2,26},{10... | collective-permute-start | bytes 172040 | tf_op jit(solution)/shard_map/ppermute | solution.py:488
  92.2 4.4 %collective-permute-start.9 = (bf16[16,1792]{1,0:T(8,128)(2,1)}, bf16[16,1792]{1,0:T(8,128)(2,1)S(1)}, u32[]{:S(2)}, u32[]{:S(2)}) collective-permute-start(bf16[16,1792]{1,0:T(8,128)(2,1)} %get-tuple-element.59), channel_id=1, source_target_pairs={{0,8},{8,0},{16,24},{24,16},{1,9},{9,1},{17,25},{25,17},{2,10},{10... | collective-permute-start | bytes 172040 | tf_op jit(solution)/shard_map/ppermute | solution.py:488

commit v4 on v3

--- a/solution.py
+++ b/solution.py
@@ -124,27 +124,33 @@
         back.wait()
 
 
-def block_part(slot, heads, length, conved, w_ref, sums, own):
-    rows = conved.shape[0]
-    qkv = dot(conved, projection(w_ref, heads), ((1,), (1,))).astype(BF)
+def qkv_of(heads, top, low, w_ref):
+    conved = jnp.concatenate([top[...], low[...]], axis=0)
+    return dot(conved, projection(w_ref, heads), ((1,), (1,))).astype(BF)
+
+
+def parts_of(qkv, heads, head):
+    at = 2 * heads * F + head * WIDE
+    return qkv[:, head * F : (head + 1) * F], qkv[:, (heads + head) * F : (heads + head + 1) * F], qkv[:, at : at + WIDE]
+
+
+def sums_of(slot, heads, head, length, qkv, pick):
+    _, k, v = parts_of(qkv, heads, head)
+    live = length - v.shape[0] * (lax.axis_index("head") ^ slot)
+    live_row = lax.broadcasted_iota(jnp.int32, v.shape, 0) < live
+    v = jnp.where(live_row, v.astype(F32), 0.0).astype(BF)
+    return dot(phi_of(k, pick).astype(BF), v, ((0,), (0,)))
+
+
+def own_of(slot, heads, head, length, qkv):
+    q, k, v = parts_of(qkv, heads, head)
+    rows = v.shape[0]
     live = length - rows * (lax.axis_index("head") ^ slot)
     row = lax.broadcasted_iota(jnp.int32, (rows, rows), 0)
     col = lax.broadcasted_iota(jnp.int32, (rows, rows), 1)
-    allowed = (col <= row) & (col < live)
-    live_row = lax.broadcasted_iota(jnp.int32, (rows, WIDE), 0) < live
-    pick = spreader()
-    keys = [qkv[:, (heads + head) * F : (heads + head) * F + F] for head in range(heads)]
-    values = [qkv[:, 2 * heads * F + head * WIDE : 2 * heads * F + (head + 1) * WIDE] for head in range(heads)]
-    for head in range(heads):
-        live_values = jnp.where(live_row, values[head].astype(F32), 0.0).astype(BF)
-        sums[head] = dot(phi_of(keys[head], pick).astype(BF), live_values, ((0,), (0,)))
-        sums.push(head)
-    for head in range(heads):
-        inner = dot(qkv[:, head * F : head * F + F], keys[head], ((1,), (1,))) * (1.0 / math.sqrt(F))
-        weights = jnp.where(allowed, 1.0 + inner + 0.5 * inner * inner, 0.0).astype(BF)
-        own[head] = dot(weights, values[head])
-        own.push(head)
-    return qkv[:, : heads * F]
+    shifted = dot(q, k, ((1,), (1,))) * (1.0 / math.sqrt(F)) + 1.0
+    weights = jnp.where((col <= row) & (col < live), 0.5 * shifted * shifted + 0.5, 0.0).astype(BF)
+    return dot(weights, v)
 
 
 def old_state(cache_ref, head):
@@ -165,80 +171,95 @@
     return jnp.where(live_row, total, 0.0).astype(BF)
 
 
-def project_part(parts, heads, w_ref, top, low, others=()):
+def project_part(parts, heads, w_ref, top, low):
     attended = jnp.concatenate(parts, axis=1)
     half = low.shape[0]
     w_out = out_projection(w_ref, heads)
-    for order, (out, rows) in enumerate(((top, attended[:half]), (low, attended[half:]))):
-        total = dot(rows, w_out)
-        if others:
-            total = total + others[order][...].astype(F32)
-        out[...] = total.astype(BF)
+    for out, rows in ((top, attended[:half]), (low, attended[half:])):
+        out[...] = dot(rows, w_out).astype(BF)
         out.push()
 
 
 def first_kernel(heads, len_ref, low, top, w_ref, sums, own, queries):
-    conved = jnp.concatenate([top[...], low[...]], axis=0)
-    queries[...] = block_part(0, heads, len_ref[0], conved, w_ref, sums, own)
-
-
-def second_kernel(
-    heads, len_ref, low1, top1, w_ref, low2, top2, cache, sums0, own1, queries1, own2, queries2, state3, bases, sums1, sums2
-):
-    conved = jnp.concatenate([top1[...], low1[...]], axis=0)
-    sums1, sums2 = Near(sums1), Near(sums2)
-    queries1[...] = block_part(1, heads, len_ref[0], conved, w_ref, sums1, own1)
-    queries1.push()
-    conved = jnp.concatenate([top2[...], low2[...]], axis=0)
-    queries2[...] = block_part(2, heads, len_ref[0], conved, w_ref, sums2, own2)
-    queries2.push()
+    qkv = qkv_of(heads, top, low, w_ref)
+    pick = spreader()
+    for head in range(heads):
+        sums[head] = sums_of(0, heads, head, len_ref[0], qkv, pick)
+    sums.push()
+    for head in range(heads):
+        own[head] = own_of(0, heads, head, len_ref[0], qkv)
+    queries[...] = qkv[:, : heads * F]
+
+
+def second_kernel(heads, len_ref, low1, top1, w_ref, low2, top2, cache, sums0, sums1, qkv1, sums2, qkv2, state3):
+    pick = spreader()
+    for slot, low, top, sums, qkv in ((1, low1, top1, sums1, qkv1), (2, low2, top2, sums2, qkv2)):
+        found = qkv_of(heads, top, low, w_ref)
+        qkv[...] = found
+        qkv.push()
+        for head in range(heads):
+            sums[head] = sums_of(slot, heads, head, len_ref[0], found, pick)
+        sums.push()
+    for head in range(heads):
+        state3[head] = state_before(3, old_state(cache, head), (sums0[head], sums1[head], sums2[head]))
+
+
+def state_before(slot, old, sums):
     mine = lax.axis_index("head")
-    for head in range(heads):
-        old, sums = old_state(cache, head), (sums0[head], sums1[head], sums2[head])
-        for slot in range(4):
-            total = old
-            for other in range(3):
-                if other != slot:
-                    total = total + ((mine ^ other) < (mine ^ slot)).astype(F32) * sums[other]
-            if slot == 3:
-                state3[head] = total.astype(BF)
-            else:
-                bases[slot, head] = total
-        bases[3, head] = old + (sums[0] + (sums[1] + sums[2]))
-
-
-def third_kernel(heads, len_ref, low, top, w_ref, state3, gain_ref, out_w_ref, top3, low3, sums3, own):
+    for other, part in enumerate(sums):
+        if other != slot:
+            old = old + ((mine ^ other) < (mine ^ slot)).astype(F32) * part
+    return old.astype(BF)
+
+
+def third_kernel(heads, len_ref, low, top, w_ref, state3, gain_ref, out_w_ref, top3, low3, qkv3):
     length = len_ref[0]
-    conved = jnp.concatenate([top[...], low[...]], axis=0)
-    own = Near(own)
-    queries = block_part(3, heads, length, conved, w_ref, sums3, own)
+    qkv = qkv_of(heads, top, low, w_ref)
+    qkv3[...] = qkv
+    qkv3.push()
     pick = spreader()
     parts = []
     for head in range(heads):
-        q = queries[:, head * F : head * F + F]
-        parts.append(attend_part(3, head, heads, length, q, own[head], state3[head], gain_ref, pick))
+        q = parts_of(qkv, heads, head)[0]
+        own = own_of(3, heads, head, length, qkv)
+        parts.append(attend_part(3, head, heads, length, q, own, state3[head], gain_ref, pick))
     project_part(parts, heads, out_w_ref, top3, low3)
 
 
-def attend_kernel(heads, slots, adds, len_ref, bases, sums3, gain_ref, out_w_ref, *refs):
-    queries, own, refs = refs[: len(slots)], refs[len(slots) : 2 * len(slots)], refs[2 * len(slots) :]
-    others, outs = refs[:adds], refs[adds:]
-    mine = lax.axis_index("head")
+def fourth_kernel(
+    heads, len_ref, qkv3, qkv1, cache, sums0, sums1, sums2, qkv2, gain_ref, out_w_ref, top1, low1, top2, low2, sums3
+):
     pick = spreader()
-    for order, slot in enumerate(slots):
+    length = len_ref[0]
+    for head in range(heads):
+        sums3[head] = sums_of(3, heads, head, length, qkv3, pick)
+    sums3.push()
+    for slot, qkv, top, low in ((1, qkv1, top1, low1), (2, qkv2, top2, low2)):
         parts = []
         for head in range(heads):
-            q = queries[order][:, head * F : (head + 1) * F]
-            state = bases[slot, head] + ((mine ^ 3) < (mine ^ slot)).astype(F32) * sums3[head]
-            parts.append(attend_part(slot, head, heads, len_ref[0], q, own[order][head], state.astype(BF), gain_ref, pick))
-        project_part(parts, heads, out_w_ref, outs[2 * order], outs[2 * order + 1], others)
-    if len(outs) > 2 * len(slots):
-        state_next = outs[-1]
-        for head in range(heads):
-            new = (bases[3, head] + sums3[head])[:, :DH]
-            state_next[0, F + 1 :, head, :] = new[:QUAD]
-            state_next[0, 1 : F + 1, head, :] = new[QUAD : QUAD + F]
-            state_next[0, 0:1, head, :] = new[QUAD + F : QUAD + F + 1]
+            q = parts_of(qkv, heads, head)[0]
+            own = own_of(slot, heads, head, length, qkv)
+            state = state_before(slot, old_state(cache, head), (sums0[head], sums1[head], sums2[head], sums3[head]))
+            parts.append(attend_part(slot, head, heads, length, q, own, state, gain_ref, pick))
+        project_part(parts, heads, out_w_ref, top, low)
+
+
+def fifth_kernel(
+    heads, len_ref, cache, sums0, sums1, sums2, sums3, queries, own, gain_ref, out_w_ref, top0, low0, state_next
+):
+    pick = spreader()
+    parts = []
+    for head in range(heads):
+        old = old_state(cache, head)
+        sums = [part[head] for part in (sums0, sums1, sums2, sums3)]
+        q = queries[:, head * F : (head + 1) * F]
+        state = state_before(0, old, sums)
+        parts.append(attend_part(0, head, heads, len_ref[0], q, own[head], state, gain_ref, pick))
+        new = (old + (sums[0] + sums[1]) + (sums[2] + sums[3]))[:, :DH]
+        state_next[0, F + 1 :, head, :] = new[:QUAD]
+        state_next[0, 1 : F + 1, head, :] = new[QUAD : QUAD + F]
+        state_next[0, 0:1, head, :] = new[QUAD + F : QUAD + F + 1]
+    project_part(parts, heads, out_w_ref, top0, low0)
 
 
 def add_kernel(top2, via_x, low1, via_y, two_y, two_x):
@@ -246,10 +267,11 @@
     two_x[...] = (low1[...].astype(F32) + via_y[...].astype(F32)).astype(BF)
 
 
-def total_kernel(dec0, dec1, dec2, dec3, top0, low0, two_y, two_x, out, decode_out):
-    half = low0.shape[0]
-    out[0, :half, :] = (top0[...].astype(F32) + two_y[...].astype(F32)).astype(BF)
-    out[0, half:, :] = (low0[...].astype(F32) + two_x[...].astype(F32)).astype(BF)
+def total_kernel(top0, one_x, two_y, low0, one_y, two_x, dec0, dec1, dec2, dec3, out, decode_out):
+    out[0] = (top0[...].astype(F32) + one_x[...].astype(F32) + two_y[...].astype(F32)).astype(BF)
+    out.push(0)
+    out[1] = (low0[...].astype(F32) + one_y[...].astype(F32) + two_x[...].astype(F32)).astype(BF)
+    out.push(1)
     total = (dec0[...].astype(F32) + dec1[...].astype(F32)) + (dec2[...].astype(F32) + dec3[...].astype(F32))
     decode_out[0] = total[: DEC // 4].astype(BF)
 
@@ -332,7 +354,7 @@
         out[:, head * WIDE + DH : (head + 1) * WIDE] = jnp.zeros((count, WIDE - DH), BF)
 
 
-def return_kernel(heads, capacity, items_ref, owner_ref, w_ref, *outs):
+def return_kernel(heads, capacity, items_ref, owner_ref, w_ref, seen_x, seen_y, *outs):
     owners = owner_ref[...]
     target = column(owners) * capacity + placing_rank(owners, 1)
     placing = lax.broadcasted_iota(jnp.int32, (DEC, items_ref.shape[0]), 1) == target
@@ -384,10 +406,14 @@
     def __setitem__(self, index, value):
         self.place[index] = value
 
-    def push(self, entry=0):
-        if entry not in self.gone:
-            self.copies[entry].start()
-            self.gone.add(entry)
+    def push(self, entry=None):
+        if (entry is None) == (len(self.copies) == 1):
+            self.send(entry or 0)
+
+    def send(self, n):
+        if n not in self.gone:
+            self.copies[n].start()
+            self.gone.add(n)
 
 
 class Near:
@@ -400,7 +426,7 @@
     def __setitem__(self, index, value):
         self.ref[index] = value
 
-    def push(self, entry=0):
+    def push(self, entry=None):
         pass
 
 
@@ -450,7 +476,7 @@
             kernel(*numbers[: len(scalars) - (picked is not None)], *ins, *done, *own)
             for n in far:
                 for entry in range(len(done[n].copies)):
-                    done[n].push(entry)
+                    done[n].send(entry)
             for n in moved:
                 for entry in range(len(ins[n].copies)):
                     ins[n].wait(entry)
@@ -556,8 +582,10 @@
         block_flops,
         size,
         scalars=[length],
-        split_out=(0, 1),
     )(low, top, w_in)
+    low_y, top_x = lax.optimization_barrier((low_y, top_x, queries0, items))[:2]
+    low_xy = across(low_y, 1)
+    top_xy = across(top_x, 2)
     (served,) = hbm_call(
         functools.partial(serve_kernel, heads),
         [shape(count, heads * WIDE)],
@@ -568,48 +596,27 @@
         scratch=[pltpu.VMEM(cache.shape[1:], F32), pltpu.SemaphoreType.DMA((cache.shape[1],))],
         waits=[queries0],
     )(items.reshape(count, wide), out_gain, cache)
-    low_y, top_x = lax.optimization_barrier((low_y, top_x, served))[:2]
-    low_xy = across(low_y, 1)
-    top_xy = across(top_x, 2)
-    own1, queries1, own2, queries2, state3, bases = hbm_call(
+    blocks = shape(rows, wide)
+    sums1, qkv1, sums2, qkv2, state3 = hbm_call(
         functools.partial(second_kernel, heads),
-        [own, queries, own, queries, shape(heads, PHI_WIDE, WIDE), shape(4, heads, PHI_WIDE, WIDE, dtype=F32)],
+        [sums, blocks, sums, blocks, shape(heads, PHI_WIDE, WIDE)],
         2 * block_flops,
         2 * size,
         scalars=[length, slot],
         picked=5,
         waits=[served],
         loose=(0, 1, 3, 4),
-        split=(6,),
-        split_out=(0, 2),
-        scratch=[pltpu.VMEM(sums.shape, F32)] * 2,
     )(low_x, top_x, w_in, low_y, top_y, cache, sums0)
-    top3, low3, sums3 = hbm_call(
+    top3, low3, qkv3 = hbm_call(
         functools.partial(third_kernel, heads),
-        [piece, piece, sums],
+        [piece, piece, blocks],
         block_flops + attend_flops,
         size,
         scalars=[length],
         loose=(0, 1),
         near=(0, 1),
-        split=(3,),
-        split_out=(2,),
-        scratch=[pltpu.VMEM(own.shape, F32)],
-        waits=[queries2],
+        waits=[qkv2],
     )(low_xy, top_xy, w_in, state3, out_gain, out_weight)
-
-    def attend(slots, *blocks, others=(), keep=False, waits=()):
-        ins = 4 + 2 * len(slots)
-        return hbm_call(
-            functools.partial(attend_kernel, heads, slots, len(others)),
-            [piece] * (2 * len(slots)) + [shape(1, PHI, heads, DH, dtype=F32)] * keep,
-            len(slots) * attend_flops,
-            size,
-            scalars=[length],
-            split=(0, 1),
-            loose=range(ins, ins + len(others)),
-            waits=waits,
-        )(bases, sums3, out_gain, out_weight, *[b[0] for b in blocks], *[b[1] for b in blocks], *others)
 
     via_x = across(top3, 1)
     via_y = across(low3, 2)
@@ -617,27 +624,48 @@
     returned = lax.all_to_all(
         served.reshape(groups, capacity, heads * WIDE), "tok", split_axis=0, concat_axis=0, tiled=True
     ).reshape(count, heads * WIDE)
-    top1, low1, top2, low2 = attend((1, 2), (queries1, own1), (queries2, own2))
+    top1, low1, top2, low2, sums3 = hbm_call(
+        functools.partial(fourth_kernel, heads),
+        [piece] * 4 + [sums],
+        2 * attend_flops,
+        size,
+        scalars=[length, slot],
+        picked=2,
+    )(qkv3, qkv1, cache, sums0, sums1, sums2, qkv2, out_gain, out_weight)
     one_x = across(top1, 1)
     one_y = across(low2, 2)
     two_y, two_x = hbm_call(add_kernel, [piece, piece], 0, size, here=(1, 3), near=(0, 1), waits=[top1])(top2, via_x, low1, via_y)
-    top0, low0, state_next = attend((0,), (queries0, own0), others=(one_x, one_y), keep=True, waits=[top1])
+    top0, low0, state_next = hbm_call(
+        functools.partial(fifth_kernel, heads),
+        [piece] * 2 + [shape(1, PHI, heads, DH, dtype=F32)],
+        attend_flops,
+        size,
+        scalars=[length, slot],
+        picked=0,
+        waits=[two_x],
+    )(cache, sums0, sums1, sums2, sums3, queries0, own0, out_gain, out_weight)
     decoded = hbm_call(
         functools.partial(return_kernel, heads, capacity),
         [shape(TILE, D)] * 4,
         2 * DEC * heads * WIDE * D,
         2 * heads * WIDE * D,
-        loose=(0,),
+        loose=(0, 3, 4),
         waits=[top0],
-    )(returned, owner_row, out_weight)
+        raw=(3, 4),
+    )(returned, owner_row, out_weight, one_x, one_y)
     shares = [decoded[0]] + [across(decoded[by], by) for by in (1, 2, 3)]
     two_y = across(two_y, 2)
     two_x = across(two_x, 1)
     state_next = jnp.transpose(state_next, (0, 2, 3, 1))
     stretch_out, decode_out = hbm_call(
-        total_kernel, [shape(1, rows, D), shape(1, DEC // 4, D)], 0, 8 * rows * D, loose=(1, 2, 3, 6, 7)
-    )(*shares, top0, low0, two_y, two_x)
-    return (stretch_out, decode_out, state_next)
+        total_kernel,
+        [shape(2, half, D), shape(1, DEC // 4, D)],
+        0,
+        8 * rows * D,
+        loose=(1, 2, 4, 5, 7, 8, 9),
+        split_out=(0,),
+    )(top0, one_x, two_y, low0, one_y, two_x, *shares)
+    return (stretch_out.reshape(1, rows, D), decode_out, state_next)
 
 
 def from_behind(array, axis, by):

time: 99.9 us -> 93.2 us (0.933)
  Pallas kernels: 56.9 us -> 53 us
  waiting for transfers between devices: 8.92 us -> 6.32 us
    pallas_call x11, Pallas kernels: 56 us -> 52.1 us  [run(): pl.pallas_call(body, out_shape=[o if n in near else pltpu.HBM(o.shape, o....]
    ppermute x15, waiting for transfers between devices: 8.92 us -> 5.71 us  [across(): return lax.ppermute(array, 'head', [(i, i ^ by) for i in range(4)])]
  transfers between devices with their start and end apart: 18 -> 18, of which waited for: 6 -> 7; matrix products, arithmetic and copies ran while one was open for 0% -> 0% of each run, Pallas kernels for 44% -> 45%
where the time goes in v4:
time: 93.2 us; the launch traced here: 92.6 us
  Pallas kernels  53 us (57%)
  starting transfers between devices  31 us (33%)
  waiting for transfers between devices  6.32 us (7%)
  between operations  2.28 us (2%)
    pallas_call x11, Pallas kernels, run(): pl.pallas_call(body, out_shape=[o if n in near else pltpu.HBM(o.shape, o....  52.1 us
    ppermute x15, starting transfers between devices, across(): return lax.ppermute(array, 'head', [(i, i ^ by) for i in range(4)])  16.3 us
    ppermute x15, waiting for transfers between devices, across(): return lax.ppermute(array, 'head', [(i, i ^ by) for i in range(4)])  5.71 us
    ppermute x1, starting transfers between devices, from_behind(): return lax.ppermute(array, axis, pairs)  4.98 us
    all_to_all x1, starting transfers between devices, local_square(): lax.all_to_all(sent.reshape(groups, capacity, wide), 'tok', split_axis=0,...  4.88 us
    all_to_all x1, starting transfers between devices, local_square(): lax.all_to_all(served.reshape(groups, capacity, heads * WIDE), 'tok', spl...  4.87 us
  transfers between devices with their start and end apart: 18, of which 7 were waited for; matrix products, arithmetic and copies ran while one was open for 0% of the time, Pallas kernels for 45%

profile of v4, /device:TPU:0, one launch (start us, length us, event | category | flops | bytes accessed | tf_op | source)
XLA Modules:
  0.0 92.6 jit_solution(6975904110074089937)
XLA Ops:
  0.6 3.1 %shard_map.157 = (bf16[128,1792]{1,0:T(8,128)(2,1)}, bf16[128,1792]{1,0:T(8,128)(2,1)}, bf16[16,1792]{1,0:T(8,128)(2,1)}, bf16[16,1792]{1,0:T(8,128)(2,1)}) custom-call(bf16[256,1792]{1,0:T(8,128)(2,1)} %bitcast.24, bf16[2,1792]{1,0:T(2,128)(2,1)} %bitcast.28, f32[1792]{0:T(1024)} %refs_2_.4, f32[3,1792]{1,0:T(4,128)} %taps_ref.1), custom_call_target="tpu_custom_call" | custom-call | flops 9175040 | bytes 1835008 | tf_op jit(solution)/shard_map/pallas_call | solution.py:491
  3.8 0.0 copy-start.1
  3.8 5.0 %collective-permute-start = (bf16[16,1792]{1,0:T(8,128)(2,1)}, bf16[16,1792]{1,0:T(8,128)(2,1)S(1)}, u32[]{:S(2)}, u32[]{:S(2)}) collective-permute-start(bf16[16,1792]{1,0:T(8,128)(2,1)} %get-tuple-element.40), channel_id=1, source_target_pairs={{0,8},{8,16},{16,24},{1,9},{9,17},{17,25},{2,10},{10,18},{18,26},{... | collective-permute-start | bytes 172040 | tf_op jit(solution)/shard_map/ppermute | solution.py:674
  8.8 1.6 %collective-permute-start.2 = (bf16[128,1792]{1,0:T(8,128)(2,1)}, bf16[128,1792]{1,0:T(8,128)(2,1)S(1)}, u32[]{:S(2)}, u32[]{:S(2)}) collective-permute-start(bf16[128,1792]{1,0:T(8,128)(2,1)} %get-tuple-element.37.refs_1_), channel_id=1, source_target_pairs={{0,16},{8,24},{16,0},{24,8},{1,17},{9,25},{17,1},{25,9},{2,18},{10... | collective-permute-start | bytes 1376264 | tf_op jit(solution)/shard_map/ppermute | solution.py:514
  10.4 3.4 %shard_map.158.wait_ref = bf16[64,640]{1,0:T(8,128)(2,1)} custom-call(bf16[32,1792]{1,0:T(8,128)(2,1)} %bitcast.27, bf16[32,2,1792]{2,1,0:T(2,128)(2,1)} %bitcast.26, f32[1792]{0:T(1024)} %refs_2_.4, f32[3,1792]{1,0:T(4,128)} %taps_ref.1, s32[1,32]{1,0:T(1,128)} %bitcast.29, s32[1,32]{1,0:T(1,128)} %refs_5_.2, bf16[4,144,1792]{2,1,0:T(8,128)(2,1)} %bitcast.20), custom_call_target="tpu_custom_call" | custom-call | flops 73400320 | bytes 2293760 | tf_op jit(solution)/shard_map/pallas_call | solution.py:491
  13.8 0.0 collective-permute-done.end_ref
  13.8 0.9 %shard_map.159.refs_2_ = bf16[128,1792]{1,0:T(8,128)(2,1)} custom-call(s32[1]{0:T(128)} %bitcast.3.first_ref, bf16[128,1792]{1,0:T(8,128)(2,1)} %get-tuple-element.38.top_ref, bf16[16,1792]{1,0:T(8,128)(2,1)} %get-tuple-element.39.begin_ref, bf16[16,1792]{1,0:T(8,128)(2,1)S(1)} %collective-permute-done.end_ref, ...), custom_call_target="tpu_custom_call", output_to_operand_aliasing={{}: (1, {})} | custom-call | flops 28672 | bytes 229376 | tf_op jit(solution)/shard_map/pallas_call | solution.py:561
  14.7 0.7 collective-permute-start.3
  15.4 0.0 copy-done.1
  15.4 1.4 %collective-permute-start.1 = (bf16[128,1792]{1,0:T(8,128)(2,1)S(1)}, bf16[128,1792]{1,0:T(8,128)(2,1)S(1)}, u32[]{:S(2)}, u32[]{:S(2)}) collective-permute-start(bf16[128,1792]{1,0:T(8,128)(2,1)S(1)} %copy-done.1), channel_id=1, source_target_pairs={{0,8},{8,0},{16,24},{24,16},{1,9},{9,1},{17,25},{25,17},{2,10},{10... | collective-permute-start | bytes 1376264 | tf_op jit(solution)/shard_map/ppermute | solution.py:514
  16.8 1.1 %collective-permute-start.4 = (bf16[128,1792]{1,0:T(8,128)(2,1)}, bf16[128,1792]{1,0:T(8,128)(2,1)S(1)}, u32[]{:S(2)}, u32[]{:S(2)}) collective-permute-start(bf16[128,1792]{1,0:T(8,128)(2,1)} %shard_map.159.refs_2_), channel_id=1, source_target_pairs={{0,16},{8,24},{16,0},{24,8},{1,17},{9,25},{17,1},{25,9},{2,18},{10... | collective-permute-start | bytes 1376264 | tf_op jit(solution)/shard_map/ppermute | solution.py:514
  18.0 4.9 %all-to-all-start = ((bf16[8,8,640]{2,1,0:T(8,128)(2,1)}), bf16[8,8,640]{2,1,0:T(8,128)(2,1)S(1)}, u32[]{:S(2)}, u32[]{:S(2)}) async-start(bf16[8,8,640]{2,1,0:T(8,128)(2,1)} %bitcast.25), calls=%async_computation | async-start | bytes 163840 | tf_op jit(solution)/shard_map/all_to_all | solution.py:576
  23.5 5.0 %shard_map.160 = (f32[4,384,128]{2,1,0:T(8,128)}, f32[4,256,128]{2,1,0:T(8,128)}, bf16[256,64]{1,0:T(8,128)(2,1)}) custom-call(s32[1]{0:T(128)S(6)} %copy.19.refs_0_, bf16[128,1792]{1,0:T(8,128)(2,1)} %get-tuple-element.37.refs_1_, bf16[128,1792]{1,0:T(8,128)(2,1)} %shard_map.159.refs_2_, bf16[4,144,1792]{2,1,0:T(8,128)(2,1)} %bitcast.21), custom_call_target="tpu_custom_call" | custom-call | flops 788529152 | bytes 1835008 | tf_op jit(solution)/shard_map/pallas_call | solution.py:491
  28.5 0.4 all-to-all-done
  29.0 0.0 collective-permute-done.2.refs_5_
  29.0 0.0 collective-permute-done.3.refs_3_
  29.0 0.9 collective-permute-start.6
  29.9 1.2 %collective-permute-start.5 = (bf16[128,1792]{1,0:T(8,128)(2,1)S(1)}, bf16[128,1792]{1,0:T(8,128)(2,1)S(1)}, u32[]{:S(2)}, u32[]{:S(2)}) collective-permute-start(bf16[128,1792]{1,0:T(8,128)(2,1)S(1)} %collective-permute-done.2.refs_5_), channel_id=1, source_target_pairs={{0,8},{8,0},{16,24},{24,16},{1,9},{9,1},{17,25},{25,17},{2,10},{10... | collective-permute-start | bytes 1376264 | tf_op jit(solution)/shard_map/ppermute | solution.py:514
  31.7 6.6 %shard_map.161.refs_9_ = bf16[64,512]{1,0:T(8,128)(2,1)} custom-call(bf16[64,640]{1,0:T(8,128)(2,1)S(1)} %bitcast.14, f32[448]{0:T(512)} %refs_9_.3, f32[1,16,273,4,112]{4,3,2,1,0:T(4,128)} %bitcast.16, bf16[256,64]{1,0:T(8,128)(2,1)} %get-tuple-element.42.refs_3_.refs_7_), custom_call_target="tpu_custom_call" | custom-call | flops 1001914368 | bytes 8945664 | tf_op jit(solution)/shard_map/pallas_call | solution.py:491
  38.4 0.0 collective-permute-done.1.refs_2_
  38.4 0.0 collective-permute-done.4.refs_6_
  38.4 7.5 %shard_map.162 = (f32[4,384,128]{2,1,0:T(8,128)}, bf16[256,640]{1,0:T(8,128)(2,1)}, f32[4,384,128]{2,1,0:T(8,128)}, bf16[256,640]{1,0:T(8,128)(2,1)}, bf16[4,384,128]{2,1,0:T(8,128)(2,1)}) custom-call(s32[1]{0:T(128)S(6)} %copy.19.refs_0_, s32[1]{0:T(128)S(6)} %copy.20.refs_1_, bf16[128,1792]{1,0:T(8,128)(2,1)S(1)} %collective-permute-done.1.refs_2_, ...), custom_call_target="tpu_custom_call" | custom-call | flops 1577058304 | bytes 3670016 | tf_op jit(solution)/shard_map/pallas_call | solution.py:491
  45.9 0.0 collective-permute-done.6.refs_2_
  46.0 0.4 collective-permute-done.5.refs_1_
  46.4 5.9 %shard_map.163 = (bf16[128,1792]{1,0:T(8,128)(2,1)S(1)}, bf16[128,1792]{1,0:T(8,128)(2,1)S(1)}, bf16[256,640]{1,0:T(8,128)(2,1)}) custom-call(s32[1]{0:T(128)S(6)} %copy.19.refs_0_, bf16[128,1792]{1,0:T(8,128)(2,1)S(1)} %collective-permute-done.5.refs_1_, bf16[128,1792]{1,0:T(8,128)(2,1)S(1)} %collective-permute-done.6.refs_2_, ...), custom_call_target="tpu_custom_call" | custom-call | flops 1358954496 | bytes 1835008 | tf_op jit(solution)/shard_map/pallas_call | solution.py:491
  52.2 1.2 %collective-permute-start.8 = (bf16[128,1792]{1,0:T(8,128)(2,1)S(1)}, bf16[128,1792]{1,0:T(8,128)(2,1)S(1)}, u32[]{:S(2)}, u32[]{:S(2)}) collective-permute-start(bf16[128,1792]{1,0:T(8,128)(2,1)S(1)} %get-tuple-element.56), channel_id=1, source_target_pairs={{0,16},{8,24},{16,0},{24,8},{1,17},{9,25},{17,1},{25,9},{2,18},{10... | collective-permute-start | bytes 1376264 | tf_op jit(solution)/shard_map/ppermute | solution.py:514
  53.4 1.5 %collective-permute-start.7 = (bf16[128,1792]{1,0:T(8,128)(2,1)S(1)}, bf16[128,1792]{1,0:T(8,128)(2,1)S(1)}, u32[]{:S(2)}, u32[]{:S(2)}) collective-permute-start(bf16[128,1792]{1,0:T(8,128)(2,1)S(1)} %get-tuple-element.54), channel_id=1, source_target_pairs={{0,8},{8,0},{16,24},{24,16},{1,9},{9,1},{17,25},{25,17},{2,10},{10... | collective-permute-start | bytes 1376264 | tf_op jit(solution)/shard_map/ppermute | solution.py:514
  54.9 8.1 %shard_map.164 = (bf16[128,1792]{1,0:T(8,128)(2,1)}, bf16[128,1792]{1,0:T(8,128)(2,1)}, bf16[128,1792]{1,0:T(8,128)(2,1)}, bf16[128,1792]{1,0:T(8,128)(2,1)}, f32[4,384,128]{2,1,0:T(8,128)}) custom-call(s32[1]{0:T(128)S(6)} %copy.19.refs_0_, s32[1]{0:T(128)S(6)} %copy.20.refs_1_, bf16[256,640]{1,0:T(8,128)(2,1)} %get-tuple-element.49.refs_2_, ...), custom_call_target="tpu_custom_call" | custom-call | flops 1140850688 | bytes 1835008 | tf_op jit(solution)/shard_map/pallas_call | solution.py:491
  63.0 0.4 collective-permute-start.11
  63.4 1.1 %collective-permute-start.9 = (bf16[128,1792]{1,0:T(8,128)(2,1)}, bf16[128,1792]{1,0:T(8,128)(2,1)S(1)}, u32[]{:S(2)}, u32[]{:S(2)}) collective-permute-start(bf16[128,1792]{1,0:T(8,128)(2,1)} %get-tuple-element.57.refs_4_), channel_id=1, source_target_pairs={{0,8},{8,0},{16,24},{24,16},{1,9},{9,1},{17,25},{25,17},{2,10},{10... | collective-permute-start | bytes 1376264 | tf_op jit(solution)/shard_map/ppermute | solution.py:514
  64.5 0.0 collective-permute-done.8.refs_3_
  64.5 1.1 %collective-permute-done.7.refs_1_ = bf16[128,1792]{1,0:T(8,128)(2,1)S(1)} collective-permute-done((bf16[128,1792]{1,0:T(8,128)(2,1)S(1)}, bf16[128,1792]{1,0:T(8,128)(2,1)S(1)}, u32[]{:S(2)}, u32[]{:S(2)}) %collective-permute-start.7) | collective-permute-done | bytes 458784 | tf_op jit(solution)/shard_map/ppermute | solution.py:514
  65.6 1.3 %shard_map.165 = (bf16[128,1792]{1,0:T(8,128)(2,1)S(1)}, bf16[128,1792]{1,0:T(8,128)(2,1)S(1)}) custom-call(bf16[128,1792]{1,0:T(8,128)(2,1)} %get-tuple-element.53.refs_0_, bf16[128,1792]{1,0:T(8,128)(2,1)S(1)} %collective-permute-done.7.refs_1_, bf16[128,1792]{1,0:T(8,128)(2,1)} %get-tuple-element.55.refs_2_, ...), custom_call_target="tpu_custom_call" | custom-call | bytes 1835008 | tf_op jit(solution)/shard_map/pallas_call | solution.py:491
  66.9 0.0 copy-start
  66.9 0.3 collective-permute-start.10
  67.2 1.3 %collective-permute-start.12 = (bf16[128,1792]{1,0:T(8,128)(2,1)S(1)}, bf16[128,1792]{1,0:T(8,128)(2,1)S(1)}, u32[]{:S(2)}, u32[]{:S(2)}) collective-permute-start(bf16[128,1792]{1,0:T(8,128)(2,1)S(1)} %get-tuple-element.58.refs_11_), channel_id=1, source_target_pairs={{0,8},{8,0},{16,24},{24,16},{1,9},{9,1},{17,25},{25,17},{2,10},{10... | collective-permute-start | bytes 1376264 | tf_op jit(solution)/shard_map/ppermute | solution.py:514
  68.5 4.9 %all-to-all-start.1 = ((bf16[8,8,512]{2,1,0:T(8,128)(2,1)}), bf16[8,8,512]{2,1,0:T(8,128)(2,1)S(1)}, u32[]{:S(2)}, u32[]{:S(2)}) async-start(bf16[8,8,512]{2,1,0:T(8,128)(2,1)} %bitcast.10), calls=%async_computation.1 | async-start | bytes 131072 | tf_op jit(solution)/shard_map/all_to_all | solution.py:624
  73.4 0.0 copy-done
  73.4 5.7 %shard_map.166 = (bf16[128,1792]{1,0:T(8,128)(2,1)}, bf16[128,1792]{1,0:T(8,128)(2,1)}, f32[1,273,4,112]{3,2,1,0:T(4,128)}) custom-call(s32[1]{0:T(128)S(6)} %copy.19.refs_0_, s32[1]{0:T(128)S(6)} %copy.20.refs_1_, f32[1,16,273,4,112]{4,3,2,1,0:T(4,128)} %bitcast.19, f32[4,384,128]{2,1,0:T(8,128)} %get-tuple-element.41.refs_8_.refs_5_.refs_3_, ...), custom_call_target="tpu_custom_call" | custom-call | flops 570425344 | bytes 1835008 | tf_op jit(solution)/shard_map/pallas_call | solution.py:491
  79.1 0.2 all-to-all-done.1
  79.3 0.0 collective-permute-done.11.refs_4_
  79.3 0.0 collective-permute-done.9.refs_3_.refs_1_
  79.3 2.7 %shard_map.167 = (bf16[16,1792]{1,0:T(8,128)(2,1)}, bf16[16,1792]{1,0:T(8,128)(2,1)}, bf16[16,1792]{1,0:T(8,128)(2,1)}, bf16[16,1792]{1,0:T(8,128)(2,1)}) custom-call(bf16[64,512]{1,0:T(8,128)(2,1)S(1)} %bitcast.15, s32[1,32]{1,0:T(1,128)} %bitcast.30, bf16[448,1792]{1,0:T(8,128)(2,1)} %refs_2_.5, ...), custom_call_target="tpu_custom_call" | custom-call | flops 58720256 | bytes 1835008 | tf_op jit(solution)/shard_map/pallas_call | solution.py:491
  82.0 0.7 collective-permute-start.13
  82.7 1.8 %collective-permute-start.14 = (bf16[16,1792]{1,0:T(8,128)(2,1)}, bf16[16,1792]{1,0:T(8,128)(2,1)S(1)}, u32[]{:S(2)}, u32[]{:S(2)}) collective-permute-start(bf16[16,1792]{1,0:T(8,128)(2,1)} %get-tuple-element.66), channel_id=1, source_target_pairs={{0,16},{8,24},{16,0},{24,8},{1,17},{9,25},{17,1},{25,9},{2,18},{10... | collective-permute-start | bytes 172040 | tf_op jit(solution)/shard_map/ppermute | solution.py:514
  84.4 1.1 %collective-permute-start.15 = (bf16[16,1792]{1,0:T(8,128)(2,1)}, bf16[16,1792]{1,0:T(8,128)(2,1)S(1)}, u32[]{:S(2)}, u32[]{:S(2)}) collective-permute-start(bf16[16,1792]{1,0:T(8,128)(2,1)} %get-tuple-element.67), channel_id=1, source_target_pairs={{0,24},{8,16},{16,8},{24,0},{1,25},{9,17},{17,9},{25,1},{2,26},{10... | collective-permute-start | bytes 172040 | tf_op jit(solution)/shard_map/ppermute | solution.py:514
  85.5 0.9 collective-permute-done.13.refs_7_
  86.4 0.6 collective-permute-done.14.refs_8_
  87.1 2.6 %collective-permute-done.15.refs_9_ = bf16[16,1792]{1,0:T(8,128)(2,1)S(1)} collective-permute-done((bf16[16,1792]{1,0:T(8,128)(2,1)}, bf16[16,1792]{1,0:T(8,128)(2,1)S(1)}, u32[]{:S(2)}, u32[]{:S(2)}) %collective-permute-start.15) | collective-permute-done | bytes 57376 | tf_op jit(solution)/shard_map/ppermute | solution.py:514
  89.7 0.0 collective-permute-done.10.refs_2_
  89.7 0.0 collective-permute-done.12.refs_5_
  89.7 2.7 %shard_map.168 = (bf16[2,128,1792]{2,1,0:T(8,128)(2,1)}, bf16[1,8,1792]{2,1,0:T(8,128)(2,1)}) custom-call(bf16[128,1792]{1,0:T(8,128)(2,1)} %get-tuple-element.59.refs_5_.refs_0_, bf16[128,1792]{1,0:T(8,128)(2,1)S(1)} %collective-permute-done.9.refs_3_.refs_1_, bf16[128,1792]{1,0:T(8,128)(2,1)S(1)} %collective-permute-done.10.refs_2_, ...), custom_call_target="tpu_custom_call" | custom-call | bytes 3670016 | tf_op jit(solution)/shard_map/pallas_call | solution.py:491
Async XLA Ops:
  3.8 11.6 %copy-start.1 = (bf16[128,1792]{1,0:T(8,128)(2,1)S(1)}, bf16[128,1792]{1,0:T(8,128)(2,1)}, u32[]{:S(2)}) copy-start(bf16[128,1792]{1,0:T(8,128)(2,1)} %get-tuple-element.37.refs_1_) | copy-start | bytes 1376260
  3.8 10.0 %collective-permute-start = (bf16[16,1792]{1,0:T(8,128)(2,1)}, bf16[16,1792]{1,0:T(8,128)(2,1)S(1)}, u32[]{:S(2)}, u32[]{:S(2)}) collective-permute-start(bf16[16,1792]{1,0:T(8,128)(2,1)} %get-tuple-element.40), channel_id=1, source_target_pairs={{0,8},{8,16},{16,24},{1,9},{9,17},{17,25},{2,10},{10,18},{18,26},{... | collective-permute-start | bytes 172040 | tf_op jit(solution)/shard_map/ppermute | solution.py:674
  8.8 20.2 %collective-permute-start.2 = (bf16[128,1792]{1,0:T(8,128)(2,1)}, bf16[128,1792]{1,0:T(8,128)(2,1)S(1)}, u32[]{:S(2)}, u32[]{:S(2)}) collective-permute-start(bf16[128,1792]{1,0:T(8,128)(2,1)} %get-tuple-element.37.refs_1_), channel_id=1, source_target_pairs={{0,16},{8,24},{16,0},{24,8},{1,17},{9,25},{17,1},{25,9},{2,18},{10... | collective-permute-start | bytes 1376264 | tf_op jit(solution)/shard_map/ppermute | solution.py:514
  14.7 14.2 %collective-permute-start.3 = (bf16[128,1792]{1,0:T(8,128)(2,1)}, bf16[128,1792]{1,0:T(8,128)(2,1)S(1)}, u32[]{:S(2)}, u32[]{:S(2)}) collective-permute-start(bf16[128,1792]{1,0:T(8,128)(2,1)} %shard_map.159.refs_2_), channel_id=1, source_target_pairs={{0,8},{8,0},{16,24},{24,16},{1,9},{9,1},{17,25},{25,17},{2,10},{10... | collective-permute-start | bytes 1376264 | tf_op jit(solution)/shard_map/ppermute | solution.py:514
  15.4 22.9 %collective-permute-start.1 = (bf16[128,1792]{1,0:T(8,128)(2,1)S(1)}, bf16[128,1792]{1,0:T(8,128)(2,1)S(1)}, u32[]{:S(2)}, u32[]{:S(2)}) collective-permute-start(bf16[128,1792]{1,0:T(8,128)(2,1)S(1)} %copy-done.1), channel_id=1, source_target_pairs={{0,8},{8,0},{16,24},{24,16},{1,9},{9,1},{17,25},{25,17},{2,10},{10... | collective-permute-start | bytes 1376264 | tf_op jit(solution)/shard_map/ppermute | solution.py:514
  16.8 21.5 %collective-permute-start.4 = (bf16[128,1792]{1,0:T(8,128)(2,1)}, bf16[128,1792]{1,0:T(8,128)(2,1)S(1)}, u32[]{:S(2)}, u32[]{:S(2)}) collective-permute-start(bf16[128,1792]{1,0:T(8,128)(2,1)} %shard_map.159.refs_2_), channel_id=1, source_target_pairs={{0,16},{8,24},{16,0},{24,8},{1,17},{9,25},{17,1},{25,9},{2,18},{10... | collective-permute-start | bytes 1376264 | tf_op jit(solution)/shard_map/ppermute | solution.py:514
  18.0 11.0 %all-to-all-start = ((bf16[8,8,640]{2,1,0:T(8,128)(2,1)}), bf16[8,8,640]{2,1,0:T(8,128)(2,1)S(1)}, u32[]{:S(2)}, u32[]{:S(2)}) async-start(bf16[8,8,640]{2,1,0:T(8,128)(2,1)} %bitcast.25), calls=%async_computation | async-start | bytes 163840 | tf_op jit(solution)/shard_map/all_to_all | solution.py:576
  29.0 17.0 %collective-permute-start.6 = (bf16[128,1792]{1,0:T(8,128)(2,1)S(1)}, bf16[128,1792]{1,0:T(8,128)(2,1)S(1)}, u32[]{:S(2)}, u32[]{:S(2)}) collective-permute-start(bf16[128,1792]{1,0:T(8,128)(2,1)S(1)} %collective-permute-done.3.refs_3_), channel_id=1, source_target_pairs={{0,16},{8,24},{16,0},{24,8},{1,17},{9,25},{17,1},{25,9},{2,18},{10... | collective-permute-start | bytes 1376264 | tf_op jit(solution)/shard_map/ppermute | solution.py:514
  29.9 16.5 %collective-permute-start.5 = (bf16[128,1792]{1,0:T(8,128)(2,1)S(1)}, bf16[128,1792]{1,0:T(8,128)(2,1)S(1)}, u32[]{:S(2)}, u32[]{:S(2)}) collective-permute-start(bf16[128,1792]{1,0:T(8,128)(2,1)S(1)} %collective-permute-done.2.refs_5_), channel_id=1, source_target_pairs={{0,8},{8,0},{16,24},{24,16},{1,9},{9,1},{17,25},{25,17},{2,10},{10... | collective-permute-start | bytes 1376264 | tf_op jit(solution)/shard_map/ppermute | solution.py:514
  52.2 12.3 %collective-permute-start.8 = (bf16[128,1792]{1,0:T(8,128)(2,1)S(1)}, bf16[128,1792]{1,0:T(8,128)(2,1)S(1)}, u32[]{:S(2)}, u32[]{:S(2)}) collective-permute-start(bf16[128,1792]{1,0:T(8,128)(2,1)S(1)} %get-tuple-element.56), channel_id=1, source_target_pairs={{0,16},{8,24},{16,0},{24,8},{1,17},{9,25},{17,1},{25,9},{2,18},{10... | collective-permute-start | bytes 1376264 | tf_op jit(solution)/shard_map/ppermute | solution.py:514
  53.4 12.1 %collective-permute-start.7 = (bf16[128,1792]{1,0:T(8,128)(2,1)S(1)}, bf16[128,1792]{1,0:T(8,128)(2,1)S(1)}, u32[]{:S(2)}, u32[]{:S(2)}) collective-permute-start(bf16[128,1792]{1,0:T(8,128)(2,1)S(1)} %get-tuple-element.54), channel_id=1, source_target_pairs={{0,8},{8,0},{16,24},{24,16},{1,9},{9,1},{17,25},{25,17},{2,10},{10... | collective-permute-start | bytes 1376264 | tf_op jit(solution)/shard_map/ppermute | solution.py:514
  63.0 16.3 %collective-permute-start.11 = (bf16[128,1792]{1,0:T(8,128)(2,1)}, bf16[128,1792]{1,0:T(8,128)(2,1)S(1)}, u32[]{:S(2)}, u32[]{:S(2)}) collective-permute-start(bf16[128,1792]{1,0:T(8,128)(2,1)} %get-tuple-element.62), channel_id=1, source_target_pairs={{0,16},{8,24},{16,0},{24,8},{1,17},{9,25},{17,1},{25,9},{2,18},{10... | collective-permute-start | bytes 1376264 | tf_op jit(solution)/shard_map/ppermute | solution.py:514
  63.4 15.9 %collective-permute-start.9 = (bf16[128,1792]{1,0:T(8,128)(2,1)}, bf16[128,1792]{1,0:T(8,128)(2,1)S(1)}, u32[]{:S(2)}, u32[]{:S(2)}) collective-permute-start(bf16[128,1792]{1,0:T(8,128)(2,1)} %get-tuple-element.57.refs_4_), channel_id=1, source_target_pairs={{0,8},{8,0},{16,24},{24,16},{1,9},{9,1},{17,25},{25,17},{2,10},{10... | collective-permute-start | bytes 1376264 | tf_op jit(solution)/shard_map/ppermute | solution.py:514
  66.9 6.5 %copy-start = (bf16[128,1792]{1,0:T(8,128)(2,1)}, bf16[128,1792]{1,0:T(8,128)(2,1)S(1)}, u32[]{:S(2)}) copy-start(bf16[128,1792]{1,0:T(8,128)(2,1)S(1)} %get-tuple-element.58.refs_11_) | copy-start | bytes 1376260
  66.9 22.8 %collective-permute-start.10 = (bf16[128,1792]{1,0:T(8,128)(2,1)S(1)}, bf16[128,1792]{1,0:T(8,128)(2,1)S(1)}, u32[]{:S(2)}, u32[]{:S(2)}) collective-permute-start(bf16[128,1792]{1,0:T(8,128)(2,1)S(1)} %get-tuple-element.60), channel_id=1, source_target_pairs={{0,16},{8,24},{16,0},{24,8},{1,17},{9,25},{17,1},{25,9},{2,18},{10... | collective-permute-start | bytes 1376264 | tf_op jit(solution)/shard_map/ppermute | solution.py:514
  67.2 22.5 %collective-permute-start.12 = (bf16[128,1792]{1,0:T(8,128)(2,1)S(1)}, bf16[128,1792]{1,0:T(8,128)(2,1)S(1)}, u32[]{:S(2)}, u32[]{:S(2)}) collective-permute-start(bf16[128,1792]{1,0:T(8,128)(2,1)S(1)} %get-tuple-element.58.refs_11_), channel_id=1, source_target_pairs={{0,8},{8,0},{16,24},{24,16},{1,9},{9,1},{17,25},{25,17},{2,10},{10... | collective-permute-start | bytes 1376264 | tf_op jit(solution)/shard_map/ppermute | solution.py:514
  68.5 10.8 %all-to-all-start.1 = ((bf16[8,8,512]{2,1,0:T(8,128)(2,1)}), bf16[8,8,512]{2,1,0:T(8,128)(2,1)S(1)}, u32[]{:S(2)}, u32[]{:S(2)}) async-start(bf16[8,8,512]{2,1,0:T(8,128)(2,1)} %bitcast.10), calls=%async_computation.1 | async-start | bytes 131072 | tf_op jit(solution)/shard_map/all_to_all | solution.py:624
  82.0 4.5 %collective-permute-start.13 = (bf16[16,1792]{1,0:T(8,128)(2,1)}, bf16[16,1792]{1,0:T(8,128)(2,1)S(1)}, u32[]{:S(2)}, u32[]{:S(2)}) collective-permute-start(bf16[16,1792]{1,0:T(8,128)(2,1)} %get-tuple-element.65), channel_id=1, source_target_pairs={{0,8},{8,0},{16,24},{24,16},{1,9},{9,1},{17,25},{25,17},{2,10},{10... | collective-permute-start | bytes 172040 | tf_op jit(solution)/shard_map/ppermute | solution.py:514
  82.7 4.4 %collective-permute-start.14 = (bf16[16,1792]{1,0:T(8,128)(2,1)}, bf16[16,1792]{1,0:T(8,128)(2,1)S(1)}, u32[]{:S(2)}, u32[]{:S(2)}) collective-permute-start(bf16[16,1792]{1,0:T(8,128)(2,1)} %get-tuple-element.66), channel_id=1, source_target_pairs={{0,16},{8,24},{16,0},{24,8},{1,17},{9,25},{17,1},{25,9},{2,18},{10... | collective-permute-start | bytes 172040 | tf_op jit(solution)/shard_map/ppermute | solution.py:514
  84.4 5.3 %collective-permute-start.15 = (bf16[16,1792]{1,0:T(8,128)(2,1)}, bf16[16,1792]{1,0:T(8,128)(2,1)S(1)}, u32[]{:S(2)}, u32[]{:S(2)}) collective-permute-start(bf16[16,1792]{1,0:T(8,128)(2,1)} %get-tuple-element.67), channel_id=1, source_target_pairs={{0,24},{8,16},{16,8},{24,0},{1,25},{9,17},{17,9},{25,1},{2,26},{10... | collective-permute-start | bytes 172040 | tf_op jit(solution)/shard_map/ppermute | solution.py:514

commit v5 on v4

--- a/solution.py
+++ b/solution.py
@@ -191,10 +191,18 @@
     queries[...] = qkv[:, : heads * F]
 
 
-def second_kernel(heads, len_ref, low1, top1, w_ref, low2, top2, cache, sums0, sums1, qkv1, sums2, qkv2, state3):
+def second_kernel(
+    heads, len_ref, low1, top1, w_ref, low2, top2, cache, sums0, items, half_total, gain_ref, cache_ref,
+    sums1, qkv1, sums2, qkv2, state3, served, state, sem
+):
+    start = 2 * sem.shape[0]
+    copies = slot_copies(heads, start, start, cache_ref, state, sem)
     pick = spreader()
     for slot, low, top, sums, qkv in ((1, low1, top1, sums1, qkv1), (2, low2, top2, sums2, qkv2)):
         found = qkv_of(heads, top, low, w_ref)
+        if slot == 1:
+            for copy in copies:
+                copy.start()
         qkv[...] = found
         qkv.push()
         for head in range(heads):
@@ -202,6 +210,8 @@
         sums.push()
     for head in range(heads):
         state3[head] = state_before(3, old_state(cache, head), (sums0[head], sums1[head], sums2[head]))
+    state3.push()
+    serve_part(heads, start, items, half_total, gain_ref, copies, state, served)
 
 
 def state_before(slot, old, sums):
@@ -309,12 +319,7 @@
     return ones_where(a == entry), ones_where((quad >= 0) & ((quad & (F - 1)) == entry))
 
 
-def serve_kernel(heads, items, gain_ref, cache_ref, out, state, sem):
-    flying = 6
-    copies = [pltpu.make_async_copy(cache_ref.at[0, n], state.at[n], sem.at[n]) for n in range(state.shape[0])]
-    for copy in copies[:flying]:
-        copy.start()
-    count = items.shape[0]
+def slot_features(heads, items):
     mark = 2 * heads * F + DH
     first, second = cache_spreaders(heads)
     phis = []
@@ -326,20 +331,53 @@
         scale = jnp.where(lane < heads * (F + 1), 1.0 / math.sqrt(math.sqrt(F)), b * (1.0 / math.sqrt(2.0 * F)))
         value = jnp.where(lane < heads, 1.0, a * scale)
         phis.append(jnp.where((lane & (heads - 1)) == head, value, 0.0).astype(BF))
-    phis = jnp.concatenate(phis, axis=0)
     slots = jnp.concatenate([items[:, mark : mark + 1].astype(F32)] * heads, axis=0)
-    zeros = jnp.zeros((PHI * heads, WIDE - DH), BF)
-    total = jnp.zeros((heads * count, WIDE), F32)
-    for n in range(0, len(copies), 2):
-        pair = []
-        for place in (n, n + 1):
-            copies[place].wait()
-            for later in copies[place + flying : place + flying + 1]:
-                later.start()
-            pair += [state[place].reshape(PHI * heads, DH).astype(BF), zeros]
-        table = dot(phis, jnp.concatenate(pair, axis=1))
-        total = total + jnp.where(slots == float(n), table[:, :WIDE], 0.0)
-        total = total + jnp.where(slots == float(n + 1), table[:, WIDE:], 0.0)
+    return jnp.concatenate(phis, axis=0), slots
+
+
+def slot_copies(heads, start, count, cache_ref, state, sem):
+    size = 2 * PHI * heads
+    return [
+        pltpu.make_async_copy(cache_ref.at[pl.ds(start * size // 2 + n * size, size)], state.at[pl.ds(n * size, size)], sem.at[n])
+        for n in range(count // 2)
+    ]
+
+
+def slot_totals(heads, start, phis, slots, copies, state, total):
+    span = PHI * heads
+    waiting = list(copies)
+    done = {}
+    for n in range(2 * len(copies)):
+        if n % 2 == 0:
+            waiting.pop(0).wait()
+        shift = n * span % 8
+        rows = -(-(span + shift) // 8) * 8
+        block = state[n * span - shift : n * span - shift + rows, :].astype(BF)
+        done.setdefault(shift, []).append((n, block))
+        if len(done[shift]) == 2:
+            zeros = jnp.zeros((rows, WIDE - DH), BF)
+            pair = [part for _, block in done[shift] for part in (block, zeros)]
+            sides = [jnp.zeros((phis.shape[0], size), BF) for size in (shift, rows - span - shift)]
+            wide = [side for side in (sides[0], phis, sides[1]) if side.shape[1] > 0]
+            table = dot(jnp.concatenate(wide, axis=1), jnp.concatenate(pair, axis=1))
+            for side, (place, _) in enumerate(done.pop(shift)):
+                here = slots == float(start + place)
+                total = total + jnp.where(here, table[:, side * WIDE : (side + 1) * WIDE], 0.0)
+    return total
+
+
+def serve_kernel(heads, items, cache_ref, total, state, sem):
+    copies = slot_copies(heads, 0, 2 * sem.shape[0], cache_ref, state, sem)
+    for copy in copies:
+        copy.start()
+    phis, slots = slot_features(heads, items)
+    total[...] = slot_totals(heads, 0, phis, slots, copies, state, jnp.zeros(total.shape, F32))
+
+
+def serve_part(heads, start, items, half_total, gain_ref, copies, state, out):
+    count = items.shape[0]
+    phis, slots = slot_features(heads, items)
+    total = slot_totals(heads, start, phis, slots, copies, state, half_total[...])
     gains = gain_ref[...].reshape(1, heads * DH)
     for head in range(heads):
         q = items[:, head * F : head * F + F].astype(F32)
@@ -583,30 +621,36 @@
         size,
         scalars=[length],
     )(low, top, w_in)
-    low_y, top_x = lax.optimization_barrier((low_y, top_x, queries0, items))[:2]
+    items = items.reshape(count, wide)
+    slots = cache.shape[1]
+    flat = cache.reshape(slots * PHI * heads, DH)
+    states = [pltpu.VMEM((slots // 2 * PHI * heads, DH), F32), pltpu.SemaphoreType.DMA((slots // 4,))]
+    serve_flops = slots * heads * heads * DH * PHI * count
+    (half_total,) = hbm_call(
+        functools.partial(serve_kernel, heads),
+        [shape(heads * count, WIDE, dtype=F32)],
+        serve_flops,
+        2 * slots * heads * WIDE * PHI,
+        loose=(0,),
+        raw=(1,),
+        scratch=states,
+        waits=[queries0],
+    )(items, flat)
+    low_y, top_x, low_x = lax.optimization_barrier((low_y, top_x, low_x, half_total))[:3]
     low_xy = across(low_y, 1)
     top_xy = across(top_x, 2)
-    (served,) = hbm_call(
-        functools.partial(serve_kernel, heads),
-        [shape(count, heads * WIDE)],
-        2 * cache.shape[1] * heads * heads * DH * PHI * count,
-        4 * cache.shape[1] * heads * WIDE * PHI,
-        loose=(0,),
-        raw=(2,),
-        scratch=[pltpu.VMEM(cache.shape[1:], F32), pltpu.SemaphoreType.DMA((cache.shape[1],))],
-        waits=[queries0],
-    )(items.reshape(count, wide), out_gain, cache)
     blocks = shape(rows, wide)
-    sums1, qkv1, sums2, qkv2, state3 = hbm_call(
+    sums1, qkv1, sums2, qkv2, state3, served = hbm_call(
         functools.partial(second_kernel, heads),
-        [sums, blocks, sums, blocks, shape(heads, PHI_WIDE, WIDE)],
-        2 * block_flops,
-        2 * size,
+        [sums, blocks, sums, blocks, shape(heads, PHI_WIDE, WIDE), shape(count, heads * WIDE)],
+        2 * block_flops + serve_flops,
+        2 * slots * heads * WIDE * PHI,
         scalars=[length, slot],
         picked=5,
-        waits=[served],
-        loose=(0, 1, 3, 4),
-    )(low_x, top_x, w_in, low_y, top_y, cache, sums0)
+        loose=(0, 1, 3, 4, 7),
+        raw=(10,),
+        scratch=states,
+    )(low_x, top_x, w_in, low_y, top_y, cache, sums0, items, half_total, out_gain, flat)
     top3, low3, qkv3 = hbm_call(
         functools.partial(third_kernel, heads),
         [piece, piece, blocks],

time: 93.2 us -> 92 us (0.987)
  Pallas kernels: 53 us -> 52 us
    pallas_call x11, Pallas kernels: 52.1 us -> 51.1 us  [run(): pl.pallas_call(body, out_shape=[o if n in near else pltpu.HBM(o.shape, o....]
  transfers between devices with their start and end apart: 18 -> 18, of which waited for: 7 -> 7; matrix products, arithmetic and copies ran while one was open for 0% -> 0% of each run, Pallas kernels for 45% -> 44%
where the time goes in v5:
time: 92 us; the launch traced here: 91.4 us
  Pallas kernels  52 us (57%)
  starting transfers between devices  30.7 us (33%)
  waiting for transfers between devices  6.38 us (7%)
  between operations  2.27 us (2%)
    pallas_call x11, Pallas kernels, run(): pl.pallas_call(body, out_shape=[o if n in near else pltpu.HBM(o.shape, o....  51.1 us
    ppermute x15, starting transfers between devices, across(): return lax.ppermute(array, 'head', [(i, i ^ by) for i in range(4)])  16.3 us
    ppermute x15, waiting for transfers between devices, across(): return lax.ppermute(array, 'head', [(i, i ^ by) for i in range(4)])  5.77 us
    all_to_all x1, starting transfers between devices, local_square(): lax.all_to_all(sent.reshape(groups, capacity, wide), 'tok', split_axis=0,...  4.88 us
    ppermute x1, starting transfers between devices, from_behind(): return lax.ppermute(array, axis, pairs)  4.84 us
    all_to_all x1, starting transfers between devices, local_square(): lax.all_to_all(served.reshape(groups, capacity, heads * WIDE), 'tok', spl...  4.74 us
  transfers between devices with their start and end apart: 18, of which 7 were waited for; matrix products, arithmetic and copies ran while one was open for 0% of the time, Pallas kernels for 44%

profile of v5, /device:TPU:0, one launch (start us, length us, event | category | flops | bytes accessed | tf_op | source)
XLA Modules:
  0.0 91.4 jit_solution(16270611120309799659)
XLA Ops:
  0.6 3.1 %shard_map.157 = (bf16[128,1792]{1,0:T(8,128)(2,1)}, bf16[128,1792]{1,0:T(8,128)(2,1)}, bf16[16,1792]{1,0:T(8,128)(2,1)}, bf16[16,1792]{1,0:T(8,128)(2,1)}) custom-call(bf16[256,1792]{1,0:T(8,128)(2,1)} %bitcast.28, bf16[2,1792]{1,0:T(2,128)(2,1)} %bitcast.32, f32[1792]{0:T(1024)} %refs_2_.4, f32[3,1792]{1,0:T(4,128)} %taps_ref.1), custom_call_target="tpu_custom_call" | custom-call | flops 9175040 | bytes 1835008 | tf_op jit(solution)/shard_map/pallas_call | solution.py:529
  3.8 4.8 %collective-permute-start = (bf16[16,1792]{1,0:T(8,128)(2,1)}, bf16[16,1792]{1,0:T(8,128)(2,1)S(1)}, u32[]{:S(2)}, u32[]{:S(2)}) collective-permute-start(bf16[16,1792]{1,0:T(8,128)(2,1)} %get-tuple-element.42), channel_id=1, source_target_pairs={{0,8},{8,16},{16,24},{1,9},{9,17},{17,25},{2,10},{10,18},{18,26},{... | collective-permute-start | bytes 172040 | tf_op jit(solution)/shard_map/ppermute | solution.py:718
  8.6 1.6 %collective-permute-start.3 = (bf16[128,1792]{1,0:T(8,128)(2,1)}, bf16[128,1792]{1,0:T(8,128)(2,1)S(1)}, u32[]{:S(2)}, u32[]{:S(2)}) collective-permute-start(bf16[128,1792]{1,0:T(8,128)(2,1)} %get-tuple-element.39.refs_1_), channel_id=1, source_target_pairs={{0,8},{8,0},{16,24},{24,16},{1,9},{9,1},{17,25},{25,17},{2,10},{10... | collective-permute-start | bytes 1376264 | tf_op jit(solution)/shard_map/ppermute | solution.py:552
  10.2 0.1 collective-permute-start.1
  10.3 3.4 %shard_map.158.wait_ref = bf16[64,640]{1,0:T(8,128)(2,1)} custom-call(bf16[32,1792]{1,0:T(8,128)(2,1)} %bitcast.31, bf16[32,2,1792]{2,1,0:T(2,128)(2,1)} %bitcast.30, f32[1792]{0:T(1024)} %refs_2_.4, f32[3,1792]{1,0:T(4,128)} %taps_ref.1, s32[1,32]{1,0:T(1,128)} %bitcast.33, s32[1,32]{1,0:T(1,128)} %refs_5_.2, bf16[4,144,1792]{2,1,0:T(8,128)(2,1)} %bitcast.24), custom_call_target="tpu_custom_call" | custom-call | flops 73400320 | bytes 2293760 | tf_op jit(solution)/shard_map/pallas_call | solution.py:529
  13.7 0.0 collective-permute-done.end_ref
  13.7 0.9 %shard_map.159.refs_2_ = bf16[128,1792]{1,0:T(8,128)(2,1)} custom-call(s32[1]{0:T(128)} %bitcast.3.first_ref, bf16[128,1792]{1,0:T(8,128)(2,1)} %get-tuple-element.40.top_ref, bf16[16,1792]{1,0:T(8,128)(2,1)} %get-tuple-element.41.begin_ref, bf16[16,1792]{1,0:T(8,128)(2,1)S(1)} %collective-permute-done.end_ref, ...), custom_call_target="tpu_custom_call", output_to_operand_aliasing={{}: (1, {})} | custom-call | flops 28672 | bytes 229376 | tf_op jit(solution)/shard_map/pallas_call | solution.py:599
  14.7 2.6 %collective-permute-start.2 = (bf16[128,1792]{1,0:T(8,128)(2,1)}, bf16[128,1792]{1,0:T(8,128)(2,1)S(1)}, u32[]{:S(2)}, u32[]{:S(2)}) collective-permute-start(bf16[128,1792]{1,0:T(8,128)(2,1)} %shard_map.159.refs_2_), channel_id=1, source_target_pairs={{0,8},{8,0},{16,24},{24,16},{1,9},{9,1},{17,25},{25,17},{2,10},{10... | collective-permute-start | bytes 1376264 | tf_op jit(solution)/shard_map/ppermute | solution.py:552
  17.3 0.5 collective-permute-start.4
  17.8 4.9 %all-to-all-start = ((bf16[8,8,640]{2,1,0:T(8,128)(2,1)}), bf16[8,8,640]{2,1,0:T(8,128)(2,1)S(1)}, u32[]{:S(2)}, u32[]{:S(2)}) async-start(bf16[8,8,640]{2,1,0:T(8,128)(2,1)} %bitcast.29), calls=%async_computation | async-start | bytes 163840 | tf_op jit(solution)/shard_map/all_to_all | solution.py:614
  23.3 5.0 %shard_map.160 = (f32[4,384,128]{2,1,0:T(8,128)}, f32[4,256,128]{2,1,0:T(8,128)}, bf16[256,64]{1,0:T(8,128)(2,1)}) custom-call(s32[1]{0:T(128)S(6)} %copy.19.refs_0_, bf16[128,1792]{1,0:T(8,128)(2,1)} %get-tuple-element.39.refs_1_, bf16[128,1792]{1,0:T(8,128)(2,1)} %shard_map.159.refs_2_, bf16[4,144,1792]{2,1,0:T(8,128)(2,1)} %bitcast.25), custom_call_target="tpu_custom_call" | custom-call | flops 788529152 | bytes 1835008 | tf_op jit(solution)/shard_map/pallas_call | solution.py:529
  28.4 0.4 all-to-all-done
  28.8 3.5 %shard_map.161.refs_10_ = f32[256,128]{1,0:T(8,128)} custom-call(bf16[64,640]{1,0:T(8,128)(2,1)S(1)} %bitcast.16, f32[17472,112]{1,0:T(8,128)} %bitcast.19, bf16[256,64]{1,0:T(8,128)(2,1)} %get-tuple-element.44.refs_2_.refs_7_), custom_call_target="tpu_custom_call" | custom-call | flops 500957184 | bytes 4472832 | tf_op jit(solution)/shard_map/pallas_call | solution.py:529
  32.3 0.0 collective-permute-done.3.refs_2_
  32.4 0.0 collective-permute-done.1.refs_5_
  32.4 0.0 collective-permute-done.2.refs_3_
  32.4 1.6 %collective-permute-start.6 = (bf16[128,1792]{1,0:T(8,128)(2,1)S(1)}, bf16[128,1792]{1,0:T(8,128)(2,1)S(1)}, u32[]{:S(2)}, u32[]{:S(2)}) collective-permute-start(bf16[128,1792]{1,0:T(8,128)(2,1)S(1)} %collective-permute-done.2.refs_3_), channel_id=1, source_target_pairs={{0,16},{8,24},{16,0},{24,8},{1,17},{9,25},{17,1},{25,9},{2,18},{10... | collective-permute-start | bytes 1376264 | tf_op jit(solution)/shard_map/ppermute | solution.py:552
  34.0 0.1 collective-permute-start.5
  34.7 0.0 collective-permute-done.4.refs_6_
  34.7 9.6 %shard_map.162 = (f32[4,384,128]{2,1,0:T(8,128)}, bf16[256,640]{1,0:T(8,128)(2,1)}, f32[4,384,128]{2,1,0:T(8,128)}, bf16[256,640]{1,0:T(8,128)(2,1)}, bf16[4,384...) custom-call(s32[1]{0:T(128)S(6)} %copy.19.refs_0_, s32[1]{0:T(128)S(6)} %copy.20.refs_1_, ...), custom_call_target="tpu_custom_call" | custom-call | flops 2078015488 | bytes 4472832 | tf_op jit(solution)/shard_map/pallas_call | solution.py:529
  44.3 0.6 collective-permute-done.6.refs_2_
  45.0 1.2 %collective-permute-done.5.refs_1_ = bf16[128,1792]{1,0:T(8,128)(2,1)S(1)} collective-permute-done((bf16[128,1792]{1,0:T(8,128)(2,1)S(1)}, bf16[128,1792]{1,0:T(8,128)(2,1)S(1)}, u32[]{:S(2)}, u32[]{:S(2)}) %collective-permute-start.5) | collective-permute-done | bytes 458784 | tf_op jit(solution)/shard_map/ppermute | solution.py:552
  46.2 5.9 %shard_map.163 = (bf16[128,1792]{1,0:T(8,128)(2,1)S(1)}, bf16[128,1792]{1,0:T(8,128)(2,1)S(1)}, bf16[256,640]{1,0:T(8,128)(2,1)}) custom-call(s32[1]{0:T(128)S(6)} %copy.19.refs_0_, bf16[128,1792]{1,0:T(8,128)(2,1)S(1)} %collective-permute-done.5.refs_1_, bf16[128,1792]{1,0:T(8,128)(2,1)S(1)} %collective-permute-done.6.refs_2_, ...), custom_call_target="tpu_custom_call" | custom-call | flops 1358954496 | bytes 1835008 | tf_op jit(solution)/shard_map/pallas_call | solution.py:529
  52.1 0.6 collective-permute-start.8
  52.7 1.5 %collective-permute-start.7 = (bf16[128,1792]{1,0:T(8,128)(2,1)S(1)}, bf16[128,1792]{1,0:T(8,128)(2,1)S(1)}, u32[]{:S(2)}, u32[]{:S(2)}) collective-permute-start(bf16[128,1792]{1,0:T(8,128)(2,1)S(1)} %get-tuple-element.57), channel_id=1, source_target_pairs={{0,8},{8,0},{16,24},{24,16},{1,9},{9,1},{17,25},{25,17},{2,10},{10... | collective-permute-start | bytes 1376264 | tf_op jit(solution)/shard_map/ppermute | solution.py:552
  54.2 8.1 %shard_map.164 = (bf16[128,1792]{1,0:T(8,128)(2,1)}, bf16[128,1792]{1,0:T(8,128)(2,1)}, bf16[128,1792]{1,0:T(8,128)(2,1)}, bf16[128,1792]{1,0:T(8,128)(2,1)}, f32[4,384,128]{2,1,0:T(8,128)}) custom-call(s32[1]{0:T(128)S(6)} %copy.19.refs_0_, s32[1]{0:T(128)S(6)} %copy.20.refs_1_, bf16[256,640]{1,0:T(8,128)(2,1)} %get-tuple-element.52.refs_2_, ...), custom_call_target="tpu_custom_call" | custom-call | flops 1140850688 | bytes 1835008 | tf_op jit(solution)/shard_map/pallas_call | solution.py:529
  62.2 0.4 collective-permute-start.11
  62.7 1.7 %collective-permute-start.9 = (bf16[128,1792]{1,0:T(8,128)(2,1)}, bf16[128,1792]{1,0:T(8,128)(2,1)S(1)}, u32[]{:S(2)}, u32[]{:S(2)}) collective-permute-start(bf16[128,1792]{1,0:T(8,128)(2,1)} %get-tuple-element.60.refs_4_), channel_id=1, source_target_pairs={{0,8},{8,0},{16,24},{24,16},{1,9},{9,1},{17,25},{25,17},{2,10},{10... | collective-permute-start | bytes 1376264 | tf_op jit(solution)/shard_map/ppermute | solution.py:552
  64.4 0.0 collective-permute-done.8.refs_3_
  64.4 0.0 collective-permute-done.7.refs_1_
  64.4 1.3 %shard_map.165 = (bf16[128,1792]{1,0:T(8,128)(2,1)S(1)}, bf16[128,1792]{1,0:T(8,128)(2,1)S(1)}) custom-call(bf16[128,1792]{1,0:T(8,128)(2,1)} %get-tuple-element.56.refs_0_, bf16[128,1792]{1,0:T(8,128)(2,1)S(1)} %collective-permute-done.7.refs_1_, bf16[128,1792]{1,0:T(8,128)(2,1)} %get-tuple-element.58.refs_2_, ...), custom_call_target="tpu_custom_call" | custom-call | bytes 1835008 | tf_op jit(solution)/shard_map/pallas_call | solution.py:529
  65.6 0.0 copy-start
  65.7 1.0 %collective-permute-start.10 = (bf16[128,1792]{1,0:T(8,128)(2,1)S(1)}, bf16[128,1792]{1,0:T(8,128)(2,1)S(1)}, u32[]{:S(2)}, u32[]{:S(2)}) collective-permute-start(bf16[128,1792]{1,0:T(8,128)(2,1)S(1)} %get-tuple-element.63), channel_id=1, source_target_pairs={{0,16},{8,24},{16,0},{24,8},{1,17},{9,25},{17,1},{25,9},{2,18},{10... | collective-permute-start | bytes 1376264 | tf_op jit(solution)/shard_map/ppermute | solution.py:552
  66.7 1.0 %collective-permute-start.12 = (bf16[128,1792]{1,0:T(8,128)(2,1)S(1)}, bf16[128,1792]{1,0:T(8,128)(2,1)S(1)}, u32[]{:S(2)}, u32[]{:S(2)}) collective-permute-start(bf16[128,1792]{1,0:T(8,128)(2,1)S(1)} %get-tuple-element.61.refs_11_), channel_id=1, source_target_pairs={{0,8},{8,0},{16,24},{24,16},{1,9},{9,1},{17,25},{25,17},{2,10},{10... | collective-permute-start | bytes 1376264 | tf_op jit(solution)/shard_map/ppermute | solution.py:552
  67.7 4.7 %all-to-all-start.1 = ((bf16[8,8,512]{2,1,0:T(8,128)(2,1)}), bf16[8,8,512]{2,1,0:T(8,128)(2,1)S(1)}, u32[]{:S(2)}, u32[]{:S(2)}) async-start(bf16[8,8,512]{2,1,0:T(8,128)(2,1)} %bitcast.11), calls=%async_computation.1 | async-start | bytes 131072 | tf_op jit(solution)/shard_map/all_to_all | solution.py:668
  72.5 0.0 copy-done
  72.5 5.7 %shard_map.166 = (bf16[128,1792]{1,0:T(8,128)(2,1)}, bf16[128,1792]{1,0:T(8,128)(2,1)}, f32[1,273,4,112]{3,2,1,0:T(4,128)}) custom-call(s32[1]{0:T(128)S(6)} %copy.19.refs_0_, s32[1]{0:T(128)S(6)} %copy.20.refs_1_, f32[1,16,273,4,112]{4,3,2,1,0:T(4,128)} %bitcast.23, f32[4,384,128]{2,1,0:T(8,128)} %get-tuple-element.43.refs_8_.refs_5_.refs_3_, ...), custom_call_target="tpu_custom_call" | custom-call | flops 570425344 | bytes 1835008 | tf_op jit(solution)/shard_map/pallas_call | solution.py:529
  78.2 0.2 all-to-all-done.1
  78.4 0.0 collective-permute-done.11.refs_4_
  78.4 0.0 collective-permute-done.9.refs_3_.refs_1_
  78.4 2.7 %shard_map.167 = (bf16[16,1792]{1,0:T(8,128)(2,1)}, bf16[16,1792]{1,0:T(8,128)(2,1)}, bf16[16,1792]{1,0:T(8,128)(2,1)}, bf16[16,1792]{1,0:T(8,128)(2,1)}) custom-call(bf16[64,512]{1,0:T(8,128)(2,1)S(1)} %bitcast.18, s32[1,32]{1,0:T(1,128)} %bitcast.34, bf16[448,1792]{1,0:T(8,128)(2,1)} %refs_2_.5, ...), custom_call_target="tpu_custom_call" | custom-call | flops 58720256 | bytes 1835008 | tf_op jit(solution)/shard_map/pallas_call | solution.py:529
  81.0 1.1 %collective-permute-start.13 = (bf16[16,1792]{1,0:T(8,128)(2,1)}, bf16[16,1792]{1,0:T(8,128)(2,1)S(1)}, u32[]{:S(2)}, u32[]{:S(2)}) collective-permute-start(bf16[16,1792]{1,0:T(8,128)(2,1)} %get-tuple-element.69), channel_id=1, source_target_pairs={{0,8},{8,0},{16,24},{24,16},{1,9},{9,1},{17,25},{25,17},{2,10},{10... | collective-permute-start | bytes 172040 | tf_op jit(solution)/shard_map/ppermute | solution.py:552
  82.1 1.1 %collective-permute-start.14 = (bf16[16,1792]{1,0:T(8,128)(2,1)}, bf16[16,1792]{1,0:T(8,128)(2,1)S(1)}, u32[]{:S(2)}, u32[]{:S(2)}) collective-permute-start(bf16[16,1792]{1,0:T(8,128)(2,1)} %get-tuple-element.70), channel_id=1, source_target_pairs={{0,16},{8,24},{16,0},{24,8},{1,17},{9,25},{17,1},{25,9},{2,18},{10... | collective-permute-start | bytes 172040 | tf_op jit(solution)/shard_map/ppermute | solution.py:552
  83.2 1.4 %collective-permute-start.15 = (bf16[16,1792]{1,0:T(8,128)(2,1)}, bf16[16,1792]{1,0:T(8,128)(2,1)S(1)}, u32[]{:S(2)}, u32[]{:S(2)}) collective-permute-start(bf16[16,1792]{1,0:T(8,128)(2,1)} %get-tuple-element.71), channel_id=1, source_target_pairs={{0,24},{8,16},{16,8},{24,0},{1,25},{9,17},{17,9},{25,1},{2,26},{10... | collective-permute-start | bytes 172040 | tf_op jit(solution)/shard_map/ppermute | solution.py:552
  84.6 0.9 collective-permute-done.13.refs_7_
  85.5 1.0 %collective-permute-done.14.refs_8_ = bf16[16,1792]{1,0:T(8,128)(2,1)S(1)} collective-permute-done((bf16[16,1792]{1,0:T(8,128)(2,1)}, bf16[16,1792]{1,0:T(8,128)(2,1)S(1)}, u32[]{:S(2)}, u32[]{:S(2)}) %collective-permute-start.14) | collective-permute-done | bytes 57376 | tf_op jit(solution)/shard_map/ppermute | solution.py:552
  86.5 2.0 %collective-permute-done.15.refs_9_ = bf16[16,1792]{1,0:T(8,128)(2,1)S(1)} collective-permute-done((bf16[16,1792]{1,0:T(8,128)(2,1)}, bf16[16,1792]{1,0:T(8,128)(2,1)S(1)}, u32[]{:S(2)}, u32[]{:S(2)}) %collective-permute-start.15) | collective-permute-done | bytes 57376 | tf_op jit(solution)/shard_map/ppermute | solution.py:552
  88.5 0.0 collective-permute-done.10.refs_2_
  88.5 0.0 collective-permute-done.12.refs_5_
  88.5 2.7 %shard_map.168 = (bf16[2,128,1792]{2,1,0:T(8,128)(2,1)}, bf16[1,8,1792]{2,1,0:T(8,128)(2,1)}) custom-call(bf16[128,1792]{1,0:T(8,128)(2,1)} %get-tuple-element.62.refs_5_.refs_0_, bf16[128,1792]{1,0:T(8,128)(2,1)S(1)} %collective-permute-done.9.refs_3_.refs_1_, bf16[128,1792]{1,0:T(8,128)(2,1)S(1)} %collective-permute-done.10.refs_2_, ...), custom_call_target="tpu_custom_call" | custom-call | bytes 3670016 | tf_op jit(solution)/shard_map/pallas_call | solution.py:529
Async XLA Ops:
  3.8 9.9 %collective-permute-start = (bf16[16,1792]{1,0:T(8,128)(2,1)}, bf16[16,1792]{1,0:T(8,128)(2,1)S(1)}, u32[]{:S(2)}, u32[]{:S(2)}) collective-permute-start(bf16[16,1792]{1,0:T(8,128)(2,1)} %get-tuple-element.42), channel_id=1, source_target_pairs={{0,8},{8,16},{16,24},{1,9},{9,17},{17,25},{2,10},{10,18},{18,26},{... | collective-permute-start | bytes 172040 | tf_op jit(solution)/shard_map/ppermute | solution.py:718
  8.6 23.7 %collective-permute-start.3 = (bf16[128,1792]{1,0:T(8,128)(2,1)}, bf16[128,1792]{1,0:T(8,128)(2,1)S(1)}, u32[]{:S(2)}, u32[]{:S(2)}) collective-permute-start(bf16[128,1792]{1,0:T(8,128)(2,1)} %get-tuple-element.39.refs_1_), channel_id=1, source_target_pairs={{0,8},{8,0},{16,24},{24,16},{1,9},{9,1},{17,25},{25,17},{2,10},{10... | collective-permute-start | bytes 1376264 | tf_op jit(solution)/shard_map/ppermute | solution.py:552
  10.2 22.2 %collective-permute-start.1 = (bf16[128,1792]{1,0:T(8,128)(2,1)}, bf16[128,1792]{1,0:T(8,128)(2,1)S(1)}, u32[]{:S(2)}, u32[]{:S(2)}) collective-permute-start(bf16[128,1792]{1,0:T(8,128)(2,1)} %get-tuple-element.39.refs_1_), channel_id=1, source_target_pairs={{0,16},{8,24},{16,0},{24,8},{1,17},{9,25},{17,1},{25,9},{2,18},{10... | collective-permute-start | bytes 1376264 | tf_op jit(solution)/shard_map/ppermute | solution.py:552
  14.7 17.7 %collective-permute-start.2 = (bf16[128,1792]{1,0:T(8,128)(2,1)}, bf16[128,1792]{1,0:T(8,128)(2,1)S(1)}, u32[]{:S(2)}, u32[]{:S(2)}) collective-permute-start(bf16[128,1792]{1,0:T(8,128)(2,1)} %shard_map.159.refs_2_), channel_id=1, source_target_pairs={{0,8},{8,0},{16,24},{24,16},{1,9},{9,1},{17,25},{25,17},{2,10},{10... | collective-permute-start | bytes 1376264 | tf_op jit(solution)/shard_map/ppermute | solution.py:552
  17.3 17.4 %collective-permute-start.4 = (bf16[128,1792]{1,0:T(8,128)(2,1)}, bf16[128,1792]{1,0:T(8,128)(2,1)S(1)}, u32[]{:S(2)}, u32[]{:S(2)}) collective-permute-start(bf16[128,1792]{1,0:T(8,128)(2,1)} %shard_map.159.refs_2_), channel_id=1, source_target_pairs={{0,16},{8,24},{16,0},{24,8},{1,17},{9,25},{17,1},{25,9},{2,18},{10... | collective-permute-start | bytes 1376264 | tf_op jit(solution)/shard_map/ppermute | solution.py:552
  17.8 11.0 %all-to-all-start = ((bf16[8,8,640]{2,1,0:T(8,128)(2,1)}), bf16[8,8,640]{2,1,0:T(8,128)(2,1)S(1)}, u32[]{:S(2)}, u32[]{:S(2)}) async-start(bf16[8,8,640]{2,1,0:T(8,128)(2,1)} %bitcast.29), calls=%async_computation | async-start | bytes 163840 | tf_op jit(solution)/shard_map/all_to_all | solution.py:614
  32.4 12.6 %collective-permute-start.6 = (bf16[128,1792]{1,0:T(8,128)(2,1)S(1)}, bf16[128,1792]{1,0:T(8,128)(2,1)S(1)}, u32[]{:S(2)}, u32[]{:S(2)}) collective-permute-start(bf16[128,1792]{1,0:T(8,128)(2,1)S(1)} %collective-permute-done.2.refs_3_), channel_id=1, source_target_pairs={{0,16},{8,24},{16,0},{24,8},{1,17},{9,25},{17,1},{25,9},{2,18},{10... | collective-permute-start | bytes 1376264 | tf_op jit(solution)/shard_map/ppermute | solution.py:552
  34.0 12.3 %collective-permute-start.5 = (bf16[128,1792]{1,0:T(8,128)(2,1)S(1)}, bf16[128,1792]{1,0:T(8,128)(2,1)S(1)}, u32[]{:S(2)}, u32[]{:S(2)}) collective-permute-start(bf16[128,1792]{1,0:T(8,128)(2,1)S(1)} %collective-permute-done.1.refs_5_), channel_id=1, source_target_pairs={{0,8},{8,0},{16,24},{24,16},{1,9},{9,1},{17,25},{25,17},{2,10},{10... | collective-permute-start | bytes 1376264 | tf_op jit(solution)/shard_map/ppermute | solution.py:552
  52.1 12.3 %collective-permute-start.8 = (bf16[128,1792]{1,0:T(8,128)(2,1)S(1)}, bf16[128,1792]{1,0:T(8,128)(2,1)S(1)}, u32[]{:S(2)}, u32[]{:S(2)}) collective-permute-start(bf16[128,1792]{1,0:T(8,128)(2,1)S(1)} %get-tuple-element.59), channel_id=1, source_target_pairs={{0,16},{8,24},{16,0},{24,8},{1,17},{9,25},{17,1},{25,9},{2,18},{10... | collective-permute-start | bytes 1376264 | tf_op jit(solution)/shard_map/ppermute | solution.py:552
  52.7 11.7 %collective-permute-start.7 = (bf16[128,1792]{1,0:T(8,128)(2,1)S(1)}, bf16[128,1792]{1,0:T(8,128)(2,1)S(1)}, u32[]{:S(2)}, u32[]{:S(2)}) collective-permute-start(bf16[128,1792]{1,0:T(8,128)(2,1)S(1)} %get-tuple-element.57), channel_id=1, source_target_pairs={{0,8},{8,0},{16,24},{24,16},{1,9},{9,1},{17,25},{25,17},{2,10},{10... | collective-permute-start | bytes 1376264 | tf_op jit(solution)/shard_map/ppermute | solution.py:552
  62.2 16.1 %collective-permute-start.11 = (bf16[128,1792]{1,0:T(8,128)(2,1)}, bf16[128,1792]{1,0:T(8,128)(2,1)S(1)}, u32[]{:S(2)}, u32[]{:S(2)}) collective-permute-start(bf16[128,1792]{1,0:T(8,128)(2,1)} %get-tuple-element.65), channel_id=1, source_target_pairs={{0,16},{8,24},{16,0},{24,8},{1,17},{9,25},{17,1},{25,9},{2,18},{10... | collective-permute-start | bytes 1376264 | tf_op jit(solution)/shard_map/ppermute | solution.py:552
  62.7 15.7 %collective-permute-start.9 = (bf16[128,1792]{1,0:T(8,128)(2,1)}, bf16[128,1792]{1,0:T(8,128)(2,1)S(1)}, u32[]{:S(2)}, u32[]{:S(2)}) collective-permute-start(bf16[128,1792]{1,0:T(8,128)(2,1)} %get-tuple-element.60.refs_4_), channel_id=1, source_target_pairs={{0,8},{8,0},{16,24},{24,16},{1,9},{9,1},{17,25},{25,17},{2,10},{10... | collective-permute-start | bytes 1376264 | tf_op jit(solution)/shard_map/ppermute | solution.py:552
  65.6 6.8 %copy-start = (bf16[128,1792]{1,0:T(8,128)(2,1)}, bf16[128,1792]{1,0:T(8,128)(2,1)S(1)}, u32[]{:S(2)}) copy-start(bf16[128,1792]{1,0:T(8,128)(2,1)S(1)} %get-tuple-element.61.refs_11_) | copy-start | bytes 1376260
  65.7 22.8 %collective-permute-start.10 = (bf16[128,1792]{1,0:T(8,128)(2,1)S(1)}, bf16[128,1792]{1,0:T(8,128)(2,1)S(1)}, u32[]{:S(2)}, u32[]{:S(2)}) collective-permute-start(bf16[128,1792]{1,0:T(8,128)(2,1)S(1)} %get-tuple-element.63), channel_id=1, source_target_pairs={{0,16},{8,24},{16,0},{24,8},{1,17},{9,25},{17,1},{25,9},{2,18},{10... | collective-permute-start | bytes 1376264 | tf_op jit(solution)/shard_map/ppermute | solution.py:552
  66.7 21.8 %collective-permute-start.12 = (bf16[128,1792]{1,0:T(8,128)(2,1)S(1)}, bf16[128,1792]{1,0:T(8,128)(2,1)S(1)}, u32[]{:S(2)}, u32[]{:S(2)}) collective-permute-start(bf16[128,1792]{1,0:T(8,128)(2,1)S(1)} %get-tuple-element.61.refs_11_), channel_id=1, source_target_pairs={{0,8},{8,0},{16,24},{24,16},{1,9},{9,1},{17,25},{25,17},{2,10},{10... | collective-permute-start | bytes 1376264 | tf_op jit(solution)/shard_map/ppermute | solution.py:552
  67.7 10.7 %all-to-all-start.1 = ((bf16[8,8,512]{2,1,0:T(8,128)(2,1)}), bf16[8,8,512]{2,1,0:T(8,128)(2,1)S(1)}, u32[]{:S(2)}, u32[]{:S(2)}) async-start(bf16[8,8,512]{2,1,0:T(8,128)(2,1)} %bitcast.11), calls=%async_computation.1 | async-start | bytes 131072 | tf_op jit(solution)/shard_map/all_to_all | solution.py:668
  81.0 4.5 %collective-permute-start.13 = (bf16[16,1792]{1,0:T(8,128)(2,1)}, bf16[16,1792]{1,0:T(8,128)(2,1)S(1)}, u32[]{:S(2)}, u32[]{:S(2)}) collective-permute-start(bf16[16,1792]{1,0:T(8,128)(2,1)} %get-tuple-element.69), channel_id=1, source_target_pairs={{0,8},{8,0},{16,24},{24,16},{1,9},{9,1},{17,25},{25,17},{2,10},{10... | collective-permute-start | bytes 172040 | tf_op jit(solution)/shard_map/ppermute | solution.py:552
  82.1 4.4 %collective-permute-start.14 = (bf16[16,1792]{1,0:T(8,128)(2,1)}, bf16[16,1792]{1,0:T(8,128)(2,1)S(1)}, u32[]{:S(2)}, u32[]{:S(2)}) collective-permute-start(bf16[16,1792]{1,0:T(8,128)(2,1)} %get-tuple-element.70), channel_id=1, source_target_pairs={{0,16},{8,24},{16,0},{24,8},{1,17},{9,25},{17,1},{25,9},{2,18},{10... | collective-permute-start | bytes 172040 | tf_op jit(solution)/shard_map/ppermute | solution.py:552
  83.2 5.3 %collective-permute-start.15 = (bf16[16,1792]{1,0:T(8,128)(2,1)}, bf16[16,1792]{1,0:T(8,128)(2,1)S(1)}, u32[]{:S(2)}, u32[]{:S(2)}) collective-permute-start(bf16[16,1792]{1,0:T(8,128)(2,1)} %get-tuple-element.71), channel_id=1, source_target_pairs={{0,24},{8,16},{16,8},{24,0},{1,25},{9,17},{17,9},{25,1},{2,26},{10... | collective-permute-start | bytes 172040 | tf_op jit(solution)/shard_map/ppermute | solution.py:552

commit v6 on v5

--- a/solution.py
+++ b/solution.py
@@ -277,13 +277,11 @@
     two_x[...] = (low1[...].astype(F32) + via_y[...].astype(F32)).astype(BF)
 
 
-def total_kernel(top0, one_x, two_y, low0, one_y, two_x, dec0, dec1, dec2, dec3, out, decode_out):
+def total_kernel(top0, one_x, two_y, low0, one_y, two_x, out):
     out[0] = (top0[...].astype(F32) + one_x[...].astype(F32) + two_y[...].astype(F32)).astype(BF)
     out.push(0)
     out[1] = (low0[...].astype(F32) + one_y[...].astype(F32) + two_x[...].astype(F32)).astype(BF)
     out.push(1)
-    total = (dec0[...].astype(F32) + dec1[...].astype(F32)) + (dec2[...].astype(F32) + dec3[...].astype(F32))
-    decode_out[0] = total[: DEC // 4].astype(BF)
 
 
 def placing_rank(owners_row, axis):
@@ -701,15 +699,18 @@
     two_y = across(two_y, 2)
     two_x = across(two_x, 1)
     state_next = jnp.transpose(state_next, (0, 2, 3, 1))
-    stretch_out, decode_out = hbm_call(
+    (stretch_out,) = hbm_call(
         total_kernel,
-        [shape(2, half, D), shape(1, DEC // 4, D)],
+        [shape(2, half, D)],
         0,
         8 * rows * D,
-        loose=(1, 2, 4, 5, 7, 8, 9),
+        loose=(1, 2, 4, 5),
         split_out=(0,),
-    )(top0, one_x, two_y, low0, one_y, two_x, *shares)
-    return (stretch_out.reshape(1, rows, D), decode_out, state_next)
+        waits=[decoded[0]],
+    )(top0, one_x, two_y, low0, one_y, two_x)
+    shares = lax.optimization_barrier((*shares, stretch_out))[:4]
+    decode_out = sum(share[: DEC // 4].astype(F32) for share in shares).astype(BF)
+    return (stretch_out.reshape(1, rows, D), decode_out[None], state_next)
 
 
 def from_behind(array, axis, by):

time: 92 us -> 89.7 us (0.975)
  waiting for transfers between devices: 6.38 us -> 3.65 us
    ppermute x15, waiting for transfers between devices: 5.77 us -> 3.04 us  [across(): return lax.ppermute(array, 'head', [(i, i ^ by) for i in range(4)])]
  transfers between devices with their start and end apart: 18 -> 18, of which waited for: 7 -> 5; matrix products, arithmetic and copies ran while one was open for 0% -> 0% of each run, Pallas kernels for 44% -> 48%
where the time goes in v6:
time: 89.7 us; the launch traced here: 89.1 us
  Pallas kernels  52 us (58%)
  starting transfers between devices  30.7 us (34%)
  waiting for transfers between devices  3.65 us (4%)
  between operations  2.13 us (2%)
    pallas_call x11, Pallas kernels, run(): pl.pallas_call(body, out_shape=[o if n in near else pltpu.HBM(o.shape, o....  51.1 us
    ppermute x15, starting transfers between devices, across(): return lax.ppermute(array, 'head', [(i, i ^ by) for i in range(4)])  16.3 us
    all_to_all x1, starting transfers between devices, local_square(): lax.all_to_all(sent.reshape(groups, capacity, wide), 'tok', split_axis=0,...  4.88 us
    ppermute x1, starting transfers between devices, from_behind(): return lax.ppermute(array, axis, pairs)  4.84 us
    all_to_all x1, starting transfers between devices, local_square(): lax.all_to_all(served.reshape(groups, capacity, heads * WIDE), 'tok', spl...  4.74 us
    ppermute x15, waiting for transfers between devices, across(): return lax.ppermute(array, 'head', [(i, i ^ by) for i in range(4)])  3.04 us
  transfers between devices with their start and end apart: 18, of which 5 were waited for; matrix products, arithmetic and copies ran while one was open for 0% of the time, Pallas kernels for 48%

profile of v6, /device:TPU:0, one launch (start us, length us, event | category | flops | bytes accessed | tf_op | source)
XLA Modules:
  0.0 89.1 jit_solution(5501115757390786363)
XLA Ops:
  0.6 3.1 %shard_map.157 = (bf16[128,1792]{1,0:T(8,128)(2,1)}, bf16[128,1792]{1,0:T(8,128)(2,1)}, bf16[16,1792]{1,0:T(8,128)(2,1)}, bf16[16,1792]{1,0:T(8,128)(2,1)}) custom-call(bf16[256,1792]{1,0:T(8,128)(2,1)} %bitcast.31, bf16[2,1792]{1,0:T(2,128)(2,1)} %bitcast.35, f32[1792]{0:T(1024)} %refs_2_.4, f32[3,1792]{1,0:T(4,128)} %taps_ref.1), custom_call_target="tpu_custom_call" | custom-call | flops 9175040 | bytes 1835008 | tf_op jit(solution)/shard_map/pallas_call | solution.py:527
  3.8 4.8 %collective-permute-start = (bf16[16,1792]{1,0:T(8,128)(2,1)}, bf16[16,1792]{1,0:T(8,128)(2,1)S(1)}, u32[]{:S(2)}, u32[]{:S(2)}) collective-permute-start(bf16[16,1792]{1,0:T(8,128)(2,1)} %get-tuple-element.44), channel_id=1, source_target_pairs={{0,8},{8,16},{16,24},{1,9},{9,17},{17,25},{2,10},{10,18},{18,26},{... | collective-permute-start | bytes 172040 | tf_op jit(solution)/shard_map/ppermute | solution.py:719
  8.6 1.6 %collective-permute-start.3 = (bf16[128,1792]{1,0:T(8,128)(2,1)}, bf16[128,1792]{1,0:T(8,128)(2,1)S(1)}, u32[]{:S(2)}, u32[]{:S(2)}) collective-permute-start(bf16[128,1792]{1,0:T(8,128)(2,1)} %get-tuple-element.41.refs_1_), channel_id=1, source_target_pairs={{0,8},{8,0},{16,24},{24,16},{1,9},{9,1},{17,25},{25,17},{2,10},{10... | collective-permute-start | bytes 1376264 | tf_op jit(solution)/shard_map/ppermute | solution.py:550
  10.2 0.1 collective-permute-start.1
  10.3 3.4 %shard_map.158.wait_ref = bf16[64,640]{1,0:T(8,128)(2,1)} custom-call(bf16[32,1792]{1,0:T(8,128)(2,1)} %bitcast.34, bf16[32,2,1792]{2,1,0:T(2,128)(2,1)} %bitcast.33, f32[1792]{0:T(1024)} %refs_2_.4, f32[3,1792]{1,0:T(4,128)} %taps_ref.1, s32[1,32]{1,0:T(1,128)} %bitcast.36, s32[1,32]{1,0:T(1,128)} %refs_5_.2, bf16[4,144,1792]{2,1,0:T(8,128)(2,1)} %bitcast.26), custom_call_target="tpu_custom_call" | custom-call | flops 73400320 | bytes 2293760 | tf_op jit(solution)/shard_map/pallas_call | solution.py:527
  13.7 0.0 collective-permute-done.end_ref
  13.7 0.9 %shard_map.159.refs_2_ = bf16[128,1792]{1,0:T(8,128)(2,1)} custom-call(s32[1]{0:T(128)} %bitcast.3.first_ref, bf16[128,1792]{1,0:T(8,128)(2,1)} %get-tuple-element.42.top_ref, bf16[16,1792]{1,0:T(8,128)(2,1)} %get-tuple-element.43.begin_ref, bf16[16,1792]{1,0:T(8,128)(2,1)S(1)} %collective-permute-done.end_ref, ...), custom_call_target="tpu_custom_call", output_to_operand_aliasing={{}: (1, {})} | custom-call | flops 28672 | bytes 229376 | tf_op jit(solution)/shard_map/pallas_call | solution.py:597
  14.7 2.6 %collective-permute-start.2 = (bf16[128,1792]{1,0:T(8,128)(2,1)}, bf16[128,1792]{1,0:T(8,128)(2,1)S(1)}, u32[]{:S(2)}, u32[]{:S(2)}) collective-permute-start(bf16[128,1792]{1,0:T(8,128)(2,1)} %shard_map.159.refs_2_), channel_id=1, source_target_pairs={{0,8},{8,0},{16,24},{24,16},{1,9},{9,1},{17,25},{25,17},{2,10},{10... | collective-permute-start | bytes 1376264 | tf_op jit(solution)/shard_map/ppermute | solution.py:550
  17.3 0.5 collective-permute-start.4
  17.8 4.9 %all-to-all-start = ((bf16[8,8,640]{2,1,0:T(8,128)(2,1)}), bf16[8,8,640]{2,1,0:T(8,128)(2,1)S(1)}, u32[]{:S(2)}, u32[]{:S(2)}) async-start(bf16[8,8,640]{2,1,0:T(8,128)(2,1)} %bitcast.32), calls=%async_computation | async-start | bytes 163840 | tf_op jit(solution)/shard_map/all_to_all | solution.py:612
  23.3 5.0 %shard_map.160 = (f32[4,384,128]{2,1,0:T(8,128)}, f32[4,256,128]{2,1,0:T(8,128)}, bf16[256,64]{1,0:T(8,128)(2,1)}) custom-call(s32[1]{0:T(128)S(6)} %copy.19.refs_0_, bf16[128,1792]{1,0:T(8,128)(2,1)} %get-tuple-element.41.refs_1_, bf16[128,1792]{1,0:T(8,128)(2,1)} %shard_map.159.refs_2_, bf16[4,144,1792]{2,1,0:T(8,128)(2,1)} %bitcast.27), custom_call_target="tpu_custom_call" | custom-call | flops 788529152 | bytes 1835008 | tf_op jit(solution)/shard_map/pallas_call | solution.py:527
  28.4 0.4 all-to-all-done
  28.8 3.5 %shard_map.161.refs_10_ = f32[256,128]{1,0:T(8,128)} custom-call(bf16[64,640]{1,0:T(8,128)(2,1)S(1)} %bitcast.18, f32[17472,112]{1,0:T(8,128)} %bitcast.21, bf16[256,64]{1,0:T(8,128)(2,1)} %get-tuple-element.46.refs_2_.refs_7_), custom_call_target="tpu_custom_call" | custom-call | flops 500957184 | bytes 4472832 | tf_op jit(solution)/shard_map/pallas_call | solution.py:527
  32.3 0.0 collective-permute-done.3.refs_2_
  32.4 0.0 collective-permute-done.1.refs_5_
  32.4 0.0 collective-permute-done.2.refs_3_
  32.4 1.6 %collective-permute-start.6 = (bf16[128,1792]{1,0:T(8,128)(2,1)S(1)}, bf16[128,1792]{1,0:T(8,128)(2,1)S(1)}, u32[]{:S(2)}, u32[]{:S(2)}) collective-permute-start(bf16[128,1792]{1,0:T(8,128)(2,1)S(1)} %collective-permute-done.2.refs_3_), channel_id=1, source_target_pairs={{0,16},{8,24},{16,0},{24,8},{1,17},{9,25},{17,1},{25,9},{2,18},{10... | collective-permute-start | bytes 1376264 | tf_op jit(solution)/shard_map/ppermute | solution.py:550
  34.0 0.1 collective-permute-start.5
  34.7 0.0 collective-permute-done.4.refs_6_
  34.7 9.6 %shard_map.162 = (f32[4,384,128]{2,1,0:T(8,128)}, bf16[256,640]{1,0:T(8,128)(2,1)}, f32[4,384,128]{2,1,0:T(8,128)}, bf16[256,640]{1,0:T(8,128)(2,1)}, bf16[4,384...) custom-call(s32[1]{0:T(128)S(6)} %copy.19.refs_0_, s32[1]{0:T(128)S(6)} %copy.20.refs_1_, ...), custom_call_target="tpu_custom_call" | custom-call | flops 2078015488 | bytes 4472832 | tf_op jit(solution)/shard_map/pallas_call | solution.py:527
  44.3 0.6 collective-permute-done.6.refs_2_
  45.0 1.2 %collective-permute-done.5.refs_1_ = bf16[128,1792]{1,0:T(8,128)(2,1)S(1)} collective-permute-done((bf16[128,1792]{1,0:T(8,128)(2,1)S(1)}, bf16[128,1792]{1,0:T(8,128)(2,1)S(1)}, u32[]{:S(2)}, u32[]{:S(2)}) %collective-permute-start.5) | collective-permute-done | bytes 458784 | tf_op jit(solution)/shard_map/ppermute | solution.py:550
  46.2 5.9 %shard_map.163 = (bf16[128,1792]{1,0:T(8,128)(2,1)S(1)}, bf16[128,1792]{1,0:T(8,128)(2,1)S(1)}, bf16[256,640]{1,0:T(8,128)(2,1)}) custom-call(s32[1]{0:T(128)S(6)} %copy.19.refs_0_, bf16[128,1792]{1,0:T(8,128)(2,1)S(1)} %collective-permute-done.5.refs_1_, bf16[128,1792]{1,0:T(8,128)(2,1)S(1)} %collective-permute-done.6.refs_2_, ...), custom_call_target="tpu_custom_call" | custom-call | flops 1358954496 | bytes 1835008 | tf_op jit(solution)/shard_map/pallas_call | solution.py:527
  52.1 0.6 collective-permute-start.8
  52.7 1.5 %collective-permute-start.7 = (bf16[128,1792]{1,0:T(8,128)(2,1)S(1)}, bf16[128,1792]{1,0:T(8,128)(2,1)S(1)}, u32[]{:S(2)}, u32[]{:S(2)}) collective-permute-start(bf16[128,1792]{1,0:T(8,128)(2,1)S(1)} %get-tuple-element.59), channel_id=1, source_target_pairs={{0,8},{8,0},{16,24},{24,16},{1,9},{9,1},{17,25},{25,17},{2,10},{10... | collective-permute-start | bytes 1376264 | tf_op jit(solution)/shard_map/ppermute | solution.py:550
  54.2 8.1 %shard_map.164 = (bf16[128,1792]{1,0:T(8,128)(2,1)}, bf16[128,1792]{1,0:T(8,128)(2,1)}, bf16[128,1792]{1,0:T(8,128)(2,1)}, bf16[128,1792]{1,0:T(8,128)(2,1)}, f32[4,384,128]{2,1,0:T(8,128)}) custom-call(s32[1]{0:T(128)S(6)} %copy.19.refs_0_, s32[1]{0:T(128)S(6)} %copy.20.refs_1_, bf16[256,640]{1,0:T(8,128)(2,1)} %get-tuple-element.54.refs_2_, ...), custom_call_target="tpu_custom_call" | custom-call | flops 1140850688 | bytes 1835008 | tf_op jit(solution)/shard_map/pallas_call | solution.py:527
  62.2 0.4 collective-permute-start.11
  62.7 1.7 %collective-permute-start.9 = (bf16[128,1792]{1,0:T(8,128)(2,1)}, bf16[128,1792]{1,0:T(8,128)(2,1)S(1)}, u32[]{:S(2)}, u32[]{:S(2)}) collective-permute-start(bf16[128,1792]{1,0:T(8,128)(2,1)} %get-tuple-element.62.refs_4_), channel_id=1, source_target_pairs={{0,8},{8,0},{16,24},{24,16},{1,9},{9,1},{17,25},{25,17},{2,10},{10... | collective-permute-start | bytes 1376264 | tf_op jit(solution)/shard_map/ppermute | solution.py:550
  64.4 0.0 collective-permute-done.8.refs_3_
  64.4 0.0 collective-permute-done.7.refs_1_
  64.4 1.3 %shard_map.165 = (bf16[128,1792]{1,0:T(8,128)(2,1)S(1)}, bf16[128,1792]{1,0:T(8,128)(2,1)S(1)}) custom-call(bf16[128,1792]{1,0:T(8,128)(2,1)} %get-tuple-element.58.refs_0_, bf16[128,1792]{1,0:T(8,128)(2,1)S(1)} %collective-permute-done.7.refs_1_, bf16[128,1792]{1,0:T(8,128)(2,1)} %get-tuple-element.60.refs_2_, ...), custom_call_target="tpu_custom_call" | custom-call | bytes 1835008 | tf_op jit(solution)/shard_map/pallas_call | solution.py:527
  65.6 0.0 copy-start
  65.7 1.0 %collective-permute-start.10 = (bf16[128,1792]{1,0:T(8,128)(2,1)S(1)}, bf16[128,1792]{1,0:T(8,128)(2,1)S(1)}, u32[]{:S(2)}, u32[]{:S(2)}) collective-permute-start(bf16[128,1792]{1,0:T(8,128)(2,1)S(1)} %get-tuple-element.65), channel_id=1, source_target_pairs={{0,16},{8,24},{16,0},{24,8},{1,17},{9,25},{17,1},{25,9},{2,18},{10... | collective-permute-start | bytes 1376264 | tf_op jit(solution)/shard_map/ppermute | solution.py:550
  66.7 1.0 %collective-permute-start.12 = (bf16[128,1792]{1,0:T(8,128)(2,1)S(1)}, bf16[128,1792]{1,0:T(8,128)(2,1)S(1)}, u32[]{:S(2)}, u32[]{:S(2)}) collective-permute-start(bf16[128,1792]{1,0:T(8,128)(2,1)S(1)} %get-tuple-element.63.refs_11_), channel_id=1, source_target_pairs={{0,8},{8,0},{16,24},{24,16},{1,9},{9,1},{17,25},{25,17},{2,10},{10... | collective-permute-start | bytes 1376264 | tf_op jit(solution)/shard_map/ppermute | solution.py:550
  67.7 4.7 %all-to-all-start.1 = ((bf16[8,8,512]{2,1,0:T(8,128)(2,1)}), bf16[8,8,512]{2,1,0:T(8,128)(2,1)S(1)}, u32[]{:S(2)}, u32[]{:S(2)}) async-start(bf16[8,8,512]{2,1,0:T(8,128)(2,1)} %bitcast.11), calls=%async_computation.1 | async-start | bytes 131072 | tf_op jit(solution)/shard_map/all_to_all | solution.py:666
  72.5 0.0 copy-done
  72.5 5.7 %shard_map.166 = (bf16[128,1792]{1,0:T(8,128)(2,1)}, bf16[128,1792]{1,0:T(8,128)(2,1)}, f32[1,273,4,112]{3,2,1,0:T(4,128)}) custom-call(s32[1]{0:T(128)S(6)} %copy.19.refs_0_, s32[1]{0:T(128)S(6)} %copy.20.refs_1_, f32[1,16,273,4,112]{4,3,2,1,0:T(4,128)} %bitcast.25, f32[4,384,128]{2,1,0:T(8,128)} %get-tuple-element.45.refs_8_.refs_5_.refs_3_, ...), custom_call_target="tpu_custom_call" | custom-call | flops 570425344 | bytes 1835008 | tf_op jit(solution)/shard_map/pallas_call | solution.py:527
  78.2 0.2 all-to-all-done.1
  78.4 0.0 collective-permute-done.11.refs_4_
  78.4 0.0 collective-permute-done.9.refs_3_.refs_1_
  78.4 2.7 %shard_map.167 = (bf16[16,1792]{1,0:T(8,128)(2,1)}, bf16[16,1792]{1,0:T(8,128)(2,1)}, bf16[16,1792]{1,0:T(8,128)(2,1)}, bf16[16,1792]{1,0:T(8,128)(2,1)}) custom-call(bf16[64,512]{1,0:T(8,128)(2,1)S(1)} %bitcast.20, s32[1,32]{1,0:T(1,128)} %bitcast.37, bf16[448,1792]{1,0:T(8,128)(2,1)} %refs_2_.5, ...), custom_call_target="tpu_custom_call" | custom-call | flops 58720256 | bytes 1835008 | tf_op jit(solution)/shard_map/pallas_call | solution.py:527
  81.1 0.0 copy-start.1
  81.1 1.1 %collective-permute-start.13 = (bf16[16,1792]{1,0:T(8,128)(2,1)}, bf16[16,1792]{1,0:T(8,128)(2,1)S(1)}, u32[]{:S(2)}, u32[]{:S(2)}) collective-permute-start(bf16[16,1792]{1,0:T(8,128)(2,1)} %get-tuple-element.71), channel_id=1, source_target_pairs={{0,8},{8,0},{16,24},{24,16},{1,9},{9,1},{17,25},{25,17},{2,10},{10... | collective-permute-start | bytes 172040 | tf_op jit(solution)/shard_map/ppermute | solution.py:550
  82.1 1.1 %collective-permute-start.14 = (bf16[16,1792]{1,0:T(8,128)(2,1)}, bf16[16,1792]{1,0:T(8,128)(2,1)S(1)}, u32[]{:S(2)}, u32[]{:S(2)}) collective-permute-start(bf16[16,1792]{1,0:T(8,128)(2,1)} %get-tuple-element.72), channel_id=1, source_target_pairs={{0,16},{8,24},{16,0},{24,8},{1,17},{9,25},{17,1},{25,9},{2,18},{10... | collective-permute-start | bytes 172040 | tf_op jit(solution)/shard_map/ppermute | solution.py:550
  83.2 1.4 %collective-permute-start.15 = (bf16[16,1792]{1,0:T(8,128)(2,1)}, bf16[16,1792]{1,0:T(8,128)(2,1)S(1)}, u32[]{:S(2)}, u32[]{:S(2)}) collective-permute-start(bf16[16,1792]{1,0:T(8,128)(2,1)} %get-tuple-element.73), channel_id=1, source_target_pairs={{0,24},{8,16},{16,8},{24,0},{1,25},{9,17},{17,9},{25,1},{2,26},{10... | collective-permute-start | bytes 172040 | tf_op jit(solution)/shard_map/ppermute | solution.py:550
  84.6 0.0 collective-permute-done.10.refs_2_
  84.6 0.0 collective-permute-done.12.refs_5_
  84.6 2.7 %shard_map.168 = bf16[2,128,1792]{2,1,0:T(8,128)(2,1)} custom-call(bf16[128,1792]{1,0:T(8,128)(2,1)} %get-tuple-element.64.refs_5_.refs_0_, bf16[128,1792]{1,0:T(8,128)(2,1)S(1)} %collective-permute-done.9.refs_3_.refs_1_, bf16[128,1792]{1,0:T(8,128)(2,1)S(1)} %collective-permute-done.10.refs_2_, bf16[128,1792]{1,0:T(8,128)(2,1)} %get-tuple-element.66.refs_3_, ...), custom_call_target="tpu_custom_call" | custom-call | bytes 3670016 | tf_op jit(solution)/shard_map/pallas_call | solution.py:527
  87.3 0.0 collective-permute-done.13
  87.3 0.0 collective-permute-done.14
  87.4 1.1 %collective-permute-done.15 = bf16[16,1792]{1,0:T(8,128)(2,1)S(1)} collective-permute-done((bf16[16,1792]{1,0:T(8,128)(2,1)}, bf16[16,1792]{1,0:T(8,128)(2,1)S(1)}, u32[]{:S(2)}, u32[]{:S(2)}) %collective-permute-start.15) | collective-permute-done | bytes 57376 | tf_op jit(solution)/shard_map/ppermute | solution.py:550
  88.5 0.0 copy-done.1
  88.5 0.6 fusion
Async XLA Ops:
  3.8 9.9 %collective-permute-start = (bf16[16,1792]{1,0:T(8,128)(2,1)}, bf16[16,1792]{1,0:T(8,128)(2,1)S(1)}, u32[]{:S(2)}, u32[]{:S(2)}) collective-permute-start(bf16[16,1792]{1,0:T(8,128)(2,1)} %get-tuple-element.44), channel_id=1, source_target_pairs={{0,8},{8,16},{16,24},{1,9},{9,17},{17,25},{2,10},{10,18},{18,26},{... | collective-permute-start | bytes 172040 | tf_op jit(solution)/shard_map/ppermute | solution.py:719
  8.6 23.7 %collective-permute-start.3 = (bf16[128,1792]{1,0:T(8,128)(2,1)}, bf16[128,1792]{1,0:T(8,128)(2,1)S(1)}, u32[]{:S(2)}, u32[]{:S(2)}) collective-permute-start(bf16[128,1792]{1,0:T(8,128)(2,1)} %get-tuple-element.41.refs_1_), channel_id=1, source_target_pairs={{0,8},{8,0},{16,24},{24,16},{1,9},{9,1},{17,25},{25,17},{2,10},{10... | collective-permute-start | bytes 1376264 | tf_op jit(solution)/shard_map/ppermute | solution.py:550
  10.2 22.2 %collective-permute-start.1 = (bf16[128,1792]{1,0:T(8,128)(2,1)}, bf16[128,1792]{1,0:T(8,128)(2,1)S(1)}, u32[]{:S(2)}, u32[]{:S(2)}) collective-permute-start(bf16[128,1792]{1,0:T(8,128)(2,1)} %get-tuple-element.41.refs_1_), channel_id=1, source_target_pairs={{0,16},{8,24},{16,0},{24,8},{1,17},{9,25},{17,1},{25,9},{2,18},{10... | collective-permute-start | bytes 1376264 | tf_op jit(solution)/shard_map/ppermute | solution.py:550
  14.7 17.7 %collective-permute-start.2 = (bf16[128,1792]{1,0:T(8,128)(2,1)}, bf16[128,1792]{1,0:T(8,128)(2,1)S(1)}, u32[]{:S(2)}, u32[]{:S(2)}) collective-permute-start(bf16[128,1792]{1,0:T(8,128)(2,1)} %shard_map.159.refs_2_), channel_id=1, source_target_pairs={{0,8},{8,0},{16,24},{24,16},{1,9},{9,1},{17,25},{25,17},{2,10},{10... | collective-permute-start | bytes 1376264 | tf_op jit(solution)/shard_map/ppermute | solution.py:550
  17.3 17.4 %collective-permute-start.4 = (bf16[128,1792]{1,0:T(8,128)(2,1)}, bf16[128,1792]{1,0:T(8,128)(2,1)S(1)}, u32[]{:S(2)}, u32[]{:S(2)}) collective-permute-start(bf16[128,1792]{1,0:T(8,128)(2,1)} %shard_map.159.refs_2_), channel_id=1, source_target_pairs={{0,16},{8,24},{16,0},{24,8},{1,17},{9,25},{17,1},{25,9},{2,18},{10... | collective-permute-start | bytes 1376264 | tf_op jit(solution)/shard_map/ppermute | solution.py:550
  17.8 11.0 %all-to-all-start = ((bf16[8,8,640]{2,1,0:T(8,128)(2,1)}), bf16[8,8,640]{2,1,0:T(8,128)(2,1)S(1)}, u32[]{:S(2)}, u32[]{:S(2)}) async-start(bf16[8,8,640]{2,1,0:T(8,128)(2,1)} %bitcast.32), calls=%async_computation | async-start | bytes 163840 | tf_op jit(solution)/shard_map/all_to_all | solution.py:612
  32.4 12.6 %collective-permute-start.6 = (bf16[128,1792]{1,0:T(8,128)(2,1)S(1)}, bf16[128,1792]{1,0:T(8,128)(2,1)S(1)}, u32[]{:S(2)}, u32[]{:S(2)}) collective-permute-start(bf16[128,1792]{1,0:T(8,128)(2,1)S(1)} %collective-permute-done.2.refs_3_), channel_id=1, source_target_pairs={{0,16},{8,24},{16,0},{24,8},{1,17},{9,25},{17,1},{25,9},{2,18},{10... | collective-permute-start | bytes 1376264 | tf_op jit(solution)/shard_map/ppermute | solution.py:550
  34.0 12.3 %collective-permute-start.5 = (bf16[128,1792]{1,0:T(8,128)(2,1)S(1)}, bf16[128,1792]{1,0:T(8,128)(2,1)S(1)}, u32[]{:S(2)}, u32[]{:S(2)}) collective-permute-start(bf16[128,1792]{1,0:T(8,128)(2,1)S(1)} %collective-permute-done.1.refs_5_), channel_id=1, source_target_pairs={{0,8},{8,0},{16,24},{24,16},{1,9},{9,1},{17,25},{25,17},{2,10},{10... | collective-permute-start | bytes 1376264 | tf_op jit(solution)/shard_map/ppermute | solution.py:550
  52.1 12.3 %collective-permute-start.8 = (bf16[128,1792]{1,0:T(8,128)(2,1)S(1)}, bf16[128,1792]{1,0:T(8,128)(2,1)S(1)}, u32[]{:S(2)}, u32[]{:S(2)}) collective-permute-start(bf16[128,1792]{1,0:T(8,128)(2,1)S(1)} %get-tuple-element.61), channel_id=1, source_target_pairs={{0,16},{8,24},{16,0},{24,8},{1,17},{9,25},{17,1},{25,9},{2,18},{10... | collective-permute-start | bytes 1376264 | tf_op jit(solution)/shard_map/ppermute | solution.py:550
  52.7 11.7 %collective-permute-start.7 = (bf16[128,1792]{1,0:T(8,128)(2,1)S(1)}, bf16[128,1792]{1,0:T(8,128)(2,1)S(1)}, u32[]{:S(2)}, u32[]{:S(2)}) collective-permute-start(bf16[128,1792]{1,0:T(8,128)(2,1)S(1)} %get-tuple-element.59), channel_id=1, source_target_pairs={{0,8},{8,0},{16,24},{24,16},{1,9},{9,1},{17,25},{25,17},{2,10},{10... | collective-permute-start | bytes 1376264 | tf_op jit(solution)/shard_map/ppermute | solution.py:550
  62.2 16.1 %collective-permute-start.11 = (bf16[128,1792]{1,0:T(8,128)(2,1)}, bf16[128,1792]{1,0:T(8,128)(2,1)S(1)}, u32[]{:S(2)}, u32[]{:S(2)}) collective-permute-start(bf16[128,1792]{1,0:T(8,128)(2,1)} %get-tuple-element.67), channel_id=1, source_target_pairs={{0,16},{8,24},{16,0},{24,8},{1,17},{9,25},{17,1},{25,9},{2,18},{10... | collective-permute-start | bytes 1376264 | tf_op jit(solution)/shard_map/ppermute | solution.py:550
  62.7 15.7 %collective-permute-start.9 = (bf16[128,1792]{1,0:T(8,128)(2,1)}, bf16[128,1792]{1,0:T(8,128)(2,1)S(1)}, u32[]{:S(2)}, u32[]{:S(2)}) collective-permute-start(bf16[128,1792]{1,0:T(8,128)(2,1)} %get-tuple-element.62.refs_4_), channel_id=1, source_target_pairs={{0,8},{8,0},{16,24},{24,16},{1,9},{9,1},{17,25},{25,17},{2,10},{10... | collective-permute-start | bytes 1376264 | tf_op jit(solution)/shard_map/ppermute | solution.py:550
  65.6 6.8 %copy-start = (bf16[128,1792]{1,0:T(8,128)(2,1)}, bf16[128,1792]{1,0:T(8,128)(2,1)S(1)}, u32[]{:S(2)}) copy-start(bf16[128,1792]{1,0:T(8,128)(2,1)S(1)} %get-tuple-element.63.refs_11_) | copy-start | bytes 1376260
  65.7 19.0 %collective-permute-start.10 = (bf16[128,1792]{1,0:T(8,128)(2,1)S(1)}, bf16[128,1792]{1,0:T(8,128)(2,1)S(1)}, u32[]{:S(2)}, u32[]{:S(2)}) collective-permute-start(bf16[128,1792]{1,0:T(8,128)(2,1)S(1)} %get-tuple-element.65), channel_id=1, source_target_pairs={{0,16},{8,24},{16,0},{24,8},{1,17},{9,25},{17,1},{25,9},{2,18},{10... | collective-permute-start | bytes 1376264 | tf_op jit(solution)/shard_map/ppermute | solution.py:550
  66.7 18.0 %collective-permute-start.12 = (bf16[128,1792]{1,0:T(8,128)(2,1)S(1)}, bf16[128,1792]{1,0:T(8,128)(2,1)S(1)}, u32[]{:S(2)}, u32[]{:S(2)}) collective-permute-start(bf16[128,1792]{1,0:T(8,128)(2,1)S(1)} %get-tuple-element.63.refs_11_), channel_id=1, source_target_pairs={{0,8},{8,0},{16,24},{24,16},{1,9},{9,1},{17,25},{25,17},{2,10},{10... | collective-permute-start | bytes 1376264 | tf_op jit(solution)/shard_map/ppermute | solution.py:550
  67.7 10.7 %all-to-all-start.1 = ((bf16[8,8,512]{2,1,0:T(8,128)(2,1)}), bf16[8,8,512]{2,1,0:T(8,128)(2,1)S(1)}, u32[]{:S(2)}, u32[]{:S(2)}) async-start(bf16[8,8,512]{2,1,0:T(8,128)(2,1)} %bitcast.11), calls=%async_computation.1 | async-start | bytes 131072 | tf_op jit(solution)/shard_map/all_to_all | solution.py:666
  81.1 7.4 %copy-start.1 = (bf16[16,1792]{1,0:T(8,128)(2,1)S(1)}, bf16[16,1792]{1,0:T(8,128)(2,1)}, u32[]{:S(2)}) copy-start(bf16[16,1792]{1,0:T(8,128)(2,1)} %get-tuple-element.74.refs_6_) | copy-start | bytes 172036
  81.1 6.3 %collective-permute-start.13 = (bf16[16,1792]{1,0:T(8,128)(2,1)}, bf16[16,1792]{1,0:T(8,128)(2,1)S(1)}, u32[]{:S(2)}, u32[]{:S(2)}) collective-permute-start(bf16[16,1792]{1,0:T(8,128)(2,1)} %get-tuple-element.71), channel_id=1, source_target_pairs={{0,8},{8,0},{16,24},{24,16},{1,9},{9,1},{17,25},{25,17},{2,10},{10... | collective-permute-start | bytes 172040 | tf_op jit(solution)/shard_map/ppermute | solution.py:550
  82.1 5.2 %collective-permute-start.14 = (bf16[16,1792]{1,0:T(8,128)(2,1)}, bf16[16,1792]{1,0:T(8,128)(2,1)S(1)}, u32[]{:S(2)}, u32[]{:S(2)}) collective-permute-start(bf16[16,1792]{1,0:T(8,128)(2,1)} %get-tuple-element.72), channel_id=1, source_target_pairs={{0,16},{8,24},{16,0},{24,8},{1,17},{9,25},{17,1},{25,9},{2,18},{10... | collective-permute-start | bytes 172040 | tf_op jit(solution)/shard_map/ppermute | solution.py:550
  83.2 5.3 %collective-permute-start.15 = (bf16[16,1792]{1,0:T(8,128)(2,1)}, bf16[16,1792]{1,0:T(8,128)(2,1)S(1)}, u32[]{:S(2)}, u32[]{:S(2)}) collective-permute-start(bf16[16,1792]{1,0:T(8,128)(2,1)} %get-tuple-element.73), channel_id=1, source_target_pairs={{0,24},{8,16},{16,8},{24,0},{1,25},{9,17},{17,9},{25,1},{2,26},{10... | collective-permute-start | bytes 172040 | tf_op jit(solution)/shard_map/ppermute | solution.py:550

commit v7 on v6

--- a/solution.py
+++ b/solution.py
@@ -192,8 +192,8 @@
 
 
 def second_kernel(
-    heads, len_ref, low1, top1, w_ref, low2, top2, cache, sums0, items, half_total, gain_ref, cache_ref,
-    sums1, qkv1, sums2, qkv2, state3, served, state, sem
+    heads, len_ref, low1, top1, w_ref, low2, top2, cache, sums0, items, half_total, gain_ref, out_w_ref, cache_ref,
+    sums1, qkv1, sums2, qkv2, state3, served, old, state, sem
 ):
     start = 2 * sem.shape[0]
     copies = slot_copies(heads, start, start, cache_ref, state, sem)
@@ -209,9 +209,11 @@
             sums[head] = sums_of(slot, heads, head, len_ref[0], found, pick)
         sums.push()
     for head in range(heads):
-        state3[head] = state_before(3, old_state(cache, head), (sums0[head], sums1[head], sums2[head]))
+        old[head] = old_state(cache, head)
+        state3[head] = state_before(3, old[head], (sums0[head], sums1[head], sums2[head]))
+    old.push()
     state3.push()
-    serve_part(heads, start, items, half_total, gain_ref, copies, state, served)
+    serve_part(heads, start, items, half_total, gain_ref, out_w_ref, copies, state, served)
 
 
 def state_before(slot, old, sums):
@@ -237,7 +239,7 @@
 
 
 def fourth_kernel(
-    heads, len_ref, qkv3, qkv1, cache, sums0, sums1, sums2, qkv2, gain_ref, out_w_ref, top1, low1, top2, low2, sums3
+    heads, len_ref, qkv3, qkv1, old, sums0, sums1, sums2, qkv2, gain_ref, out_w_ref, top1, low1, top2, low2, sums3
 ):
     pick = spreader()
     length = len_ref[0]
@@ -249,18 +251,18 @@
         for head in range(heads):
             q = parts_of(qkv, heads, head)[0]
             own = own_of(slot, heads, head, length, qkv)
-            state = state_before(slot, old_state(cache, head), (sums0[head], sums1[head], sums2[head], sums3[head]))
+            state = state_before(slot, old[head], (sums0[head], sums1[head], sums2[head], sums3[head]))
             parts.append(attend_part(slot, head, heads, length, q, own, state, gain_ref, pick))
         project_part(parts, heads, out_w_ref, top, low)
 
 
 def fifth_kernel(
-    heads, len_ref, cache, sums0, sums1, sums2, sums3, queries, own, gain_ref, out_w_ref, top0, low0, state_next
+    heads, len_ref, olds, sums0, sums1, sums2, sums3, queries, own, gain_ref, out_w_ref, top0, low0, state_next
 ):
     pick = spreader()
     parts = []
     for head in range(heads):
-        old = old_state(cache, head)
+        old = olds[head]
         sums = [part[head] for part in (sums0, sums1, sums2, sums3)]
         q = queries[:, head * F : (head + 1) * F]
         state = state_before(0, old, sums)
@@ -277,10 +279,10 @@
     two_x[...] = (low1[...].astype(F32) + via_y[...].astype(F32)).astype(BF)
 
 
-def total_kernel(top0, one_x, two_y, low0, one_y, two_x, out):
-    out[0] = (top0[...].astype(F32) + one_x[...].astype(F32) + two_y[...].astype(F32)).astype(BF)
+def total_kernel(top0, two_y, low0, two_x, out):
+    out[0] = (top0[...].astype(F32) + two_y[...].astype(F32)).astype(BF)
     out.push(0)
-    out[1] = (low0[...].astype(F32) + one_y[...].astype(F32) + two_x[...].astype(F32)).astype(BF)
+    out[1] = (low0[...].astype(F32) + two_x[...].astype(F32)).astype(BF)
     out.push(1)
 
 
@@ -372,7 +374,8 @@
     total[...] = slot_totals(heads, 0, phis, slots, copies, state, jnp.zeros(total.shape, F32))
 
 
-def serve_part(heads, start, items, half_total, gain_ref, copies, state, out):
+def serve_part(heads, start, items, half_total, gain_ref, w_ref, copies, state, out):
+    attended = []
     count = items.shape[0]
     phis, slots = slot_features(heads, items)
     total = slot_totals(heads, start, phis, slots, copies, state, half_total[...])
@@ -386,23 +389,27 @@
         value = total[head * count : (head + 1) * count, :DH] + (1.0 + inner + 0.5 * inner * inner) * v
         square = jnp.sum(value * value, axis=-1, keepdims=True)
         value = value * lax.rsqrt(square * (1.0 / DH) + 1e-05) * gains[:, head * DH : (head + 1) * DH]
-        out[:, head * WIDE : head * WIDE + DH] = value.astype(BF)
-        out[:, head * WIDE + DH : (head + 1) * WIDE] = jnp.zeros((count, WIDE - DH), BF)
-
-
-def return_kernel(heads, capacity, items_ref, owner_ref, w_ref, seen_x, seen_y, *outs):
+        attended += [value.astype(BF), jnp.zeros((count, WIDE - DH), BF)]
+    out[...] = dot(jnp.concatenate(attended, axis=1), out_projection(w_ref, heads)).astype(BF)
+
+
+def return_kernel(capacity, items_ref, owner_ref, top0, one_x, low0, one_y, *outs):
+    top, low = outs[4:]
     owners = owner_ref[...]
     target = column(owners) * capacity + placing_rank(owners, 1)
     placing = lax.broadcasted_iota(jnp.int32, (DEC, items_ref.shape[0]), 1) == target
-    attended = dot(ones_where(placing), items_ref[...]).astype(BF)
     row = lax.broadcasted_iota(jnp.int32, (4 * TILE, DEC), 0)
     entry = lax.broadcasted_iota(jnp.int32, (4 * TILE, DEC), 1)
     device = lax.axis_index("head") ^ (row // TILE)
     wanted = ((row % TILE) < DEC // 4) & (entry == device * (DEC // 4) + row % TILE)
-    attended = dot(ones_where(wanted), attended).astype(BF)
-    shares = dot(attended, out_projection(w_ref, heads)).astype(BF)
-    for slot, out in enumerate(outs):
+    wanted = dot(ones_where(wanted), ones_where(placing)).astype(BF)
+    shares = dot(wanted, items_ref[...]).astype(BF)
+    for slot, out in enumerate(outs[:4]):
         out[...] = shares[slot * TILE : (slot + 1) * TILE]
+        out.push()
+    top[...] = (top0[...].astype(F32) + one_x[...].astype(F32)).astype(BF)
+    top.push()
+    low[...] = (low0[...].astype(F32) + one_y[...].astype(F32)).astype(BF)
 
 
 def far_off(array):
@@ -638,17 +645,17 @@
     low_xy = across(low_y, 1)
     top_xy = across(top_x, 2)
     blocks = shape(rows, wide)
-    sums1, qkv1, sums2, qkv2, state3, served = hbm_call(
+    sums1, qkv1, sums2, qkv2, state3, served, old = hbm_call(
         functools.partial(second_kernel, heads),
-        [sums, blocks, sums, blocks, shape(heads, PHI_WIDE, WIDE), shape(count, heads * WIDE)],
+        [sums, blocks, sums, blocks, shape(heads, PHI_WIDE, WIDE), shape(count, D), sums],
         2 * block_flops + serve_flops,
         2 * slots * heads * WIDE * PHI,
         scalars=[length, slot],
         picked=5,
         loose=(0, 1, 3, 4, 7),
-        raw=(10,),
+        raw=(11,),
         scratch=states,
-    )(low_x, top_x, w_in, low_y, top_y, cache, sums0, items, half_total, out_gain, flat)
+    )(low_x, top_x, w_in, low_y, top_y, cache, sums0, items, half_total, out_gain, out_weight, flat)
     top3, low3, qkv3 = hbm_call(
         functools.partial(third_kernel, heads),
         [piece, piece, blocks],
@@ -663,17 +670,15 @@
     via_x = across(top3, 1)
     via_y = across(low3, 2)
     served = lax.optimization_barrier((served, top3))[0]
-    returned = lax.all_to_all(
-        served.reshape(groups, capacity, heads * WIDE), "tok", split_axis=0, concat_axis=0, tiled=True
-    ).reshape(count, heads * WIDE)
+    returned = lax.all_to_all(served.reshape(groups, capacity, D), "tok", split_axis=0, concat_axis=0, tiled=True)
+    returned = returned.reshape(count, D)
     top1, low1, top2, low2, sums3 = hbm_call(
         functools.partial(fourth_kernel, heads),
         [piece] * 4 + [sums],
         2 * attend_flops,
         size,
-        scalars=[length, slot],
-        picked=2,
-    )(qkv3, qkv1, cache, sums0, sums1, sums2, qkv2, out_gain, out_weight)
+        scalars=[length],
+    )(qkv3, qkv1, old, sums0, sums1, sums2, qkv2, out_gain, out_weight)
     one_x = across(top1, 1)
     one_y = across(low2, 2)
     two_y, two_x = hbm_call(add_kernel, [piece, piece], 0, size, here=(1, 3), near=(0, 1), waits=[top1])(top2, via_x, low1, via_y)
@@ -682,19 +687,16 @@
         [piece] * 2 + [shape(1, PHI, heads, DH, dtype=F32)],
         attend_flops,
         size,
-        scalars=[length, slot],
-        picked=0,
+        scalars=[length],
         waits=[two_x],
-    )(cache, sums0, sums1, sums2, sums3, queries0, own0, out_gain, out_weight)
-    decoded = hbm_call(
-        functools.partial(return_kernel, heads, capacity),
-        [shape(TILE, D)] * 4,
-        2 * DEC * heads * WIDE * D,
-        2 * heads * WIDE * D,
-        loose=(0, 3, 4),
-        waits=[top0],
-        raw=(3, 4),
-    )(returned, owner_row, out_weight, one_x, one_y)
+    )(old, sums0, sums1, sums2, sums3, queries0, own0, out_gain, out_weight)
+    *decoded, top0, low0 = hbm_call(
+        functools.partial(return_kernel, capacity),
+        [shape(TILE, D)] * 4 + [piece] * 2,
+        2 * DEC * count * D,
+        4 * count * D,
+        loose=(0, 3, 5),
+    )(returned, owner_row, top0, one_x, low0, one_y)
     shares = [decoded[0]] + [across(decoded[by], by) for by in (1, 2, 3)]
     two_y = across(two_y, 2)
     two_x = across(two_x, 1)
@@ -704,10 +706,10 @@
         [shape(2, half, D)],
         0,
         8 * rows * D,
-        loose=(1, 2, 4, 5),
+        loose=(1, 3),
         split_out=(0,),
         waits=[decoded[0]],
-    )(top0, one_x, two_y, low0, one_y, two_x)
+    )(top0, two_y, low0, two_x)
     shares = lax.optimization_barrier((*shares, stretch_out))[:4]
     decode_out = sum(share[: DEC // 4].astype(F32) for share in shares).astype(BF)
     return (stretch_out.reshape(1, rows, D), decode_out[None], state_next)

time: 89.7 us -> 88.8 us (0.990)
  transfers between devices with their start and end apart: 18 -> 18, of which waited for: 5 -> 6; matrix products, arithmetic and copies ran while one was open for 0% -> 0% of each run, Pallas kernels for 48% -> 48%
where the time goes in v7:
time: 88.8 us; the launch traced here: 88.2 us
  Pallas kernels  51.3 us (58%)
  starting transfers between devices  30.7 us (35%)
  waiting for transfers between devices  3.45 us (4%)
  between operations  2.13 us (2%)
    pallas_call x11, Pallas kernels, run(): pl.pallas_call(body, out_shape=[o if n in near else pltpu.HBM(o.shape, o....  50.3 us
    ppermute x15, starting transfers between devices, across(): return lax.ppermute(array, 'head', [(i, i ^ by) for i in range(4)])  16.3 us
    all_to_all x1, starting transfers between devices, local_square(): lax.all_to_all(sent.reshape(groups, capacity, wide), 'tok', split_axis=0,...  4.88 us
    ppermute x1, starting transfers between devices, from_behind(): return lax.ppermute(array, axis, pairs)  4.84 us
    all_to_all x1, starting transfers between devices, local_square(): lax.all_to_all(served.reshape(groups, capacity, D), 'tok', split_axis=0,...  4.72 us
    ppermute x15, waiting for transfers between devices, across(): return lax.ppermute(array, 'head', [(i, i ^ by) for i in range(4)])  2.95 us
  transfers between devices with their start and end apart: 18, of which 6 were waited for; matrix products, arithmetic and copies ran while one was open for 0% of the time, Pallas kernels for 48%

profile of v7, /device:TPU:0, one launch (start us, length us, event | category | flops | bytes accessed | tf_op | source)
XLA Modules:
  0.0 88.2 jit_solution(16774970884740500178)
XLA Ops:
  0.6 3.1 %shard_map.157 = (bf16[128,1792]{1,0:T(8,128)(2,1)}, bf16[128,1792]{1,0:T(8,128)(2,1)}, bf16[16,1792]{1,0:T(8,128)(2,1)}, bf16[16,1792]{1,0:T(8,128)(2,1)}) custom-call(bf16[256,1792]{1,0:T(8,128)(2,1)} %bitcast.28, bf16[2,1792]{1,0:T(2,128)(2,1)} %bitcast.33, f32[1792]{0:T(1024)} %refs_2_.3, f32[3,1792]{1,0:T(4,128)} %taps_ref.1), custom_call_target="tpu_custom_call" | custom-call | flops 9175040 | bytes 1835008 | tf_op jit(solution)/shard_map/pallas_call | solution.py:534
  3.8 4.8 %collective-permute-start.1 = (bf16[16,1792]{1,0:T(8,128)(2,1)}, bf16[16,1792]{1,0:T(8,128)(2,1)S(1)}, u32[]{:S(2)}, u32[]{:S(2)}) collective-permute-start(bf16[16,1792]{1,0:T(8,128)(2,1)} %get-tuple-element.47), channel_id=1, source_target_pairs={{0,8},{8,16},{16,24},{1,9},{9,17},{17,25},{2,10},{10,18},{18,26},{... | collective-permute-start | bytes 172040 | tf_op jit(solution)/shard_map/ppermute | solution.py:721
  8.6 1.6 %collective-permute-start.3 = (bf16[128,1792]{1,0:T(8,128)(2,1)}, bf16[128,1792]{1,0:T(8,128)(2,1)S(1)}, u32[]{:S(2)}, u32[]{:S(2)}) collective-permute-start(bf16[128,1792]{1,0:T(8,128)(2,1)} %get-tuple-element.44.refs_1_), channel_id=1, source_target_pairs={{0,8},{8,0},{16,24},{24,16},{1,9},{9,1},{17,25},{25,17},{2,10},{10... | collective-permute-start | bytes 1376264 | tf_op jit(solution)/shard_map/ppermute | solution.py:557
  10.2 0.1 collective-permute-start
  10.3 3.4 %shard_map.158.wait_ref = bf16[64,640]{1,0:T(8,128)(2,1)} custom-call(bf16[32,1792]{1,0:T(8,128)(2,1)} %bitcast.32, bf16[32,2,1792]{2,1,0:T(2,128)(2,1)} %bitcast.31, f32[1792]{0:T(1024)} %refs_2_.3, f32[3,1792]{1,0:T(4,128)} %taps_ref.1, s32[1,32]{1,0:T(1,128)} %bitcast.34, s32[1,32]{1,0:T(1,128)} %refs_5_.2, bf16[4,144,1792]{2,1,0:T(8,128)(2,1)} %bitcast.24), custom_call_target="tpu_custom_call" | custom-call | flops 73400320 | bytes 2293760 | tf_op jit(solution)/shard_map/pallas_call | solution.py:534
  13.7 0.0 collective-permute-done.1.end_ref
  13.7 0.9 %shard_map.159.refs_2_ = bf16[128,1792]{1,0:T(8,128)(2,1)} custom-call(s32[1]{0:T(128)} %bitcast.2.first_ref, bf16[128,1792]{1,0:T(8,128)(2,1)} %get-tuple-element.45.top_ref, bf16[16,1792]{1,0:T(8,128)(2,1)} %get-tuple-element.46.begin_ref, bf16[16,1792]{1,0:T(8,128)(2,1)S(1)} %collective-permute-done.1.end_ref, ...), custom_call_target="tpu_custom_call", output_to_operand_aliasing={{}: (1, {})} | custom-call | flops 28672 | bytes 229376 | tf_op jit(solution)/shard_map/pallas_call | solution.py:604
  14.7 2.6 %collective-permute-start.2 = (bf16[128,1792]{1,0:T(8,128)(2,1)}, bf16[128,1792]{1,0:T(8,128)(2,1)S(1)}, u32[]{:S(2)}, u32[]{:S(2)}) collective-permute-start(bf16[128,1792]{1,0:T(8,128)(2,1)} %shard_map.159.refs_2_), channel_id=1, source_target_pairs={{0,8},{8,0},{16,24},{24,16},{1,9},{9,1},{17,25},{25,17},{2,10},{10... | collective-permute-start | bytes 1376264 | tf_op jit(solution)/shard_map/ppermute | solution.py:557
  17.3 0.5 collective-permute-start.4
  17.8 4.9 %all-to-all-start = ((bf16[8,8,640]{2,1,0:T(8,128)(2,1)}), bf16[8,8,640]{2,1,0:T(8,128)(2,1)S(1)}, u32[]{:S(2)}, u32[]{:S(2)}) async-start(bf16[8,8,640]{2,1,0:T(8,128)(2,1)} %bitcast.30), calls=%async_computation | async-start | bytes 163840 | tf_op jit(solution)/shard_map/all_to_all | solution.py:619
  23.3 5.0 %shard_map.160 = (f32[4,384,128]{2,1,0:T(8,128)}, f32[4,256,128]{2,1,0:T(8,128)}, bf16[256,64]{1,0:T(8,128)(2,1)}) custom-call(s32[1]{0:T(128)S(6)} %copy.19.refs_0_, bf16[128,1792]{1,0:T(8,128)(2,1)} %get-tuple-element.44.refs_1_, bf16[128,1792]{1,0:T(8,128)(2,1)} %shard_map.159.refs_2_, bf16[4,144,1792]{2,1,0:T(8,128)(2,1)} %bitcast.25), custom_call_target="tpu_custom_call" | custom-call | flops 788529152 | bytes 1835008 | tf_op jit(solution)/shard_map/pallas_call | solution.py:534
  28.4 0.4 all-to-all-done
  28.8 3.5 %shard_map.161.refs_10_ = f32[256,128]{1,0:T(8,128)} custom-call(bf16[64,640]{1,0:T(8,128)(2,1)S(1)} %bitcast.19, f32[17472,112]{1,0:T(8,128)} %bitcast.21, bf16[256,64]{1,0:T(8,128)(2,1)} %get-tuple-element.48.refs_2_.refs_6_), custom_call_target="tpu_custom_call" | custom-call | flops 500957184 | bytes 4472832 | tf_op jit(solution)/shard_map/pallas_call | solution.py:534
  32.3 0.0 collective-permute-done.3.refs_2_
  32.4 0.0 collective-permute-done.refs_5_
  32.4 0.0 collective-permute-done.2.refs_3_
  32.4 1.6 %collective-permute-start.6 = (bf16[128,1792]{1,0:T(8,128)(2,1)S(1)}, bf16[128,1792]{1,0:T(8,128)(2,1)S(1)}, u32[]{:S(2)}, u32[]{:S(2)}) collective-permute-start(bf16[128,1792]{1,0:T(8,128)(2,1)S(1)} %collective-permute-done.2.refs_3_), channel_id=1, source_target_pairs={{0,16},{8,24},{16,0},{24,8},{1,17},{9,25},{17,1},{25,9},{2,18},{10... | collective-permute-start | bytes 1376264 | tf_op jit(solution)/shard_map/ppermute | solution.py:557
  34.0 0.1 collective-permute-start.5
  34.7 0.0 collective-permute-done.4.refs_6_
  34.7 10.1 %shard_map.162 = (f32[4,384,128]{2,1,0:T(8,128)}, bf16[256,640]{1,0:T(8,128)(2,1)}, f32[4,384,128]{2,1,0:T(8,128)}, bf16[256,640]{1,0:T(8,128)(2,1)}, bf16[4,384...) custom-call(s32[1]{0:T(128)S(6)} %copy.19.refs_0_, s32[1]{0:T(128)S(6)} %copy.20.refs_1_, ...), custom_call_target="tpu_custom_call" | custom-call | flops 2078015488 | bytes 4472832 | tf_op jit(solution)/shard_map/pallas_call | solution.py:534
  44.8 0.2 collective-permute-done.6.refs_2_
  45.0 1.2 %collective-permute-done.5.refs_1_ = bf16[128,1792]{1,0:T(8,128)(2,1)S(1)} collective-permute-done((bf16[128,1792]{1,0:T(8,128)(2,1)S(1)}, bf16[128,1792]{1,0:T(8,128)(2,1)S(1)}, u32[]{:S(2)}, u32[]{:S(2)}) %collective-permute-start.5) | collective-permute-done | bytes 458784 | tf_op jit(solution)/shard_map/ppermute | solution.py:557
  46.2 5.9 %shard_map.163 = (bf16[128,1792]{1,0:T(8,128)(2,1)S(1)}, bf16[128,1792]{1,0:T(8,128)(2,1)S(1)}, bf16[256,640]{1,0:T(8,128)(2,1)}) custom-call(s32[1]{0:T(128)S(6)} %copy.19.refs_0_, bf16[128,1792]{1,0:T(8,128)(2,1)S(1)} %collective-permute-done.5.refs_1_, bf16[128,1792]{1,0:T(8,128)(2,1)S(1)} %collective-permute-done.6.refs_2_, ...), custom_call_target="tpu_custom_call" | custom-call | flops 1358954496 | bytes 1835008 | tf_op jit(solution)/shard_map/pallas_call | solution.py:534
  52.1 0.6 collective-permute-start.8
  52.7 1.5 %collective-permute-start.7 = (bf16[128,1792]{1,0:T(8,128)(2,1)S(1)}, bf16[128,1792]{1,0:T(8,128)(2,1)S(1)}, u32[]{:S(2)}, u32[]{:S(2)}) collective-permute-start(bf16[128,1792]{1,0:T(8,128)(2,1)S(1)} %get-tuple-element.56), channel_id=1, source_target_pairs={{0,8},{8,0},{16,24},{24,16},{1,9},{9,1},{17,25},{25,17},{2,10},{10... | collective-permute-start | bytes 1376264 | tf_op jit(solution)/shard_map/ppermute | solution.py:557
  54.2 7.5 %shard_map.164 = (bf16[128,1792]{1,0:T(8,128)(2,1)}, bf16[128,1792]{1,0:T(8,128)(2,1)}, bf16[128,1792]{1,0:T(8,128)(2,1)}, bf16[128,1792]{1,0:T(8,128)(2,1)}, f32[4,384,128]{2,1,0:T(8,128)}) custom-call(s32[1]{0:T(128)S(6)} %copy.19.refs_0_, bf16[256,640]{1,0:T(8,128)(2,1)} %get-tuple-element.61.refs_1_, bf16[256,640]{1,0:T(8,128)(2,1)} %get-tuple-element.62.refs_2_, ...), custom_call_target="tpu_custom_call" | custom-call | flops 1140850688 | bytes 1835008 | tf_op jit(solution)/shard_map/pallas_call | solution.py:534
  61.7 0.7 collective-permute-start.10
  62.3 1.5 %collective-permute-start.9 = (bf16[128,1792]{1,0:T(8,128)(2,1)}, bf16[128,1792]{1,0:T(8,128)(2,1)S(1)}, u32[]{:S(2)}, u32[]{:S(2)}) collective-permute-start(bf16[128,1792]{1,0:T(8,128)(2,1)} %get-tuple-element.68.refs_4_), channel_id=1, source_target_pairs={{0,8},{8,0},{16,24},{24,16},{1,9},{9,1},{17,25},{25,17},{2,10},{10... | collective-permute-start | bytes 1376264 | tf_op jit(solution)/shard_map/ppermute | solution.py:557
  63.8 4.7 %all-to-all-start.1 = ((bf16[8,8,1792]{2,1,0:T(8,128)(2,1)}), bf16[8,8,1792]{2,1,0:T(8,128)(2,1)S(1)}, u32[]{:S(2)}, u32[]{:S(2)}) async-start(bf16[8,8,1792]{2,1,0:T(8,128)(2,1)} %bitcast.11), calls=%async_computation.1 | async-start | bytes 458752 | tf_op jit(solution)/shard_map/all_to_all | solution.py:673
  68.5 0.0 collective-permute-done.8.refs_3_
  68.5 0.0 collective-permute-done.7.refs_1_
  68.5 1.3 %shard_map.165 = (bf16[128,1792]{1,0:T(8,128)(2,1)S(1)}, bf16[128,1792]{1,0:T(8,128)(2,1)S(1)}) custom-call(bf16[128,1792]{1,0:T(8,128)(2,1)} %get-tuple-element.65.refs_0_, bf16[128,1792]{1,0:T(8,128)(2,1)S(1)} %collective-permute-done.7.refs_1_, bf16[128,1792]{1,0:T(8,128)(2,1)} %get-tuple-element.66.refs_2_, ...), custom_call_target="tpu_custom_call" | custom-call | bytes 1835008 | tf_op jit(solution)/shard_map/pallas_call | solution.py:534
  69.8 0.0 copy-start
  69.8 0.6 collective-permute-start.11
  70.4 1.5 %collective-permute-start.12 = (bf16[128,1792]{1,0:T(8,128)(2,1)S(1)}, bf16[128,1792]{1,0:T(8,128)(2,1)S(1)}, u32[]{:S(2)}, u32[]{:S(2)}) collective-permute-start(bf16[128,1792]{1,0:T(8,128)(2,1)S(1)} %get-tuple-element.69.refs_10_), channel_id=1, source_target_pairs={{0,8},{8,0},{16,24},{24,16},{1,9},{9,1},{17,25},{25,17},{2,10},{10... | collective-permute-start | bytes 1376264 | tf_op jit(solution)/shard_map/ppermute | solution.py:557
  71.9 0.0 copy-done
  71.9 5.6 %shard_map.166 = (bf16[128,1792]{1,0:T(8,128)(2,1)}, bf16[128,1792]{1,0:T(8,128)(2,1)}, f32[1,273,4,112]{3,2,1,0:T(4,128)}) custom-call(s32[1]{0:T(128)S(6)} %copy.19.refs_0_, f32[4,384,128]{2,1,0:T(8,128)} %get-tuple-element.58.refs_3_.refs_1_, f32[4,384,128]{2,1,0:T(8,128)} %get-tuple-element.52.refs_8_.refs_4_.refs_2_, ...), custom_call_target="tpu_custom_call" | custom-call | flops 570425344 | bytes 1835008 | tf_op jit(solution)/shard_map/pallas_call | solution.py:534
  77.5 0.1 all-to-all-done.1
  77.5 0.0 collective-permute-done.10.refs_5_
  77.5 0.0 collective-permute-done.9.refs_3_
  77.5 2.6 %shard_map.167 = (bf16[16,1792]{1,0:T(8,128)(2,1)}, bf16[16,1792]{1,0:T(8,128)(2,1)}, bf16[16,1792]{1,0:T(8,128)(2,1)}, bf16[16,1792]{1,0:T(8,128)(2,1)}, bf16[1...) custom-call(bf16[64,1792]{1,0:T(8,128)(2,1)S(1)} %bitcast.18, s32[1,32]{1,0:T(1,128)} %bitcast.35, ...), custom_call_target="tpu_custom_call" | custom-call | flops 7340032 | bytes 458752 | tf_op jit(solution)/shard_map/pallas_call | solution.py:534
  80.2 0.0 copy-start.1
  80.2 0.6 collective-permute-start.13
  80.8 1.5 %collective-permute-start.14 = (bf16[16,1792]{1,0:T(8,128)(2,1)}, bf16[16,1792]{1,0:T(8,128)(2,1)S(1)}, u32[]{:S(2)}, u32[]{:S(2)}) collective-permute-start(bf16[16,1792]{1,0:T(8,128)(2,1)} %get-tuple-element.78), channel_id=1, source_target_pairs={{0,16},{8,24},{16,0},{24,8},{1,17},{9,25},{17,1},{25,9},{2,18},{10... | collective-permute-start | bytes 172040 | tf_op jit(solution)/shard_map/ppermute | solution.py:557
  82.3 1.5 %collective-permute-start.15 = (bf16[16,1792]{1,0:T(8,128)(2,1)}, bf16[16,1792]{1,0:T(8,128)(2,1)S(1)}, u32[]{:S(2)}, u32[]{:S(2)}) collective-permute-start(bf16[16,1792]{1,0:T(8,128)(2,1)} %get-tuple-element.79), channel_id=1, source_target_pairs={{0,24},{8,16},{16,8},{24,0},{1,25},{9,17},{17,9},{25,1},{2,26},{10... | collective-permute-start | bytes 172040 | tf_op jit(solution)/shard_map/ppermute | solution.py:557
  83.7 0.0 collective-permute-done.11.refs_1_
  83.7 1.2 %collective-permute-done.12.refs_3_ = bf16[128,1792]{1,0:T(8,128)(2,1)S(1)} collective-permute-done((bf16[128,1792]{1,0:T(8,128)(2,1)S(1)}, bf16[128,1792]{1,0:T(8,128)(2,1)S(1)}, u32[]{:S(2)}, u32[]{:S(2)}) %collective-permute-start.12) | collective-permute-done | bytes 458784 | tf_op jit(solution)/shard_map/ppermute | solution.py:557
  84.9 2.3 %shard_map.168 = bf16[2,128,1792]{2,1,0:T(8,128)(2,1)} custom-call(bf16[128,1792]{1,0:T(8,128)(2,1)} %get-tuple-element.73.refs_0_, bf16[128,1792]{1,0:T(8,128)(2,1)S(1)} %collective-permute-done.11.refs_1_, bf16[128,1792]{1,0:T(8,128)(2,1)} %get-tuple-element.75.refs_2_, bf16[128,1792]{1,0:T(8,128)(2,1)S(1)} %collective-permute-done.12.refs_3_, ...), custom_call_target="tpu_custom_call" | custom-call | bytes 3670016 | tf_op jit(solution)/shard_map/pallas_call | solution.py:534
  87.2 0.0 collective-permute-done.13
  87.2 0.0 collective-permute-done.14
  87.2 0.3 collective-permute-done.15
  87.6 0.0 copy-done.1
  87.6 0.6 fusion
Async XLA Ops:
  3.8 9.9 %collective-permute-start.1 = (bf16[16,1792]{1,0:T(8,128)(2,1)}, bf16[16,1792]{1,0:T(8,128)(2,1)S(1)}, u32[]{:S(2)}, u32[]{:S(2)}) collective-permute-start(bf16[16,1792]{1,0:T(8,128)(2,1)} %get-tuple-element.47), channel_id=1, source_target_pairs={{0,8},{8,16},{16,24},{1,9},{9,17},{17,25},{2,10},{10,18},{18,26},{... | collective-permute-start | bytes 172040 | tf_op jit(solution)/shard_map/ppermute | solution.py:721
  8.6 23.7 %collective-permute-start.3 = (bf16[128,1792]{1,0:T(8,128)(2,1)}, bf16[128,1792]{1,0:T(8,128)(2,1)S(1)}, u32[]{:S(2)}, u32[]{:S(2)}) collective-permute-start(bf16[128,1792]{1,0:T(8,128)(2,1)} %get-tuple-element.44.refs_1_), channel_id=1, source_target_pairs={{0,8},{8,0},{16,24},{24,16},{1,9},{9,1},{17,25},{25,17},{2,10},{10... | collective-permute-start | bytes 1376264 | tf_op jit(solution)/shard_map/ppermute | solution.py:557
  10.2 22.2 %collective-permute-start = (bf16[128,1792]{1,0:T(8,128)(2,1)}, bf16[128,1792]{1,0:T(8,128)(2,1)S(1)}, u32[]{:S(2)}, u32[]{:S(2)}) collective-permute-start(bf16[128,1792]{1,0:T(8,128)(2,1)} %get-tuple-element.44.refs_1_), channel_id=1, source_target_pairs={{0,16},{8,24},{16,0},{24,8},{1,17},{9,25},{17,1},{25,9},{2,18},{10... | collective-permute-start | bytes 1376264 | tf_op jit(solution)/shard_map/ppermute | solution.py:557
  14.7 17.7 %collective-permute-start.2 = (bf16[128,1792]{1,0:T(8,128)(2,1)}, bf16[128,1792]{1,0:T(8,128)(2,1)S(1)}, u32[]{:S(2)}, u32[]{:S(2)}) collective-permute-start(bf16[128,1792]{1,0:T(8,128)(2,1)} %shard_map.159.refs_2_), channel_id=1, source_target_pairs={{0,8},{8,0},{16,24},{24,16},{1,9},{9,1},{17,25},{25,17},{2,10},{10... | collective-permute-start | bytes 1376264 | tf_op jit(solution)/shard_map/ppermute | solution.py:557
  17.3 17.4 %collective-permute-start.4 = (bf16[128,1792]{1,0:T(8,128)(2,1)}, bf16[128,1792]{1,0:T(8,128)(2,1)S(1)}, u32[]{:S(2)}, u32[]{:S(2)}) collective-permute-start(bf16[128,1792]{1,0:T(8,128)(2,1)} %shard_map.159.refs_2_), channel_id=1, source_target_pairs={{0,16},{8,24},{16,0},{24,8},{1,17},{9,25},{17,1},{25,9},{2,18},{10... | collective-permute-start | bytes 1376264 | tf_op jit(solution)/shard_map/ppermute | solution.py:557
  17.8 11.0 %all-to-all-start = ((bf16[8,8,640]{2,1,0:T(8,128)(2,1)}), bf16[8,8,640]{2,1,0:T(8,128)(2,1)S(1)}, u32[]{:S(2)}, u32[]{:S(2)}) async-start(bf16[8,8,640]{2,1,0:T(8,128)(2,1)} %bitcast.30), calls=%async_computation | async-start | bytes 163840 | tf_op jit(solution)/shard_map/all_to_all | solution.py:619
  32.4 12.6 %collective-permute-start.6 = (bf16[128,1792]{1,0:T(8,128)(2,1)S(1)}, bf16[128,1792]{1,0:T(8,128)(2,1)S(1)}, u32[]{:S(2)}, u32[]{:S(2)}) collective-permute-start(bf16[128,1792]{1,0:T(8,128)(2,1)S(1)} %collective-permute-done.2.refs_3_), channel_id=1, source_target_pairs={{0,16},{8,24},{16,0},{24,8},{1,17},{9,25},{17,1},{25,9},{2,18},{10... | collective-permute-start | bytes 1376264 | tf_op jit(solution)/shard_map/ppermute | solution.py:557
  34.0 12.3 %collective-permute-start.5 = (bf16[128,1792]{1,0:T(8,128)(2,1)S(1)}, bf16[128,1792]{1,0:T(8,128)(2,1)S(1)}, u32[]{:S(2)}, u32[]{:S(2)}) collective-permute-start(bf16[128,1792]{1,0:T(8,128)(2,1)S(1)} %collective-permute-done.refs_5_), channel_id=1, source_target_pairs={{0,8},{8,0},{16,24},{24,16},{1,9},{9,1},{17,25},{25,17},{2,10},{10... | collective-permute-start | bytes 1376264 | tf_op jit(solution)/shard_map/ppermute | solution.py:557
  52.1 16.4 %collective-permute-start.8 = (bf16[128,1792]{1,0:T(8,128)(2,1)S(1)}, bf16[128,1792]{1,0:T(8,128)(2,1)S(1)}, u32[]{:S(2)}, u32[]{:S(2)}) collective-permute-start(bf16[128,1792]{1,0:T(8,128)(2,1)S(1)} %get-tuple-element.67), channel_id=1, source_target_pairs={{0,16},{8,24},{16,0},{24,8},{1,17},{9,25},{17,1},{25,9},{2,18},{10... | collective-permute-start | bytes 1376264 | tf_op jit(solution)/shard_map/ppermute | solution.py:557
  52.7 15.8 %collective-permute-start.7 = (bf16[128,1792]{1,0:T(8,128)(2,1)S(1)}, bf16[128,1792]{1,0:T(8,128)(2,1)S(1)}, u32[]{:S(2)}, u32[]{:S(2)}) collective-permute-start(bf16[128,1792]{1,0:T(8,128)(2,1)S(1)} %get-tuple-element.56), channel_id=1, source_target_pairs={{0,8},{8,0},{16,24},{24,16},{1,9},{9,1},{17,25},{25,17},{2,10},{10... | collective-permute-start | bytes 1376264 | tf_op jit(solution)/shard_map/ppermute | solution.py:557
  61.7 15.9 %collective-permute-start.10 = (bf16[128,1792]{1,0:T(8,128)(2,1)}, bf16[128,1792]{1,0:T(8,128)(2,1)S(1)}, u32[]{:S(2)}, u32[]{:S(2)}) collective-permute-start(bf16[128,1792]{1,0:T(8,128)(2,1)} %get-tuple-element.72), channel_id=1, source_target_pairs={{0,16},{8,24},{16,0},{24,8},{1,17},{9,25},{17,1},{25,9},{2,18},{10... | collective-permute-start | bytes 1376264 | tf_op jit(solution)/shard_map/ppermute | solution.py:557
  62.3 15.2 %collective-permute-start.9 = (bf16[128,1792]{1,0:T(8,128)(2,1)}, bf16[128,1792]{1,0:T(8,128)(2,1)S(1)}, u32[]{:S(2)}, u32[]{:S(2)}) collective-permute-start(bf16[128,1792]{1,0:T(8,128)(2,1)} %get-tuple-element.68.refs_4_), channel_id=1, source_target_pairs={{0,8},{8,0},{16,24},{24,16},{1,9},{9,1},{17,25},{25,17},{2,10},{10... | collective-permute-start | bytes 1376264 | tf_op jit(solution)/shard_map/ppermute | solution.py:557
  63.8 13.8 %all-to-all-start.1 = ((bf16[8,8,1792]{2,1,0:T(8,128)(2,1)}), bf16[8,8,1792]{2,1,0:T(8,128)(2,1)S(1)}, u32[]{:S(2)}, u32[]{:S(2)}) async-start(bf16[8,8,1792]{2,1,0:T(8,128)(2,1)} %bitcast.11), calls=%async_computation.1 | async-start | bytes 458752 | tf_op jit(solution)/shard_map/all_to_all | solution.py:673
  69.8 2.1 %copy-start = (bf16[128,1792]{1,0:T(8,128)(2,1)}, bf16[128,1792]{1,0:T(8,128)(2,1)S(1)}, u32[]{:S(2)}) copy-start(bf16[128,1792]{1,0:T(8,128)(2,1)S(1)} %get-tuple-element.69.refs_10_) | copy-start | bytes 1376260
  69.8 13.9 %collective-permute-start.11 = (bf16[128,1792]{1,0:T(8,128)(2,1)S(1)}, bf16[128,1792]{1,0:T(8,128)(2,1)S(1)}, u32[]{:S(2)}, u32[]{:S(2)}) collective-permute-start(bf16[128,1792]{1,0:T(8,128)(2,1)S(1)} %get-tuple-element.74), channel_id=1, source_target_pairs={{0,16},{8,24},{16,0},{24,8},{1,17},{9,25},{17,1},{25,9},{2,18},{10... | collective-permute-start | bytes 1376264 | tf_op jit(solution)/shard_map/ppermute | solution.py:557
  70.4 14.5 %collective-permute-start.12 = (bf16[128,1792]{1,0:T(8,128)(2,1)S(1)}, bf16[128,1792]{1,0:T(8,128)(2,1)S(1)}, u32[]{:S(2)}, u32[]{:S(2)}) collective-permute-start(bf16[128,1792]{1,0:T(8,128)(2,1)S(1)} %get-tuple-element.69.refs_10_), channel_id=1, source_target_pairs={{0,8},{8,0},{16,24},{24,16},{1,9},{9,1},{17,25},{25,17},{2,10},{10... | collective-permute-start | bytes 1376264 | tf_op jit(solution)/shard_map/ppermute | solution.py:557
  80.2 7.4 %copy-start.1 = (bf16[16,1792]{1,0:T(8,128)(2,1)S(1)}, bf16[16,1792]{1,0:T(8,128)(2,1)}, u32[]{:S(2)}) copy-start(bf16[16,1792]{1,0:T(8,128)(2,1)} %get-tuple-element.80.refs_4_) | copy-start | bytes 172036
  80.2 7.0 %collective-permute-start.13 = (bf16[16,1792]{1,0:T(8,128)(2,1)}, bf16[16,1792]{1,0:T(8,128)(2,1)S(1)}, u32[]{:S(2)}, u32[]{:S(2)}) collective-permute-start(bf16[16,1792]{1,0:T(8,128)(2,1)} %get-tuple-element.77), channel_id=1, source_target_pairs={{0,8},{8,0},{16,24},{24,16},{1,9},{9,1},{17,25},{25,17},{2,10},{10... | collective-permute-start | bytes 172040 | tf_op jit(solution)/shard_map/ppermute | solution.py:557
  80.8 6.4 %collective-permute-start.14 = (bf16[16,1792]{1,0:T(8,128)(2,1)}, bf16[16,1792]{1,0:T(8,128)(2,1)S(1)}, u32[]{:S(2)}, u32[]{:S(2)}) collective-permute-start(bf16[16,1792]{1,0:T(8,128)(2,1)} %get-tuple-element.78), channel_id=1, source_target_pairs={{0,16},{8,24},{16,0},{24,8},{1,17},{9,25},{17,1},{25,9},{2,18},{10... | collective-permute-start | bytes 172040 | tf_op jit(solution)/shard_map/ppermute | solution.py:557
  82.3 5.3 %collective-permute-start.15 = (bf16[16,1792]{1,0:T(8,128)(2,1)}, bf16[16,1792]{1,0:T(8,128)(2,1)S(1)}, u32[]{:S(2)}, u32[]{:S(2)}) collective-permute-start(bf16[16,1792]{1,0:T(8,128)(2,1)} %get-tuple-element.79), channel_id=1, source_target_pairs={{0,24},{8,16},{16,8},{24,0},{1,25},{9,17},{17,9},{25,1},{2,26},{10... | collective-permute-start | bytes 172040 | tf_op jit(solution)/shard_map/ppermute | solution.py:557

commit v8 on v7

--- a/solution.py
+++ b/solution.py
@@ -653,6 +653,7 @@
         scalars=[length, slot],
         picked=5,
         loose=(0, 1, 3, 4, 7),
+        here=(2,),
         raw=(11,),
         scratch=states,
     )(low_x, top_x, w_in, low_y, top_y, cache, sums0, items, half_total, out_gain, out_weight, flat)
@@ -664,6 +665,7 @@
         scalars=[length],
         loose=(0, 1),
         near=(0, 1),
+        here=(2, 5),
         waits=[qkv2],
     )(low_xy, top_xy, w_in, state3, out_gain, out_weight)
 
@@ -678,6 +680,7 @@
         2 * attend_flops,
         size,
         scalars=[length],
+        here=(8,),
     )(qkv3, qkv1, old, sums0, sums1, sums2, qkv2, out_gain, out_weight)
     one_x = across(top1, 1)
     one_y = across(low2, 2)

time: 88.8 us -> 87.1 us (0.981)
  Pallas kernels: 51.3 us -> 48.8 us
    pallas_call x11, Pallas kernels: 50.3 us -> 47.8 us  [run(): pl.pallas_call(body, out_shape=[o if n in near else pltpu.HBM(o.shape, o....]
where the time goes in v8:
time: 87.1 us; the launch traced here: 86.6 us
  Pallas kernels  48.8 us (56%)
  starting transfers between devices  30.7 us (35%)
  waiting for transfers between devices  4.32 us (5%)
  between operations  2.15 us (2%)
    pallas_call x11, Pallas kernels, run(): pl.pallas_call(body, out_shape=[o if n in near else pltpu.HBM(o.shape, o....  47.8 us
    ppermute x15, starting transfers between devices, across(): return lax.ppermute(array, 'head', [(i, i ^ by) for i in range(4)])  16.3 us
    all_to_all x1, starting transfers between devices, local_square(): lax.all_to_all(sent.reshape(groups, capacity, wide), 'tok', split_axis=0,...  4.87 us
    ppermute x1, starting transfers between devices, from_behind(): return lax.ppermute(array, axis, pairs)  4.84 us
    all_to_all x1, starting transfers between devices, local_square(): lax.all_to_all(served.reshape(groups, capacity, D), 'tok', split_axis=0,...  4.72 us
    ppermute x15, waiting for transfers between devices, across(): return lax.ppermute(array, 'head', [(i, i ^ by) for i in range(4)])  3.83 us
  transfers between devices with their start and end apart: 18, of which 6 were waited for; matrix products, arithmetic and copies ran while one was open for 0% of the time, Pallas kernels for 48%

profile of v8, /device:TPU:0, one launch (start us, length us, event | category | flops | bytes accessed | tf_op | source)
XLA Modules:
  0.0 86.6 jit_solution(13680948488955651613)
XLA Ops:
  0.6 3.2 %shard_map.157 = (bf16[128,1792]{1,0:T(8,128)(2,1)}, bf16[128,1792]{1,0:T(8,128)(2,1)}, bf16[16,1792]{1,0:T(8,128)(2,1)}, bf16[16,1792]{1,0:T(8,128)(2,1)}) custom-call(bf16[256,1792]{1,0:T(8,128)(2,1)} %bitcast.28, bf16[2,1792]{1,0:T(2,128)(2,1)} %bitcast.33, f32[1792]{0:T(1024)} %refs_2_.3, f32[3,1792]{1,0:T(4,128)} %taps_ref.1), custom_call_target="tpu_custom_call" | custom-call | flops 9175040 | bytes 1835008 | tf_op jit(solution)/shard_map/pallas_call | solution.py:534
  3.8 4.8 %collective-permute-start.1 = (bf16[16,1792]{1,0:T(8,128)(2,1)}, bf16[16,1792]{1,0:T(8,128)(2,1)S(1)}, u32[]{:S(2)}, u32[]{:S(2)}) collective-permute-start(bf16[16,1792]{1,0:T(8,128)(2,1)} %get-tuple-element.47), channel_id=1, source_target_pairs={{0,8},{8,16},{16,24},{1,9},{9,17},{17,25},{2,10},{10,18},{18,26},{... | collective-permute-start | bytes 172040 | tf_op jit(solution)/shard_map/ppermute | solution.py:724
  8.6 1.6 %collective-permute-start.3 = (bf16[128,1792]{1,0:T(8,128)(2,1)}, bf16[128,1792]{1,0:T(8,128)(2,1)S(1)}, u32[]{:S(2)}, u32[]{:S(2)}) collective-permute-start(bf16[128,1792]{1,0:T(8,128)(2,1)} %get-tuple-element.44.refs_1_), channel_id=1, source_target_pairs={{0,8},{8,0},{16,24},{24,16},{1,9},{9,1},{17,25},{25,17},{2,10},{10... | collective-permute-start | bytes 1376264 | tf_op jit(solution)/shard_map/ppermute | solution.py:557
  10.2 0.1 collective-permute-start
  10.3 3.4 %shard_map.158.wait_ref = bf16[64,640]{1,0:T(8,128)(2,1)} custom-call(bf16[32,1792]{1,0:T(8,128)(2,1)} %bitcast.32, bf16[32,2,1792]{2,1,0:T(2,128)(2,1)} %bitcast.31, f32[1792]{0:T(1024)} %refs_2_.3, f32[3,1792]{1,0:T(4,128)} %taps_ref.1, s32[1,32]{1,0:T(1,128)} %bitcast.34, s32[1,32]{1,0:T(1,128)} %refs_5_.2, bf16[4,144,1792]{2,1,0:T(8,128)(2,1)} %bitcast.18), custom_call_target="tpu_custom_call" | custom-call | flops 73400320 | bytes 2293760 | tf_op jit(solution)/shard_map/pallas_call | solution.py:534
  13.7 0.0 collective-permute-done.1.end_ref
  13.7 0.9 %shard_map.159.refs_2_ = bf16[128,1792]{1,0:T(8,128)(2,1)} custom-call(s32[1]{0:T(128)} %bitcast.2.first_ref, bf16[128,1792]{1,0:T(8,128)(2,1)} %get-tuple-element.45.top_ref, bf16[16,1792]{1,0:T(8,128)(2,1)} %get-tuple-element.46.begin_ref, bf16[16,1792]{1,0:T(8,128)(2,1)S(1)} %collective-permute-done.1.end_ref, ...), custom_call_target="tpu_custom_call", output_to_operand_aliasing={{}: (1, {})} | custom-call | flops 28672 | bytes 229376 | tf_op jit(solution)/shard_map/pallas_call | solution.py:604
  14.7 2.6 %collective-permute-start.2 = (bf16[128,1792]{1,0:T(8,128)(2,1)}, bf16[128,1792]{1,0:T(8,128)(2,1)S(1)}, u32[]{:S(2)}, u32[]{:S(2)}) collective-permute-start(bf16[128,1792]{1,0:T(8,128)(2,1)} %shard_map.159.refs_2_), channel_id=1, source_target_pairs={{0,8},{8,0},{16,24},{24,16},{1,9},{9,1},{17,25},{25,17},{2,10},{10... | collective-permute-start | bytes 1376264 | tf_op jit(solution)/shard_map/ppermute | solution.py:557
  17.3 0.5 collective-permute-start.4
  17.8 4.9 %all-to-all-start = ((bf16[8,8,640]{2,1,0:T(8,128)(2,1)}), bf16[8,8,640]{2,1,0:T(8,128)(2,1)S(1)}, u32[]{:S(2)}, u32[]{:S(2)}) async-start(bf16[8,8,640]{2,1,0:T(8,128)(2,1)} %bitcast.30), calls=%async_computation | async-start | bytes 163840 | tf_op jit(solution)/shard_map/all_to_all | solution.py:619
  23.3 5.0 %shard_map.160 = (f32[4,384,128]{2,1,0:T(8,128)}, f32[4,256,128]{2,1,0:T(8,128)}, bf16[256,64]{1,0:T(8,128)(2,1)}) custom-call(s32[1]{0:T(128)S(6)} %copy.19.refs_0_, bf16[128,1792]{1,0:T(8,128)(2,1)} %get-tuple-element.44.refs_1_, bf16[128,1792]{1,0:T(8,128)(2,1)} %shard_map.159.refs_2_, bf16[4,144,1792]{2,1,0:T(8,128)(2,1)} %bitcast.19), custom_call_target="tpu_custom_call" | custom-call | flops 788529152 | bytes 1835008 | tf_op jit(solution)/shard_map/pallas_call | solution.py:534
  28.4 0.4 all-to-all-done
  28.8 0.0 copy-start
  28.8 3.7 %shard_map.161.refs_10_ = f32[256,128]{1,0:T(8,128)} custom-call(bf16[64,640]{1,0:T(8,128)(2,1)S(1)} %bitcast.23, f32[17472,112]{1,0:T(8,128)} %bitcast.25, bf16[256,64]{1,0:T(8,128)(2,1)} %get-tuple-element.48.refs_2_.refs_6_), custom_call_target="tpu_custom_call" | custom-call | flops 500957184 | bytes 4472832 | tf_op jit(solution)/shard_map/pallas_call | solution.py:534
  32.5 0.0 collective-permute-done.3.refs_2_
  32.5 0.0 collective-permute-done.refs_5_
  32.5 0.0 collective-permute-done.2.refs_3_
  32.5 1.6 %collective-permute-start.6 = (bf16[128,1792]{1,0:T(8,128)(2,1)S(1)}, bf16[128,1792]{1,0:T(8,128)(2,1)S(1)}, u32[]{:S(2)}, u32[]{:S(2)}) collective-permute-start(bf16[128,1792]{1,0:T(8,128)(2,1)S(1)} %collective-permute-done.2.refs_3_), channel_id=1, source_target_pairs={{0,16},{8,24},{16,0},{24,8},{1,17},{9,25},{17,1},{25,9},{2,18},{10... | collective-permute-start | bytes 1376264 | tf_op jit(solution)/shard_map/ppermute | solution.py:557
  34.1 0.1 collective-permute-start.5
  34.9 0.0 collective-permute-done.4.refs_6_
  34.9 0.0 copy-done
  34.9 0.0 copy-start.1
  34.9 9.2 %shard_map.162 = (f32[4,384,128]{2,1,0:T(8,128)}, bf16[256,640]{1,0:T(8,128)(2,1)}, f32[4,384,128]{2,1,0:T(8,128)}, bf16[256,640]{1,0:T(8,128)(2,1)}, bf16[4,384...) custom-call(s32[1]{0:T(128)S(6)} %copy.19.refs_0_, s32[1]{0:T(128)S(6)} %copy.20.refs_1_, ...), custom_call_target="tpu_custom_call" | custom-call | flops 2078015488 | bytes 4472832 | tf_op jit(solution)/shard_map/pallas_call | solution.py:534
  44.1 1.0 %collective-permute-done.6.refs_2_ = bf16[128,1792]{1,0:T(8,128)(2,1)S(1)} collective-permute-done((bf16[128,1792]{1,0:T(8,128)(2,1)S(1)}, bf16[128,1792]{1,0:T(8,128)(2,1)S(1)}, u32[]{:S(2)}, u32[]{:S(2)}) %collective-permute-start.6) | collective-permute-done | bytes 458784 | tf_op jit(solution)/shard_map/ppermute | solution.py:557
  45.1 1.2 %collective-permute-done.5.refs_1_ = bf16[128,1792]{1,0:T(8,128)(2,1)S(1)} collective-permute-done((bf16[128,1792]{1,0:T(8,128)(2,1)S(1)}, bf16[128,1792]{1,0:T(8,128)(2,1)S(1)}, u32[]{:S(2)}, u32[]{:S(2)}) %collective-permute-start.5) | collective-permute-done | bytes 458784 | tf_op jit(solution)/shard_map/ppermute | solution.py:557
  46.4 0.0 copy-done.1
  46.4 4.2 %shard_map.163 = (bf16[128,1792]{1,0:T(8,128)(2,1)S(1)}, bf16[128,1792]{1,0:T(8,128)(2,1)S(1)}, bf16[256,640]{1,0:T(8,128)(2,1)}) custom-call(s32[1]{0:T(128)S(6)} %copy.19.refs_0_, bf16[128,1792]{1,0:T(8,128)(2,1)S(1)} %collective-permute-done.5.refs_1_, bf16[128,1792]{1,0:T(8,128)(2,1)S(1)} %collective-permute-done.6.refs_2_, ...), custom_call_target="tpu_custom_call" | custom-call | flops 1358954496 | bytes 1835008 | tf_op jit(solution)/shard_map/pallas_call | solution.py:534
  50.6 0.6 collective-permute-start.8
  51.2 1.5 %collective-permute-start.7 = (bf16[128,1792]{1,0:T(8,128)(2,1)S(1)}, bf16[128,1792]{1,0:T(8,128)(2,1)S(1)}, u32[]{:S(2)}, u32[]{:S(2)}) collective-permute-start(bf16[128,1792]{1,0:T(8,128)(2,1)S(1)} %get-tuple-element.56), channel_id=1, source_target_pairs={{0,8},{8,0},{16,24},{24,16},{1,9},{9,1},{17,25},{25,17},{2,10},{10... | collective-permute-start | bytes 1376264 | tf_op jit(solution)/shard_map/ppermute | solution.py:557
  52.7 7.4 %shard_map.164 = (bf16[128,1792]{1,0:T(8,128)(2,1)}, bf16[128,1792]{1,0:T(8,128)(2,1)}, bf16[128,1792]{1,0:T(8,128)(2,1)}, bf16[128,1792]{1,0:T(8,128)(2,1)}, f32[4,384,128]{2,1,0:T(8,128)}) custom-call(s32[1]{0:T(128)S(6)} %copy.19.refs_0_, bf16[256,640]{1,0:T(8,128)(2,1)} %get-tuple-element.61.refs_1_, bf16[256,640]{1,0:T(8,128)(2,1)} %get-tuple-element.62.refs_2_, ...), custom_call_target="tpu_custom_call" | custom-call | flops 1140850688 | bytes 1835008 | tf_op jit(solution)/shard_map/pallas_call | solution.py:534
  60.0 0.4 collective-permute-start.10
  60.5 1.7 %collective-permute-start.9 = (bf16[128,1792]{1,0:T(8,128)(2,1)}, bf16[128,1792]{1,0:T(8,128)(2,1)S(1)}, u32[]{:S(2)}, u32[]{:S(2)}) collective-permute-start(bf16[128,1792]{1,0:T(8,128)(2,1)} %get-tuple-element.68.refs_4_), channel_id=1, source_target_pairs={{0,8},{8,0},{16,24},{24,16},{1,9},{9,1},{17,25},{25,17},{2,10},{10... | collective-permute-start | bytes 1376264 | tf_op jit(solution)/shard_map/ppermute | solution.py:557
  62.2 4.7 %all-to-all-start.1 = ((bf16[8,8,1792]{2,1,0:T(8,128)(2,1)}), bf16[8,8,1792]{2,1,0:T(8,128)(2,1)S(1)}, u32[]{:S(2)}, u32[]{:S(2)}) async-start(bf16[8,8,1792]{2,1,0:T(8,128)(2,1)} %bitcast.11), calls=%async_computation.1 | async-start | bytes 458752 | tf_op jit(solution)/shard_map/all_to_all | solution.py:675
  66.9 0.0 collective-permute-done.8.refs_3_
  66.9 0.0 collective-permute-done.7.refs_1_
  66.9 1.3 %shard_map.165 = (bf16[128,1792]{1,0:T(8,128)(2,1)S(1)}, bf16[128,1792]{1,0:T(8,128)(2,1)S(1)}) custom-call(bf16[128,1792]{1,0:T(8,128)(2,1)} %get-tuple-element.65.refs_0_, bf16[128,1792]{1,0:T(8,128)(2,1)S(1)} %collective-permute-done.7.refs_1_, bf16[128,1792]{1,0:T(8,128)(2,1)} %get-tuple-element.66.refs_2_, ...), custom_call_target="tpu_custom_call" | custom-call | bytes 1835008 | tf_op jit(solution)/shard_map/pallas_call | solution.py:534
  68.2 0.0 copy-start.2
  68.2 0.6 collective-permute-start.11
  68.8 1.5 %collective-permute-start.12 = (bf16[128,1792]{1,0:T(8,128)(2,1)S(1)}, bf16[128,1792]{1,0:T(8,128)(2,1)S(1)}, u32[]{:S(2)}, u32[]{:S(2)}) collective-permute-start(bf16[128,1792]{1,0:T(8,128)(2,1)S(1)} %get-tuple-element.69.refs_10_), channel_id=1, source_target_pairs={{0,8},{8,0},{16,24},{24,16},{1,9},{9,1},{17,25},{25,17},{2,10},{10... | collective-permute-start | bytes 1376264 | tf_op jit(solution)/shard_map/ppermute | solution.py:557
  70.3 0.0 copy-done.2
  70.3 5.6 %shard_map.166 = (bf16[128,1792]{1,0:T(8,128)(2,1)}, bf16[128,1792]{1,0:T(8,128)(2,1)}, f32[1,273,4,112]{3,2,1,0:T(4,128)}) custom-call(s32[1]{0:T(128)S(6)} %copy.19.refs_0_, f32[4,384,128]{2,1,0:T(8,128)} %get-tuple-element.58.refs_3_.refs_1_, f32[4,384,128]{2,1,0:T(8,128)} %get-tuple-element.52.refs_8_.refs_4_.refs_2_, ...), custom_call_target="tpu_custom_call" | custom-call | flops 570425344 | bytes 1835008 | tf_op jit(solution)/shard_map/pallas_call | solution.py:534
  75.9 0.1 all-to-all-done.1
  75.9 0.0 collective-permute-done.10.refs_5_
  75.9 0.0 collective-permute-done.9.refs_3_
  75.9 2.6 %shard_map.167 = (bf16[16,1792]{1,0:T(8,128)(2,1)}, bf16[16,1792]{1,0:T(8,128)(2,1)}, bf16[16,1792]{1,0:T(8,128)(2,1)}, bf16[16,1792]{1,0:T(8,128)(2,1)}, bf16[1...) custom-call(bf16[64,1792]{1,0:T(8,128)(2,1)S(1)} %bitcast.22, s32[1,32]{1,0:T(1,128)} %bitcast.35, ...), custom_call_target="tpu_custom_call" | custom-call | flops 7340032 | bytes 458752 | tf_op jit(solution)/shard_map/pallas_call | solution.py:534
  78.6 0.0 copy-start.3
  78.6 0.6 collective-permute-start.13
  79.1 1.5 %collective-permute-start.14 = (bf16[16,1792]{1,0:T(8,128)(2,1)}, bf16[16,1792]{1,0:T(8,128)(2,1)S(1)}, u32[]{:S(2)}, u32[]{:S(2)}) collective-permute-start(bf16[16,1792]{1,0:T(8,128)(2,1)} %get-tuple-element.78), channel_id=1, source_target_pairs={{0,16},{8,24},{16,0},{24,8},{1,17},{9,25},{17,1},{25,9},{2,18},{10... | collective-permute-start | bytes 172040 | tf_op jit(solution)/shard_map/ppermute | solution.py:557
  80.7 1.5 %collective-permute-start.15 = (bf16[16,1792]{1,0:T(8,128)(2,1)}, bf16[16,1792]{1,0:T(8,128)(2,1)S(1)}, u32[]{:S(2)}, u32[]{:S(2)}) collective-permute-start(bf16[16,1792]{1,0:T(8,128)(2,1)} %get-tuple-element.79), channel_id=1, source_target_pairs={{0,24},{8,16},{16,8},{24,0},{1,25},{9,17},{17,9},{25,1},{2,26},{10... | collective-permute-start | bytes 172040 | tf_op jit(solution)/shard_map/ppermute | solution.py:557
  82.1 0.0 collective-permute-done.11.refs_1_
  82.1 0.5 collective-permute-done.12.refs_3_
  82.6 2.3 %shard_map.168 = bf16[2,128,1792]{2,1,0:T(8,128)(2,1)} custom-call(bf16[128,1792]{1,0:T(8,128)(2,1)} %get-tuple-element.73.refs_0_, bf16[128,1792]{1,0:T(8,128)(2,1)S(1)} %collective-permute-done.11.refs_1_, bf16[128,1792]{1,0:T(8,128)(2,1)} %get-tuple-element.75.refs_2_, bf16[128,1792]{1,0:T(8,128)(2,1)S(1)} %collective-permute-done.12.refs_3_, ...), custom_call_target="tpu_custom_call" | custom-call | bytes 3670016 | tf_op jit(solution)/shard_map/pallas_call | solution.py:534
  84.9 0.0 collective-permute-done.13
  84.9 0.0 collective-permute-done.14
  84.9 1.0 %collective-permute-done.15 = bf16[16,1792]{1,0:T(8,128)(2,1)S(1)} collective-permute-done((bf16[16,1792]{1,0:T(8,128)(2,1)}, bf16[16,1792]{1,0:T(8,128)(2,1)S(1)}, u32[]{:S(2)}, u32[]{:S(2)}) %collective-permute-start.15) | collective-permute-done | bytes 57376 | tf_op jit(solution)/shard_map/ppermute | solution.py:557
  85.9 0.0 copy-done.3
  85.9 0.6 fusion
Async XLA Ops:
  3.8 9.9 %collective-permute-start.1 = (bf16[16,1792]{1,0:T(8,128)(2,1)}, bf16[16,1792]{1,0:T(8,128)(2,1)S(1)}, u32[]{:S(2)}, u32[]{:S(2)}) collective-permute-start(bf16[16,1792]{1,0:T(8,128)(2,1)} %get-tuple-element.47), channel_id=1, source_target_pairs={{0,8},{8,16},{16,24},{1,9},{9,17},{17,25},{2,10},{10,18},{18,26},{... | collective-permute-start | bytes 172040 | tf_op jit(solution)/shard_map/ppermute | solution.py:724
  8.6 23.9 %collective-permute-start.3 = (bf16[128,1792]{1,0:T(8,128)(2,1)}, bf16[128,1792]{1,0:T(8,128)(2,1)S(1)}, u32[]{:S(2)}, u32[]{:S(2)}) collective-permute-start(bf16[128,1792]{1,0:T(8,128)(2,1)} %get-tuple-element.44.refs_1_), channel_id=1, source_target_pairs={{0,8},{8,0},{16,24},{24,16},{1,9},{9,1},{17,25},{25,17},{2,10},{10... | collective-permute-start | bytes 1376264 | tf_op jit(solution)/shard_map/ppermute | solution.py:557
  10.2 22.3 %collective-permute-start = (bf16[128,1792]{1,0:T(8,128)(2,1)}, bf16[128,1792]{1,0:T(8,128)(2,1)S(1)}, u32[]{:S(2)}, u32[]{:S(2)}) collective-permute-start(bf16[128,1792]{1,0:T(8,128)(2,1)} %get-tuple-element.44.refs_1_), channel_id=1, source_target_pairs={{0,16},{8,24},{16,0},{24,8},{1,17},{9,25},{17,1},{25,9},{2,18},{10... | collective-permute-start | bytes 1376264 | tf_op jit(solution)/shard_map/ppermute | solution.py:557
  14.7 17.9 %collective-permute-start.2 = (bf16[128,1792]{1,0:T(8,128)(2,1)}, bf16[128,1792]{1,0:T(8,128)(2,1)S(1)}, u32[]{:S(2)}, u32[]{:S(2)}) collective-permute-start(bf16[128,1792]{1,0:T(8,128)(2,1)} %shard_map.159.refs_2_), channel_id=1, source_target_pairs={{0,8},{8,0},{16,24},{24,16},{1,9},{9,1},{17,25},{25,17},{2,10},{10... | collective-permute-start | bytes 1376264 | tf_op jit(solution)/shard_map/ppermute | solution.py:557
  17.3 17.6 %collective-permute-start.4 = (bf16[128,1792]{1,0:T(8,128)(2,1)}, bf16[128,1792]{1,0:T(8,128)(2,1)S(1)}, u32[]{:S(2)}, u32[]{:S(2)}) collective-permute-start(bf16[128,1792]{1,0:T(8,128)(2,1)} %shard_map.159.refs_2_), channel_id=1, source_target_pairs={{0,16},{8,24},{16,0},{24,8},{1,17},{9,25},{17,1},{25,9},{2,18},{10... | collective-permute-start | bytes 1376264 | tf_op jit(solution)/shard_map/ppermute | solution.py:557
  17.8 11.0 %all-to-all-start = ((bf16[8,8,640]{2,1,0:T(8,128)(2,1)}), bf16[8,8,640]{2,1,0:T(8,128)(2,1)S(1)}, u32[]{:S(2)}, u32[]{:S(2)}) async-start(bf16[8,8,640]{2,1,0:T(8,128)(2,1)} %bitcast.30), calls=%async_computation | async-start | bytes 163840 | tf_op jit(solution)/shard_map/all_to_all | solution.py:619
  28.8 6.1 %copy-start = (bf16[1792,4,144]{0,2,1:T(8,128)(2,1)S(1)}, bf16[1792,4,144]{0,2,1:T(8,128)(2,1)}, u32[]{:S(2)}) copy-start(bf16[1792,4,144]{0,2,1:T(8,128)(2,1)} %param.20) | copy-start | bytes 6193156
  32.5 12.6 %collective-permute-start.6 = (bf16[128,1792]{1,0:T(8,128)(2,1)S(1)}, bf16[128,1792]{1,0:T(8,128)(2,1)S(1)}, u32[]{:S(2)}, u32[]{:S(2)}) collective-permute-start(bf16[128,1792]{1,0:T(8,128)(2,1)S(1)} %collective-permute-done.2.refs_3_), channel_id=1, source_target_pairs={{0,16},{8,24},{16,0},{24,8},{1,17},{9,25},{17,1},{25,9},{2,18},{10... | collective-permute-start | bytes 1376264 | tf_op jit(solution)/shard_map/ppermute | solution.py:557
  34.1 12.3 %collective-permute-start.5 = (bf16[128,1792]{1,0:T(8,128)(2,1)S(1)}, bf16[128,1792]{1,0:T(8,128)(2,1)S(1)}, u32[]{:S(2)}, u32[]{:S(2)}) collective-permute-start(bf16[128,1792]{1,0:T(8,128)(2,1)S(1)} %collective-permute-done.refs_5_), channel_id=1, source_target_pairs={{0,8},{8,0},{16,24},{24,16},{1,9},{9,1},{17,25},{25,17},{2,10},{10... | collective-permute-start | bytes 1376264 | tf_op jit(solution)/shard_map/ppermute | solution.py:557
  34.9 11.5 %copy-start.1 = (bf16[448,1792]{1,0:T(8,128)(2,1)S(1)}, bf16[448,1792]{1,0:T(8,128)(2,1)}, u32[]{:S(2)}) copy-start(bf16[448,1792]{1,0:T(8,128)(2,1)} %refs_9_.3) | copy-start | bytes 4816900
  50.6 16.3 %collective-permute-start.8 = (bf16[128,1792]{1,0:T(8,128)(2,1)S(1)}, bf16[128,1792]{1,0:T(8,128)(2,1)S(1)}, u32[]{:S(2)}, u32[]{:S(2)}) collective-permute-start(bf16[128,1792]{1,0:T(8,128)(2,1)S(1)} %get-tuple-element.67), channel_id=1, source_target_pairs={{0,16},{8,24},{16,0},{24,8},{1,17},{9,25},{17,1},{25,9},{2,18},{10... | collective-permute-start | bytes 1376264 | tf_op jit(solution)/shard_map/ppermute | solution.py:557
  51.2 15.7 %collective-permute-start.7 = (bf16[128,1792]{1,0:T(8,128)(2,1)S(1)}, bf16[128,1792]{1,0:T(8,128)(2,1)S(1)}, u32[]{:S(2)}, u32[]{:S(2)}) collective-permute-start(bf16[128,1792]{1,0:T(8,128)(2,1)S(1)} %get-tuple-element.56), channel_id=1, source_target_pairs={{0,8},{8,0},{16,24},{24,16},{1,9},{9,1},{17,25},{25,17},{2,10},{10... | collective-permute-start | bytes 1376264 | tf_op jit(solution)/shard_map/ppermute | solution.py:557
  60.0 15.9 %collective-permute-start.10 = (bf16[128,1792]{1,0:T(8,128)(2,1)}, bf16[128,1792]{1,0:T(8,128)(2,1)S(1)}, u32[]{:S(2)}, u32[]{:S(2)}) collective-permute-start(bf16[128,1792]{1,0:T(8,128)(2,1)} %get-tuple-element.72), channel_id=1, source_target_pairs={{0,16},{8,24},{16,0},{24,8},{1,17},{9,25},{17,1},{25,9},{2,18},{10... | collective-permute-start | bytes 1376264 | tf_op jit(solution)/shard_map/ppermute | solution.py:557
  60.5 15.5 %collective-permute-start.9 = (bf16[128,1792]{1,0:T(8,128)(2,1)}, bf16[128,1792]{1,0:T(8,128)(2,1)S(1)}, u32[]{:S(2)}, u32[]{:S(2)}) collective-permute-start(bf16[128,1792]{1,0:T(8,128)(2,1)} %get-tuple-element.68.refs_4_), channel_id=1, source_target_pairs={{0,8},{8,0},{16,24},{24,16},{1,9},{9,1},{17,25},{25,17},{2,10},{10... | collective-permute-start | bytes 1376264 | tf_op jit(solution)/shard_map/ppermute | solution.py:557
  62.2 13.8 %all-to-all-start.1 = ((bf16[8,8,1792]{2,1,0:T(8,128)(2,1)}), bf16[8,8,1792]{2,1,0:T(8,128)(2,1)S(1)}, u32[]{:S(2)}, u32[]{:S(2)}) async-start(bf16[8,8,1792]{2,1,0:T(8,128)(2,1)} %bitcast.11), calls=%async_computation.1 | async-start | bytes 458752 | tf_op jit(solution)/shard_map/all_to_all | solution.py:675
  68.2 2.1 %copy-start.2 = (bf16[128,1792]{1,0:T(8,128)(2,1)}, bf16[128,1792]{1,0:T(8,128)(2,1)S(1)}, u32[]{:S(2)}) copy-start(bf16[128,1792]{1,0:T(8,128)(2,1)S(1)} %get-tuple-element.69.refs_10_) | copy-start | bytes 1376260
  68.2 13.9 %collective-permute-start.11 = (bf16[128,1792]{1,0:T(8,128)(2,1)S(1)}, bf16[128,1792]{1,0:T(8,128)(2,1)S(1)}, u32[]{:S(2)}, u32[]{:S(2)}) collective-permute-start(bf16[128,1792]{1,0:T(8,128)(2,1)S(1)} %get-tuple-element.74), channel_id=1, source_target_pairs={{0,16},{8,24},{16,0},{24,8},{1,17},{9,25},{17,1},{25,9},{2,18},{10... | collective-permute-start | bytes 1376264 | tf_op jit(solution)/shard_map/ppermute | solution.py:557
  68.8 13.8 %collective-permute-start.12 = (bf16[128,1792]{1,0:T(8,128)(2,1)S(1)}, bf16[128,1792]{1,0:T(8,128)(2,1)S(1)}, u32[]{:S(2)}, u32[]{:S(2)}) collective-permute-start(bf16[128,1792]{1,0:T(8,128)(2,1)S(1)} %get-tuple-element.69.refs_10_), channel_id=1, source_target_pairs={{0,8},{8,0},{16,24},{24,16},{1,9},{9,1},{17,25},{25,17},{2,10},{10... | collective-permute-start | bytes 1376264 | tf_op jit(solution)/shard_map/ppermute | solution.py:557
  78.6 7.4 %copy-start.3 = (bf16[16,1792]{1,0:T(8,128)(2,1)S(1)}, bf16[16,1792]{1,0:T(8,128)(2,1)}, u32[]{:S(2)}) copy-start(bf16[16,1792]{1,0:T(8,128)(2,1)} %get-tuple-element.80.refs_4_) | copy-start | bytes 172036
  78.6 6.3 %collective-permute-start.13 = (bf16[16,1792]{1,0:T(8,128)(2,1)}, bf16[16,1792]{1,0:T(8,128)(2,1)S(1)}, u32[]{:S(2)}, u32[]{:S(2)}) collective-permute-start(bf16[16,1792]{1,0:T(8,128)(2,1)} %get-tuple-element.77), channel_id=1, source_target_pairs={{0,8},{8,0},{16,24},{24,16},{1,9},{9,1},{17,25},{25,17},{2,10},{10... | collective-permute-start | bytes 172040 | tf_op jit(solution)/shard_map/ppermute | solution.py:557
  79.1 5.8 %collective-permute-start.14 = (bf16[16,1792]{1,0:T(8,128)(2,1)}, bf16[16,1792]{1,0:T(8,128)(2,1)S(1)}, u32[]{:S(2)}, u32[]{:S(2)}) collective-permute-start(bf16[16,1792]{1,0:T(8,128)(2,1)} %get-tuple-element.78), channel_id=1, source_target_pairs={{0,16},{8,24},{16,0},{24,8},{1,17},{9,25},{17,1},{25,9},{2,18},{10... | collective-permute-start | bytes 172040 | tf_op jit(solution)/shard_map/ppermute | solution.py:557
  80.7 5.3 %collective-permute-start.15 = (bf16[16,1792]{1,0:T(8,128)(2,1)}, bf16[16,1792]{1,0:T(8,128)(2,1)S(1)}, u32[]{:S(2)}, u32[]{:S(2)}) collective-permute-start(bf16[16,1792]{1,0:T(8,128)(2,1)} %get-tuple-element.79), channel_id=1, source_target_pairs={{0,24},{8,16},{16,8},{24,0},{1,25},{9,17},{17,9},{25,1},{2,26},{10... | collective-permute-start | bytes 172040 | tf_op jit(solution)/shard_map/ppermute | solution.py:557

commit v9 on v8

--- a/solution.py
+++ b/solution.py
@@ -654,6 +654,7 @@
         picked=5,
         loose=(0, 1, 3, 4, 7),
         here=(2,),
+        near=(4,),
         raw=(11,),
         scratch=states,
     )(low_x, top_x, w_in, low_y, top_y, cache, sums0, items, half_total, out_gain, out_weight, flat)
@@ -665,7 +666,7 @@
         scalars=[length],
         loose=(0, 1),
         near=(0, 1),
-        here=(2, 5),
+        here=(2, 3, 5),
         waits=[qkv2],
     )(low_xy, top_xy, w_in, state3, out_gain, out_weight)
 

time: 87.1 us -> 86.8 us (level)
  no operation moved by 1% of the time
where the time goes in v9:
time: 86.8 us; the launch traced here: 86.3 us
  Pallas kernels  48.4 us (56%)
  starting transfers between devices  30.7 us (35%)
  waiting for transfers between devices  4.35 us (5%)
  between operations  2.15 us (2%)
    pallas_call x11, Pallas kernels, run(): pl.pallas_call(body, out_shape=[o if n in near else pltpu.HBM(o.shape, o....  47.5 us
    ppermute x15, starting transfers between devices, across(): return lax.ppermute(array, 'head', [(i, i ^ by) for i in range(4)])  16.2 us
    all_to_all x1, starting transfers between devices, local_square(): lax.all_to_all(sent.reshape(groups, capacity, wide), 'tok', split_axis=0,...  4.87 us
    ppermute x1, starting transfers between devices, from_behind(): return lax.ppermute(array, axis, pairs)  4.84 us
    all_to_all x1, starting transfers between devices, local_square(): lax.all_to_all(served.reshape(groups, capacity, D), 'tok', split_axis=0,...  4.74 us
    ppermute x15, waiting for transfers between devices, across(): return lax.ppermute(array, 'head', [(i, i ^ by) for i in range(4)])  3.84 us
  transfers between devices with their start and end apart: 18, of which 6 were waited for; matrix products, arithmetic and copies ran while one was open for 0% of the time, Pallas kernels for 48%

profile of v9, /device:TPU:0, one launch (start us, length us, event | category | flops | bytes accessed | tf_op | source)
XLA Modules:
  0.0 86.3 jit_solution(1195128637604779383)
XLA Ops:
  0.6 3.2 %shard_map.157 = (bf16[128,1792]{1,0:T(8,128)(2,1)}, bf16[128,1792]{1,0:T(8,128)(2,1)}, bf16[16,1792]{1,0:T(8,128)(2,1)}, bf16[16,1792]{1,0:T(8,128)(2,1)}) custom-call(bf16[256,1792]{1,0:T(8,128)(2,1)} %bitcast.28, bf16[2,1792]{1,0:T(2,128)(2,1)} %bitcast.33, f32[1792]{0:T(1024)} %refs_2_.3, f32[3,1792]{1,0:T(4,128)} %taps_ref.1), custom_call_target="tpu_custom_call" | custom-call | flops 9175040 | bytes 1835008 | tf_op jit(solution)/shard_map/pallas_call | solution.py:534
  3.8 4.8 %collective-permute-start.1 = (bf16[16,1792]{1,0:T(8,128)(2,1)}, bf16[16,1792]{1,0:T(8,128)(2,1)S(1)}, u32[]{:S(2)}, u32[]{:S(2)}) collective-permute-start(bf16[16,1792]{1,0:T(8,128)(2,1)} %get-tuple-element.47), channel_id=1, source_target_pairs={{0,8},{8,16},{16,24},{1,9},{9,17},{17,25},{2,10},{10,18},{18,26},{... | collective-permute-start | bytes 172040 | tf_op jit(solution)/shard_map/ppermute | solution.py:725
  8.6 1.6 %collective-permute-start.3 = (bf16[128,1792]{1,0:T(8,128)(2,1)}, bf16[128,1792]{1,0:T(8,128)(2,1)S(1)}, u32[]{:S(2)}, u32[]{:S(2)}) collective-permute-start(bf16[128,1792]{1,0:T(8,128)(2,1)} %get-tuple-element.44.refs_1_), channel_id=1, source_target_pairs={{0,8},{8,0},{16,24},{24,16},{1,9},{9,1},{17,25},{25,17},{2,10},{10... | collective-permute-start | bytes 1376264 | tf_op jit(solution)/shard_map/ppermute | solution.py:557
  10.2 0.1 collective-permute-start
  10.3 3.4 %shard_map.158.wait_ref = bf16[64,640]{1,0:T(8,128)(2,1)} custom-call(bf16[32,1792]{1,0:T(8,128)(2,1)} %bitcast.32, bf16[32,2,1792]{2,1,0:T(2,128)(2,1)} %bitcast.31, f32[1792]{0:T(1024)} %refs_2_.3, f32[3,1792]{1,0:T(4,128)} %taps_ref.1, s32[1,32]{1,0:T(1,128)} %bitcast.34, s32[1,32]{1,0:T(1,128)} %refs_5_.2, bf16[4,144,1792]{2,1,0:T(8,128)(2,1)} %bitcast.18), custom_call_target="tpu_custom_call" | custom-call | flops 73400320 | bytes 2293760 | tf_op jit(solution)/shard_map/pallas_call | solution.py:534
  13.7 0.0 collective-permute-done.1.end_ref
  13.7 0.9 %shard_map.159.refs_2_ = bf16[128,1792]{1,0:T(8,128)(2,1)} custom-call(s32[1]{0:T(128)} %bitcast.2.first_ref, bf16[128,1792]{1,0:T(8,128)(2,1)} %get-tuple-element.45.top_ref, bf16[16,1792]{1,0:T(8,128)(2,1)} %get-tuple-element.46.begin_ref, bf16[16,1792]{1,0:T(8,128)(2,1)S(1)} %collective-permute-done.1.end_ref, ...), custom_call_target="tpu_custom_call", output_to_operand_aliasing={{}: (1, {})} | custom-call | flops 28672 | bytes 229376 | tf_op jit(solution)/shard_map/pallas_call | solution.py:604
  14.7 2.6 %collective-permute-start.2 = (bf16[128,1792]{1,0:T(8,128)(2,1)}, bf16[128,1792]{1,0:T(8,128)(2,1)S(1)}, u32[]{:S(2)}, u32[]{:S(2)}) collective-permute-start(bf16[128,1792]{1,0:T(8,128)(2,1)} %shard_map.159.refs_2_), channel_id=1, source_target_pairs={{0,8},{8,0},{16,24},{24,16},{1,9},{9,1},{17,25},{25,17},{2,10},{10... | collective-permute-start | bytes 1376264 | tf_op jit(solution)/shard_map/ppermute | solution.py:557
  17.3 0.5 collective-permute-start.4
  17.8 4.9 %all-to-all-start = ((bf16[8,8,640]{2,1,0:T(8,128)(2,1)}), bf16[8,8,640]{2,1,0:T(8,128)(2,1)S(1)}, u32[]{:S(2)}, u32[]{:S(2)}) async-start(bf16[8,8,640]{2,1,0:T(8,128)(2,1)} %bitcast.30), calls=%async_computation | async-start | bytes 163840 | tf_op jit(solution)/shard_map/all_to_all | solution.py:619
  23.3 5.0 %shard_map.160 = (f32[4,384,128]{2,1,0:T(8,128)}, f32[4,256,128]{2,1,0:T(8,128)}, bf16[256,64]{1,0:T(8,128)(2,1)}) custom-call(s32[1]{0:T(128)S(6)} %copy.19.refs_0_, bf16[128,1792]{1,0:T(8,128)(2,1)} %get-tuple-element.44.refs_1_, bf16[128,1792]{1,0:T(8,128)(2,1)} %shard_map.159.refs_2_, bf16[4,144,1792]{2,1,0:T(8,128)(2,1)} %bitcast.19), custom_call_target="tpu_custom_call" | custom-call | flops 788529152 | bytes 1835008 | tf_op jit(solution)/shard_map/pallas_call | solution.py:534
  28.4 0.4 all-to-all-done
  28.8 0.0 copy-start
  28.8 3.7 %shard_map.161.refs_10_ = f32[256,128]{1,0:T(8,128)} custom-call(bf16[64,640]{1,0:T(8,128)(2,1)S(1)} %bitcast.23, f32[17472,112]{1,0:T(8,128)} %bitcast.25, bf16[256,64]{1,0:T(8,128)(2,1)} %get-tuple-element.48.refs_2_.refs_6_), custom_call_target="tpu_custom_call" | custom-call | flops 500957184 | bytes 4472832 | tf_op jit(solution)/shard_map/pallas_call | solution.py:534
  32.5 0.0 collective-permute-done.3.refs_2_
  32.5 0.0 collective-permute-done.refs_5_
  32.5 0.0 collective-permute-done.2.refs_3_
  32.5 1.6 %collective-permute-start.6 = (bf16[128,1792]{1,0:T(8,128)(2,1)S(1)}, bf16[128,1792]{1,0:T(8,128)(2,1)S(1)}, u32[]{:S(2)}, u32[]{:S(2)}) collective-permute-start(bf16[128,1792]{1,0:T(8,128)(2,1)S(1)} %collective-permute-done.2.refs_3_), channel_id=1, source_target_pairs={{0,16},{8,24},{16,0},{24,8},{1,17},{9,25},{17,1},{25,9},{2,18},{10... | collective-permute-start | bytes 1376264 | tf_op jit(solution)/shard_map/ppermute | solution.py:557
  34.1 0.1 collective-permute-start.5
  34.9 0.0 collective-permute-done.4.refs_6_
  34.9 0.0 copy-done
  34.9 0.0 copy-start.1
  34.9 9.2 %shard_map.162 = (f32[4,384,128]{2,1,0:T(8,128)}, bf16[256,640]{1,0:T(8,128)(2,1)}, f32[4,384,128]{2,1,0:T(8,128)}, bf16[256,640]{1,0:T(8,128)(2,1)}, bf16[4,384...) custom-call(s32[1]{0:T(128)S(6)} %copy.19.refs_0_, s32[1]{0:T(128)S(6)} %copy.20.refs_1_, ...), custom_call_target="tpu_custom_call" | custom-call | flops 2078015488 | bytes 4472832 | tf_op jit(solution)/shard_map/pallas_call | solution.py:534
  44.1 1.0 %collective-permute-done.6.refs_2_ = bf16[128,1792]{1,0:T(8,128)(2,1)S(1)} collective-permute-done((bf16[128,1792]{1,0:T(8,128)(2,1)S(1)}, bf16[128,1792]{1,0:T(8,128)(2,1)S(1)}, u32[]{:S(2)}, u32[]{:S(2)}) %collective-permute-start.6) | collective-permute-done | bytes 458784 | tf_op jit(solution)/shard_map/ppermute | solution.py:557
  45.1 1.2 %collective-permute-done.5.refs_1_ = bf16[128,1792]{1,0:T(8,128)(2,1)S(1)} collective-permute-done((bf16[128,1792]{1,0:T(8,128)(2,1)S(1)}, bf16[128,1792]{1,0:T(8,128)(2,1)S(1)}, u32[]{:S(2)}, u32[]{:S(2)}) %collective-permute-start.5) | collective-permute-done | bytes 458784 | tf_op jit(solution)/shard_map/ppermute | solution.py:557
  46.4 0.0 copy-done.1
  46.4 3.9 %shard_map.163 = (bf16[128,1792]{1,0:T(8,128)(2,1)S(1)}, bf16[128,1792]{1,0:T(8,128)(2,1)S(1)}, bf16[256,640]{1,0:T(8,128)(2,1)}) custom-call(s32[1]{0:T(128)S(6)} %copy.19.refs_0_, bf16[128,1792]{1,0:T(8,128)(2,1)S(1)} %collective-permute-done.5.refs_1_, bf16[128,1792]{1,0:T(8,128)(2,1)S(1)} %collective-permute-done.6.refs_2_, ...), custom_call_target="tpu_custom_call" | custom-call | flops 1358954496 | bytes 1835008 | tf_op jit(solution)/shard_map/pallas_call | solution.py:534
  50.3 0.6 collective-permute-start.8
  50.9 1.5 %collective-permute-start.7 = (bf16[128,1792]{1,0:T(8,128)(2,1)S(1)}, bf16[128,1792]{1,0:T(8,128)(2,1)S(1)}, u32[]{:S(2)}, u32[]{:S(2)}) collective-permute-start(bf16[128,1792]{1,0:T(8,128)(2,1)S(1)} %get-tuple-element.56), channel_id=1, source_target_pairs={{0,8},{8,0},{16,24},{24,16},{1,9},{9,1},{17,25},{25,17},{2,10},{10... | collective-permute-start | bytes 1376264 | tf_op jit(solution)/shard_map/ppermute | solution.py:557
  52.3 7.4 %shard_map.164 = (bf16[128,1792]{1,0:T(8,128)(2,1)}, bf16[128,1792]{1,0:T(8,128)(2,1)}, bf16[128,1792]{1,0:T(8,128)(2,1)}, bf16[128,1792]{1,0:T(8,128)(2,1)}, f32[4,384,128]{2,1,0:T(8,128)}) custom-call(s32[1]{0:T(128)S(6)} %copy.19.refs_0_, bf16[256,640]{1,0:T(8,128)(2,1)} %get-tuple-element.61.refs_1_, bf16[256,640]{1,0:T(8,128)(2,1)} %get-tuple-element.62.refs_2_, ...), custom_call_target="tpu_custom_call" | custom-call | flops 1140850688 | bytes 1835008 | tf_op jit(solution)/shard_map/pallas_call | solution.py:534
  59.7 0.4 collective-permute-start.10
  60.1 1.7 %collective-permute-start.9 = (bf16[128,1792]{1,0:T(8,128)(2,1)}, bf16[128,1792]{1,0:T(8,128)(2,1)S(1)}, u32[]{:S(2)}, u32[]{:S(2)}) collective-permute-start(bf16[128,1792]{1,0:T(8,128)(2,1)} %get-tuple-element.68.refs_4_), channel_id=1, source_target_pairs={{0,8},{8,0},{16,24},{24,16},{1,9},{9,1},{17,25},{25,17},{2,10},{10... | collective-permute-start | bytes 1376264 | tf_op jit(solution)/shard_map/ppermute | solution.py:557
  61.8 4.7 %all-to-all-start.1 = ((bf16[8,8,1792]{2,1,0:T(8,128)(2,1)}), bf16[8,8,1792]{2,1,0:T(8,128)(2,1)S(1)}, u32[]{:S(2)}, u32[]{:S(2)}) async-start(bf16[8,8,1792]{2,1,0:T(8,128)(2,1)} %bitcast.11), calls=%async_computation.1 | async-start | bytes 458752 | tf_op jit(solution)/shard_map/all_to_all | solution.py:676
  66.6 0.0 collective-permute-done.8.refs_3_
  66.6 0.0 collective-permute-done.7.refs_1_
  66.6 1.3 %shard_map.165 = (bf16[128,1792]{1,0:T(8,128)(2,1)S(1)}, bf16[128,1792]{1,0:T(8,128)(2,1)S(1)}) custom-call(bf16[128,1792]{1,0:T(8,128)(2,1)} %get-tuple-element.65.refs_0_, bf16[128,1792]{1,0:T(8,128)(2,1)S(1)} %collective-permute-done.7.refs_1_, bf16[128,1792]{1,0:T(8,128)(2,1)} %get-tuple-element.66.refs_2_, ...), custom_call_target="tpu_custom_call" | custom-call | bytes 1835008 | tf_op jit(solution)/shard_map/pallas_call | solution.py:534
  67.9 0.0 copy-start.2
  67.9 0.6 collective-permute-start.11
  68.5 1.5 %collective-permute-start.12 = (bf16[128,1792]{1,0:T(8,128)(2,1)S(1)}, bf16[128,1792]{1,0:T(8,128)(2,1)S(1)}, u32[]{:S(2)}, u32[]{:S(2)}) collective-permute-start(bf16[128,1792]{1,0:T(8,128)(2,1)S(1)} %get-tuple-element.69.refs_10_), channel_id=1, source_target_pairs={{0,8},{8,0},{16,24},{24,16},{1,9},{9,1},{17,25},{25,17},{2,10},{10... | collective-permute-start | bytes 1376264 | tf_op jit(solution)/shard_map/ppermute | solution.py:557
  69.9 0.0 copy-done.2
  69.9 5.6 %shard_map.166 = (bf16[128,1792]{1,0:T(8,128)(2,1)}, bf16[128,1792]{1,0:T(8,128)(2,1)}, f32[1,273,4,112]{3,2,1,0:T(4,128)}) custom-call(s32[1]{0:T(128)S(6)} %copy.19.refs_0_, f32[4,384,128]{2,1,0:T(8,128)} %get-tuple-element.58.refs_3_.refs_1_, f32[4,384,128]{2,1,0:T(8,128)} %get-tuple-element.52.refs_8_.refs_4_.refs_2_, ...), custom_call_target="tpu_custom_call" | custom-call | flops 570425344 | bytes 1835008 | tf_op jit(solution)/shard_map/pallas_call | solution.py:534
  75.5 0.1 all-to-all-done.1
  75.6 0.0 collective-permute-done.10.refs_5_
  75.6 0.0 collective-permute-done.9.refs_3_
  75.6 2.6 %shard_map.167 = (bf16[16,1792]{1,0:T(8,128)(2,1)}, bf16[16,1792]{1,0:T(8,128)(2,1)}, bf16[16,1792]{1,0:T(8,128)(2,1)}, bf16[16,1792]{1,0:T(8,128)(2,1)}, bf16[1...) custom-call(bf16[64,1792]{1,0:T(8,128)(2,1)S(1)} %bitcast.22, s32[1,32]{1,0:T(1,128)} %bitcast.35, ...), custom_call_target="tpu_custom_call" | custom-call | flops 7340032 | bytes 458752 | tf_op jit(solution)/shard_map/pallas_call | solution.py:534
  78.3 0.0 copy-start.3
  78.3 0.6 collective-permute-start.13
  78.8 1.5 %collective-permute-start.14 = (bf16[16,1792]{1,0:T(8,128)(2,1)}, bf16[16,1792]{1,0:T(8,128)(2,1)S(1)}, u32[]{:S(2)}, u32[]{:S(2)}) collective-permute-start(bf16[16,1792]{1,0:T(8,128)(2,1)} %get-tuple-element.78), channel_id=1, source_target_pairs={{0,16},{8,24},{16,0},{24,8},{1,17},{9,25},{17,1},{25,9},{2,18},{10... | collective-permute-start | bytes 172040 | tf_op jit(solution)/shard_map/ppermute | solution.py:557
  80.4 1.5 %collective-permute-start.15 = (bf16[16,1792]{1,0:T(8,128)(2,1)}, bf16[16,1792]{1,0:T(8,128)(2,1)S(1)}, u32[]{:S(2)}, u32[]{:S(2)}) collective-permute-start(bf16[16,1792]{1,0:T(8,128)(2,1)} %get-tuple-element.79), channel_id=1, source_target_pairs={{0,24},{8,16},{16,8},{24,0},{1,25},{9,17},{17,9},{25,1},{2,26},{10... | collective-permute-start | bytes 172040 | tf_op jit(solution)/shard_map/ppermute | solution.py:557
  81.8 0.0 collective-permute-done.11.refs_1_
  81.8 0.5 collective-permute-done.12.refs_3_
  82.3 2.3 %shard_map.168 = bf16[2,128,1792]{2,1,0:T(8,128)(2,1)} custom-call(bf16[128,1792]{1,0:T(8,128)(2,1)} %get-tuple-element.73.refs_0_, bf16[128,1792]{1,0:T(8,128)(2,1)S(1)} %collective-permute-done.11.refs_1_, bf16[128,1792]{1,0:T(8,128)(2,1)} %get-tuple-element.75.refs_2_, bf16[128,1792]{1,0:T(8,128)(2,1)S(1)} %collective-permute-done.12.refs_3_, ...), custom_call_target="tpu_custom_call" | custom-call | bytes 3670016 | tf_op jit(solution)/shard_map/pallas_call | solution.py:534
  84.6 0.0 collective-permute-done.13
  84.6 0.0 collective-permute-done.14
  84.6 1.1 %collective-permute-done.15 = bf16[16,1792]{1,0:T(8,128)(2,1)S(1)} collective-permute-done((bf16[16,1792]{1,0:T(8,128)(2,1)}, bf16[16,1792]{1,0:T(8,128)(2,1)S(1)}, u32[]{:S(2)}, u32[]{:S(2)}) %collective-permute-start.15) | collective-permute-done | bytes 57376 | tf_op jit(solution)/shard_map/ppermute | solution.py:557
  85.6 0.0 copy-done.3
  85.6 0.6 fusion
Async XLA Ops:
  3.8 9.9 %collective-permute-start.1 = (bf16[16,1792]{1,0:T(8,128)(2,1)}, bf16[16,1792]{1,0:T(8,128)(2,1)S(1)}, u32[]{:S(2)}, u32[]{:S(2)}) collective-permute-start(bf16[16,1792]{1,0:T(8,128)(2,1)} %get-tuple-element.47), channel_id=1, source_target_pairs={{0,8},{8,16},{16,24},{1,9},{9,17},{17,25},{2,10},{10,18},{18,26},{... | collective-permute-start | bytes 172040 | tf_op jit(solution)/shard_map/ppermute | solution.py:725
  8.6 23.9 %collective-permute-start.3 = (bf16[128,1792]{1,0:T(8,128)(2,1)}, bf16[128,1792]{1,0:T(8,128)(2,1)S(1)}, u32[]{:S(2)}, u32[]{:S(2)}) collective-permute-start(bf16[128,1792]{1,0:T(8,128)(2,1)} %get-tuple-element.44.refs_1_), channel_id=1, source_target_pairs={{0,8},{8,0},{16,24},{24,16},{1,9},{9,1},{17,25},{25,17},{2,10},{10... | collective-permute-start | bytes 1376264 | tf_op jit(solution)/shard_map/ppermute | solution.py:557
  10.2 22.3 %collective-permute-start = (bf16[128,1792]{1,0:T(8,128)(2,1)}, bf16[128,1792]{1,0:T(8,128)(2,1)S(1)}, u32[]{:S(2)}, u32[]{:S(2)}) collective-permute-start(bf16[128,1792]{1,0:T(8,128)(2,1)} %get-tuple-element.44.refs_1_), channel_id=1, source_target_pairs={{0,16},{8,24},{16,0},{24,8},{1,17},{9,25},{17,1},{25,9},{2,18},{10... | collective-permute-start | bytes 1376264 | tf_op jit(solution)/shard_map/ppermute | solution.py:557
  14.7 17.9 %collective-permute-start.2 = (bf16[128,1792]{1,0:T(8,128)(2,1)}, bf16[128,1792]{1,0:T(8,128)(2,1)S(1)}, u32[]{:S(2)}, u32[]{:S(2)}) collective-permute-start(bf16[128,1792]{1,0:T(8,128)(2,1)} %shard_map.159.refs_2_), channel_id=1, source_target_pairs={{0,8},{8,0},{16,24},{24,16},{1,9},{9,1},{17,25},{25,17},{2,10},{10... | collective-permute-start | bytes 1376264 | tf_op jit(solution)/shard_map/ppermute | solution.py:557
  17.3 17.6 %collective-permute-start.4 = (bf16[128,1792]{1,0:T(8,128)(2,1)}, bf16[128,1792]{1,0:T(8,128)(2,1)S(1)}, u32[]{:S(2)}, u32[]{:S(2)}) collective-permute-start(bf16[128,1792]{1,0:T(8,128)(2,1)} %shard_map.159.refs_2_), channel_id=1, source_target_pairs={{0,16},{8,24},{16,0},{24,8},{1,17},{9,25},{17,1},{25,9},{2,18},{10... | collective-permute-start | bytes 1376264 | tf_op jit(solution)/shard_map/ppermute | solution.py:557
  17.8 11.0 %all-to-all-start = ((bf16[8,8,640]{2,1,0:T(8,128)(2,1)}), bf16[8,8,640]{2,1,0:T(8,128)(2,1)S(1)}, u32[]{:S(2)}, u32[]{:S(2)}) async-start(bf16[8,8,640]{2,1,0:T(8,128)(2,1)} %bitcast.30), calls=%async_computation | async-start | bytes 163840 | tf_op jit(solution)/shard_map/all_to_all | solution.py:619
  28.8 6.1 %copy-start = (bf16[1792,4,144]{0,2,1:T(8,128)(2,1)S(1)}, bf16[1792,4,144]{0,2,1:T(8,128)(2,1)}, u32[]{:S(2)}) copy-start(bf16[1792,4,144]{0,2,1:T(8,128)(2,1)} %param.20) | copy-start | bytes 6193156
  32.5 12.6 %collective-permute-start.6 = (bf16[128,1792]{1,0:T(8,128)(2,1)S(1)}, bf16[128,1792]{1,0:T(8,128)(2,1)S(1)}, u32[]{:S(2)}, u32[]{:S(2)}) collective-permute-start(bf16[128,1792]{1,0:T(8,128)(2,1)S(1)} %collective-permute-done.2.refs_3_), channel_id=1, source_target_pairs={{0,16},{8,24},{16,0},{24,8},{1,17},{9,25},{17,1},{25,9},{2,18},{10... | collective-permute-start | bytes 1376264 | tf_op jit(solution)/shard_map/ppermute | solution.py:557
  34.1 12.3 %collective-permute-start.5 = (bf16[128,1792]{1,0:T(8,128)(2,1)S(1)}, bf16[128,1792]{1,0:T(8,128)(2,1)S(1)}, u32[]{:S(2)}, u32[]{:S(2)}) collective-permute-start(bf16[128,1792]{1,0:T(8,128)(2,1)S(1)} %collective-permute-done.refs_5_), channel_id=1, source_target_pairs={{0,8},{8,0},{16,24},{24,16},{1,9},{9,1},{17,25},{25,17},{2,10},{10... | collective-permute-start | bytes 1376264 | tf_op jit(solution)/shard_map/ppermute | solution.py:557
  34.9 11.5 %copy-start.1 = (bf16[448,1792]{1,0:T(8,128)(2,1)S(1)}, bf16[448,1792]{1,0:T(8,128)(2,1)}, u32[]{:S(2)}) copy-start(bf16[448,1792]{1,0:T(8,128)(2,1)} %refs_9_.3) | copy-start | bytes 4816900
  50.3 16.3 %collective-permute-start.8 = (bf16[128,1792]{1,0:T(8,128)(2,1)S(1)}, bf16[128,1792]{1,0:T(8,128)(2,1)S(1)}, u32[]{:S(2)}, u32[]{:S(2)}) collective-permute-start(bf16[128,1792]{1,0:T(8,128)(2,1)S(1)} %get-tuple-element.67), channel_id=1, source_target_pairs={{0,16},{8,24},{16,0},{24,8},{1,17},{9,25},{17,1},{25,9},{2,18},{10... | collective-permute-start | bytes 1376264 | tf_op jit(solution)/shard_map/ppermute | solution.py:557
  50.9 15.7 %collective-permute-start.7 = (bf16[128,1792]{1,0:T(8,128)(2,1)S(1)}, bf16[128,1792]{1,0:T(8,128)(2,1)S(1)}, u32[]{:S(2)}, u32[]{:S(2)}) collective-permute-start(bf16[128,1792]{1,0:T(8,128)(2,1)S(1)} %get-tuple-element.56), channel_id=1, source_target_pairs={{0,8},{8,0},{16,24},{24,16},{1,9},{9,1},{17,25},{25,17},{2,10},{10... | collective-permute-start | bytes 1376264 | tf_op jit(solution)/shard_map/ppermute | solution.py:557
  59.7 15.9 %collective-permute-start.10 = (bf16[128,1792]{1,0:T(8,128)(2,1)}, bf16[128,1792]{1,0:T(8,128)(2,1)S(1)}, u32[]{:S(2)}, u32[]{:S(2)}) collective-permute-start(bf16[128,1792]{1,0:T(8,128)(2,1)} %get-tuple-element.72), channel_id=1, source_target_pairs={{0,16},{8,24},{16,0},{24,8},{1,17},{9,25},{17,1},{25,9},{2,18},{10... | collective-permute-start | bytes 1376264 | tf_op jit(solution)/shard_map/ppermute | solution.py:557
  60.1 15.5 %collective-permute-start.9 = (bf16[128,1792]{1,0:T(8,128)(2,1)}, bf16[128,1792]{1,0:T(8,128)(2,1)S(1)}, u32[]{:S(2)}, u32[]{:S(2)}) collective-permute-start(bf16[128,1792]{1,0:T(8,128)(2,1)} %get-tuple-element.68.refs_4_), channel_id=1, source_target_pairs={{0,8},{8,0},{16,24},{24,16},{1,9},{9,1},{17,25},{25,17},{2,10},{10... | collective-permute-start | bytes 1376264 | tf_op jit(solution)/shard_map/ppermute | solution.py:557
  61.8 13.8 %all-to-all-start.1 = ((bf16[8,8,1792]{2,1,0:T(8,128)(2,1)}), bf16[8,8,1792]{2,1,0:T(8,128)(2,1)S(1)}, u32[]{:S(2)}, u32[]{:S(2)}) async-start(bf16[8,8,1792]{2,1,0:T(8,128)(2,1)} %bitcast.11), calls=%async_computation.1 | async-start | bytes 458752 | tf_op jit(solution)/shard_map/all_to_all | solution.py:676
  67.9 2.1 %copy-start.2 = (bf16[128,1792]{1,0:T(8,128)(2,1)}, bf16[128,1792]{1,0:T(8,128)(2,1)S(1)}, u32[]{:S(2)}) copy-start(bf16[128,1792]{1,0:T(8,128)(2,1)S(1)} %get-tuple-element.69.refs_10_) | copy-start | bytes 1376260
  67.9 13.9 %collective-permute-start.11 = (bf16[128,1792]{1,0:T(8,128)(2,1)S(1)}, bf16[128,1792]{1,0:T(8,128)(2,1)S(1)}, u32[]{:S(2)}, u32[]{:S(2)}) collective-permute-start(bf16[128,1792]{1,0:T(8,128)(2,1)S(1)} %get-tuple-element.74), channel_id=1, source_target_pairs={{0,16},{8,24},{16,0},{24,8},{1,17},{9,25},{17,1},{25,9},{2,18},{10... | collective-permute-start | bytes 1376264 | tf_op jit(solution)/shard_map/ppermute | solution.py:557
  68.5 13.8 %collective-permute-start.12 = (bf16[128,1792]{1,0:T(8,128)(2,1)S(1)}, bf16[128,1792]{1,0:T(8,128)(2,1)S(1)}, u32[]{:S(2)}, u32[]{:S(2)}) collective-permute-start(bf16[128,1792]{1,0:T(8,128)(2,1)S(1)} %get-tuple-element.69.refs_10_), channel_id=1, source_target_pairs={{0,8},{8,0},{16,24},{24,16},{1,9},{9,1},{17,25},{25,17},{2,10},{10... | collective-permute-start | bytes 1376264 | tf_op jit(solution)/shard_map/ppermute | solution.py:557
  78.3 7.4 %copy-start.3 = (bf16[16,1792]{1,0:T(8,128)(2,1)S(1)}, bf16[16,1792]{1,0:T(8,128)(2,1)}, u32[]{:S(2)}) copy-start(bf16[16,1792]{1,0:T(8,128)(2,1)} %get-tuple-element.80.refs_4_) | copy-start | bytes 172036
  78.3 6.3 %collective-permute-start.13 = (bf16[16,1792]{1,0:T(8,128)(2,1)}, bf16[16,1792]{1,0:T(8,128)(2,1)S(1)}, u32[]{:S(2)}, u32[]{:S(2)}) collective-permute-start(bf16[16,1792]{1,0:T(8,128)(2,1)} %get-tuple-element.77), channel_id=1, source_target_pairs={{0,8},{8,0},{16,24},{24,16},{1,9},{9,1},{17,25},{25,17},{2,10},{10... | collective-permute-start | bytes 172040 | tf_op jit(solution)/shard_map/ppermute | solution.py:557
  78.8 5.8 %collective-permute-start.14 = (bf16[16,1792]{1,0:T(8,128)(2,1)}, bf16[16,1792]{1,0:T(8,128)(2,1)S(1)}, u32[]{:S(2)}, u32[]{:S(2)}) collective-permute-start(bf16[16,1792]{1,0:T(8,128)(2,1)} %get-tuple-element.78), channel_id=1, source_target_pairs={{0,16},{8,24},{16,0},{24,8},{1,17},{9,25},{17,1},{25,9},{2,18},{10... | collective-permute-start | bytes 172040 | tf_op jit(solution)/shard_map/ppermute | solution.py:557
  80.4 5.3 %collective-permute-start.15 = (bf16[16,1792]{1,0:T(8,128)(2,1)}, bf16[16,1792]{1,0:T(8,128)(2,1)S(1)}, u32[]{:S(2)}, u32[]{:S(2)}) collective-permute-start(bf16[16,1792]{1,0:T(8,128)(2,1)} %get-tuple-element.79), channel_id=1, source_target_pairs={{0,24},{8,16},{16,8},{24,0},{1,25},{9,17},{17,9},{25,1},{2,26},{10... | collective-permute-start | bytes 172040 | tf_op jit(solution)/shard_map/ppermute | solution.py:557
